TPU v7x, 128 devices: a whole 4x4x4 slice. The times are simulated.
128 devices in a mesh: dp: 16 (over x, z), tx: 2 (over core), ty: 4 (over y).
Axes of the slice: x: 4, y: 4, z: 4, core: 2. Of those that a mesh axis runs over, the one named last changes fastest.
Arguments:
- latent: bfloat16 [16, 64, 64, 4], P('dp', 'tx', 'ty'), may hold values from -6 to 6
- condition: bfloat16 [16, 1152], P(None, ('dp', 'tx', 'ty')), may hold values from -6 to 6
- routed_ids: int32 [16, 512], P('dp'), may hold values from 0 to 1023, as said below
- embed_weight: bfloat16 [16, 1152], P(None, ('dp', 'tx', 'ty')), may hold values from -1.5 to 1.5
- embed_bias: bfloat16 [1152], P(('dp', 'tx', 'ty')), may hold values from -1.5 to 1.5
- modulation_weight: bfloat16 [2, 1152, 6912], P(None, ('dp', 'tx', 'ty')), may hold values from -0.1875 to 0.1875
- modulation_bias: bfloat16 [2, 6912], P(None, ('dp', 'tx', 'ty')), may hold values from -1.5 to 1.5
- attention_weight: bfloat16 [2, 1152, 3, 1152], P(None, ('dp', 'tx', 'ty')), may hold values from -0.1875 to 0.1875
- attention_bias: bfloat16 [2, 2304], P(None, ('dp', 'tx', 'ty')), may hold values from -1.5 to 1.5
- merge_weight: bfloat16 [2, 1152, 1152], P(None, ('dp', 'tx', 'ty')), may hold values from -0.75 to 0.75
- merge_bias: bfloat16 [2, 1152], P(None, ('dp', 'tx', 'ty')), may hold values from -1.5 to 1.5
- expand_weight: bfloat16 [2, 1152, 4608], P(None, ('dp', 'tx', 'ty')), may hold values from -0.1875 to 0.1875
- expand_bias: bfloat16 [2, 4608], P(None, ('dp', 'tx', 'ty')), may hold values from -1.5 to 1.5
- reduce_weight: bfloat16 [2, 1152, 4608], P(None, ('dp', 'tx', 'ty')), may hold values from -0.09375 to 0.09375
- reduce_bias: bfloat16 [2, 1152], P(None, ('dp', 'tx', 'ty')), may hold values from -1.5 to 1.5
- final_modulation: bfloat16 [1152, 2304], P(('dp', 'tx', 'ty')), may hold values from -0.1875 to 0.1875
- final_offsets: bfloat16 [2304], P(('dp', 'tx', 'ty')), may hold values from -1.5 to 1.5
- unpatch_weight: bfloat16 [1152, 32], P(('dp', 'tx', 'ty')), may hold values from -0.1875 to 0.1875
- unpatch_bias: bfloat16 [32], replicated, may hold values from -1.5 to 1.5
- pred_cotangent: bfloat16 [16, 64, 64, 8], P('dp', 'tx', 'ty'), may hold values from -6 to 6
Outputs:
- predicted: bfloat16 [16, 64, 64, 8], P('dp', 'tx', 'ty')
- latent_grad: float32 [16, 64, 64, 4], P('dp', 'tx', 'ty')
- condition_grad: float32 [16, 1152], P(None, ('dp', 'tx', 'ty'))
- embed_weight_grad: float32 [16, 1152], P(None, ('dp', 'tx', 'ty'))
- embed_bias_grad: float32 [1152], P(('dp', 'tx', 'ty'))
- modulation_weight_grad: float32 [2, 1152, 6912], P(None, ('dp', 'tx', 'ty'))
- modulation_bias_grad: float32 [2, 6912], P(None, ('dp', 'tx', 'ty'))
- attention_weight_grad: float32 [2, 1152, 3, 1152], P(None, ('dp', 'tx', 'ty'))
- attention_bias_grad: float32 [2, 2304], P(None, ('dp', 'tx', 'ty'))
- merge_weight_grad: float32 [2, 1152, 1152], P(None, ('dp', 'tx', 'ty'))
- merge_bias_grad: float32 [2, 1152], P(None, ('dp', 'tx', 'ty'))
- expand_weight_grad: float32 [2, 1152, 4608], P(None, ('dp', 'tx', 'ty'))
- expand_bias_grad: float32 [2, 4608], P(None, ('dp', 'tx', 'ty'))
- reduce_weight_grad: float32 [2, 1152, 4608], P(None, ('dp', 'tx', 'ty'))
- reduce_bias_grad: float32 [2, 1152], P(None, ('dp', 'tx', 'ty'))
- final_modulation_grad: float32 [1152, 2304], P(('dp', 'tx', 'ty'))
- final_offsets_grad: float32 [2304], P(('dp', 'tx', 'ty'))
- unpatch_weight_grad: float32 [1152, 32], P(('dp', 'tx', 'ty'))
- unpatch_bias_grad: float32 [32], replicated
Inputs may be any that keep to these rules, and one draw needn't show every extreme that they name: `routed_ids`: each row lists 512 different token numbers of one image in rising order, token r * 32 + c sitting at patch row r and column c; of the 128 tokens of one device's tile (patch rows split over tx, columns over ty) at most 112 and at least 16 are listed, and in every image some tile holds exactly 112.
All inputs are finite; a program needn't handle non-finite values.
Results may differ from a plain program's by a relative error of at most 0.024.
Values may be sent and summed in bfloat16 or wider, within the bound.
A program may use at most 192 MiB of HBM per device.

v0:
```python
import math

import jax
import jax.numpy as jnp
from jax import lax
from jax.sharding import Mesh
from jax.sharding import PartitionSpec as P

D = 1152
HEADS = 16
FF = 4608
DP = ("dp_0", "dp_1")
DP_TX_TY = ("dp_0", "dp_1", "tx", "ty")


def from_everyone(array, axis):
    copies = jnp.broadcast_to(array, (lax.axis_size(axis), *array.shape))
    return lax.all_to_all(copies, axis, split_axis=0, concat_axis=0, tiled=True)


def in_order(parts, dim):
    parts = jnp.moveaxis(parts, 0, dim)
    shape = parts.shape
    return parts.reshape(*shape[:dim], shape[dim] * shape[dim + 1], *shape[dim + 2 :])


def gather_directly(array, axis, dim):
    parts = from_everyone(array, axis)
    return in_order(parts, dim)


def cut_along(array, dim, peers):
    before, after = (array.shape[:dim], array.shape[dim + 1 :])
    return jnp.moveaxis(array.reshape(*before, peers, -1, *after), dim, 0)


def sum_at_owner(array, axis, dim):
    peers = lax.axis_size(axis)
    parts = lax.all_to_all(cut_along(array, dim, peers), axis, 0, 0, tiled=True)
    return jnp.sum(parts.astype(jnp.float32), axis=0)


def in_one_piece(arrays, axis, split_dim, concat_dim, along):
    both = jnp.concatenate(arrays, axis=along)
    result, at, gathered = (
        lax.all_to_all(both, axis, split_axis=split_dim, concat_axis=concat_dim, tiled=True),
        0,
        [],
    )
    for a in arrays:
        gathered.append(lax.slice_in_dim(result, at, at + a.shape[along], axis=along))
        at += a.shape[along]
    return tuple(gathered)


def side_by_side(arrays, axis, dim, along):
    columns = [a.reshape(*a.shape[:along], -1) for a in arrays]
    both = jnp.concatenate(columns, axis=along)
    result, at, gathered = (lax.all_gather(both, axis, axis=dim, tiled=True), 0, [])
    for a, column in zip(arrays, columns):
        share = result[..., at : at + column.shape[along]]
        gathered.append(share.reshape(*share.shape[:along], *a.shape[along:]))
        at += column.shape[along]
    return tuple(gathered)


def sent_together(arrays, axis, dim, along):
    columns = [a.reshape(*a.shape[:along], -1) for a in arrays]
    both = jnp.concatenate(columns, axis=along)
    result, at, gathered = (lax.psum_scatter(both, axis, scatter_dimension=dim, tiled=True), 0, [])
    for a, column in zip(arrays, columns):
        share = result[..., at : at + column.shape[along]]
        gathered.append(share.reshape(*share.shape[:along], *a.shape[along:]))
        at += column.shape[along]
    return tuple(gathered)


def whole_of(array, axes, dim):
    far, near = axes
    first = from_everyone(array, far)
    parts = jnp.swapaxes(from_everyone(first, near), 0, 1)
    return in_order(parts.reshape(-1, *array.shape), dim)


def in_one_piece_2(arrays, axis, dim, along):
    both = jnp.concatenate(arrays, axis=along)
    result, at, gathered = (whole_of(both, axis, dim), 0, [])
    for a in arrays:
        gathered.append(lax.slice_in_dim(result, at, at + a.shape[along], axis=along))
        at += a.shape[along]
    return tuple(gathered)


def side_by_side_2(arrays, axis, dim, along):
    widths = [math.prod(a.shape[along:]) for a in arrays]
    both = jnp.concatenate(
        [a.reshape(*a.shape[:along], w) for a, w in zip(arrays, widths)], axis=along
    )
    result = whole_of(both, axis, dim)
    parts = jnp.split(result, [sum(widths[:k]) for k in range(1, len(widths))], axis=along)
    return tuple(
        (b.reshape(*result.shape[:along], *a.shape[along:]) for a, b in zip(arrays, parts))
    )


def filled_up(lines, peers):
    spare = -len(lines) % peers
    return jnp.pad(lines, [(0, spare)] + [(0, 0)] * (lines.ndim - 1))


def summed_on_arrival(array, axis, dim):
    peers = lax.axis_size(axis)
    parts = lax.all_to_all(cut_along(array, dim, peers), axis, 0, 0, tiled=True)
    return jnp.sum(parts, axis=0)


def sum_in_two_steps(array, axes, dim):
    far, near = axes
    own = summed_on_arrival(cut_along(array, dim, lax.axis_size(far)), near, dim + 1)
    return jnp.sum(lax.all_to_all(own, far, 0, 0, tiled=True), axis=0)


def total_of(array, axes):
    padded = filled_up(array, lax.axis_size(axes[0]) * lax.axis_size(axes[1]))
    whole = whole_of(sum_in_two_steps(padded, axes, 0), axes, 0)
    return lax.slice_in_dim(whole, 0, len(array)).reshape(array.shape)


def together(arrays, axis):
    ravelled, at, gathered = (jnp.concatenate([a.reshape(-1) for a in arrays]), 0, [])
    subtotal = total_of(ravelled, axis)
    for a in arrays:
        gathered.append(subtotal[at : at + a.size].reshape(a.shape))
        at += a.size
    return tuple(gathered)


def side_by_side_3(arrays, axis, dim, along):
    columns = [a.reshape(*a.shape[:along], -1) for a in arrays]
    both = jnp.concatenate(columns, axis=along)
    result, at, gathered = (sum_in_two_steps(both, axis, dim), 0, [])
    for a, column in zip(arrays, columns):
        share = result[..., at : at + column.shape[along]]
        gathered.append(share.reshape(*share.shape[:along], *a.shape[along:]))
        at += column.shape[along]
    return tuple(gathered)


def layer_stats(value_rows):
    centered = value_rows - jnp.mean(value_rows, axis=-1, keepdims=True)
    inv_std = lax.rsqrt(jnp.mean(centered * centered, axis=-1, keepdims=True) + 1e-06)
    return (centered * inv_std, inv_std)


def layer_back(upstream, normed, inv_std):
    return inv_std * (
        upstream
        - jnp.mean(upstream, axis=-1, keepdims=True)
        - normed * jnp.mean(upstream * normed, axis=-1, keepdims=True)
    )


def smooth_gate(value_rows):
    return jax.nn.gelu(value_rows, approximate=True)


def sincos_table(row_pos, col_pos, width):
    quarter = width // 4
    freqs = jnp.power(10000.0, -jnp.arange(quarter, dtype=jnp.float32) / quarter)
    row_angle = row_pos[:, None] * freqs[None, :]
    col_angle = col_pos[:, None] * freqs[None, :]
    row_embed = jnp.concatenate([jnp.sin(row_angle), jnp.cos(row_angle)], axis=-1)
    col_embed = jnp.concatenate([jnp.sin(col_angle), jnp.cos(col_angle)], axis=-1)
    row_full = jnp.broadcast_to(
        row_embed[:, None, :], (row_pos.shape[0], col_pos.shape[0], width // 2)
    )
    col_full = jnp.broadcast_to(
        col_embed[None, :, :], (row_pos.shape[0], col_pos.shape[0], width // 2)
    )
    return jnp.concatenate([row_full, col_full], axis=-1).reshape(
        row_pos.shape[0] * col_pos.shape[0], width
    )


def to_patches(pixels):
    count, height, breadth, depth = pixels.shape
    shaped = pixels.reshape(count, height // 2, 2, breadth // 2, 2, depth)
    return shaped.transpose(0, 1, 3, 2, 4, 5).reshape(
        count, height // 2 * (breadth // 2), 4 * depth
    )


def from_patches(token_rows, tile_rows, tile_cols):
    count = token_rows.shape[0]
    depth = token_rows.shape[2] // 4
    shaped = token_rows.reshape(count, tile_rows, tile_cols, 2, 2, depth)
    return shaped.transpose(0, 1, 3, 2, 4, 5).reshape(count, 2 * tile_rows, 2 * tile_cols, depth)


def split_mod(mod, width):
    return [mod[:, None, piece * width : (piece + 1) * width] for piece in range(6)]


def compact_plan(routed, capacity):
    count, tokens = routed.shape
    flags = routed > 0
    position = jnp.cumsum(flags.astype(jnp.int32), axis=1) - 1
    slots = jnp.where(flags, position, capacity)
    batch_index = jnp.broadcast_to(jnp.arange(count, dtype=jnp.int32)[:, None], (count, tokens))
    token_ids = jnp.arange(tokens, dtype=jnp.int32)[None, :]
    owner = (
        jnp.zeros((count, capacity), jnp.int32).at[batch_index, slots].set(token_ids, mode="drop")
    )
    filled = jnp.sum(flags.astype(jnp.int32), axis=1, keepdims=True)
    valid = (jnp.arange(capacity, dtype=jnp.int32)[None, :] < filled).astype(jnp.float32)
    return (jnp.where(flags, position, 0), owner, valid)


def pick_rows(value_rows, index):
    return jax.vmap(lambda table, where: jnp.take(table, where, axis=0))(value_rows, index)


def score_block(query, keys, key_marks, heads, scale):
    count, rows, width = query.shape
    size = width // heads
    q_heads = query.reshape(count, rows, heads, size)
    k_heads = keys.reshape(count, keys.shape[1], heads, size)
    scores = (
        jnp.einsum("bqhe,bkhe->bhqk", q_heads, k_heads, preferred_element_type=jnp.float32) * scale
    )
    return jnp.where(key_marks[:, None, None, :] > 0, scores, -1e30)


def attend(query, keys, vals, key_marks, heads, scale):
    count, rows, width = query.shape
    size = width // heads
    scores = score_block(query, keys, key_marks, heads, scale)
    highest = jnp.max(scores, axis=-1, keepdims=True)
    shifted = jnp.exp(scores - highest)
    summed = jnp.sum(shifted, axis=-1, keepdims=True)
    probs16 = (shifted / summed).astype(jnp.bfloat16)
    log_sum = highest + jnp.log(summed)
    v_heads = vals.reshape(count, vals.shape[1], heads, size)
    attended = jnp.einsum("bhqk,bkhe->bqhe", probs16, v_heads, preferred_element_type=jnp.float32)
    return (attended.reshape(count, rows, width).astype(jnp.bfloat16), log_sum)


def attend_back(query, keys, vals, key_marks, log_sum, attended_grad16, heads, scale):
    count, rows, width = query.shape
    size = width // heads
    key_count = keys.shape[1]
    scores = score_block(query, keys, key_marks, heads, scale)
    probs = jnp.exp(scores - log_sum)
    probs16 = probs.astype(jnp.bfloat16)
    grad_heads = attended_grad16.reshape(count, rows, heads, size)
    v_heads = vals.reshape(count, key_count, heads, size)
    k_heads = keys.reshape(count, key_count, heads, size)
    q_heads = query.reshape(count, rows, heads, size)
    grad_probs = jnp.einsum(
        "bqhe,bkhe->bhqk", grad_heads, v_heads, preferred_element_type=jnp.float32
    )
    grad_values = jnp.einsum(
        "bhqk,bqhe->bkhe", probs16, grad_heads, preferred_element_type=jnp.float32
    )
    weighted = jnp.sum(probs * grad_probs, axis=-1, keepdims=True)
    score_grad16 = (probs * (grad_probs - weighted)).astype(jnp.bfloat16)
    grad_query = (
        jnp.einsum("bhqk,bkhe->bqhe", score_grad16, k_heads, preferred_element_type=jnp.float32)
        * scale
    )
    grad_keys = (
        jnp.einsum("bhqk,bqhe->bkhe", score_grad16, q_heads, preferred_element_type=jnp.float32)
        * scale
    )
    return (
        grad_query.reshape(count, rows, width),
        grad_keys.reshape(count, key_count, width),
        grad_values.reshape(count, key_count, width),
    )


def gather_image(rows16):
    return gather_directly(rows16, ("tx", "ty"), 1)


def sum_image(partial_value):
    return sum_at_owner(partial_value.astype(jnp.bfloat16), ("tx", "ty"), 1)


def spread_forward(value_rows, mod, params, biases, marks_all, scale):
    attn_p, merge_p, expand_p, reduce_p = params
    attn_b, merge_b, expand_b, reduce_b = biases
    width = value_rows.shape[2]
    head_width = attn_p.shape[2]
    hidden_width = expand_p.shape[2]
    heads = head_width // (D // HEADS)
    group = lax.axis_index(("tx", "ty"))
    shift1, scale1, gate1, shift2, scale2, gate2 = split_mod(mod, width)
    normed1, inv_one = layer_stats(value_rows)
    input16 = (normed1 * (1.0 + scale1) + shift1).astype(jnp.bfloat16)
    input_all = gather_image(input16)
    joined = jnp.einsum("btd,dke->btke", input_all, attn_p, preferred_element_type=jnp.float32)
    q_bias = lax.dynamic_slice_in_dim(attn_b, group * head_width, head_width).astype(jnp.float32)
    v_bias = lax.dynamic_slice_in_dim(attn_b, width + group * head_width, head_width).astype(
        jnp.float32
    )
    query = (joined[:, :, 0] + q_bias).astype(jnp.bfloat16)
    keys = joined[:, :, 1].astype(jnp.bfloat16)
    vals = (joined[:, :, 2] + v_bias).astype(jnp.bfloat16)
    attended, log_sum = attend(query, keys, vals, marks_all, heads, scale)
    branch = sum_image(
        jnp.einsum("bth,dh->btd", attended, merge_p[:, 0, :], preferred_element_type=jnp.float32)
    )
    branch = branch + merge_b.astype(jnp.float32)
    middle = value_rows + gate1 * branch
    normed2, inv_two = layer_stats(middle)
    second16 = (normed2 * (1.0 + scale2) + shift2).astype(jnp.bfloat16)
    second_all = gather_image(second16)
    e_bias = lax.dynamic_slice_in_dim(expand_b, group * hidden_width, hidden_width).astype(
        jnp.float32
    )
    pre = (
        jnp.einsum("btd,df->btf", second_all, expand_p[:, 0, :], preferred_element_type=jnp.float32)
        + e_bias
    )
    hidden16 = smooth_gate(pre).astype(jnp.bfloat16)
    mlp = sum_image(
        jnp.einsum("btf,df->btd", hidden16, reduce_p[:, 0, :], preferred_element_type=jnp.float32)
    )
    mlp = mlp + reduce_b.astype(jnp.float32)
    output = middle + gate2 * mlp
    saved = (
        normed1,
        inv_one,
        input_all,
        query,
        keys,
        vals,
        marks_all,
        log_sum,
        attended,
        branch,
        normed2,
        inv_two,
        second_all,
        pre,
        hidden16,
        mlp,
    )
    return (output, saved)


def spread_backward(upstream, saved, mod, params, marks, scale):
    attn_p, merge_p, expand_p, reduce_p = params
    (
        normed1,
        inv_one,
        input_all,
        query,
        keys,
        vals,
        marks_all,
        log_sum,
        attended,
        branch,
        normed2,
        inv_two,
        second_all,
        pre,
        hidden16,
        mlp,
    ) = saved
    width = upstream.shape[2]
    head_width = attn_p.shape[2]
    hidden_width = expand_p.shape[2]
    heads = head_width // (D // HEADS)
    group = lax.axis_index(("tx", "ty"))
    shift1, scale1, gate1, shift2, scale2, gate2 = split_mod(mod, width)
    grad_out = upstream * marks[:, :, None]
    grad_gate2 = jnp.sum(grad_out * mlp, axis=1)
    mlp_grad16 = (grad_out * gate2).astype(jnp.bfloat16)
    grad_reduce_b = jnp.sum(mlp_grad16.astype(jnp.float32), axis=(0, 1))
    mlp_grad_all = gather_image(mlp_grad16)
    grad_reduce_p = jnp.einsum(
        "btd,btf->df", mlp_grad_all, hidden16, preferred_element_type=jnp.float32
    )[:, None, :]
    grad_hidden = jnp.einsum(
        "btd,df->btf", mlp_grad_all, reduce_p[:, 0, :], preferred_element_type=jnp.float32
    )
    gate_value, gate_pull = jax.vjp(smooth_gate, pre)
    pre_grad16 = gate_pull(grad_hidden)[0].astype(jnp.bfloat16)
    grad_expand_p = jnp.einsum(
        "btd,btf->df", second_all, pre_grad16, preferred_element_type=jnp.float32
    )[:, None, :]
    grad_expand_b = lax.dynamic_update_slice_in_dim(
        jnp.zeros((FF,), jnp.float32),
        jnp.sum(pre_grad16.astype(jnp.float32), axis=(0, 1)),
        group * hidden_width,
        0,
    )
    grad_second = sum_image(
        jnp.einsum("btf,df->btd", pre_grad16, expand_p[:, 0, :], preferred_element_type=jnp.float32)
    )
    grad_shift2 = jnp.sum(grad_second, axis=1)
    grad_scale2 = jnp.sum(grad_second * normed2, axis=1)
    grad_middle = grad_out + layer_back(grad_second * (1.0 + scale2), normed2, inv_two)
    grad_gate1 = jnp.sum(grad_middle * branch, axis=1)
    branch_grad16 = (grad_middle * gate1).astype(jnp.bfloat16)
    grad_merge_b = jnp.sum(branch_grad16.astype(jnp.float32), axis=(0, 1))
    branch_grad_all = gather_image(branch_grad16)
    grad_merge_p = jnp.einsum(
        "btd,bth->dh", branch_grad_all, attended, preferred_element_type=jnp.float32
    )[:, None, :]
    attended_grad16 = jnp.einsum(
        "btd,dh->bth", branch_grad_all, merge_p[:, 0, :], preferred_element_type=jnp.float32
    ).astype(jnp.bfloat16)
    grad_query, grad_keys, grad_values = attend_back(
        query, keys, vals, marks_all, log_sum, attended_grad16, heads, scale
    )
    joined_grad16 = jnp.stack([grad_query, grad_keys, grad_values], axis=2).astype(jnp.bfloat16)
    grad_attn_p = jnp.einsum(
        "btd,btke->dke", input_all, joined_grad16, preferred_element_type=jnp.float32
    )
    bias_zero = jnp.zeros((2 * width,), jnp.float32)
    grad_attn_b = lax.dynamic_update_slice_in_dim(
        bias_zero,
        jnp.sum(joined_grad16[:, :, 0].astype(jnp.float32), axis=(0, 1)),
        group * head_width,
        0,
    )
    grad_attn_b = lax.dynamic_update_slice_in_dim(
        grad_attn_b,
        jnp.sum(joined_grad16[:, :, 2].astype(jnp.float32), axis=(0, 1)),
        width + group * head_width,
        0,
    )
    grad_input = sum_image(
        jnp.einsum("btke,dke->btd", joined_grad16, attn_p, preferred_element_type=jnp.float32)
    )
    grad_shift1 = jnp.sum(grad_input, axis=1)
    grad_scale1 = jnp.sum(grad_input * normed1, axis=1)
    grad_values_in = grad_middle + layer_back(grad_input * (1.0 + scale1), normed1, inv_one)
    grad_mod = jnp.concatenate(
        [grad_shift1, grad_scale1, grad_gate1, grad_shift2, grad_scale2, grad_gate2], axis=-1
    )
    return (
        grad_values_in,
        grad_mod,
        (grad_attn_p, grad_merge_p, grad_expand_p, grad_reduce_p),
        (grad_attn_b, grad_merge_b, grad_expand_b, grad_reduce_b),
    )


def fetch_columns(attention_weight, merge_weight, expand_weight, reduce_weight, layer_params):
    moved = (
        *in_one_piece(
            (attention_weight[layer_params], merge_weight[layer_params][:, None, :]),
            ("tx", "ty"),
            2,
            0,
            1,
        ),
        *in_one_piece(
            (expand_weight[layer_params][:, None, :], reduce_weight[layer_params][:, None, :]),
            ("tx", "ty"),
            2,
            0,
            1,
        ),
    )
    return side_by_side((moved[0], moved[1], moved[2], moved[3]), DP, 0, 1)


def return_columns(grads):
    summed = tuple(
        (
            part.astype(jnp.float32)
            for part in sent_together(
                (
                    grads[0].astype(jnp.bfloat16),
                    grads[1].astype(jnp.bfloat16),
                    grads[2].astype(jnp.bfloat16),
                    grads[3].astype(jnp.bfloat16),
                ),
                DP,
                0,
                1,
            )
        )
    )
    back = (
        *tuple(
            (
                part.astype(jnp.float32)
                for part in in_one_piece(
                    (summed[0].astype(jnp.bfloat16), summed[1].astype(jnp.bfloat16)),
                    ("tx", "ty"),
                    0,
                    2,
                    1,
                )
            )
        ),
        *tuple(
            (
                part.astype(jnp.float32)
                for part in in_one_piece(
                    (summed[2].astype(jnp.bfloat16), summed[3].astype(jnp.bfloat16)),
                    ("tx", "ty"),
                    0,
                    2,
                    1,
                )
            )
        ),
    )
    return (back[0], back[1][:, 0, :], back[2][:, 0, :], back[3][:, 0, :])


def shards(
    latent,
    condition,
    routed_ids,
    embed_weight,
    embed_bias,
    modulation_weight,
    modulation_bias,
    attention_weight,
    attention_bias,
    merge_weight,
    merge_bias,
    expand_weight,
    expand_bias,
    reduce_weight,
    reduce_bias,
    final_modulation,
    final_offsets,
    unpatch_weight,
    unpatch_bias,
    pred_cotangent,
):
    count = latent.shape[0]
    tile_rows = latent.shape[1] // 2
    tile_cols = latent.shape[2] // 2
    tile_tokens = tile_rows * tile_cols
    rows_tiles = lax.axis_size("tx")
    cols_tiles = lax.axis_size("ty")
    tiles = rows_tiles * cols_tiles
    grid_side = tile_rows * rows_tiles
    row_index = lax.axis_index("tx") * tile_rows + jnp.arange(tile_rows, dtype=jnp.int32)
    col_index = lax.axis_index("ty") * tile_cols + jnp.arange(tile_cols, dtype=jnp.int32)
    token_index = (row_index[:, None] * grid_side + col_index[None, :]).reshape(tile_tokens)
    routed = jnp.sum(
        (routed_ids[:, :, None] == token_index[None, None, :]).astype(jnp.float32), axis=1
    )
    capacity = 7 * tile_tokens // 8
    id_tiles = (
        routed_ids // grid_side // tile_rows * cols_tiles + routed_ids % grid_side // tile_cols
    )
    tile_loads = jnp.sum(
        (id_tiles[:, :, None] == jnp.arange(tiles, dtype=jnp.int32)[None, None, :]).astype(
            jnp.int32
        ),
        axis=1,
    )
    routed_marks = jnp.arange(capacity, dtype=jnp.int32)[None, None, :] < tile_loads[:, :, None]
    routed_marks = routed_marks.astype(jnp.float32).reshape(count, tiles * capacity)
    everyone = jnp.ones((count, tile_tokens), jnp.float32)
    everyone_all = jnp.ones((count, tiles * tile_tokens), jnp.float32)
    position, owner, valid = compact_plan(routed, capacity)
    width = D
    scale = (D // HEADS) ** (-0.5)
    whole_index = lax.axis_index(DP_TX_TY)
    image_start = lax.axis_index(DP) * count
    small = (
        *in_one_piece_2((condition, embed_weight), (("dp_0", "dp_1"), ("tx", "ty")), 1, 0),
        *side_by_side_2((embed_bias, unpatch_weight), (("dp_0", "dp_1"), ("tx", "ty")), 0, 1),
        whole_of(modulation_bias, (("dp_0", "dp_1"), ("tx", "ty")), 1),
        whole_of(attention_bias, (("dp_0", "dp_1"), ("tx", "ty")), 1),
        whole_of(merge_bias, (("dp_0", "dp_1"), ("tx", "ty")), 1),
        whole_of(expand_bias, (("dp_0", "dp_1"), ("tx", "ty")), 1),
        whole_of(reduce_bias, (("dp_0", "dp_1"), ("tx", "ty")), 1),
        whole_of(final_offsets, (("dp_0", "dp_1"), ("tx", "ty")), 0),
    )
    cond_all, embed_w, embed_b, unpatch_w, mod_b, attn_b, merge_b, expand_b, reduce_b, final_b = (
        small
    )
    cond16 = jax.nn.silu(cond_all.astype(jnp.float32)).astype(jnp.bfloat16)
    local_rows = modulation_weight.shape[1]
    cond_rows = lax.dynamic_slice_in_dim(cond16, whole_index * local_rows, local_rows, 1)
    mod_parts = together(
        (
            jnp.dot(cond_rows, modulation_weight[0], preferred_element_type=jnp.float32),
            jnp.dot(cond_rows, modulation_weight[1], preferred_element_type=jnp.float32),
            jnp.dot(cond_rows, final_modulation, preferred_element_type=jnp.float32),
        ),
        (("dp_0", "dp_1"), ("tx", "ty")),
    )
    mod_one = lax.dynamic_slice_in_dim(
        mod_parts[0] + mod_b[0].astype(jnp.float32), image_start, count, 0
    )
    mod_two = lax.dynamic_slice_in_dim(
        mod_parts[1] + mod_b[1].astype(jnp.float32), image_start, count, 0
    )
    head_mod = lax.dynamic_slice_in_dim(
        mod_parts[2] + final_b.astype(jnp.float32), image_start, count, 0
    )
    placed = sincos_table(row_index.astype(jnp.float32), col_index.astype(jnp.float32), width)
    patches = to_patches(latent)
    initial_tokens = (
        jnp.einsum("btp,pd->btd", patches, embed_w, preferred_element_type=jnp.float32)
        + embed_b.astype(jnp.float32)
        + placed[None, :, :]
    )
    first_params = fetch_columns(attention_weight, merge_weight, expand_weight, reduce_weight, 0)
    second_params = fetch_columns(attention_weight, merge_weight, expand_weight, reduce_weight, 1)
    first_biases = (attn_b[0], merge_b[0], expand_b[0], reduce_b[0])
    second_biases = (attn_b[1], merge_b[1], expand_b[1], reduce_b[1])
    middle_one, saved_one = spread_forward(
        initial_tokens, mod_one, first_params, first_biases, everyone_all, scale
    )
    selected_rows = pick_rows(middle_one, owner)
    middle_two, saved_two = spread_forward(
        selected_rows, mod_two, second_params, second_biases, routed_marks, scale
    )
    keep_mask = routed[:, :, None] > 0
    ended = jnp.where(keep_mask, pick_rows(middle_two, position), middle_one)
    head_shift = head_mod[:, None, :width]
    head_scale = head_mod[:, None, width:]
    normed_end, inv_end = layer_stats(ended)
    final16 = (normed_end * (1.0 + head_scale) + head_shift).astype(jnp.bfloat16)
    outputs = jnp.einsum(
        "btd,do->bto", final16, unpatch_w, preferred_element_type=jnp.float32
    ) + unpatch_bias.astype(jnp.float32)
    predicted = from_patches(outputs.astype(jnp.bfloat16), tile_rows, tile_cols)
    cotangent = to_patches(pred_cotangent)
    grad_unpatch_w = jnp.einsum(
        "btd,bto->do", final16, cotangent, preferred_element_type=jnp.float32
    )
    grad_unpatch_b = jnp.sum(cotangent.astype(jnp.float32), axis=(0, 1))
    grad_final = jnp.einsum("bto,do->btd", cotangent, unpatch_w, preferred_element_type=jnp.float32)
    head_grad_mod = jnp.concatenate(
        [jnp.sum(grad_final, axis=1), jnp.sum(grad_final * normed_end, axis=1)], axis=-1
    )
    grad_ended = layer_back(grad_final * (1.0 + head_scale), normed_end, inv_end)
    grad_chosen = pick_rows(grad_ended, owner)
    grad_two, mod_grad_two, weights_two, biases_two = spread_backward(
        grad_chosen, saved_two, mod_two, second_params, valid, scale
    )
    shards_two = return_columns(weights_two)
    grad_middle = jnp.where(keep_mask, pick_rows(grad_two, position), grad_ended)
    grad_start, mod_grad_one, weights_one, biases_one = spread_backward(
        grad_middle, saved_one, mod_one, first_params, everyone, scale
    )
    shards_one = return_columns(weights_one)
    start_grad16 = grad_start.astype(jnp.bfloat16)
    grad_embed_w = jnp.einsum(
        "btp,btd->pd", patches, start_grad16, preferred_element_type=jnp.float32
    )
    grad_embed_b = jnp.sum(start_grad16.astype(jnp.float32), axis=(0, 1))
    latent_tokens = jnp.einsum(
        "btd,pd->btp", start_grad16, embed_w, preferred_element_type=jnp.float32
    )
    latent_grad = from_patches(latent_tokens, tile_rows, tile_cols)
    bias_grads = [jnp.stack([biases_one[member], biases_two[member]]) for member in range(4)]
    small_sums = (
        sum_in_two_steps(grad_embed_w, (("dp_0", "dp_1"), ("tx", "ty")), 1),
        *side_by_side_3((grad_embed_b, grad_unpatch_w), (("dp_0", "dp_1"), ("tx", "ty")), 0, 1),
        sum_in_two_steps(bias_grads[0], (("dp_0", "dp_1"), ("tx", "ty")), 1),
        sum_in_two_steps(bias_grads[1], (("dp_0", "dp_1"), ("tx", "ty")), 1),
        sum_in_two_steps(bias_grads[2], (("dp_0", "dp_1"), ("tx", "ty")), 1),
        sum_in_two_steps(bias_grads[3], (("dp_0", "dp_1"), ("tx", "ty")), 1),
    )
    images = cond_all.shape[0]

    def place(grad_mod):
        return lax.dynamic_update_slice_in_dim(
            jnp.zeros((images, grad_mod.shape[1]), jnp.float32), grad_mod, image_start, 0
        )

    mod_back = together(
        (place(mod_grad_one), place(mod_grad_two), place(head_grad_mod), grad_unpatch_b),
        (("dp_0", "dp_1"), ("tx", "ty")),
    )
    one16 = mod_back[0].astype(jnp.bfloat16)
    two16 = mod_back[1].astype(jnp.bfloat16)
    head16 = mod_back[2].astype(jnp.bfloat16)
    mod_weight_grad = jnp.stack(
        [
            jnp.einsum("id,ie->de", cond_rows, one16, preferred_element_type=jnp.float32),
            jnp.einsum("id,ie->de", cond_rows, two16, preferred_element_type=jnp.float32),
        ]
    )
    mod_piece = modulation_bias.shape[1]
    mod_bias_grad = jnp.stack(
        [
            lax.dynamic_slice_in_dim(
                jnp.sum(one16.astype(jnp.float32), axis=0), whole_index * mod_piece, mod_piece
            ),
            lax.dynamic_slice_in_dim(
                jnp.sum(two16.astype(jnp.float32), axis=0), whole_index * mod_piece, mod_piece
            ),
        ]
    )
    final_mod_grad = jnp.einsum("id,ie->de", cond_rows, head16, preferred_element_type=jnp.float32)
    final_piece = final_offsets.shape[0]
    final_bias_grad = lax.dynamic_slice_in_dim(
        jnp.sum(head16.astype(jnp.float32), axis=0), whole_index * final_piece, final_piece
    )
    cond_terms = (
        jnp.einsum("ie,de->id", one16, modulation_weight[0], preferred_element_type=jnp.float32)
        + jnp.einsum("ie,de->id", two16, modulation_weight[1], preferred_element_type=jnp.float32)
        + jnp.einsum("ie,de->id", head16, final_modulation, preferred_element_type=jnp.float32)
    )
    silu_value, silu_pull = jax.vjp(jax.nn.silu, condition.astype(jnp.float32))
    condition_grad = silu_pull(cond_terms)[0]
    stacked = [jnp.stack([shards_one[member], shards_two[member]]) for member in range(4)]
    return (
        predicted,
        latent_grad,
        condition_grad,
        small_sums[0],
        small_sums[1],
        mod_weight_grad,
        mod_bias_grad,
        stacked[0],
        small_sums[3],
        stacked[1],
        small_sums[4],
        stacked[2],
        small_sums[5],
        stacked[3],
        small_sums[6],
        final_mod_grad,
        final_bias_grad,
        small_sums[2],
        mod_back[3],
    )


def solution(mesh):
    torus = Mesh(
        mesh.devices.reshape(4, 4, mesh.shape["tx"], mesh.shape["ty"]), ("dp_0", "dp_1", "tx", "ty")
    )
    return jax.shard_map(
        shards,
        mesh=torus,
        in_specs=(
            P(DP, "tx", "ty", None),
            P(None, DP_TX_TY),
            P(DP, None),
            P(None, DP_TX_TY),
            P(DP_TX_TY),
            P(None, DP_TX_TY, None),
            P(None, DP_TX_TY),
            P(None, DP_TX_TY, None, None),
            P(None, DP_TX_TY),
            P(None, DP_TX_TY, None),
            P(None, DP_TX_TY),
            P(None, DP_TX_TY, None),
            P(None, DP_TX_TY),
            P(None, DP_TX_TY, None),
            P(None, DP_TX_TY),
            P(DP_TX_TY, None),
            P(DP_TX_TY),
            P(DP_TX_TY, None),
            P(),
            P(DP, "tx", "ty", None),
        ),
        out_specs=(
            P(DP, "tx", "ty", None),
            P(DP, "tx", "ty", None),
            P(None, DP_TX_TY),
            P(None, DP_TX_TY),
            P(DP_TX_TY),
            P(None, DP_TX_TY, None),
            P(None, DP_TX_TY),
            P(None, DP_TX_TY, None, None),
            P(None, DP_TX_TY),
            P(None, DP_TX_TY, None),
            P(None, DP_TX_TY),
            P(None, DP_TX_TY, None),
            P(None, DP_TX_TY),
            P(None, DP_TX_TY, None),
            P(None, DP_TX_TY),
            P(DP_TX_TY, None),
            P(DP_TX_TY),
            P(DP_TX_TY, None),
            P(),
        ),
        check_vma=False,
    )
```

profile of v0, /device:TPU:1, one launch (start us, length us, event | category | flops | bytes accessed | tf_op | source)
XLA Modules:
  0.0 1226.6 jit_solution(9011504941415470149)
XLA Ops:
  8.5 8.4 all-to-all-start.8
  29.5 6.7 all-to-all-start
  36.2 6.4 all-to-all-done
  43.6 7.1 all-to-all-start.1
  70.6 6.1 all-to-all-done.2
  209.9 26.9 %all-to-all-done.10 = bf16[8,1,128,1152]{3,2,1,0:T(8,128)(2,1)S(1)} async-done(((bf16[8,1,128,1152]{3,2,1,0:T(8,128)(2,1)}), bf16[8,1,128,1152]{3,2,1,0:T(8,128)(2,1)S(1)}, u32[]{:S(2)}, u32[]{:S(2)}) %all-to-all-start.10) | async-done | bytes 2359328 | tf_op jit(solution)/shard_map/all_to_all | solution.py:18
  281.5 11.9 all-to-all-done.15
  293.9 6.9 all-to-all-start.22
  355.4 15.3 %all-to-all-done.18 = bf16[8,1,128,1152]{3,2,1,0:T(8,128)(2,1)} async-done(((bf16[8,1,128,1152]{3,2,1,0:T(8,128)(2,1)}), bf16[8,1,128,1152]{3,2,1,0:T(8,128)(2,1)}, u32[]{:S(2)}, u32[]{:S(2)}) %all-to-all-start.18) | async-done | bytes 2359328 | tf_op jit(solution)/shard_map/all_to_all | solution.py:18
  394.0 24.9 %all-to-all-done.21 = bf16[8,1,128,1152]{3,2,1,0:T(8,128)(2,1)} async-done(((bf16[8,1,128,1152]{3,2,1,0:T(8,128)(2,1)}), bf16[8,1,128,1152]{3,2,1,0:T(8,128)(2,1)}, u32[]{:S(2)}, u32[]{:S(2)}) %all-to-all-start.21) | async-done | bytes 2359328 | tf_op jit(solution)/shard_map/all_to_all | solution.py:39
  431.6 25.4 %all-to-all-done.24 = bf16[8,1,112,1152]{3,2,1,0:T(8,128)(2,1)} async-done(((bf16[8,1,112,1152]{3,2,1,0:T(8,128)(2,1)}), bf16[8,1,112,1152]{3,2,1,0:T(8,128)(2,1)}, u32[]{:S(2)}, u32[]{:S(2)}) %all-to-all-start.24) | async-done | bytes 2064416 | tf_op jit(solution)/shard_map/all_to_all | solution.py:18
  474.6 25.7 %all-to-all-done.27 = bf16[8,1,112,1152]{3,2,1,0:T(8,128)(2,1)} async-done(((bf16[8,1,112,1152]{3,2,1,0:T(8,128)(2,1)}), bf16[8,1,112,1152]{3,2,1,0:T(8,128)(2,1)}, u32[]{:S(2)}, u32[]{:S(2)}) %all-to-all-start.27) | async-done | bytes 2064416 | tf_op jit(solution)/shard_map/all_to_all | solution.py:39
  521.9 22.1 %all-to-all-done.28 = bf16[8,1,112,1152]{3,2,1,0:T(8,128)(2,1)} async-done(((bf16[8,1,112,1152]{3,2,1,0:T(8,128)(2,1)}), bf16[8,1,112,1152]{3,2,1,0:T(8,128)(2,1)}, u32[]{:S(2)}, u32[]{:S(2)}) %all-to-all-start.28) | async-done | bytes 2064416 | tf_op jit(solution)/shard_map/all_to_all | solution.py:18
  572.9 16.7 %all-to-all-done.29 = bf16[8,1,112,1152]{3,2,1,0:T(8,128)(2,1)} async-done(((bf16[8,1,112,1152]{3,2,1,0:T(8,128)(2,1)}), bf16[8,1,112,1152]{3,2,1,0:T(8,128)(2,1)}, u32[]{:S(2)}, u32[]{:S(2)}) %all-to-all-start.29) | async-done | bytes 2064416 | tf_op jit(solution)/shard_map/all_to_all | solution.py:39
  602.3 29.6 %all_to_all.424 = bf16[8,1,112,1152]{3,2,1,0:T(8,128)(2,1)S(1)} all-to-all(bf16[8,1,112,1152]{3,2,1,0:T(8,128)(2,1)S(1)} %broadcast_in_dim.155), channel_id=1, replica_groups=mesh['dp_0'=4,'dp_1'=4,'tx'=2,'ty'=4] {'tx','ty'}, dimensions={0} | all-to-all | bytes 4128768 | tf_op jit(solution)/shard_map/all_to_all | solution.py:18
  638.1 29.0 %all_to_all.425 = bf16[8,1,112,1152]{3,2,1,0:T(8,128)(2,1)S(1)} all-to-all(bf16[8,1,112,1152]{3,2,1,0:T(8,128)(2,1)S(1)} %bitcast.739), channel_id=1, replica_groups=mesh['dp_0'=4,'dp_1'=4,'tx'=2,'ty'=4] {'tx','ty'}, dimensions={0} | all-to-all | bytes 4128768 | tf_op jit(solution)/shard_map/all_to_all | solution.py:39
  684.0 19.8 %all-to-all-done.34 = bf16[8,1,112,1152]{3,2,1,0:T(8,128)(2,1)} async-done(((bf16[8,1,112,1152]{3,2,1,0:T(8,128)(2,1)}), bf16[8,1,112,1152]{3,2,1,0:T(8,128)(2,1)}, u32[]{:S(2)}, u32[]{:S(2)}) %all-to-all-start.34) | async-done | bytes 2064416 | tf_op jit(solution)/shard_map/all_to_all | solution.py:18
  720.6 29.2 %all_to_all.426 = bf16[8,1,112,1152]{3,2,1,0:T(8,128)(2,1)S(1)} all-to-all(bf16[8,1,112,1152]{3,2,1,0:T(8,128)(2,1)S(1)} %bitcast.738), channel_id=1, replica_groups=mesh['dp_0'=4,'dp_1'=4,'tx'=2,'ty'=4] {'tx','ty'}, dimensions={0} | all-to-all | bytes 4128768 | tf_op jit(solution)/shard_map/all_to_all | solution.py:39
  767.7 25.1 %all-to-all-done.36 = bf16[8,1,128,1152]{3,2,1,0:T(8,128)(2,1)} async-done(((bf16[8,1,128,1152]{3,2,1,0:T(8,128)(2,1)}), bf16[8,1,128,1152]{3,2,1,0:T(8,128)(2,1)}, u32[]{:S(2)}, u32[]{:S(2)}) %all-to-all-start.36) | async-done | bytes 2359328 | tf_op jit(solution)/shard_map/all_to_all | solution.py:18
  792.8 6.2 convert_reduce_fusion.10
  826.1 9.2 pad_maximum_fusion.1
  864.1 23.1 %all-to-all-done.38 = bf16[8,1,128,1152]{3,2,1,0:T(8,128)(2,1)} async-done(((bf16[8,1,128,1152]{3,2,1,0:T(8,128)(2,1)}), bf16[8,1,128,1152]{3,2,1,0:T(8,128)(2,1)}, u32[]{:S(2)}, u32[]{:S(2)}) %all-to-all-start.38) | async-done | bytes 2359328 | tf_op jit(solution)/shard_map/all_to_all | solution.py:18
  954.6 7.1 all-to-all-done.39
  973.4 6.6 all-to-all-start.57
  980.0 6.4 all-to-all-done.57
  990.0 6.4 all-to-all-done.53
  1006.8 7.9 all-to-all-start.44
  1023.5 8.3 pad_maximum_fusion
  1052.3 7.8 all-to-all-done.41
  1085.2 6.4 all-to-all-done.47
  1092.7 8.2 all-to-all-start.43
  1126.1 43.2 %all-reduce.7.cloned.1.call-done = (bf16[1152,1728]{0,1:T(8,128)(2,1)}, bf16[1152,1728]{0,1:T(8,128)(2,1)}) async-done(((bf16[1152,1728]{0,1:T(8,128)(2,1)}, bf16[1152,1728]{0,1:T(8,128)(2,1)}), (bf16[1152,1728]{0,1:T(8,128)(2,1)}, bf16[1152,1728]{0,1:T(8,128)(2,1)})) %all-reduce.7.cloned.1.call-update) | async-done | bytes 7962640
  (1066 shorter events, 717.4 us)
Async XLA Ops:
  8.5 20.9 %all-to-all-start.8 = ((bf16[16,2,54]{2,1,0:T(2,128)(2,1)}), bf16[16,2,54]{2,1,0:T(2,128)(2,1)S(1)}, u32[]{:S(2)}, u32[]{:S(2)}) async-start(bf16[16,2,54]{2,1,0:T(2,128)(2,1)} %broadcast_in_dim.135), calls=%async_computation.8 | async-start | bytes 16384 | tf_op jit(solution)/shard_map/all_to_all | solution.py:18
  29.5 13.1 %all-to-all-start = ((bf16[16,2,144]{2,1,0:T(2,128)(2,1)}), bf16[16,2,144]{2,1,0:T(2,128)(2,1)S(1)}, u32[]{:S(2)}, u32[]{:S(2)}) async-start(bf16[16,2,144]{2,1,0:T(2,128)(2,1)} %reshape.2409), calls=%async_computation | async-start | bytes 32768 | tf_op jit(solution)/shard_map/all_to_all | solution.py:18
  43.6 12.1 all-to-all-start.1
  88.1 20.6 %all-to-all-start.4 = ((f32[8,16,2016]{2,1,0:T(8,128)}), f32[8,16,2016]{2,1,0:T(8,128)S(1)}, u32[]{:S(2)}, u32[]{:S(2)}) async-start(f32[8,16,2016]{2,1,0:T(8,128)} %copy.1106), calls=%async_computation.4 | async-start | bytes 2097152 | tf_op jit(solution)/shard_map/all_to_all | solution.py:113
  161.1 19.6 %all-to-all-start.7 = ((f32[8,16,2016]{2,1,0:T(8,128)}), f32[8,16,2016]{2,1,0:T(8,128)}, u32[]{:S(2)}, u32[]{:S(2)}) async-start(f32[8,16,2016]{2,1,0:T(8,128)} %broadcast_in_dim.134), calls=%async_computation.7 | async-start | bytes 2097152 | tf_op jit(solution)/shard_map/all_to_all | solution.py:18
  165.6 76.1 %all-gather.3.cloned.1.call-start = ((), (), s32[]{:S(2)}) async-start(), calls=%async_computation.60 | async-start | bytes 4386816 | tf_op jit(solution)/shard_map/all_gather | solution.py:59
  203.7 33.1 %all-to-all-start.10 = ((bf16[8,1,128,1152]{3,2,1,0:T(8,128)(2,1)}), bf16[8,1,128,1152]{3,2,1,0:T(8,128)(2,1)S(1)}, u32[]{:S(2)}, u32[]{:S(2)}) async-start(bf16[8,1,128,1152]{3,2,1,0:T(8,128)(2,1)} %broadcast_in_dim.137), calls=%async_computation.10 | async-start | bytes 4718592 | tf_op jit(solution)/shard_map/all_to_all | solution.py:18
  237.5 13.8 %all-to-all-start.19 = ((bf16[16,2,36]{2,1,0:T(2,128)(2,1)}), bf16[16,2,36]{2,1,0:T(2,128)(2,1)S(1)}, u32[]{:S(2)}, u32[]{:S(2)}) async-start(bf16[16,2,36]{2,1,0:T(2,128)(2,1)} %broadcast_in_dim.143), calls=%async_computation.19 | async-start | bytes 16384 | tf_op jit(solution)/shard_map/all_to_all | solution.py:18
  260.2 33.1 %all-to-all-start.15 = ((bf16[8,1,128,1152]{3,2,1,0:T(8,128)(2,1)}), bf16[8,1,128,1152]{3,2,1,0:T(8,128)(2,1)S(1)}, u32[]{:S(2)}, u32[]{:S(2)}) async-start(bf16[8,1,128,1152]{3,2,1,0:T(8,128)(2,1)} %bitcast.695), calls=%async_computation.15 | async-start | bytes 4718592 | tf_op jit(solution)/shard_map/all_to_all | solution.py:39
  293.9 13.3 %all-to-all-start.22 = ((bf16[16,2,9]{2,1,0:T(2,128)(2,1)}), bf16[16,2,9]{2,1,0:T(2,128)(2,1)S(1)}, u32[]{:S(2)}, u32[]{:S(2)}) async-start(bf16[16,2,9]{2,1,0:T(2,128)(2,1)} %broadcast_in_dim.145), calls=%async_computation.22 | async-start | bytes 16384 | tf_op jit(solution)/shard_map/all_to_all | solution.py:18
  336.8 33.9 %all-to-all-start.18 = ((bf16[8,1,128,1152]{3,2,1,0:T(8,128)(2,1)}), bf16[8,1,128,1152]{3,2,1,0:T(8,128)(2,1)}, u32[]{:S(2)}, u32[]{:S(2)}) async-start(bf16[8,1,128,1152]{3,2,1,0:T(8,128)(2,1)} %broadcast_in_dim.142), calls=%async_computation.18 | async-start | bytes 4718592 | tf_op jit(solution)/shard_map/all_to_all | solution.py:18
  341.6 90.0 %all-gather.5.cloned.1.call-start = ((), (), s32[]{:S(2)}) async-start(), calls=%async_computation.61 | async-start | bytes 4386816 | tf_op jit(solution)/shard_map/all_gather | solution.py:59
  370.7 14.2 %all-to-all-start.23 = ((bf16[8,2,144]{2,1,0:T(2,128)(2,1)}), bf16[8,2,144]{2,1,0:T(2,128)(2,1)S(1)}, u32[]{:S(2)}, u32[]{:S(2)}) async-start(bf16[8,2,144]{2,1,0:T(2,128)(2,1)} %reshape.2427), calls=%async_computation.23 | async-start | bytes 16384 | tf_op jit(solution)/shard_map/all_to_all | solution.py:18
  384.9 33.9 %all-to-all-start.21 = ((bf16[8,1,128,1152]{3,2,1,0:T(8,128)(2,1)}), bf16[8,1,128,1152]{3,2,1,0:T(8,128)(2,1)}, u32[]{:S(2)}, u32[]{:S(2)}) async-start(bf16[8,1,128,1152]{3,2,1,0:T(8,128)(2,1)} %bitcast.61), calls=%async_computation.21 | async-start | bytes 4718592 | tf_op jit(solution)/shard_map/all_to_all | solution.py:39
  426.3 30.7 %all-to-all-start.24 = ((bf16[8,1,112,1152]{3,2,1,0:T(8,128)(2,1)}), bf16[8,1,112,1152]{3,2,1,0:T(8,128)(2,1)}, u32[]{:S(2)}, u32[]{:S(2)}) async-start(bf16[8,1,112,1152]{3,2,1,0:T(8,128)(2,1)} %broadcast_in_dim.149), calls=%async_computation.24 | async-start | bytes 4128768 | tf_op jit(solution)/shard_map/all_to_all | solution.py:18
  469.5 30.7 %all-to-all-start.27 = ((bf16[8,1,112,1152]{3,2,1,0:T(8,128)(2,1)}), bf16[8,1,112,1152]{3,2,1,0:T(8,128)(2,1)}, u32[]{:S(2)}, u32[]{:S(2)}) async-start(bf16[8,1,112,1152]{3,2,1,0:T(8,128)(2,1)} %bitcast.700), calls=%async_computation.27 | async-start | bytes 4128768 | tf_op jit(solution)/shard_map/all_to_all | solution.py:39
  512.1 31.9 %all-to-all-start.28 = ((bf16[8,1,112,1152]{3,2,1,0:T(8,128)(2,1)}), bf16[8,1,112,1152]{3,2,1,0:T(8,128)(2,1)}, u32[]{:S(2)}, u32[]{:S(2)}) async-start(bf16[8,1,112,1152]{3,2,1,0:T(8,128)(2,1)} %broadcast_in_dim.152), calls=%async_computation.28 | async-start | bytes 4128768 | tf_op jit(solution)/shard_map/all_to_all | solution.py:18
  544.0 14.8 %all-to-all-start.31 = ((bf16[8,2,144]{2,1,0:T(2,128)(2,1)}), bf16[8,2,144]{2,1,0:T(2,128)(2,1)S(1)}, u32[]{:S(2)}, u32[]{:S(2)}) async-start(bf16[8,2,144]{2,1,0:T(2,128)(2,1)} %reshape.2433), calls=%async_computation.31 | async-start | bytes 16384 | tf_op jit(solution)/shard_map/all_to_all | solution.py:18
  558.7 30.9 %all-to-all-start.29 = ((bf16[8,1,112,1152]{3,2,1,0:T(8,128)(2,1)}), bf16[8,1,112,1152]{3,2,1,0:T(8,128)(2,1)}, u32[]{:S(2)}, u32[]{:S(2)}) async-start(bf16[8,1,112,1152]{3,2,1,0:T(8,128)(2,1)} %bitcast.737), calls=%async_computation.29 | async-start | bytes 4128768 | tf_op jit(solution)/shard_map/all_to_all | solution.py:39
  672.7 31.0 %all-to-all-start.34 = ((bf16[8,1,112,1152]{3,2,1,0:T(8,128)(2,1)}), bf16[8,1,112,1152]{3,2,1,0:T(8,128)(2,1)}, u32[]{:S(2)}, u32[]{:S(2)}) async-start(bf16[8,1,112,1152]{3,2,1,0:T(8,128)(2,1)} %broadcast_in_dim.156), calls=%async_computation.34 | async-start | bytes 4128768 | tf_op jit(solution)/shard_map/all_to_all | solution.py:18
  758.7 34.1 %all-to-all-start.36 = ((bf16[8,1,128,1152]{3,2,1,0:T(8,128)(2,1)}), bf16[8,1,128,1152]{3,2,1,0:T(8,128)(2,1)}, u32[]{:S(2)}, u32[]{:S(2)}) async-start(bf16[8,1,128,1152]{3,2,1,0:T(8,128)(2,1)} %broadcast_in_dim.157), calls=%async_computation.36 | async-start | bytes 4718592 | tf_op jit(solution)/shard_map/all_to_all | solution.py:18
  803.1 33.4 %all-to-all-start.37 = ((bf16[8,1,128,1152]{3,2,1,0:T(8,128)(2,1)}), bf16[8,1,128,1152]{3,2,1,0:T(8,128)(2,1)S(1)}, u32[]{:S(2)}, u32[]{:S(2)}) async-start(bf16[8,1,128,1152]{3,2,1,0:T(8,128)(2,1)} %bitcast.725), calls=%async_computation.37 | async-start | bytes 4718592 | tf_op jit(solution)/shard_map/all_to_all | solution.py:39
  836.6 14.9 %all-to-all-start.58 = ((f32[8,1,288]{2,1,0:T(1,128)}), f32[8,1,288]{2,1,0:T(1,128)S(1)}, u32[]{:S(2)}, u32[]{:S(2)}) async-start(f32[8,1,288]{2,1,0:T(1,128)} %reshape.2449), calls=%async_computation.58 | async-start | bytes 24576 | tf_op jit(solution)/shard_map/all_to_all | solution.py:113
  853.2 34.1 %all-to-all-start.38 = ((bf16[8,1,128,1152]{3,2,1,0:T(8,128)(2,1)}), bf16[8,1,128,1152]{3,2,1,0:T(8,128)(2,1)}, u32[]{:S(2)}, u32[]{:S(2)}) async-start(bf16[8,1,128,1152]{3,2,1,0:T(8,128)(2,1)} %broadcast_in_dim.158), calls=%async_computation.38 | async-start | bytes 4718592 | tf_op jit(solution)/shard_map/all_to_all | solution.py:18
  887.2 22.2 %all-to-all-start.56 = ((f32[8,1,1152]{2,1,0:T(1,128)}), f32[8,1,1152]{2,1,0:T(1,128)S(1)}, u32[]{:S(2)}, u32[]{:S(2)}) async-start(f32[8,1,1152]{2,1,0:T(1,128)} %reshape.2447), calls=%async_computation.56 | async-start | bytes 73728 | tf_op jit(solution)/shard_map/all_to_all | solution.py:113
  927.9 33.8 %all-to-all-start.39 = ((bf16[8,1,128,1152]{3,2,1,0:T(8,128)(2,1)}), bf16[8,1,128,1152]{3,2,1,0:T(8,128)(2,1)}, u32[]{:S(2)}, u32[]{:S(2)}) async-start(bf16[8,1,128,1152]{3,2,1,0:T(8,128)(2,1)} %bitcast.726), calls=%async_computation.39 | async-start | bytes 4718592 | tf_op jit(solution)/shard_map/all_to_all | solution.py:39
  973.4 13.1 %all-to-all-start.57 = ((f32[16,2,36]{2,1,0:T(2,128)}), f32[16,2,36]{2,1,0:T(2,128)S(1)}, u32[]{:S(2)}, u32[]{:S(2)}) async-start(f32[16,2,36]{2,1,0:T(2,128)} %copy.1217), calls=%async_computation.57 | async-start | bytes 32768 | tf_op jit(solution)/shard_map/all_to_all | solution.py:120
  1006.8 12.8 %all-to-all-start.44 = ((f32[8,1,2304]{2,1,0:T(1,128)}), f32[8,1,2304]{2,1,0:T(1,128)S(1)}, u32[]{:S(2)}, u32[]{:S(2)}) async-start(f32[8,1,2304]{2,1,0:T(1,128)} %reshape.2435), calls=%async_computation.44 | async-start | bytes 147456 | tf_op jit(solution)/shard_map/all_to_all | solution.py:113
  1019.6 18.9 %all-to-all-start.40 = ((f32[8,16,2017]{2,1,0:T(8,128)}), f32[8,16,2017]{2,1,0:T(8,128)S(1)}, u32[]{:S(2)}, u32[]{:S(2)}) async-start(f32[8,16,2017]{2,1,0:T(8,128)} %copy.1191), calls=%async_computation.40 | async-start | bytes 2097152 | tf_op jit(solution)/shard_map/all_to_all | solution.py:113
  1023.5 145.7 %all-reduce.7.cloned.1.call-start = ((), (), s32[]{:S(2)}) async-start(), calls=%async_computation.62 | async-start | bytes 15925248
  1048.0 12.1 all-to-all-start.41
  1092.7 23.2 %all-to-all-start.43 = ((f32[8,16,2017]{2,1,0:T(8,128)}), f32[8,16,2017]{2,1,0:T(8,128)S(1)}, u32[]{:S(2)}, u32[]{:S(2)}) async-start(f32[8,16,2017]{2,1,0:T(8,128)} %broadcast_in_dim.286), calls=%async_computation.43 | async-start | bytes 2097152 | tf_op jit(solution)/shard_map/all_to_all | solution.py:18
  (230 other events, 3271.3 us)
Sparse Core Ops, SparseCore 0:
  174.9 50.2 all-gather.2
  354.4 48.6 all-gather.4
  1032.0 137.1 all-reduce.6
where the time goes:
time: 1240 us; the launch traced here: 1230 us
  waiting for transfers between devices  438 us (35%)
  starting transfers between devices  265 us (21%)
  local copies, waits for them, and re-layouts  196 us (16%)
  matrix products  130 us (10%)
  other arithmetic  90.9 us (7%)
  blocking collectives  87.8 us (7%)
  between operations  19.2 us (2%)
    all_to_all x27, waiting for transfers between devices, from_everyone(): return lax.all_to_all(copies, axis, split_axis=0, concat_axis=0, tiled=True)  220 us
    all_to_all x27, starting transfers between devices, from_everyone(): return lax.all_to_all(copies, axis, split_axis=0, concat_axis=0, tiled=True)  135 us
    all_to_all x6, waiting for transfers between devices, sum_at_owner(): parts = lax.all_to_all(cut_along(array, dim, peers), axis, 0, 0, tiled=True)  86.3 us
    unnamed x489, local copies, waits for them, and re-layouts  69.5 us
    all_to_all x2, blocking collectives, sum_at_owner(): parts = lax.all_to_all(cut_along(array, dim, peers), axis, 0, 0, tiled=True)  58.2 us
    unnamed x4, waiting for transfers between devices  43.2 us
    all_to_all x8, waiting for transfers between devices, sum_in_two_steps(): return jnp.sum(lax.all_to_all(own, far, 0, 0, tiled=True), axis=0)  41.4 us
    all_to_all x8, starting transfers between devices, summed_on_arrival(): parts = lax.all_to_all(cut_along(array, dim, peers), axis, 0, 0, tiled=True)  37 us
  transfers between devices with their start and end apart: 60, of which 49 were waited for; matrix products, arithmetic and copies ran while one was open for 25% of the time, Pallas kernels for 0%

commit v1 on v0

v1 whole, which is shorter than its diff:
```python
import functools

import jax
import jax.numpy as jnp
from jax import lax
from jax.experimental import pallas as pl
from jax.experimental.pallas import tpu as pltpu
from jax.sharding import Mesh
from jax.sharding import PartitionSpec as P

D = 1152
HEADS = 16
FF = 4608
HW = D // 8
FW = FF // 8
DP = ("dp_0", "dp_1")
DP_TX_TY = ("dp_0", "dp_1", "tx", "ty")
MESH = pl.DeviceIdType.MESH
VMEM = pl.BlockSpec(memory_space=pltpu.VMEM)
F32 = jnp.float32
BF16 = jnp.bfloat16
ATT_COLS = 640
FFN_COLS = 2 * FW
ALL_COLS = 2 * (ATT_COLS + FFN_COLS)
PIECE = 512
PIECES = ALL_COLS // PIECE
MOD_ALL = 14 * D
SMALL_IN = (16 * 9, 9, 9 * 32, 2 * 18, 2 * 9, 2 * 36, 2 * 9)


def enter(peers):
    barrier = pltpu.get_barrier_semaphore()
    for peer in peers:
        pl.semaphore_signal(barrier, inc=1, device_id=peer, device_id_type=MESH)
    pl.semaphore_wait(barrier, len(peers))


def send(src, dst, sems, k, peer):
    copy = pltpu.make_async_remote_copy(
        src_ref=src,
        dst_ref=dst,
        send_sem=sems[0].at[k],
        recv_sem=sems[1].at[k],
        device_id=peer,
        device_id_type=MESH,
    )
    copy.start()
    return copy


def group_peers():
    c, y = lax.axis_index("tx"), lax.axis_index("ty")
    found = []
    for dc in range(2):
        for dy in range(4):
            if dc or dy:
                oc, oy = lax.rem(c + dc, 2), lax.rem(y + dy, 4)
                found.append(({"tx": oc, "ty": oy}, oc * 4 + oy))
    return found


def image_peers():
    x, z = lax.axis_index("dp_0"), lax.axis_index("dp_1")
    found = []
    for dx in range(4):
        for dz in range(4):
            if dx or dz:
                ox, oz = lax.rem(x + dx, 4), lax.rem(z + dz, 4)
                found.append(({"dp_0": ox, "dp_1": oz}, ox * 4 + oz))
    return found


def own_group():
    return lax.axis_index("tx") * 4 + lax.axis_index("ty")


def own_image():
    return lax.axis_index("dp_0") * 4 + lax.axis_index("dp_1")


def dma_sems(n):
    return [pltpu.SemaphoreType.DMA((n,)), pltpu.SemaphoreType.DMA((n,))]


def collective(kernel, cid, outs, scratch, *operands, vmem=48 << 20):
    return pl.pallas_call(
        kernel,
        out_shape=outs,
        in_specs=[VMEM] * len(operands),
        out_specs=jax.tree.map(lambda _: VMEM, outs),
        scratch_shapes=scratch,
        compiler_params=pltpu.CompilerParams(
            collective_id=cid, has_side_effects=True, vmem_limit_bytes=vmem
        ),
    )(*operands)


def ring_peers():
    c, y = lax.axis_index("tx"), lax.axis_index("ty")
    return (
        {"tx": 1 - c},
        {"ty": lax.rem(y + 1, 4)},
        {"ty": lax.rem(y + 3, 4)},
        {"ty": lax.rem(y + 2, 4)},
    )


def gather_kernel(x_ref, o_ref, ss, rs):
    tokens = x_ref.shape[0]
    half = (tokens // 2 + 15) // 16 * 16
    c, y = lax.axis_index("tx"), lax.axis_index("ty")
    sib, up, down, _ = ring_peers()
    enter([sib, up, down])
    sems = (ss, rs)
    me = c * 4 + y
    above, below, across = (c * 4 + lax.rem(y + k, 4) for k in (1, 3, 2))
    a1 = send(x_ref.at[0:half], o_ref.at[me, 0:half], sems, 0, up)
    b1 = send(x_ref.at[half:tokens], o_ref.at[me, half:tokens], sems, 1, down)
    a2 = send(x_ref.at[half:tokens], o_ref.at[me, half:tokens], sems, 2, up)
    b2 = send(x_ref.at[0:half], o_ref.at[me, 0:half], sems, 3, down)
    s0 = send(x_ref, o_ref.at[me], sems, 4, sib)
    o_ref[me] = x_ref[...]
    a1.wait_recv()
    f1 = send(o_ref.at[below, 0:half], o_ref.at[below, 0:half], sems, 5, up)
    b1.wait_recv()
    f2 = send(o_ref.at[above, half:tokens], o_ref.at[above, half:tokens], sems, 6, down)
    a2.wait_recv()
    s1 = send(o_ref.at[below], o_ref.at[below], sems, 7, sib)
    b2.wait_recv()
    s2 = send(o_ref.at[above], o_ref.at[above], sems, 8, sib)
    f1.wait_recv()
    f2.wait_recv()
    s3 = send(o_ref.at[across], o_ref.at[across], sems, 9, sib)
    for copy in (s0, s1, s2, s3):
        copy.wait()
    for copy in (a1, a2, b1, b2, f1, f2):
        copy.wait_send()


def sum_kernel(x_ref, o_ref, sib_buf, mine, got, ss, rs):
    c, y = lax.axis_index("tx"), lax.axis_index("ty")
    sib, up, down, far = ring_peers()
    enter([sib, up, down, far])
    sems = (ss, rs)
    to = {1: up, 2: far, 3: down}
    order = (2, 1, 3, 0)
    swaps = [
        send(x_ref.at[(1 - c) * 4 + lax.rem(y + d, 4)], sib_buf.at[d], sems, d, sib) for d in order
    ]
    sends = {}
    for d, swap in zip(order, swaps):
        swap.wait_recv()
        total = x_ref[c * 4 + lax.rem(y + d, 4)].astype(F32) + sib_buf[d].astype(F32)
        if d:
            mine[d] = total.astype(BF16)
            sends[d] = send(mine.at[d], got.at[d], sems, 3 + d, to[d])
        else:
            o_ref[...] = total
    for d in (1, 3, 2):
        sends[d].wait_recv()
        o_ref[...] = o_ref[...] + got[d].astype(F32)
    for d in (1, 3, 2):
        sends[d].wait_send()
    for swap in swaps:
        swap.wait_send()


def gather_image(rows16, cid):
    tokens = rows16.shape[1]
    out = jax.ShapeDtypeStruct((8, tokens, D), BF16)
    parts = collective(gather_kernel, cid, out, dma_sems(10), rows16[0])
    return parts.reshape(1, 8 * tokens, D)


def sum_image(partial_value, cid):
    tokens = partial_value.shape[1] // 8
    out = jax.ShapeDtypeStruct((tokens, D), F32)
    scratch = [pltpu.VMEM((4, tokens, D), BF16)] * 3 + dma_sems(8)
    parts = partial_value.astype(BF16).reshape(8, tokens, D)
    return collective(sum_kernel, cid, out, scratch, parts)[None]


def spread_kernel(w_ref, m_ref, s_ref, w_out, m_out, s_out, m_got, m_two, ss, rs):
    group, image = group_peers(), image_peers()
    enter([peer for peer, _ in group + image])
    sems = (ss, rs)
    me, mine = own_group(), own_image()
    first = []
    for k, (peer, at) in enumerate(image):
        first.append(send(m_ref.at[at], m_got.at[mine], sems, k, peer))
        first.append(send(s_ref, s_out.at[me, mine], sems, 15 + k, peer))
    weights = [send(w_ref.at[at], w_out.at[me], sems, 30 + k, p) for k, (p, at) in enumerate(group)]
    w_out[me] = w_ref[me]
    s_out[me, mine] = s_ref[...]
    m_got[mine] = m_ref[mine]
    for copy in first:
        copy.wait_recv()
    total = m_got[0]
    for k in range(1, 16):
        total = total + m_got[k]
    m_two[me] = total
    second = []
    for k, (peer, _) in enumerate(group):
        second.append(send(m_two.at[me], m_two.at[me], sems, 37 + k, peer))
        second.append(send(s_out.at[me], s_out.at[me], sems, 44 + k, peer))
    for copy in second:
        copy.wait_recv()
    total = m_two[0]
    for k in range(1, 8):
        total = total + m_two[k]
    m_out[...] = total
    for copy in weights:
        copy.wait_recv()
    for copy in first + second + weights:
        copy.wait_send()


def spread(weights, mods, small):
    outs = (
        jax.ShapeDtypeStruct(weights.shape, BF16),
        jax.ShapeDtypeStruct((128, 128), F32),
        jax.ShapeDtypeStruct((8, 16, *small.shape), BF16),
    )
    scratch = [pltpu.VMEM((16, 128, 128), F32), pltpu.VMEM((8, 128, 128), F32)] + dma_sems(51)
    return collective(spread_kernel, 1, outs, scratch, weights, mods, small)


def fetch_kernel(w_ref, o_ref, ss, rs):
    image = image_peers()
    enter([peer for peer, _ in image])
    mine = own_image()
    copies = [
        send(w_ref, o_ref.at[mine], (ss, rs), k, peer) for k, (peer, _) in enumerate(image)
    ]
    o_ref[mine] = w_ref[...]
    for copy in copies:
        copy.wait()


def fetch_rows(rows, cid):
    padded = jnp.pad(rows, [(0, 8), (0, 0)])
    out = jax.ShapeDtypeStruct((16, *padded.shape), BF16)
    slabs = collective(fetch_kernel, cid, out, dma_sems(15), padded)
    return slabs[:, :72].reshape(D, rows.shape[1])


def reduce_kernel(g_ref, o_ref, got, ss, rs):
    image = image_peers()
    enter([peer for peer, _ in image])
    mine = own_image()
    copies = [
        send(g_ref.at[at], got.at[mine], (ss, rs), k, peer) for k, (peer, at) in enumerate(image)
    ]
    got[mine] = g_ref[mine]
    for copy in copies:
        copy.wait_recv()

    @pl.loop(0, g_ref.shape[1] // 16)
    def _(piece):
        rows = pl.ds(pl.multiple_of(piece * 16, 16), 16)
        total = got[0, rows, :].astype(F32)
        for k in range(1, 16):
            total = total + got[k, rows, :].astype(F32)
        o_ref[rows, :] = total.astype(BF16)

    for copy in copies:
        copy.wait_send()


def reduce_rows(grads, cid):
    slabs = jnp.pad(grads.reshape(16, 72, -1), [(0, 0), (0, 8), (0, 0)])
    out = jax.ShapeDtypeStruct(slabs.shape[1:], BF16)
    scratch = [pltpu.VMEM(slabs.shape, BF16)] + dma_sems(15)
    return collective(reduce_kernel, cid, out, scratch, slabs)[:72]


def finish_kernel(g_ref, m_ref, s_ref, g_out, m_out, s_out, m_got, s_got, s_mine, s_two, ss, rs):
    group, image = group_peers(), image_peers()
    enter([peer for peer, _ in group + image])
    sems = (ss, rs)
    me, mine = own_group(), own_image()
    first = [send(m_ref.at[at], m_got.at[me], sems, k, p) for k, (p, at) in enumerate(group)]
    small = [send(s_ref.at[at], s_got.at[mine], sems, 7 + k, p) for k, (p, at) in enumerate(image)]
    weights = [send(g_ref.at[at], g_out.at[me], sems, 22 + k, p) for k, (p, at) in enumerate(group)]
    m_got[me] = m_ref[me]
    s_got[mine] = s_ref[mine]
    g_out[me] = g_ref[me]
    for copy in first:
        copy.wait_recv()
    total = m_got[0]
    for k in range(1, 8):
        total = total + m_got[k]
    m_out[me, mine] = total.astype(BF16)
    second = [
        send(m_out.at[me, mine], m_out.at[me, mine], sems, 29 + k, p)
        for k, (p, _) in enumerate(image)
    ]
    for copy in small:
        copy.wait_recv()
    total = s_got[0]
    for k in range(1, 16):
        total = total + s_got[k]
    s_mine[...] = total
    pieces = [send(s_mine.at[at], s_two.at[me], sems, 44 + k, p) for k, (p, at) in enumerate(group)]
    s_two[me] = s_mine[me]
    for copy in second:
        copy.wait_recv()
    third = [send(m_out.at[me], m_out.at[me], sems, 51 + k, p) for k, (p, _) in enumerate(group)]
    for copy in pieces:
        copy.wait_recv()
    total = s_two[0]
    for k in range(1, 8):
        total = total + s_two[k]
    s_out[...] = total
    for copy in weights + third:
        copy.wait_recv()
    for copy in first + small + weights + second + pieces + third:
        copy.wait_send()


def finish(grads, mods, small):
    outs = (
        jax.ShapeDtypeStruct(grads.shape, BF16),
        jax.ShapeDtypeStruct((8, 16, 16, 128), BF16),
        jax.ShapeDtypeStruct((8, 128), F32),
    )
    scratch = [
        pltpu.VMEM((8, 16, 128), F32),
        pltpu.VMEM((16, 8, 8, 128), F32),
        pltpu.VMEM((8, 8, 128), F32),
        pltpu.VMEM((8, 8, 128), F32),
    ] + dma_sems(58)
    return collective(finish_kernel, 2, outs, scratch, grads, mods, small)


def layer_stats(value_rows):
    centered = value_rows - jnp.mean(value_rows, axis=-1, keepdims=True)
    inv_std = lax.rsqrt(jnp.mean(centered * centered, axis=-1, keepdims=True) + 1e-06)
    return (centered * inv_std, inv_std)


def layer_back(upstream, normed, inv_std):
    return inv_std * (
        upstream
        - jnp.mean(upstream, axis=-1, keepdims=True)
        - normed * jnp.mean(upstream * normed, axis=-1, keepdims=True)
    )


def smooth_gate(value_rows):
    return jax.nn.gelu(value_rows, approximate=True)


def sincos_table(row_pos, col_pos, width):
    quarter = width // 4
    freqs = jnp.power(10000.0, -jnp.arange(quarter, dtype=jnp.float32) / quarter)
    row_angle = row_pos[:, None] * freqs[None, :]
    col_angle = col_pos[:, None] * freqs[None, :]
    row_embed = jnp.concatenate([jnp.sin(row_angle), jnp.cos(row_angle)], axis=-1)
    col_embed = jnp.concatenate([jnp.sin(col_angle), jnp.cos(col_angle)], axis=-1)
    row_full = jnp.broadcast_to(
        row_embed[:, None, :], (row_pos.shape[0], col_pos.shape[0], width // 2)
    )
    col_full = jnp.broadcast_to(
        col_embed[None, :, :], (row_pos.shape[0], col_pos.shape[0], width // 2)
    )
    return jnp.concatenate([row_full, col_full], axis=-1).reshape(
        row_pos.shape[0] * col_pos.shape[0], width
    )


def to_patches(pixels):
    count, height, breadth, depth = pixels.shape
    shaped = pixels.reshape(count, height // 2, 2, breadth // 2, 2, depth)
    return shaped.transpose(0, 1, 3, 2, 4, 5).reshape(
        count, height // 2 * (breadth // 2), 4 * depth
    )


def from_patches(token_rows, tile_rows, tile_cols):
    count = token_rows.shape[0]
    depth = token_rows.shape[2] // 4
    shaped = token_rows.reshape(count, tile_rows, tile_cols, 2, 2, depth)
    return shaped.transpose(0, 1, 3, 2, 4, 5).reshape(count, 2 * tile_rows, 2 * tile_cols, depth)


def split_mod(mod, width):
    return [mod[:, None, piece * width : (piece + 1) * width] for piece in range(6)]


def compact_plan(routed, capacity):
    count, tokens = routed.shape
    flags = routed > 0
    position = jnp.cumsum(flags.astype(jnp.int32), axis=1) - 1
    slots = jnp.where(flags, position, capacity)
    batch_index = jnp.broadcast_to(jnp.arange(count, dtype=jnp.int32)[:, None], (count, tokens))
    token_ids = jnp.arange(tokens, dtype=jnp.int32)[None, :]
    owner = (
        jnp.zeros((count, capacity), jnp.int32).at[batch_index, slots].set(token_ids, mode="drop")
    )
    filled = jnp.sum(flags.astype(jnp.int32), axis=1, keepdims=True)
    valid = (jnp.arange(capacity, dtype=jnp.int32)[None, :] < filled).astype(jnp.float32)
    return (jnp.where(flags, position, 0), owner, valid)


def pick_rows(value_rows, index):
    return jax.vmap(lambda table, where: jnp.take(table, where, axis=0))(value_rows, index)


def score_block(query, keys, key_marks, heads, scale):
    count, rows, width = query.shape
    size = width // heads
    q_heads = query.reshape(count, rows, heads, size)
    k_heads = keys.reshape(count, keys.shape[1], heads, size)
    scores = (
        jnp.einsum("bqhe,bkhe->bhqk", q_heads, k_heads, preferred_element_type=jnp.float32) * scale
    )
    return jnp.where(key_marks[:, None, None, :] > 0, scores, -1e30)


def attend(query, keys, vals, key_marks, heads, scale):
    count, rows, width = query.shape
    size = width // heads
    scores = score_block(query, keys, key_marks, heads, scale)
    highest = jnp.max(scores, axis=-1, keepdims=True)
    shifted = jnp.exp(scores - highest)
    summed = jnp.sum(shifted, axis=-1, keepdims=True)
    probs16 = (shifted / summed).astype(jnp.bfloat16)
    log_sum = highest + jnp.log(summed)
    v_heads = vals.reshape(count, vals.shape[1], heads, size)
    attended = jnp.einsum("bhqk,bkhe->bqhe", probs16, v_heads, preferred_element_type=jnp.float32)
    return (attended.reshape(count, rows, width).astype(jnp.bfloat16), log_sum)


def attend_back(query, keys, vals, key_marks, log_sum, attended_grad16, heads, scale):
    count, rows, width = query.shape
    size = width // heads
    key_count = keys.shape[1]
    scores = score_block(query, keys, key_marks, heads, scale)
    probs = jnp.exp(scores - log_sum)
    probs16 = probs.astype(jnp.bfloat16)
    grad_heads = attended_grad16.reshape(count, rows, heads, size)
    v_heads = vals.reshape(count, key_count, heads, size)
    k_heads = keys.reshape(count, key_count, heads, size)
    q_heads = query.reshape(count, rows, heads, size)
    grad_probs = jnp.einsum(
        "bqhe,bkhe->bhqk", grad_heads, v_heads, preferred_element_type=jnp.float32
    )
    grad_values = jnp.einsum(
        "bhqk,bqhe->bkhe", probs16, grad_heads, preferred_element_type=jnp.float32
    )
    weighted = jnp.sum(probs * grad_probs, axis=-1, keepdims=True)
    score_grad16 = (probs * (grad_probs - weighted)).astype(jnp.bfloat16)
    grad_query = (
        jnp.einsum("bhqk,bkhe->bqhe", score_grad16, k_heads, preferred_element_type=jnp.float32)
        * scale
    )
    grad_keys = (
        jnp.einsum("bhqk,bqhe->bkhe", score_grad16, q_heads, preferred_element_type=jnp.float32)
        * scale
    )
    return (
        grad_query.reshape(count, rows, width),
        grad_keys.reshape(count, key_count, width),
        grad_values.reshape(count, key_count, width),
    )


def spread_forward(value_rows, mod, params, biases, marks_all, scale, cid):
    attn_p, merge_p, expand_p, reduce_p = params
    attn_b, merge_b, expand_b, reduce_b = biases
    width = value_rows.shape[2]
    head_width = attn_p.shape[2]
    hidden_width = expand_p.shape[1]
    heads = head_width // (D // HEADS)
    group = lax.axis_index(("tx", "ty"))
    shift1, scale1, gate1, shift2, scale2, gate2 = split_mod(mod, width)
    normed1, inv_one = layer_stats(value_rows)
    input16 = (normed1 * (1.0 + scale1) + shift1).astype(jnp.bfloat16)
    input_all = gather_image(input16, cid + 0)
    joined = jnp.einsum("btd,dke->btke", input_all, attn_p, preferred_element_type=jnp.float32)
    q_bias = lax.dynamic_slice_in_dim(attn_b, group * head_width, head_width).astype(jnp.float32)
    v_bias = lax.dynamic_slice_in_dim(attn_b, width + group * head_width, head_width).astype(
        jnp.float32
    )
    query = (joined[:, :, 0] + q_bias).astype(jnp.bfloat16)
    keys = joined[:, :, 1].astype(jnp.bfloat16)
    vals = (joined[:, :, 2] + v_bias).astype(jnp.bfloat16)
    attended, log_sum = attend(query, keys, vals, marks_all, heads, scale)
    branch = sum_image(
        jnp.einsum("bth,dh->btd", attended, merge_p, preferred_element_type=jnp.float32),
        cid + 2,
    )
    branch = branch + merge_b.astype(jnp.float32)
    middle = value_rows + gate1 * branch
    normed2, inv_two = layer_stats(middle)
    second16 = (normed2 * (1.0 + scale2) + shift2).astype(jnp.bfloat16)
    second_all = gather_image(second16, cid + 1)
    e_bias = lax.dynamic_slice_in_dim(expand_b, group * hidden_width, hidden_width).astype(
        jnp.float32
    )
    pre = (
        jnp.einsum("btd,df->btf", second_all, expand_p, preferred_element_type=jnp.float32)
        + e_bias
    )
    hidden16 = smooth_gate(pre).astype(jnp.bfloat16)
    mlp = sum_image(
        jnp.einsum("btf,df->btd", hidden16, reduce_p, preferred_element_type=jnp.float32),
        cid + 3,
    )
    mlp = mlp + reduce_b.astype(jnp.float32)
    output = middle + gate2 * mlp
    saved = (
        normed1,
        inv_one,
        input_all,
        query,
        keys,
        vals,
        marks_all,
        log_sum,
        attended,
        branch,
        normed2,
        inv_two,
        second_all,
        pre,
        hidden16,
        mlp,
    )
    return (output, saved)


def spread_backward(upstream, saved, mod, params, marks, scale, cid):
    attn_p, merge_p, expand_p, reduce_p = params
    (
        normed1,
        inv_one,
        input_all,
        query,
        keys,
        vals,
        marks_all,
        log_sum,
        attended,
        branch,
        normed2,
        inv_two,
        second_all,
        pre,
        hidden16,
        mlp,
    ) = saved
    width = upstream.shape[2]
    head_width = attn_p.shape[2]
    hidden_width = expand_p.shape[1]
    heads = head_width // (D // HEADS)
    group = lax.axis_index(("tx", "ty"))
    shift1, scale1, gate1, shift2, scale2, gate2 = split_mod(mod, width)
    grad_out = upstream * marks[:, :, None]
    grad_gate2 = jnp.sum(grad_out * mlp, axis=1)
    mlp_grad16 = (grad_out * gate2).astype(jnp.bfloat16)
    grad_reduce_b = jnp.sum(mlp_grad16.astype(jnp.float32), axis=(0, 1))
    mlp_grad_all = gather_image(mlp_grad16, cid + 4)
    grad_reduce_p = jnp.einsum(
        "btd,btf->df", mlp_grad_all, hidden16, preferred_element_type=jnp.float32
    )
    grad_hidden = jnp.einsum(
        "btd,df->btf", mlp_grad_all, reduce_p, preferred_element_type=jnp.float32
    )
    gate_value, gate_pull = jax.vjp(smooth_gate, pre)
    pre_grad16 = gate_pull(grad_hidden)[0].astype(jnp.bfloat16)
    grad_expand_p = jnp.einsum(
        "btd,btf->df", second_all, pre_grad16, preferred_element_type=jnp.float32
    )
    grad_expand_b = lax.dynamic_update_slice_in_dim(
        jnp.zeros((FF,), jnp.float32),
        jnp.sum(pre_grad16.astype(jnp.float32), axis=(0, 1)),
        group * hidden_width,
        0,
    )
    grad_second = sum_image(
        jnp.einsum("btf,df->btd", pre_grad16, expand_p, preferred_element_type=jnp.float32),
        cid + 5,
    )
    grad_shift2 = jnp.sum(grad_second, axis=1)
    grad_scale2 = jnp.sum(grad_second * normed2, axis=1)
    grad_middle = grad_out + layer_back(grad_second * (1.0 + scale2), normed2, inv_two)
    grad_gate1 = jnp.sum(grad_middle * branch, axis=1)
    branch_grad16 = (grad_middle * gate1).astype(jnp.bfloat16)
    grad_merge_b = jnp.sum(branch_grad16.astype(jnp.float32), axis=(0, 1))
    branch_grad_all = gather_image(branch_grad16, cid + 6)
    grad_merge_p = jnp.einsum(
        "btd,bth->dh", branch_grad_all, attended, preferred_element_type=jnp.float32
    )
    attended_grad16 = jnp.einsum(
        "btd,dh->bth", branch_grad_all, merge_p, preferred_element_type=jnp.float32
    ).astype(jnp.bfloat16)
    grad_query, grad_keys, grad_values = attend_back(
        query, keys, vals, marks_all, log_sum, attended_grad16, heads, scale
    )
    joined_grad16 = jnp.stack([grad_query, grad_keys, grad_values], axis=2).astype(jnp.bfloat16)
    grad_attn_p = jnp.einsum(
        "btd,btke->dke", input_all, joined_grad16, preferred_element_type=jnp.float32
    )
    bias_zero = jnp.zeros((2 * width,), jnp.float32)
    grad_attn_b = lax.dynamic_update_slice_in_dim(
        bias_zero,
        jnp.sum(joined_grad16[:, :, 0].astype(jnp.float32), axis=(0, 1)),
        group * head_width,
        0,
    )
    grad_attn_b = lax.dynamic_update_slice_in_dim(
        grad_attn_b,
        jnp.sum(joined_grad16[:, :, 2].astype(jnp.float32), axis=(0, 1)),
        width + group * head_width,
        0,
    )
    grad_input = sum_image(
        jnp.einsum("btke,dke->btd", joined_grad16, attn_p, preferred_element_type=jnp.float32),
        cid + 7,
    )
    grad_shift1 = jnp.sum(grad_input, axis=1)
    grad_scale1 = jnp.sum(grad_input * normed1, axis=1)
    grad_values_in = grad_middle + layer_back(grad_input * (1.0 + scale1), normed1, inv_one)
    grad_mod = jnp.concatenate(
        [grad_shift1, grad_scale1, grad_gate1, grad_shift2, grad_scale2, grad_gate2], axis=-1
    )
    return (
        grad_values_in,
        grad_mod,
        (grad_attn_p, grad_merge_p, grad_expand_p, grad_reduce_p),
        (grad_attn_b, grad_merge_b, grad_expand_b, grad_reduce_b),
    )


def pack_weights(attention_weight, merge_weight, expand_weight, reduce_weight):
    def by_group(array):
        parts = array.reshape(*array.shape[:-1], 8, array.shape[-1] // 8)
        return jnp.moveaxis(parts, -2, 0)

    attn, merge = by_group(attention_weight), by_group(merge_weight)
    expand, reduce = by_group(expand_weight), by_group(reduce_weight)
    spare = jnp.zeros((8, 9, ATT_COLS - 4 * HW), BF16)
    columns = []
    for b in range(2):
        columns += [attn[:, b].reshape(8, 9, 3 * HW), merge[:, b], spare]
    for b in range(2):
        columns += [expand[:, b], reduce[:, b]]
    return pack_pieces(jnp.concatenate(columns, axis=2))


def pack_pieces(columns):
    pieces = columns.reshape(8, 9, PIECES, PIECE).swapaxes(1, 2)
    return jnp.pad(pieces.reshape(8, 9 * PIECES, PIECE), [(0, 0), (0, 1), (0, 0)])


def unpack_pieces(packed):
    pieces = packed[:, : 9 * PIECES].reshape(8, PIECES, 9, PIECE)
    return pieces.swapaxes(1, 2).reshape(8, 9, ALL_COLS)


def unpack_rows(packed):
    return unpack_pieces(packed).reshape(72, ALL_COLS)


def block_params(attn, ffn):
    return (
        attn[:, : 3 * HW].reshape(D, 3, HW),
        attn[:, 3 * HW : 4 * HW],
        ffn[:, :FW],
        ffn[:, FW:],
    )


def join_grads(grads):
    attn, merge, expand, reduce = (g.astype(BF16) for g in grads)
    spare = jnp.zeros((D, ATT_COLS - 4 * HW), BF16)
    return jnp.concatenate([attn.reshape(D, 3 * HW), merge, spare, expand, reduce], axis=1)


def pack_grads(one, two):
    columns = jnp.concatenate(
        [one[:, :ATT_COLS], two[:, :ATT_COLS], one[:, ATT_COLS:], two[:, ATT_COLS:]], axis=1
    )
    return pack_pieces(columns.reshape(8, 9, ALL_COLS))


def unpack_grads(packed):
    columns = unpack_pieces(packed)

    def whole(at, width, inner):
        parts = columns[:, :, at : at + inner * width].reshape(8, 9, inner, width)
        return parts.transpose(1, 2, 0, 3).reshape(9, inner, 8 * width).astype(F32)

    starts = (0, ATT_COLS), (2 * ATT_COLS, 2 * ATT_COLS + FFN_COLS)
    return (
        jnp.stack([whole(at, HW, 3) for at in starts[0]]),
        jnp.stack([whole(at + 3 * HW, HW, 1)[:, 0] for at in starts[0]]),
        jnp.stack([whole(at, FW, 1)[:, 0] for at in starts[1]]),
        jnp.stack([whole(at + FW, FW, 1)[:, 0] for at in starts[1]]),
    )


def pack_small(parts):
    flat = jnp.concatenate([part.reshape(-1) for part in parts])
    return jnp.pad(flat, (0, 2048 - flat.shape[0])).reshape(16, 128)


def by_owner(array, dim):
    before, after = array.shape[:dim], array.shape[dim + 1 :]
    parts = array.reshape(*before, 128, array.shape[dim] // 128, *after)
    return jnp.moveaxis(parts, dim, 0).reshape(128, -1)


def from_owner(parts, shape, dim):
    split = parts.reshape(128, *shape[:dim], shape[dim] // 128, *shape[dim + 1 :])
    return jnp.moveaxis(split, 0, dim).reshape(shape)


def shards(
    latent,
    condition,
    routed_ids,
    embed_weight,
    embed_bias,
    modulation_weight,
    modulation_bias,
    attention_weight,
    attention_bias,
    merge_weight,
    merge_bias,
    expand_weight,
    expand_bias,
    reduce_weight,
    reduce_bias,
    final_modulation,
    final_offsets,
    unpatch_weight,
    unpatch_bias,
    pred_cotangent,
):
    count = latent.shape[0]
    tile_rows = latent.shape[1] // 2
    tile_cols = latent.shape[2] // 2
    tile_tokens = tile_rows * tile_cols
    rows_tiles = lax.axis_size("tx")
    cols_tiles = lax.axis_size("ty")
    tiles = rows_tiles * cols_tiles
    grid_side = tile_rows * rows_tiles
    row_index = lax.axis_index("tx") * tile_rows + jnp.arange(tile_rows, dtype=jnp.int32)
    col_index = lax.axis_index("ty") * tile_cols + jnp.arange(tile_cols, dtype=jnp.int32)
    token_index = (row_index[:, None] * grid_side + col_index[None, :]).reshape(tile_tokens)
    routed = jnp.sum(
        (routed_ids[:, :, None] == token_index[None, None, :]).astype(jnp.float32), axis=1
    )
    capacity = 7 * tile_tokens // 8
    id_tiles = (
        routed_ids // grid_side // tile_rows * cols_tiles + routed_ids % grid_side // tile_cols
    )
    tile_loads = jnp.sum(
        (id_tiles[:, :, None] == jnp.arange(tiles, dtype=jnp.int32)[None, None, :]).astype(
            jnp.int32
        ),
        axis=1,
    )
    routed_marks = jnp.arange(capacity, dtype=jnp.int32)[None, None, :] < tile_loads[:, :, None]
    routed_marks = routed_marks.astype(jnp.float32).reshape(count, tiles * capacity)
    everyone = jnp.ones((count, tile_tokens), jnp.float32)
    everyone_all = jnp.ones((count, tiles * tile_tokens), jnp.float32)
    position, owner, valid = compact_plan(routed, capacity)
    width = D
    scale = (D // HEADS) ** (-0.5)
    whole_index = lax.axis_index(DP_TX_TY)
    small_parts = (
        embed_weight,
        embed_bias,
        unpatch_weight,
        attention_bias,
        merge_bias,
        expand_bias,
        reduce_bias,
    )
    cond_rows = jax.nn.silu(condition.astype(F32)).astype(BF16)
    mod_cuts = (6 * D, 12 * D, 14 * D)
    mod_piece = modulation_bias.shape[1]
    final_piece = final_offsets.shape[0]
    placed_bias = jnp.zeros((MOD_ALL,), F32)
    for bias, at in (
        (modulation_bias[0], whole_index * mod_piece),
        (modulation_bias[1], 6 * D + whole_index * mod_piece),
        (final_offsets, 12 * D + whole_index * final_piece),
    ):
        placed_bias = lax.dynamic_update_slice_in_dim(placed_bias, bias.astype(F32), at, 0)
    mod_parts = jnp.concatenate(
        [
            jnp.dot(cond_rows, modulation_weight[0], preferred_element_type=F32),
            jnp.dot(cond_rows, modulation_weight[1], preferred_element_type=F32),
            jnp.dot(cond_rows, final_modulation, preferred_element_type=F32),
        ],
        axis=1,
    )
    mod_parts = jnp.pad(mod_parts + placed_bias[None], [(0, 0), (0, 16384 - MOD_ALL)])
    packed = pack_weights(attention_weight, merge_weight, expand_weight, reduce_weight)
    packed, mods, small = spread(packed, mod_parts.reshape(16, 128, 128), pack_small(small_parts))
    mods = mods.reshape(1, 16384)
    mod_one = mods[:, : 6 * D]
    mod_two = mods[:, 6 * D : 12 * D]
    head_mod = mods[:, 12 * D : 14 * D]
    small = small.transpose(1, 0, 2, 3).reshape(128, 2048)
    pieces = jnp.split(small, [sum(SMALL_IN[:k]) for k in range(1, 8)], axis=1)
    embed_w = from_owner(pieces[0], (16, D), 1)
    embed_b = from_owner(pieces[1], (D,), 0)
    unpatch_w = from_owner(pieces[2], (D, 32), 0)
    attn_b = from_owner(pieces[3], (2, 2 * D), 1)
    merge_b = from_owner(pieces[4], (2, D), 1)
    expand_b = from_owner(pieces[5], (2, FF), 1)
    reduce_b = from_owner(pieces[6], (2, D), 1)
    rows = unpack_rows(packed)
    first_attn = fetch_rows(rows[:, :ATT_COLS], 3)
    first_ffn = lax.all_gather(
        rows[:, 2 * ATT_COLS : 2 * ATT_COLS + FFN_COLS], DP, axis=0, tiled=True
    )
    second_all = lax.all_gather(
        jnp.concatenate(
            [rows[:, ATT_COLS : 2 * ATT_COLS], rows[:, 2 * ATT_COLS + FFN_COLS :]], axis=1
        ),
        DP,
        axis=0,
        tiled=True,
    )
    placed = sincos_table(row_index.astype(jnp.float32), col_index.astype(jnp.float32), width)
    patches = to_patches(latent)
    initial_tokens = (
        jnp.einsum("btp,pd->btd", patches, embed_w, preferred_element_type=jnp.float32)
        + embed_b.astype(jnp.float32)
        + placed[None, :, :]
    )
    first_params = block_params(first_attn, first_ffn)
    second_params = block_params(second_all[:, :ATT_COLS], second_all[:, ATT_COLS:])
    first_biases = (attn_b[0], merge_b[0], expand_b[0], reduce_b[0])
    second_biases = (attn_b[1], merge_b[1], expand_b[1], reduce_b[1])
    middle_one, saved_one = spread_forward(
        initial_tokens, mod_one, first_params, first_biases, everyone_all, scale, 10
    )
    selected_rows = pick_rows(middle_one, owner)
    middle_two, saved_two = spread_forward(
        selected_rows, mod_two, second_params, second_biases, routed_marks, scale, 20
    )
    keep_mask = routed[:, :, None] > 0
    ended = jnp.where(keep_mask, pick_rows(middle_two, position), middle_one)
    head_shift = head_mod[:, None, :width]
    head_scale = head_mod[:, None, width:]
    normed_end, inv_end = layer_stats(ended)
    final16 = (normed_end * (1.0 + head_scale) + head_shift).astype(jnp.bfloat16)
    outputs = jnp.einsum(
        "btd,do->bto", final16, unpatch_w, preferred_element_type=jnp.float32
    ) + unpatch_bias.astype(jnp.float32)
    predicted = from_patches(outputs.astype(jnp.bfloat16), tile_rows, tile_cols)
    cotangent = to_patches(pred_cotangent)
    grad_unpatch_w = jnp.einsum(
        "btd,bto->do", final16, cotangent, preferred_element_type=jnp.float32
    )
    grad_unpatch_b = jnp.sum(cotangent.astype(jnp.float32), axis=(0, 1))
    grad_final = jnp.einsum("bto,do->btd", cotangent, unpatch_w, preferred_element_type=jnp.float32)
    head_grad_mod = jnp.concatenate(
        [jnp.sum(grad_final, axis=1), jnp.sum(grad_final * normed_end, axis=1)], axis=-1
    )
    grad_ended = layer_back(grad_final * (1.0 + head_scale), normed_end, inv_end)
    grad_chosen = pick_rows(grad_ended, owner)
    grad_two, mod_grad_two, weights_two, biases_two = spread_backward(
        grad_chosen, saved_two, mod_two, second_params, valid, scale, 20
    )
    summed_two = reduce_rows(join_grads(weights_two), 4)
    grad_middle = jnp.where(keep_mask, pick_rows(grad_two, position), grad_ended)
    grad_start, mod_grad_one, weights_one, biases_one = spread_backward(
        grad_middle, saved_one, mod_one, first_params, everyone, scale, 10
    )
    summed_one = reduce_rows(join_grads(weights_one), 5)
    start_grad16 = grad_start.astype(jnp.bfloat16)
    grad_embed_w = jnp.einsum(
        "btp,btd->pd", patches, start_grad16, preferred_element_type=jnp.float32
    )
    grad_embed_b = jnp.sum(start_grad16.astype(jnp.float32), axis=(0, 1))
    latent_tokens = jnp.einsum(
        "btd,pd->btp", start_grad16, embed_w, preferred_element_type=jnp.float32
    )
    latent_grad = from_patches(latent_tokens, tile_rows, tile_cols)
    bias_grads = [jnp.stack([biases_one[member], biases_two[member]]) for member in range(4)]
    small_out = jnp.concatenate(
        [
            by_owner(grad_embed_w, 1),
            by_owner(grad_embed_b, 0),
            by_owner(grad_unpatch_w, 0),
            by_owner(bias_grads[0], 1),
            by_owner(bias_grads[1], 1),
            by_owner(bias_grads[2], 1),
            by_owner(bias_grads[3], 1),
            jnp.broadcast_to(grad_unpatch_b[None], (128, 32)),
        ],
        axis=1,
    )
    small_out = jnp.pad(small_out, [(0, 0), (0, 1024 - small_out.shape[1])])
    grad_mods = jnp.concatenate([mod_grad_one, mod_grad_two, head_grad_mod], axis=1)
    grad_mods = jnp.pad(grad_mods.reshape(8, MOD_ALL // 8), [(0, 0), (0, 2048 - MOD_ALL // 8)])
    packed_grads, mod_back, small_back = finish(
        pack_grads(summed_one, summed_two),
        grad_mods.reshape(8, 16, 128),
        small_out.reshape(16, 8, 8, 128),
    )
    small_back = small_back.reshape(1024)
    small_sizes = (*SMALL_IN, 32)
    small_sums = jnp.split(small_back, [sum(small_sizes[:k]) for k in range(1, 9)])
    mod_back = mod_back.reshape(8, 16, 2048)[:, :, : MOD_ALL // 8]
    mod_back = mod_back.transpose(1, 0, 2).reshape(16, MOD_ALL)
    one16 = mod_back[:, : mod_cuts[0]]
    two16 = mod_back[:, mod_cuts[0] : mod_cuts[1]]
    head16 = mod_back[:, mod_cuts[1] :]
    stacked = unpack_grads(packed_grads)
    mod_weight_grad = jnp.stack(
        [
            jnp.einsum("id,ie->de", cond_rows, one16, preferred_element_type=jnp.float32),
            jnp.einsum("id,ie->de", cond_rows, two16, preferred_element_type=jnp.float32),
        ]
    )
    mod_bias_grad = jnp.stack(
        [
            lax.dynamic_slice_in_dim(
                jnp.sum(one16.astype(jnp.float32), axis=0), whole_index * mod_piece, mod_piece
            ),
            lax.dynamic_slice_in_dim(
                jnp.sum(two16.astype(jnp.float32), axis=0), whole_index * mod_piece, mod_piece
            ),
        ]
    )
    final_mod_grad = jnp.einsum("id,ie->de", cond_rows, head16, preferred_element_type=jnp.float32)
    final_bias_grad = lax.dynamic_slice_in_dim(
        jnp.sum(head16.astype(jnp.float32), axis=0), whole_index * final_piece, final_piece
    )
    cond_terms = (
        jnp.einsum("ie,de->id", one16, modulation_weight[0], preferred_element_type=jnp.float32)
        + jnp.einsum("ie,de->id", two16, modulation_weight[1], preferred_element_type=jnp.float32)
        + jnp.einsum("ie,de->id", head16, final_modulation, preferred_element_type=jnp.float32)
    )
    silu_value, silu_pull = jax.vjp(jax.nn.silu, condition.astype(jnp.float32))
    condition_grad = silu_pull(cond_terms)[0]
    return (
        predicted,
        latent_grad,
        condition_grad,
        small_sums[0].reshape(16, 9),
        small_sums[1],
        mod_weight_grad,
        mod_bias_grad,
        stacked[0],
        small_sums[3].reshape(2, 18),
        stacked[1],
        small_sums[4].reshape(2, 9),
        stacked[2],
        small_sums[5].reshape(2, 36),
        stacked[3],
        small_sums[6].reshape(2, 9),
        final_mod_grad,
        final_bias_grad,
        small_sums[2].reshape(9, 32),
        small_sums[7],
    )


def solution(mesh):
    torus = Mesh(
        mesh.devices.reshape(4, 4, mesh.shape["tx"], mesh.shape["ty"]), ("dp_0", "dp_1", "tx", "ty")
    )
    return jax.shard_map(
        shards,
        mesh=torus,
        in_specs=(
            P(DP, "tx", "ty", None),
            P(None, DP_TX_TY),
            P(DP, None),
            P(None, DP_TX_TY),
            P(DP_TX_TY),
            P(None, DP_TX_TY, None),
            P(None, DP_TX_TY),
            P(None, DP_TX_TY, None, None),
            P(None, DP_TX_TY),
            P(None, DP_TX_TY, None),
            P(None, DP_TX_TY),
            P(None, DP_TX_TY, None),
            P(None, DP_TX_TY),
            P(None, DP_TX_TY, None),
            P(None, DP_TX_TY),
            P(DP_TX_TY, None),
            P(DP_TX_TY),
            P(DP_TX_TY, None),
            P(),
            P(DP, "tx", "ty", None),
        ),
        out_specs=(
            P(DP, "tx", "ty", None),
            P(DP, "tx", "ty", None),
            P(None, DP_TX_TY),
            P(None, DP_TX_TY),
            P(DP_TX_TY),
            P(None, DP_TX_TY, None),
            P(None, DP_TX_TY),
            P(None, DP_TX_TY, None, None),
            P(None, DP_TX_TY),
            P(None, DP_TX_TY, None),
            P(None, DP_TX_TY),
            P(None, DP_TX_TY, None),
            P(None, DP_TX_TY),
            P(None, DP_TX_TY, None),
            P(None, DP_TX_TY),
            P(DP_TX_TY, None),
            P(DP_TX_TY),
            P(DP_TX_TY, None),
            P(),
        ),
        check_vma=False,
    )
```

time: 1240 us -> 838 us (0.68)
  Pallas kernels: 0 us -> 517 us
  waiting for transfers between devices: 438 us -> 0.08 us
  starting transfers between devices: 265 us -> 0.26 us
  blocking collectives: 87.8 us -> 0 us
  other arithmetic: 90.9 us -> 46 us
  matrix products: 130 us -> 88.4 us
  local copies, waits for them, and re-layouts: 196 us -> 162 us
    pallas_call x0 -> x21, Pallas kernels: none -> 517 us  [collective(): pl.pallas_call(kernel, out_shape=outs, in_specs=[VMEM] * len(operands), o...]
    all_to_all x57 -> x0, waiting for transfers between devices: 395 us -> none  [the longest x27 220 us: from_everyone(): return lax.all_to_all(copies, axis, split_axis=0, concat_axis=0, tiled=True)]
    all_to_all x57 -> x0, starting transfers between devices: 264 us -> none  [the longest x27 135 us: from_everyone(): return lax.all_to_all(copies, axis, split_axis=0, concat_axis=0, tiled=True)]
    all_to_all x3 -> x0, blocking collectives: 87.8 us -> none  [the longest x2 58.2 us: sum_at_owner(): parts = lax.all_to_all(cut_along(array, dim, peers), axis, 0, 0, tiled=True)]
    unnamed x489 -> x368, local copies, waits for them, and re-layouts: 69.5 us -> 17 us
    unnamed x4 -> x2, waiting for transfers between devices: 43.2 us -> 0.03 us
    concatenate x15 -> x3, other arithmetic: 23.3 us -> 0.92 us  [the longest x1 0.72 us: shards(): jnp.concatenate([rows[:, ATT_COLS:2 * ATT_COLS], rows[:, 2 * ATT_COLS + F...]
    dot_general x15, matrix products: 49.1 us -> 29.7 us  [the longest x2 8.48 us: spread_backward(): jnp.einsum('btd,df->btf', mlp_grad_all, reduce_p, preferred_element_type=...]
  transfers between devices with their start and end apart: 60 -> 2, of which waited for: 49 -> 0; matrix products, arithmetic and copies ran while one was open for 25% -> 10% of each run, Pallas kernels for 0% -> 14%
where the time goes in v1:
time: 838 us; the launch traced here: 831 us
  Pallas kernels  517 us (62%)
  local copies, waits for them, and re-layouts  162 us (19%)
  matrix products  88.4 us (11%)
  other arithmetic  46 us (5%)
  between operations  17.7 us (2%)
    pallas_call x21, Pallas kernels, collective(): pl.pallas_call(kernel, out_shape=outs, in_specs=[VMEM] * len(operands), o...  517 us
    concatenate x7, local copies, waits for them, and re-layouts, join_grads(): jnp.concatenate([attn.reshape(D, 3 * HW), merge, spare, expand, reduce],...  31 us
    unnamed x368, local copies, waits for them, and re-layouts  17 us
  transfers between devices with their start and end apart: 2, of which 0 were waited for; matrix products, arithmetic and copies ran while one was open for 10% of the time, Pallas kernels for 14%

profile of v1, /device:TPU:1, one launch (start us, length us, event | category | flops | bytes accessed | tf_op | source)
XLA Modules:
  0.0 831.3 jit_solution(2083777194126321432)
XLA Ops:
  21.3 37.5 %shard_map.342 = (bf16[8,64,512]{2,1,0:T(8,128)(2,1)S(1)}, f32[128,128]{1,0:T(8,128)S(1)}, bf16[8,16,16,128]{3,2,1,0:T(8,128)(2,1)S(1)}) custom-call(bf16[8,64,512]{2,1,0:T(8,128)(2,1)S(1)} %pad.35.w_ref, f32[16,128,128]{2,1,0:T(8,128)S(1)} %bitcast.587, bf16[16,128]{1,0:T(8,128)(2,1)S(1)} %pad_bitcast_fusion.3.s_ref), custom_call_target="tpu_custom_call" | custom-call | tf_op jit(solution)/shard_map/pallas_call | solution.py:86
  72.4 30.2 %shard_map.344 = bf16[16,80,640]{2,1,0:T(8,128)(2,1)S(1)} custom-call(bf16[80,640]{1,0:T(8,128)(2,1)S(1)} %pad.38.w_ref), custom_call_target="tpu_custom_call" | custom-call | tf_op jit(solution)/shard_map/pallas_call | solution.py:86
  104.3 15.2 %shard_map.343 = bf16[8,128,1152]{2,1,0:T(8,128)(2,1)S(1)} custom-call(bf16[128,1152]{1,0:T(8,128)(2,1)S(1)} %add_convert_fusion.4.x_ref), custom_call_target="tpu_custom_call" | custom-call | tf_op jit(solution)/shard_map/pallas_call | solution.py:86
  177.4 18.9 %shard_map.345 = f32[128,1152]{1,0:T(8,128)S(1)} custom-call(bf16[8,128,1152]{2,1,0:T(8,128)(2,1)S(1)} %bitcast.585), custom_call_target="tpu_custom_call" | custom-call | tf_op jit(solution)/shard_map/pallas_call | solution.py:86
  197.5 15.2 %shard_map.346 = bf16[8,128,1152]{2,1,0:T(8,128)(2,1)S(1)} custom-call(bf16[128,1152]{1,0:T(8,128)(2,1)S(1)} %add_convert_fusion.1.x_ref), custom_call_target="tpu_custom_call" | custom-call | tf_op jit(solution)/shard_map/pallas_call | solution.py:86
  224.3 18.9 %shard_map.347 = f32[128,1152]{1,0:T(8,128)S(1)} custom-call(bf16[8,128,1152]{2,1,0:T(8,128)(2,1)S(1)} %bitcast.596), custom_call_target="tpu_custom_call" | custom-call | tf_op jit(solution)/shard_map/pallas_call | solution.py:86
  245.8 14.3 %shard_map.348 = bf16[8,112,1152]{2,1,0:T(8,128)(2,1)S(1)} custom-call(bf16[112,1152]{1,0:T(8,128)(2,1)S(1)} %fusion.84.x_ref), custom_call_target="tpu_custom_call" | custom-call | tf_op jit(solution)/shard_map/pallas_call | solution.py:86
  260.2 3.4 fusion.133
  271.7 17.2 %shard_map.349 = f32[112,1152]{1,0:T(8,128)S(1)} custom-call(bf16[8,112,1152]{2,1,0:T(8,128)(2,1)S(1)} %bitcast.586), custom_call_target="tpu_custom_call" | custom-call | tf_op jit(solution)/shard_map/pallas_call | solution.py:86
  289.6 14.3 %shard_map.350 = bf16[8,112,1152]{2,1,0:T(8,128)(2,1)S(1)} custom-call(bf16[112,1152]{1,0:T(8,128)(2,1)S(1)} %fusion.85.x_ref), custom_call_target="tpu_custom_call" | custom-call | tf_op jit(solution)/shard_map/pallas_call | solution.py:86
  308.6 17.2 %shard_map.351 = f32[112,1152]{1,0:T(8,128)S(1)} custom-call(bf16[8,112,1152]{2,1,0:T(8,128)(2,1)S(1)} %bitcast.605), custom_call_target="tpu_custom_call" | custom-call | tf_op jit(solution)/shard_map/pallas_call | solution.py:86
  334.2 14.3 %shard_map.352 = bf16[8,112,1152]{2,1,0:T(8,128)(2,1)S(1)} custom-call(bf16[112,1152]{1,0:T(8,128)(2,1)S(1)} %fusion.125.x_ref), custom_call_target="tpu_custom_call" | custom-call | tf_op jit(solution)/shard_map/pallas_call | solution.py:86
  348.6 3.4 convolution_convert_fusion.8
  352.0 4.1 convert_reduce_fusion.1
  360.8 17.2 %shard_map.353 = f32[112,1152]{1,0:T(8,128)S(1)} custom-call(bf16[8,112,1152]{2,1,0:T(8,128)(2,1)S(1)} %bitcast.604), custom_call_target="tpu_custom_call" | custom-call | tf_op jit(solution)/shard_map/pallas_call | solution.py:86
  381.4 14.3 %shard_map.354 = bf16[8,112,1152]{2,1,0:T(8,128)(2,1)S(1)} custom-call(bf16[112,1152]{1,0:T(8,128)(2,1)S(1)} %fusion.98.x_ref), custom_call_target="tpu_custom_call" | custom-call | tf_op jit(solution)/shard_map/pallas_call | solution.py:86
  400.0 4.6 multiply_reduce_fusion.2
  404.5 4.3 multiply_convert_fusion.1
  419.2 17.2 %shard_map.355 = f32[112,1152]{1,0:T(8,128)S(1)} custom-call(bf16[8,112,1152]{2,1,0:T(8,128)(2,1)S(1)} %bitcast.603), custom_call_target="tpu_custom_call" | custom-call | tf_op jit(solution)/shard_map/pallas_call | solution.py:86
  448.6 5.1 concatenate.99
  456.8 8.2 concatenate.103
  467.5 79.5 %shard_map.361 = bf16[80,1792]{1,0:T(8,128)(2,1)S(1)} custom-call(bf16[16,80,1792]{2,1,0:T(8,128)(2,1)S(1)} %pad.40.g_ref), custom_call_target="tpu_custom_call" | custom-call | tf_op jit(solution)/shard_map/pallas_call | solution.py:86
  552.6 15.2 %shard_map.356 = bf16[8,128,1152]{2,1,0:T(8,128)(2,1)S(1)} custom-call(bf16[128,1152]{1,0:T(8,128)(2,1)S(1)} %fusion.95.x_ref), custom_call_target="tpu_custom_call" | custom-call | tf_op jit(solution)/shard_map/pallas_call | solution.py:86
  567.8 3.4 convolution_convert_fusion.6
  571.2 4.4 convert_reduce_fusion
  579.6 18.9 %shard_map.357 = f32[128,1152]{1,0:T(8,128)S(1)} custom-call(bf16[8,128,1152]{2,1,0:T(8,128)(2,1)S(1)} %bitcast.595), custom_call_target="tpu_custom_call" | custom-call | tf_op jit(solution)/shard_map/pallas_call | solution.py:86
  600.4 15.6 %shard_map.358 = bf16[8,128,1152]{2,1,0:T(8,128)(2,1)S(1)} custom-call(bf16[128,1152]{1,0:T(8,128)(2,1)S(1)} %fusion.96.x_ref), custom_call_target="tpu_custom_call" | custom-call | tf_op jit(solution)/shard_map/pallas_call | solution.py:86
  637.8 4.4 concatenate.93
  644.5 7.9 concatenate.98
  654.9 81.5 %shard_map.360 = bf16[80,1792]{1,0:T(8,128)(2,1)S(1)} custom-call(bf16[16,80,1792]{2,1,0:T(8,128)(2,1)S(1)} %pad.39.g_ref), custom_call_target="tpu_custom_call" | custom-call | tf_op jit(solution)/shard_map/pallas_call | solution.py:86
  745.6 19.1 %shard_map.359 = f32[128,1152]{1,0:T(8,128)S(1)} custom-call(bf16[8,128,1152]{2,1,0:T(8,128)(2,1)S(1)} %bitcast.594), custom_call_target="tpu_custom_call" | custom-call | tf_op jit(solution)/shard_map/pallas_call | solution.py:86
  768.7 25.2 %shard_map.362 = (bf16[8,64,512]{2,1,0:T(8,128)(2,1)S(1)}, bf16[8,16,16,128]{3,2,1,0:T(8,128)(2,1)S(1)}, f32[8,128]{1,0:T(8,128)S(1)}) custom-call(bf16[8,64,512]{2,1,0:T(8,128)(2,1)S(1)} %pad.41.g_ref, f32[8,16,128]{2,1,0:T(8,128)S(1)} %bitcast.608, f32[16,8,8,128]{3,2,1,0:T(8,128)S(1)} %copy.424), custom_call_target="tpu_custom_call" | custom-call | tf_op jit(solution)/shard_map/pallas_call | solution.py:86
  (745 shorter events, 243.8 us)
Async XLA Ops:
  7.2 210.5 %all-gather.3.cloned.1.call-start = ((), (), s32[]{:S(2)}) async-start(), calls=%async_computation | async-start | bytes 2820096 | tf_op jit(solution)/shard_map/all_gather | solution.py:821
  60.2 200.0 %all-gather.5.cloned.1.call-start = ((), (), s32[]{:S(2)}) async-start(), calls=%async_computation.1 | async-start | bytes 4386816 | tf_op jit(solution)/shard_map/all_gather | solution.py:824
  71.4 32.7 %copy-start.82 = (f32[1152]{0:T(1024)}, f32[1152]{0:T(1024)S(1)}, u32[]{:S(2)}) copy-start(f32[1152]{0:T(1024)S(1)} %get-tuple-element.168) | copy-start | bytes 13828
  72.2 124.1 %copy-start.18 = (f32[128,1152]{1,0:T(8,128)}, f32[128,1152]{1,0:T(8,128)S(1)}, u32[]{:S(2)}) copy-start(f32[128,1152]{1,0:T(8,128)S(1)} %get-tuple-element.236) | copy-start | bytes 1769476
  72.2 31.9 %copy-start.125 = (f32[128]{0:T(128)}, f32[128]{0:T(128)S(1)}, u32[]{:S(2)}) copy-start(f32[128]{0:T(128)S(1)} %broadcast_multiply_fusion.14) | copy-start | bytes 1540
  72.4 31.7 %copy-start.127 = (f32[128]{0:T(128)}, f32[128]{0:T(128)S(1)}, u32[]{:S(2)}) copy-start(f32[128]{0:T(128)S(1)} %add_rsqrt_fusion.4) | copy-start | bytes 1540
  102.8 73.3 %copy-start.22 = (bf16[16,72,640]{2,1,0:T(8,128)(2,1)}, bf16[16,72,640]{2,1,0:T(8,128)(2,1)S(1)}, u32[]{:S(2)}) copy-start(bf16[16,72,640]{2,1,0:T(8,128)(2,1)S(1)} %slice.283) | copy-start | bytes 4423684
  121.0 44.4 %copy-start.33 = (bf16[1,1024,1,144]{1,3,2,0:T(8,128)(2,1)}, bf16[1,1024,1,144]{1,3,2,0:T(8,128)(2,1)S(1)}, u32[]{:S(2)}) copy-start(bf16[1,1024,1,144]{1,3,2,0:T(8,128)(2,1)S(1)} %slice.514) | copy-start | bytes 884740
  121.9 43.5 %copy-start.31 = (f32[1,1024,1,144]{1,3,2,0:T(8,128)}, f32[1,1024,1,144]{1,3,2,0:T(8,128)S(1)}, u32[]{:S(2)}) copy-start(f32[1,1024,1,144]{1,3,2,0:T(8,128)S(1)} %get-tuple-element.186) | copy-start | bytes 1769476
  176.1 20.2 %copy-start.84 = (f32[1152]{0:T(1024)S(1)}, f32[1152]{0:T(1024)}, u32[]{:S(2)}) copy-start(f32[1152]{0:T(1024)} %get-tuple-element.169) | copy-start | bytes 13828
  177.4 19.9 %copy-start.85 = (f32[1152]{0:T(1024)S(1)}, f32[1152]{0:T(1024)}, u32[]{:S(2)}) copy-start(f32[1152]{0:T(1024)} %get-tuple-element.165) | copy-start | bytes 13828
  177.4 19.9 %copy-start.97 = (f32[1152]{0:T(1024)S(1)}, f32[1152]{0:T(1024)}, u32[]{:S(2)}) copy-start(f32[1152]{0:T(1024)} %get-tuple-element.164) | copy-start | bytes 13828
  196.5 21.1 %copy-start.118 = (s32[896]{0:T(1024)S(1)}, s32[896]{0:T(1024)}, u32[]{:S(2)}) copy-start(s32[896]{0:T(1024)} %lt.117) | copy-start | bytes 10756
  196.5 21.1 %copy-start.119 = (s32[896]{0:T(1024)S(1)}, s32[896]{0:T(1024)}, u32[]{:S(2)}) copy-start(s32[896]{0:T(1024)} %lt.114) | copy-start | bytes 10756
  196.5 21.1 %copy-start.92 = (f32[2,1024]{1,0:T(2,128)S(1)}, f32[2,1024]{1,0:T(2,128)}, u32[]{:S(2)}) copy-start(f32[2,1024]{1,0:T(2,128)} %copy-done.91) | copy-start | bytes 24580
  196.5 21.1 %copy-start.115 = (f32[2,1024]{1,0:T(2,128)S(1)}, f32[2,1024]{1,0:T(2,128)}, u32[]{:S(2)}) copy-start(f32[2,1024]{1,0:T(2,128)} %copy-done.114) | copy-start | bytes 24580
  196.8 24.2 %copy-start.129 = (f32[128]{0:T(128)}, f32[128]{0:T(128)S(1)}, u32[]{:S(2)}) copy-start(f32[128]{0:T(128)S(1)} %add_rsqrt_fusion.3) | copy-start | bytes 1540
  216.8 88.9 %copy-start.141 = (f32[576]{0:T(1024)}, f32[576]{0:T(1024)S(1)}, u32[]{:S(2)}) copy-start(f32[576]{0:T(1024)S(1)} %dynamic-slice_convert_fusion) | copy-start | bytes 6916
  289.2 36.7 %copy-start.20 = (f32[1,112,1152]{2,1,0:T(8,128)}, f32[1,112,1152]{2,1,0:T(8,128)S(1)}, u32[]{:S(2)}) copy-start(f32[1,112,1152]{2,1,0:T(8,128)S(1)} %get-tuple-element.182) | copy-start | bytes 1548292
  378.1 19.9 %slice-start.2 = ((s8[6422528]{0:T(1024)(128)(4,1)}), s8[4194304]{0:T(1024)(128)(4,1)S(1)}, s32[]{:S(2)}) async-start(s8[6422528]{0:T(1024)(128)(4,1)} %bitcast.619), calls=%async_computation.4 | async-start | bytes 8388608
  467.5 80.8 %copy-start.36 = (f32[1,112,1152]{2,1,0:T(8,128)S(1)}, f32[1,112,1152]{2,1,0:T(8,128)}, u32[]{:S(2)}) copy-start(f32[1,112,1152]{2,1,0:T(8,128)} %copy-done.35) | copy-start | bytes 1548292
  577.3 41.4 %slice-start = ((s8[8388608]{0:T(1024)(128)(4,1)}), s8[4194304]{0:T(1024)(128)(4,1)S(1)}, s32[]{:S(2)}) async-start(s8[8388608]{0:T(1024)(128)(4,1)} %bitcast.617), calls=%async_computation.2 | async-start | bytes 8388608
  579.6 39.2 %slice-start.1 = ((s8[8388608]{0:T(1024)(128)(4,1)}), s8[4194304]{0:T(1024)(128)(4,1)S(1)}, s32[]{:S(2)}) async-start(s8[8388608]{0:T(1024)(128)(4,1)} %bitcast.617), calls=%async_computation.3 | async-start | bytes 8388608
  654.9 82.3 %copy-start.24 = (f32[1152,128]{0,1:T(8,128)S(1)}, f32[1152,128]{0,1:T(8,128)}, u32[]{:S(2)}) copy-start(f32[1152,128]{0,1:T(8,128)} %copy-done.23) | copy-start | bytes 1769476
  654.9 83.0 %copy-start.42 = (bf16[128,1152]{1,0:T(8,128)(2,1)S(1)}, bf16[128,1152]{1,0:T(8,128)(2,1)}, u32[]{:S(2)}) copy-start(bf16[128,1152]{1,0:T(8,128)(2,1)} %get-tuple-element.190) | copy-start | bytes 884740
  654.9 83.0 %copy-start.90 = (bf16[128,32]{0,1:T(8,128)(2,1)S(1)}, bf16[128,32]{0,1:T(8,128)(2,1)}, u32[]{:S(2)}) copy-start(bf16[128,32]{0,1:T(8,128)(2,1)} %reshape.1953) | copy-start | bytes 24580
  745.6 19.2 %copy-start.19 = (f32[128,1152]{1,0:T(8,128)S(1)}, f32[128,1152]{1,0:T(8,128)}, u32[]{:S(2)}) copy-start(f32[128,1152]{1,0:T(8,128)} %copy-done.18) | copy-start | bytes 1769476
  745.6 19.2 %copy-start.83 = (f32[1152]{0:T(1024)S(1)}, f32[1152]{0:T(1024)}, u32[]{:S(2)}) copy-start(f32[1152]{0:T(1024)} %copy-done.82) | copy-start | bytes 13828
  745.6 19.2 %copy-start.126 = (f32[128]{0:T(128)S(1)}, f32[128]{0:T(128)}, u32[]{:S(2)}) copy-start(f32[128]{0:T(128)} %copy-done.125) | copy-start | bytes 1540
  745.6 19.2 %copy-start.128 = (f32[128]{0:T(128)S(1)}, f32[128]{0:T(128)}, u32[]{:S(2)}) copy-start(f32[128]{0:T(128)} %copy-done.127) | copy-start | bytes 1540
  745.6 19.6 %copy-start.30 = (f32[1,128,1152]{2,1,0:T(8,128)S(1)}, f32[1,128,1152]{2,1,0:T(8,128)}, u32[]{:S(2)}) copy-start(f32[1,128,1152]{2,1,0:T(8,128)} %copy-done.29) | copy-start | bytes 1769476
  768.7 29.5 %copy-start.67 = (bf16[1,9,6912]{2,0,1:T(2,128)(2,1)S(1)}, bf16[1,9,6912]{2,0,1:T(2,128)(2,1)}, u32[]{:S(2)}) copy-start(bf16[1,9,6912]{2,0,1:T(2,128)(2,1)} %copy-done.66) | copy-start | bytes 373252
  (138 other events, 854.9 us)
Sparse Core Ops, SparseCore 0:
  60.3 59.0 all-gather.2
  122.2 50.8 all-gather.4

commit v2 on v1

--- a/solution.py
+++ b/solution.py
@@ -103,81 +103,6 @@
         {"ty": lax.rem(y + 3, 4)},
         {"ty": lax.rem(y + 2, 4)},
     )
-
-
-def gather_kernel(x_ref, o_ref, ss, rs):
-    tokens = x_ref.shape[0]
-    half = (tokens // 2 + 15) // 16 * 16
-    c, y = lax.axis_index("tx"), lax.axis_index("ty")
-    sib, up, down, _ = ring_peers()
-    enter([sib, up, down])
-    sems = (ss, rs)
-    me = c * 4 + y
-    above, below, across = (c * 4 + lax.rem(y + k, 4) for k in (1, 3, 2))
-    a1 = send(x_ref.at[0:half], o_ref.at[me, 0:half], sems, 0, up)
-    b1 = send(x_ref.at[half:tokens], o_ref.at[me, half:tokens], sems, 1, down)
-    a2 = send(x_ref.at[half:tokens], o_ref.at[me, half:tokens], sems, 2, up)
-    b2 = send(x_ref.at[0:half], o_ref.at[me, 0:half], sems, 3, down)
-    s0 = send(x_ref, o_ref.at[me], sems, 4, sib)
-    o_ref[me] = x_ref[...]
-    a1.wait_recv()
-    f1 = send(o_ref.at[below, 0:half], o_ref.at[below, 0:half], sems, 5, up)
-    b1.wait_recv()
-    f2 = send(o_ref.at[above, half:tokens], o_ref.at[above, half:tokens], sems, 6, down)
-    a2.wait_recv()
-    s1 = send(o_ref.at[below], o_ref.at[below], sems, 7, sib)
-    b2.wait_recv()
-    s2 = send(o_ref.at[above], o_ref.at[above], sems, 8, sib)
-    f1.wait_recv()
-    f2.wait_recv()
-    s3 = send(o_ref.at[across], o_ref.at[across], sems, 9, sib)
-    for copy in (s0, s1, s2, s3):
-        copy.wait()
-    for copy in (a1, a2, b1, b2, f1, f2):
-        copy.wait_send()
-
-
-def sum_kernel(x_ref, o_ref, sib_buf, mine, got, ss, rs):
-    c, y = lax.axis_index("tx"), lax.axis_index("ty")
-    sib, up, down, far = ring_peers()
-    enter([sib, up, down, far])
-    sems = (ss, rs)
-    to = {1: up, 2: far, 3: down}
-    order = (2, 1, 3, 0)
-    swaps = [
-        send(x_ref.at[(1 - c) * 4 + lax.rem(y + d, 4)], sib_buf.at[d], sems, d, sib) for d in order
-    ]
-    sends = {}
-    for d, swap in zip(order, swaps):
-        swap.wait_recv()
-        total = x_ref[c * 4 + lax.rem(y + d, 4)].astype(F32) + sib_buf[d].astype(F32)
-        if d:
-            mine[d] = total.astype(BF16)
-            sends[d] = send(mine.at[d], got.at[d], sems, 3 + d, to[d])
-        else:
-            o_ref[...] = total
-    for d in (1, 3, 2):
-        sends[d].wait_recv()
-        o_ref[...] = o_ref[...] + got[d].astype(F32)
-    for d in (1, 3, 2):
-        sends[d].wait_send()
-    for swap in swaps:
-        swap.wait_send()
-
-
-def gather_image(rows16, cid):
-    tokens = rows16.shape[1]
-    out = jax.ShapeDtypeStruct((8, tokens, D), BF16)
-    parts = collective(gather_kernel, cid, out, dma_sems(10), rows16[0])
-    return parts.reshape(1, 8 * tokens, D)
-
-
-def sum_image(partial_value, cid):
-    tokens = partial_value.shape[1] // 8
-    out = jax.ShapeDtypeStruct((tokens, D), F32)
-    scratch = [pltpu.VMEM((4, tokens, D), BF16)] * 3 + dma_sems(8)
-    parts = partial_value.astype(BF16).reshape(8, tokens, D)
-    return collective(sum_kernel, cid, out, scratch, parts)[None]
 
 
 def spread_kernel(w_ref, m_ref, s_ref, w_out, m_out, s_out, m_got, m_two, ss, rs):
@@ -347,10 +272,6 @@
     )
 
 
-def smooth_gate(value_rows):
-    return jax.nn.gelu(value_rows, approximate=True)
-
-
 def sincos_table(row_pos, col_pos, width):
     quarter = width // 4
     freqs = jnp.power(10000.0, -jnp.arange(quarter, dtype=jnp.float32) / quarter)
@@ -384,10 +305,6 @@
     return shaped.transpose(0, 1, 3, 2, 4, 5).reshape(count, 2 * tile_rows, 2 * tile_cols, depth)
 
 
-def split_mod(mod, width):
-    return [mod[:, None, piece * width : (piece + 1) * width] for piece in range(6)]
-
-
 def compact_plan(routed, capacity):
     count, tokens = routed.shape
     flags = routed > 0
@@ -407,231 +324,491 @@
     return jax.vmap(lambda table, where: jnp.take(table, where, axis=0))(value_rows, index)
 
 
-def score_block(query, keys, key_marks, heads, scale):
-    count, rows, width = query.shape
-    size = width // heads
-    q_heads = query.reshape(count, rows, heads, size)
-    k_heads = keys.reshape(count, keys.shape[1], heads, size)
-    scores = (
-        jnp.einsum("bqhe,bkhe->bhqk", q_heads, k_heads, preferred_element_type=jnp.float32) * scale
-    )
-    return jnp.where(key_marks[:, None, None, :] > 0, scores, -1e30)
-
-
-def attend(query, keys, vals, key_marks, heads, scale):
-    count, rows, width = query.shape
-    size = width // heads
-    scores = score_block(query, keys, key_marks, heads, scale)
-    highest = jnp.max(scores, axis=-1, keepdims=True)
-    shifted = jnp.exp(scores - highest)
-    summed = jnp.sum(shifted, axis=-1, keepdims=True)
-    probs16 = (shifted / summed).astype(jnp.bfloat16)
-    log_sum = highest + jnp.log(summed)
-    v_heads = vals.reshape(count, vals.shape[1], heads, size)
-    attended = jnp.einsum("bhqk,bkhe->bqhe", probs16, v_heads, preferred_element_type=jnp.float32)
-    return (attended.reshape(count, rows, width).astype(jnp.bfloat16), log_sum)
-
-
-def attend_back(query, keys, vals, key_marks, log_sum, attended_grad16, heads, scale):
-    count, rows, width = query.shape
-    size = width // heads
-    key_count = keys.shape[1]
-    scores = score_block(query, keys, key_marks, heads, scale)
-    probs = jnp.exp(scores - log_sum)
-    probs16 = probs.astype(jnp.bfloat16)
-    grad_heads = attended_grad16.reshape(count, rows, heads, size)
-    v_heads = vals.reshape(count, key_count, heads, size)
-    k_heads = keys.reshape(count, key_count, heads, size)
-    q_heads = query.reshape(count, rows, heads, size)
-    grad_probs = jnp.einsum(
-        "bqhe,bkhe->bhqk", grad_heads, v_heads, preferred_element_type=jnp.float32
-    )
-    grad_values = jnp.einsum(
-        "bhqk,bqhe->bkhe", probs16, grad_heads, preferred_element_type=jnp.float32
-    )
-    weighted = jnp.sum(probs * grad_probs, axis=-1, keepdims=True)
-    score_grad16 = (probs * (grad_probs - weighted)).astype(jnp.bfloat16)
-    grad_query = (
-        jnp.einsum("bhqk,bkhe->bqhe", score_grad16, k_heads, preferred_element_type=jnp.float32)
-        * scale
-    )
-    grad_keys = (
-        jnp.einsum("bhqk,bqhe->bkhe", score_grad16, q_heads, preferred_element_type=jnp.float32)
-        * scale
-    )
-    return (
-        grad_query.reshape(count, rows, width),
-        grad_keys.reshape(count, key_count, width),
-        grad_values.reshape(count, key_count, width),
-    )
-
-
-def spread_forward(value_rows, mod, params, biases, marks_all, scale, cid):
-    attn_p, merge_p, expand_p, reduce_p = params
-    attn_b, merge_b, expand_b, reduce_b = biases
-    width = value_rows.shape[2]
-    head_width = attn_p.shape[2]
-    hidden_width = expand_p.shape[1]
-    heads = head_width // (D // HEADS)
-    group = lax.axis_index(("tx", "ty"))
-    shift1, scale1, gate1, shift2, scale2, gate2 = split_mod(mod, width)
-    normed1, inv_one = layer_stats(value_rows)
-    input16 = (normed1 * (1.0 + scale1) + shift1).astype(jnp.bfloat16)
-    input_all = gather_image(input16, cid + 0)
-    joined = jnp.einsum("btd,dke->btke", input_all, attn_p, preferred_element_type=jnp.float32)
-    q_bias = lax.dynamic_slice_in_dim(attn_b, group * head_width, head_width).astype(jnp.float32)
-    v_bias = lax.dynamic_slice_in_dim(attn_b, width + group * head_width, head_width).astype(
-        jnp.float32
-    )
-    query = (joined[:, :, 0] + q_bias).astype(jnp.bfloat16)
-    keys = joined[:, :, 1].astype(jnp.bfloat16)
-    vals = (joined[:, :, 2] + v_bias).astype(jnp.bfloat16)
-    attended, log_sum = attend(query, keys, vals, marks_all, heads, scale)
-    branch = sum_image(
-        jnp.einsum("bth,dh->btd", attended, merge_p, preferred_element_type=jnp.float32),
-        cid + 2,
-    )
-    branch = branch + merge_b.astype(jnp.float32)
-    middle = value_rows + gate1 * branch
-    normed2, inv_two = layer_stats(middle)
-    second16 = (normed2 * (1.0 + scale2) + shift2).astype(jnp.bfloat16)
-    second_all = gather_image(second16, cid + 1)
-    e_bias = lax.dynamic_slice_in_dim(expand_b, group * hidden_width, hidden_width).astype(
-        jnp.float32
-    )
-    pre = (
-        jnp.einsum("btd,df->btf", second_all, expand_p, preferred_element_type=jnp.float32)
-        + e_bias
-    )
-    hidden16 = smooth_gate(pre).astype(jnp.bfloat16)
-    mlp = sum_image(
-        jnp.einsum("btf,df->btd", hidden16, reduce_p, preferred_element_type=jnp.float32),
-        cid + 3,
-    )
-    mlp = mlp + reduce_b.astype(jnp.float32)
-    output = middle + gate2 * mlp
-    saved = (
-        normed1,
-        inv_one,
-        input_all,
-        query,
-        keys,
-        vals,
-        marks_all,
-        log_sum,
-        attended,
-        branch,
-        normed2,
-        inv_two,
-        second_all,
-        pre,
-        hidden16,
-        mlp,
-    )
-    return (output, saved)
-
-
-def spread_backward(upstream, saved, mod, params, marks, scale, cid):
-    attn_p, merge_p, expand_p, reduce_p = params
-    (
-        normed1,
-        inv_one,
-        input_all,
-        query,
-        keys,
-        vals,
-        marks_all,
-        log_sum,
-        attended,
-        branch,
-        normed2,
-        inv_two,
-        second_all,
-        pre,
-        hidden16,
-        mlp,
-    ) = saved
-    width = upstream.shape[2]
-    head_width = attn_p.shape[2]
-    hidden_width = expand_p.shape[1]
-    heads = head_width // (D // HEADS)
-    group = lax.axis_index(("tx", "ty"))
-    shift1, scale1, gate1, shift2, scale2, gate2 = split_mod(mod, width)
-    grad_out = upstream * marks[:, :, None]
-    grad_gate2 = jnp.sum(grad_out * mlp, axis=1)
-    mlp_grad16 = (grad_out * gate2).astype(jnp.bfloat16)
-    grad_reduce_b = jnp.sum(mlp_grad16.astype(jnp.float32), axis=(0, 1))
-    mlp_grad_all = gather_image(mlp_grad16, cid + 4)
-    grad_reduce_p = jnp.einsum(
-        "btd,btf->df", mlp_grad_all, hidden16, preferred_element_type=jnp.float32
-    )
-    grad_hidden = jnp.einsum(
-        "btd,df->btf", mlp_grad_all, reduce_p, preferred_element_type=jnp.float32
-    )
-    gate_value, gate_pull = jax.vjp(smooth_gate, pre)
-    pre_grad16 = gate_pull(grad_hidden)[0].astype(jnp.bfloat16)
-    grad_expand_p = jnp.einsum(
-        "btd,btf->df", second_all, pre_grad16, preferred_element_type=jnp.float32
+def rows_at(index, tokens):
+    return pl.ds(pl.multiple_of(index * tokens, 16), tokens)
+
+
+def ring_scratch(tokens):
+    half = (tokens // 2 + 15) // 16 * 16
+    return [
+        pltpu.VMEM((4, tokens, D), F32),
+        pltpu.VMEM((4, tokens, D), BF16),
+        pltpu.VMEM((4, tokens, D), BF16),
+        pltpu.VMEM((3, tokens, D), BF16),
+        pltpu.VMEM((2, tokens, D), BF16),
+        pltpu.VMEM((half, D), BF16),
+        pltpu.VMEM((tokens - half, D), BF16),
+        pltpu.SemaphoreType.DMA((20,)),
+        pltpu.SemaphoreType.DMA((20,)),
+    ]
+
+
+class Ring:
+    def __init__(self, tokens, scratch):
+        self.tokens = tokens
+        self.half = (tokens // 2 + 15) // 16 * 16
+        self.kept, self.sib_out, self.sib_in, self.out, self.got = scratch[:5]
+        self.far_low, self.far_high = scratch[5:7]
+        self.sems = tuple(scratch[7:9])
+        c, y = lax.axis_index("tx"), lax.axis_index("ty")
+        self.sib, self.up, self.down, _ = ring_peers()
+        self.own = [c * 4 + lax.rem(y + d, 4) for d in range(4)]
+        self.other = [(1 - c) * 4 + lax.rem(y + d, 4) for d in range(4)]
+        self.sent = []
+
+    def enter(self):
+        enter([self.sib, self.up, self.down])
+
+    def send(self, src, dst, k, peer):
+        copy = send(src, dst, self.sems, k, peer)
+        self.sent.append(copy)
+        return copy
+
+    def rows(self, index, start=0, stop=None):
+        stop = self.tokens if stop is None else stop
+        at = pl.multiple_of(index * self.tokens + start, 16)
+        return pl.ds(at, stop - start)
+
+    def gather(self, x_ref, all_ref, visit):
+        half, tokens = self.half, self.tokens
+        me, above, across, below = self.own
+        first, last = slice(0, half), slice(half, tokens)
+
+        def pass_on(index, k, peer, start=0, stop=None):
+            part = all_ref.at[self.rows(index, start, stop)]
+            return self.send(part, part, k, peer)
+
+        def own_part(rows, k, peer):
+            part = all_ref.at[self.rows(me, rows.start, rows.stop)]
+            return self.send(x_ref.at[rows], part, k, peer)
+
+        a1 = own_part(first, 0, self.up)
+        b1 = own_part(last, 1, self.down)
+        a2 = own_part(last, 2, self.up)
+        b2 = own_part(first, 3, self.down)
+        s0 = self.send(x_ref, all_ref.at[self.rows(me)], 4, self.sib)
+        all_ref[self.rows(me), :] = x_ref[...]
+        visit(True, 0)
+        s0.wait_recv()
+        visit(False, 0)
+        a1.wait_recv()
+        f1 = pass_on(below, 5, self.up, 0, half)
+        b1.wait_recv()
+        f2 = pass_on(above, 6, self.down, half, tokens)
+        a2.wait_recv()
+        s1 = pass_on(below, 7, self.sib)
+        b2.wait_recv()
+        s2 = pass_on(above, 8, self.sib)
+        visit(True, 3)
+        visit(True, 1)
+        s1.wait_recv()
+        visit(False, 3)
+        s2.wait_recv()
+        visit(False, 1)
+        f1.wait_recv()
+        f2.wait_recv()
+        s3 = pass_on(across, 9, self.sib)
+        visit(True, 2)
+        s3.wait_recv()
+        visit(False, 2)
+
+    def put(self, own, d, value):
+        if own:
+            self.kept[d] = value
+        else:
+            self.sib_out[d] = value.astype(BF16)
+            self.swaps[d] = self.send(self.sib_out.at[d], self.sib_in.at[d], 10 + d, self.sib)
+
+    def start_sums(self):
+        self.swaps = {}
+
+    def chip_sum(self, d):
+        self.swaps[d].wait_recv()
+        return self.kept[d] + self.sib_in[d].astype(F32)
+
+    def near(self):
+        half = self.half
+        first, last = slice(0, half), slice(half, self.tokens)
+        total = self.chip_sum(1)
+        self.kept[1] = total
+        self.out[0, last] = total[half:].astype(BF16)
+        self.n1 = self.send(self.out.at[0, last], self.got.at[0, last], 14, self.up)
+        total = self.chip_sum(3)
+        self.kept[3] = total
+        self.out[1, first] = total[:half].astype(BF16)
+        self.n2 = self.send(self.out.at[1, first], self.got.at[1, first], 15, self.down)
+
+    def far(self):
+        half = self.half
+        self.out[2] = self.chip_sum(2).astype(BF16)
+        self.f1 = self.send(self.out.at[2, 0:half], self.far_low, 16, self.up)
+        self.f2 = self.send(self.out.at[2, half : self.tokens], self.far_high, 17, self.down)
+
+    def relay(self):
+        half = self.half
+        first, last = slice(0, half), slice(half, self.tokens)
+        self.f1.wait_recv()
+        self.out[0, first] = (self.kept[1, first] + self.far_low[...].astype(F32)).astype(BF16)
+        self.r1 = self.send(self.out.at[0, first], self.got.at[0, first], 18, self.up)
+        self.f2.wait_recv()
+        self.out[1, last] = (self.kept[3, last] + self.far_high[...].astype(F32)).astype(BF16)
+        self.r2 = self.send(self.out.at[1, last], self.got.at[1, last], 19, self.down)
+
+    def total(self):
+        value = self.chip_sum(0)
+        for copy in (self.n1, self.n2, self.r1, self.r2):
+            copy.wait_recv()
+        return value + self.got[0].astype(F32) + self.got[1].astype(F32)
+
+    def leave(self):
+        for copy in self.sent:
+            copy.wait_send()
+
+
+def dot_nn(left, right):
+    return lax.dot_general(left, right, (((1,), (0,)), ((), ())), preferred_element_type=F32)
+
+
+def dot_nt(left, right):
+    return lax.dot_general(left, right, (((1,), (1,)), ((), ())), preferred_element_type=F32)
+
+
+def dot_tn(left, right):
+    return lax.dot_general(left, right, (((0,), (0,)), ((), ())), preferred_element_type=F32)
+
+
+def gelu_both(pre):
+    root = 0.7978845608028654
+    square = pre * pre
+    bent = jnp.tanh(root * pre * (1.0 + 0.044715 * square))
+    value = 0.5 * pre * (1.0 + bent)
+    slope = 0.5 * (1.0 + bent) + 0.5 * pre * (1.0 - bent * bent) * root * (1.0 + 0.134145 * square)
+    return value, slope
+
+
+def ffn_forward_kernel(
+    x_ref, vec_ref, bias_ref, we_ref, wr_ref, out_ref, mlp_ref, all_ref, hid_ref, slope_ref, x16, *scratch
+):
+    tokens = x_ref.shape[0]
+    ring = Ring(tokens, scratch)
+    normed, _ = layer_stats(x_ref[...])
+    x16[...] = (normed * (1.0 + vec_ref[1:2]) + vec_ref[0:1]).astype(BF16)
+    ring.enter()
+    ring.start_sums()
+
+    def visit(own, d):
+        rows = ring.rows((ring.own if own else ring.other)[d])
+        pre = dot_nn(all_ref[rows, :], we_ref[...]) + bias_ref[...]
+        value, slope = gelu_both(pre)
+        hidden = value.astype(BF16)
+        hid_ref[rows, :] = hidden
+        slope_ref[rows, :] = slope.astype(BF16)
+        ring.put(own, d, dot_nt(hidden, wr_ref[...]))
+        if not own and d == 1:
+            ring.near()
+
+    ring.gather(x16, all_ref, visit)
+    ring.far()
+    ring.relay()
+    mlp = ring.total() + vec_ref[3:4]
+    mlp_ref[...] = mlp
+    out_ref[...] = x_ref[...] + vec_ref[2:3] * mlp
+    ring.leave()
+
+
+def ffn_forward(x, vecs, bias, we, wr, cid):
+    tokens = x.shape[0]
+    outs = (
+        jax.ShapeDtypeStruct((tokens, D), F32),
+        jax.ShapeDtypeStruct((tokens, D), F32),
+        jax.ShapeDtypeStruct((8 * tokens, D), BF16),
+        jax.ShapeDtypeStruct((8 * tokens, FW), BF16),
+        jax.ShapeDtypeStruct((8 * tokens, FW), BF16),
+    )
+    scratch = [pltpu.VMEM((tokens, D), BF16)] + ring_scratch(tokens)
+    return collective(ffn_forward_kernel, cid, outs, scratch, x, vecs, bias, we, wr)
+
+
+def sum_rows(value):
+    return jnp.sum(value, axis=0, keepdims=True)
+
+
+def ffn_backward_kernel(
+    g_ref, x_ref, mlp_ref, vec_ref, valid_ref, second_ref, hid_ref, slope_ref, we_ref, wr_ref,
+    out_ref, vecs_ref, bias_ref, dw_ref, g16, g_all, pre_all, *scratch
+):
+    tokens = x_ref.shape[0]
+    ring = Ring(tokens, scratch)
+    grad = g_ref[...] * valid_ref[...]
+    g16[...] = (grad * vec_ref[2:3]).astype(BF16)
+    ring.enter()
+    ring.start_sums()
+    bias_ref[...] = jnp.zeros_like(bias_ref)
+
+    def visit(own, d):
+        rows = ring.rows((ring.own if own else ring.other)[d])
+        pre_grad = (
+            dot_nn(g_all[rows, :], wr_ref[...]) * slope_ref[rows, :].astype(F32)
+        ).astype(BF16)
+        pre_all[rows, :] = pre_grad
+        bias_ref[...] += sum_rows(pre_grad.astype(F32))
+        ring.put(own, d, dot_nt(pre_grad, we_ref[...]))
+        if not own and d == 1:
+            ring.near()
+
+    ring.gather(g16, g_all, visit)
+    ring.far()
+    vecs_ref[2:3] = sum_rows(grad * mlp_ref[...])
+    vecs_ref[3:4] = sum_rows(g16[...].astype(F32))
+    vecs_ref[4:8] = jnp.zeros((4, D), F32)
+    ring.relay()
+
+    @pl.loop(0, D // 128)
+    def _(k):
+        at = pl.ds(pl.multiple_of(k * 128, 128), 128)
+        dw_ref[at, :] = jnp.concatenate(
+            [
+                dot_tn(second_ref[:, at], pre_all[...]),
+                dot_tn(g_all[:, at], hid_ref[...]),
+            ],
+            axis=1,
+        ).astype(BF16)
+
+    second_grad = ring.total()
+    normed, inv_std = layer_stats(x_ref[...])
+    vecs_ref[0:1] = sum_rows(second_grad)
+    vecs_ref[1:2] = sum_rows(second_grad * normed)
+    out_ref[...] = grad + layer_back(second_grad * (1.0 + vec_ref[1:2]), normed, inv_std)
+    ring.leave()
+
+
+def ffn_backward(g, x, mlp, vecs, valid, second, hid, slope, we, wr, cid):
+    tokens = x.shape[0]
+    outs = (
+        jax.ShapeDtypeStruct((tokens, D), F32),
+        jax.ShapeDtypeStruct((8, D), F32),
+        jax.ShapeDtypeStruct((1, FW), F32),
+        jax.ShapeDtypeStruct((D, FFN_COLS), BF16),
+    )
+    scratch = [
+        pltpu.VMEM((tokens, D), BF16),
+        pltpu.VMEM((8 * tokens, D), BF16),
+        pltpu.VMEM((8 * tokens, FW), BF16),
+    ] + ring_scratch(tokens)
+    return collective(
+        ffn_backward_kernel, cid, outs, scratch, g, x, mlp, vecs, valid, second, hid, slope, we, wr
+    )
+
+
+HEAD = D // HEADS
+SCALE = HEAD ** (-0.5)
+
+
+def head_cols(h, start=0):
+    return slice(start + h * HEAD, start + (h + 1) * HEAD)
+
+
+def attn_forward_kernel(
+    x_ref, vec_ref, bias_ref, mask_ref, wqkv_ref, wm_ref,
+    out_ref, branch_ref, all_ref, q_ref, k_ref, v_ref, lse_ref, att_ref, x16, *scratch
+):
+    tokens = x_ref.shape[0]
+    ring = Ring(tokens, scratch)
+    normed, _ = layer_stats(x_ref[...])
+    x16[...] = (normed * (1.0 + vec_ref[1:2]) + vec_ref[0:1]).astype(BF16)
+    ring.enter()
+    ring.start_sums()
+
+    def visit(own, d):
+        rows = ring.rows((ring.own if own else ring.other)[d])
+        joined = (dot_nn(all_ref[rows, :], wqkv_ref[...]) + bias_ref[...]).astype(BF16)
+        for h in range(2):
+            q_ref[h, rows, :] = joined[:, head_cols(h)]
+            k_ref[h, rows, :] = joined[:, head_cols(h, HW)]
+            v_ref[h, rows, :] = joined[:, head_cols(h, 2 * HW)]
+
+    def attend(own, d):
+        rows = ring.rows((ring.own if own else ring.other)[d])
+        parts = []
+        for h in range(2):
+            scores = dot_nt(q_ref[h, rows, :], k_ref[h]) * SCALE + mask_ref[...]
+            highest = jnp.max(scores, axis=-1, keepdims=True)
+            shifted = jnp.exp(scores - highest)
+            summed = jnp.sum(shifted, axis=-1, keepdims=True)
+            probs = (shifted * (1.0 / summed)).astype(BF16)
+            lse_ref[rows, h : h + 1] = highest + jnp.log(summed)
+            parts.append(dot_nn(probs, v_ref[h]).astype(BF16))
+        attended = jnp.concatenate(parts, axis=1)
+        att_ref[rows, :] = attended
+        ring.put(own, d, dot_nt(attended, wm_ref[...]))
+
+    ring.gather(x16, all_ref, visit)
+    attend(False, 2)
+    attend(True, 2)
+    ring.far()
+    for d in (1, 3):
+        attend(False, d)
+        attend(True, d)
+    ring.near()
+    ring.relay()
+    attend(False, 0)
+    attend(True, 0)
+    branch = ring.total() + vec_ref[3:4]
+    branch_ref[...] = branch
+    out_ref[...] = x_ref[...] + vec_ref[2:3] * branch
+    ring.leave()
+
+
+def attn_forward(x, vecs, bias, mask, wqkv, wm, cid):
+    tokens = x.shape[0]
+    heads = jax.ShapeDtypeStruct((2, 8 * tokens, HEAD), BF16)
+    outs = (
+        jax.ShapeDtypeStruct((tokens, D), F32),
+        jax.ShapeDtypeStruct((tokens, D), F32),
+        jax.ShapeDtypeStruct((8 * tokens, D), BF16),
+        heads,
+        heads,
+        heads,
+        jax.ShapeDtypeStruct((8 * tokens, 2), F32),
+        jax.ShapeDtypeStruct((8 * tokens, HW), BF16),
+    )
+    scratch = [pltpu.VMEM((tokens, D), BF16)] + ring_scratch(tokens)
+    return collective(attn_forward_kernel, cid, outs, scratch, x, vecs, bias, mask, wqkv, wm)
+
+
+def attn_backward_kernel(
+    g_ref, x_ref, branch_ref, vec_ref, mask_ref, in_ref, q_ref, k_ref, v_ref, lse_ref, att_ref,
+    wqkv_ref, wm_ref, out_ref, vecs_ref, bias_ref, dw_ref,
+    g16, g_all, joined, dk, dv, *scratch
+):
+    tokens = x_ref.shape[0]
+    ring = Ring(tokens, scratch)
+    g16[...] = (g_ref[...] * vec_ref[2:3]).astype(BF16)
+    ring.enter()
+    ring.start_sums()
+    dk[...] = jnp.zeros_like(dk)
+    dv[...] = jnp.zeros_like(dv)
+
+    def visit(own, d):
+        rows = ring.rows((ring.own if own else ring.other)[d])
+        grad = dot_nn(g_all[rows, :], wm_ref[...]).astype(BF16)
+        queries = []
+        for h in range(2):
+            part = grad[:, head_cols(h)]
+            query = q_ref[h, rows, :]
+            scores = dot_nt(query, k_ref[h]) * SCALE + mask_ref[...]
+            probs = jnp.exp(scores - lse_ref[rows, h : h + 1])
+            grad_probs = dot_nt(part, v_ref[h])
+            weighted = jnp.sum(probs * grad_probs, axis=-1, keepdims=True)
+            score_grad = (probs * (grad_probs - weighted)).astype(BF16)
+            queries.append((dot_nn(score_grad, k_ref[h]) * SCALE).astype(BF16))
+            dk[h] += dot_tn(score_grad, query)
+            dv[h] += dot_tn(probs.astype(BF16), part)
+        joined[rows, 0:HW] = jnp.concatenate(queries, axis=1)
+
+    def back(own, d):
+        rows = ring.rows((ring.own if own else ring.other)[d])
+        ring.put(own, d, dot_nt(joined[rows, :], wqkv_ref[...]))
+
+    ring.gather(g16, g_all, visit)
+    later = [(dk[h] * SCALE).astype(BF16) for h in range(2)] + [dv[h].astype(BF16) for h in range(2)]
+    joined[:, HW : 3 * HW] = jnp.concatenate(later, axis=1)
+    back(False, 2)
+    back(True, 2)
+    ring.far()
+    for d in (1, 3):
+        back(False, d)
+        back(True, d)
+    ring.near()
+    back(False, 0)
+    back(True, 0)
+    bias_ref[...] = sum_rows(joined[...].astype(F32))
+    vecs_ref[2:3] = sum_rows(g_ref[...] * branch_ref[...])
+    vecs_ref[3:4] = sum_rows(g16[...].astype(F32))
+    vecs_ref[4:8] = jnp.zeros((4, D), F32)
+    ring.relay()
+
+    @pl.loop(0, D // 128)
+    def _(k):
+        at = pl.ds(pl.multiple_of(k * 128, 128), 128)
+        dw_ref[at, :] = jnp.concatenate(
+            [
+                dot_tn(in_ref[:, at], joined[...]),
+                dot_tn(g_all[:, at], att_ref[...]),
+                jnp.zeros((128, ATT_COLS - 4 * HW), F32),
+            ],
+            axis=1,
+        ).astype(BF16)
+
+    input_grad = ring.total()
+    normed, inv_std = layer_stats(x_ref[...])
+    vecs_ref[0:1] = sum_rows(input_grad)
+    vecs_ref[1:2] = sum_rows(input_grad * normed)
+    out_ref[...] = g_ref[...] + layer_back(input_grad * (1.0 + vec_ref[1:2]), normed, inv_std)
+    ring.leave()
+
+
+def attn_backward(g, x, branch, vecs, mask, inputs, q, k, v, lse, att, wqkv, wm, cid):
+    tokens = x.shape[0]
+    outs = (
+        jax.ShapeDtypeStruct((tokens, D), F32),
+        jax.ShapeDtypeStruct((8, D), F32),
+        jax.ShapeDtypeStruct((1, 3 * HW), F32),
+        jax.ShapeDtypeStruct((D, ATT_COLS), BF16),
+    )
+    scratch = [
+        pltpu.VMEM((tokens, D), BF16),
+        pltpu.VMEM((8 * tokens, D), BF16),
+        pltpu.VMEM((8 * tokens, 3 * HW), BF16),
+        pltpu.VMEM((2, 8 * tokens, HEAD), F32),
+        pltpu.VMEM((2, 8 * tokens, HEAD), F32),
+    ] + ring_scratch(tokens)
+    operands = (g, x, branch, vecs, mask, inputs, q, k, v, lse, att, wqkv, wm)
+    return collective(attn_backward_kernel, cid, outs, scratch, *operands)
+
+
+def block_forward(x, mod, params, biases, mask, cid):
+    wqkv, wm, we, wr = params
+    attn_b, merge_b, expand_b, reduce_b = (b.astype(F32) for b in biases)
+    group = own_group()
+    zeros = jnp.zeros((4, D), F32)
+    vec_one = jnp.concatenate([mod[0:3], merge_b[None], zeros])
+    vec_two = jnp.concatenate([mod[3:6], reduce_b[None], zeros])
+    bias = jnp.concatenate(
+        [
+            lax.dynamic_slice_in_dim(attn_b, group * HW, HW),
+            jnp.zeros((HW,), F32),
+            lax.dynamic_slice_in_dim(attn_b, D + group * HW, HW),
+        ]
+    )[None]
+    middle, branch, *kept = attn_forward(x, vec_one, bias, mask, wqkv, wm, cid)
+    e_bias = lax.dynamic_slice_in_dim(expand_b, group * FW, FW)[None]
+    output, mlp, *more = ffn_forward(middle, vec_two, e_bias, we, wr, cid + 1)
+    return output, (x, vec_one, mask, middle, branch, kept, vec_two, mlp, more)
+
+
+def block_backward(grad, saved, params, valid, cid):
+    x, vec_one, mask, middle, branch, kept, vec_two, mlp, more = saved
+    wqkv, wm, we, wr = params
+    group = own_group()
+    grad, mod_two, bias_two, dw_ffn = ffn_backward(
+        grad, middle, mlp, vec_two, valid, *more, we, wr, cid + 2
+    )
+    grad, mod_one, bias_one, dw_attn = attn_backward(
+        grad, x, branch, vec_one, mask, *kept, wqkv, wm, cid + 3
     )
     grad_expand_b = lax.dynamic_update_slice_in_dim(
-        jnp.zeros((FF,), jnp.float32),
-        jnp.sum(pre_grad16.astype(jnp.float32), axis=(0, 1)),
-        group * hidden_width,
-        0,
-    )
-    grad_second = sum_image(
-        jnp.einsum("btf,df->btd", pre_grad16, expand_p, preferred_element_type=jnp.float32),
-        cid + 5,
-    )
-    grad_shift2 = jnp.sum(grad_second, axis=1)
-    grad_scale2 = jnp.sum(grad_second * normed2, axis=1)
-    grad_middle = grad_out + layer_back(grad_second * (1.0 + scale2), normed2, inv_two)
-    grad_gate1 = jnp.sum(grad_middle * branch, axis=1)
-    branch_grad16 = (grad_middle * gate1).astype(jnp.bfloat16)
-    grad_merge_b = jnp.sum(branch_grad16.astype(jnp.float32), axis=(0, 1))
-    branch_grad_all = gather_image(branch_grad16, cid + 6)
-    grad_merge_p = jnp.einsum(
-        "btd,bth->dh", branch_grad_all, attended, preferred_element_type=jnp.float32
-    )
-    attended_grad16 = jnp.einsum(
-        "btd,dh->bth", branch_grad_all, merge_p, preferred_element_type=jnp.float32
-    ).astype(jnp.bfloat16)
-    grad_query, grad_keys, grad_values = attend_back(
-        query, keys, vals, marks_all, log_sum, attended_grad16, heads, scale
-    )
-    joined_grad16 = jnp.stack([grad_query, grad_keys, grad_values], axis=2).astype(jnp.bfloat16)
-    grad_attn_p = jnp.einsum(
-        "btd,btke->dke", input_all, joined_grad16, preferred_element_type=jnp.float32
-    )
-    bias_zero = jnp.zeros((2 * width,), jnp.float32)
+        jnp.zeros((FF,), F32), bias_two[0], group * FW, 0
+    )
     grad_attn_b = lax.dynamic_update_slice_in_dim(
-        bias_zero,
-        jnp.sum(joined_grad16[:, :, 0].astype(jnp.float32), axis=(0, 1)),
-        group * head_width,
-        0,
+        jnp.zeros((2 * D,), F32), bias_one[0, :HW], group * HW, 0
     )
     grad_attn_b = lax.dynamic_update_slice_in_dim(
-        grad_attn_b,
-        jnp.sum(joined_grad16[:, :, 2].astype(jnp.float32), axis=(0, 1)),
-        width + group * head_width,
-        0,
-    )
-    grad_input = sum_image(
-        jnp.einsum("btke,dke->btd", joined_grad16, attn_p, preferred_element_type=jnp.float32),
-        cid + 7,
-    )
-    grad_shift1 = jnp.sum(grad_input, axis=1)
-    grad_scale1 = jnp.sum(grad_input * normed1, axis=1)
-    grad_values_in = grad_middle + layer_back(grad_input * (1.0 + scale1), normed1, inv_one)
-    grad_mod = jnp.concatenate(
-        [grad_shift1, grad_scale1, grad_gate1, grad_shift2, grad_scale2, grad_gate2], axis=-1
-    )
-    return (
-        grad_values_in,
-        grad_mod,
-        (grad_attn_p, grad_merge_p, grad_expand_p, grad_reduce_p),
-        (grad_attn_b, grad_merge_b, grad_expand_b, grad_reduce_b),
-    )
+        grad_attn_b, bias_one[0, 2 * HW :], D + group * HW, 0
+    )
+    mod_grad = jnp.concatenate([mod_one[0:3].reshape(-1), mod_two[0:3].reshape(-1)])
+    biases = (grad_attn_b, mod_one[3], grad_expand_b, mod_two[3])
+    return grad, mod_grad, (dw_attn, dw_ffn), biases
 
 
 def pack_weights(attention_weight, merge_weight, expand_weight, reduce_weight):
@@ -665,18 +842,7 @@
 
 
 def block_params(attn, ffn):
-    return (
-        attn[:, : 3 * HW].reshape(D, 3, HW),
-        attn[:, 3 * HW : 4 * HW],
-        ffn[:, :FW],
-        ffn[:, FW:],
-    )
-
-
-def join_grads(grads):
-    attn, merge, expand, reduce = (g.astype(BF16) for g in grads)
-    spare = jnp.zeros((D, ATT_COLS - 4 * HW), BF16)
-    return jnp.concatenate([attn.reshape(D, 3 * HW), merge, spare, expand, reduce], axis=1)
+    return attn[:, : 3 * HW], attn[:, 3 * HW : 4 * HW], ffn[:, :FW], ffn[:, FW:]
 
 
 def pack_grads(one, two):
@@ -767,10 +933,8 @@
     routed_marks = jnp.arange(capacity, dtype=jnp.int32)[None, None, :] < tile_loads[:, :, None]
     routed_marks = routed_marks.astype(jnp.float32).reshape(count, tiles * capacity)
     everyone = jnp.ones((count, tile_tokens), jnp.float32)
-    everyone_all = jnp.ones((count, tiles * tile_tokens), jnp.float32)
     position, owner, valid = compact_plan(routed, capacity)
     width = D
-    scale = (D // HEADS) ** (-0.5)
     whole_index = lax.axis_index(DP_TX_TY)
     small_parts = (
         embed_weight,
@@ -840,13 +1004,17 @@
     second_params = block_params(second_all[:, :ATT_COLS], second_all[:, ATT_COLS:])
     first_biases = (attn_b[0], merge_b[0], expand_b[0], reduce_b[0])
     second_biases = (attn_b[1], merge_b[1], expand_b[1], reduce_b[1])
-    middle_one, saved_one = spread_forward(
-        initial_tokens, mod_one, first_params, first_biases, everyone_all, scale, 10
-    )
+    mask_one = jnp.zeros((1, tiles * tile_tokens), F32)
+    mask_two = jnp.where(routed_marks > 0, 0.0, -1e30).astype(F32)
+    middle_one, saved_one = block_forward(
+        initial_tokens[0], mod_one.reshape(6, D), first_params, first_biases, mask_one, 10
+    )
+    middle_one = middle_one[None]
     selected_rows = pick_rows(middle_one, owner)
-    middle_two, saved_two = spread_forward(
-        selected_rows, mod_two, second_params, second_biases, routed_marks, scale, 20
-    )
+    middle_two, saved_two = block_forward(
+        selected_rows[0], mod_two.reshape(6, D), second_params, second_biases, mask_two, 20
+    )
+    middle_two = middle_two[None]
     keep_mask = routed[:, :, None] > 0
     ended = jnp.where(keep_mask, pick_rows(middle_two, position), middle_one)
     head_shift = head_mod[:, None, :width]
@@ -868,15 +1036,16 @@
     )
     grad_ended = layer_back(grad_final * (1.0 + head_scale), normed_end, inv_end)
     grad_chosen = pick_rows(grad_ended, owner)
-    grad_two, mod_grad_two, weights_two, biases_two = spread_backward(
-        grad_chosen, saved_two, mod_two, second_params, valid, scale, 20
-    )
-    summed_two = reduce_rows(join_grads(weights_two), 4)
-    grad_middle = jnp.where(keep_mask, pick_rows(grad_two, position), grad_ended)
-    grad_start, mod_grad_one, weights_one, biases_one = spread_backward(
-        grad_middle, saved_one, mod_one, first_params, everyone, scale, 10
-    )
-    summed_one = reduce_rows(join_grads(weights_one), 5)
+    grad_two, mod_grad_two, weights_two, biases_two = block_backward(
+        grad_chosen[0], saved_two, second_params, valid[0][:, None], 20
+    )
+    summed_two = reduce_rows(jnp.concatenate(weights_two, axis=1), 4)
+    grad_middle = jnp.where(keep_mask, pick_rows(grad_two[None], position), grad_ended)
+    grad_start, mod_grad_one, weights_one, biases_one = block_backward(
+        grad_middle[0], saved_one, first_params, everyone[0][:, None], 10
+    )
+    grad_start = grad_start[None]
+    summed_one = reduce_rows(jnp.concatenate(weights_one, axis=1), 5)
     start_grad16 = grad_start.astype(jnp.bfloat16)
     grad_embed_w = jnp.einsum(
         "btp,btd->pd", patches, start_grad16, preferred_element_type=jnp.float32
@@ -901,7 +1070,7 @@
         axis=1,
     )
     small_out = jnp.pad(small_out, [(0, 0), (0, 1024 - small_out.shape[1])])
-    grad_mods = jnp.concatenate([mod_grad_one, mod_grad_two, head_grad_mod], axis=1)
+    grad_mods = jnp.concatenate([mod_grad_one, mod_grad_two, head_grad_mod[0]])
     grad_mods = jnp.pad(grad_mods.reshape(8, MOD_ALL // 8), [(0, 0), (0, 2048 - MOD_ALL // 8)])
     packed_grads, mod_back, small_back = finish(
         pack_grads(summed_one, summed_two),

time: 838 us -> 659 us (0.79)
  matrix products: 88.4 us -> 7.53 us
  local copies, waits for them, and re-layouts: 162 us -> 81.4 us
  other arithmetic: 46 us -> 17.1 us
  Pallas kernels: 517 us -> 531 us
    dot_general x32 -> x0, matrix products: 71.1 us -> none  [the longest x2 8.48 us: spread_backward(): jnp.einsum('btd,df->btf', mlp_grad_all, reduce_p, preferred_element_type=...]
    concatenate x8 -> x2, local copies, waits for them, and re-layouts: 31 us -> 0.08 us  [the longest x1 0.08 us: block_forward(): vec_one = jnp.concatenate([mod[0:3], merge_b[None], zeros])]
    pallas_call x21 -> x13, Pallas kernels: 517 us -> 531 us  [collective(): pl.pallas_call(kernel, out_shape=outs, in_specs=[VMEM] * len(operands), o...]
    convert_element_type x14 -> x16, local copies, waits for them, and re-layouts: 13.1 us -> 2.17 us  [block_forward(): attn_b, merge_b, expand_b, reduce_b = (b.astype(F32) for b in biases)]
    reduce_sum x12 -> x1, other arithmetic: 11 us -> 0.27 us  [shards(): jnp.sum(grad_final * normed_end, axis=1)]
    convert_element_type x10 -> x4, other arithmetic: 10.7 us -> 0.02 us  [block_forward(): attn_b, merge_b, expand_b, reduce_b = (b.astype(F32) for b in biases)]
    unnamed x4 -> x0, matrix products: 9.16 us -> none
    unnamed x368 -> x209, local copies, waits for them, and re-layouts: 17 us -> 25.1 us
  transfers between devices with their start and end apart: 2 -> 2, of which waited for: 0 -> 0; matrix products, arithmetic and copies ran while one was open for 10% -> 4% of each run, Pallas kernels for 14% -> 15%
where the time goes in v2:
time: 659 us; the launch traced here: 654 us
  Pallas kernels  531 us (81%)
  local copies, waits for them, and re-layouts  81.4 us (12%)
  other arithmetic  17.1 us (3%)
  between operations  16.6 us (3%)
  matrix products  7.53 us (1%)
    pallas_call x13, Pallas kernels, collective(): pl.pallas_call(kernel, out_shape=outs, in_specs=[VMEM] * len(operands), o...  531 us
    unnamed x209, local copies, waits for them, and re-layouts  25.1 us
  transfers between devices with their start and end apart: 2, of which 0 were waited for; matrix products, arithmetic and copies ran while one was open for 4% of the time, Pallas kernels for 15%

profile of v2, /device:TPU:1, one launch (start us, length us, event | category | flops | bytes accessed | tf_op | source)
XLA Modules:
  0.0 653.8 jit_solution(1640602345363154555)
XLA Ops:
  7.3 1.3 reshape.974
  15.7 37.5 %shard_map.342 = (bf16[8,64,512]{2,1,0:T(8,128)(2,1)S(1)}, f32[128,128]{1,0:T(8,128)S(1)}, bf16[8,16,16,128]{3,2,1,0:T(8,128)(2,1)S(1)}) custom-call(bf16[8,64,512]{2,1,0:T(8,128)(2,1)S(1)} %pad.35.w_ref, f32[16,128,128]{2,1,0:T(8,128)S(1)} %bitcast.362, bf16[16,128]{1,0:T(8,128)(2,1)S(1)} %pad_bitcast_fusion.3.s_ref), custom_call_target="tpu_custom_call" | custom-call | tf_op jit(solution)/shard_map/pallas_call | solution.py:86
  57.5 30.2 %shard_map.343 = bf16[16,80,640]{2,1,0:T(8,128)(2,1)S(1)} custom-call(bf16[80,640]{1,0:T(8,128)(2,1)S(1)} %pad.38.w_ref), custom_call_target="tpu_custom_call" | custom-call | tf_op jit(solution)/shard_map/pallas_call | solution.py:86
  89.4 1.3 reshape.1114
  97.9 1.7 scatter_custom_fusion
  100.7 34.3 %shard_map.344 = (f32[128,1152]{1,0:T(8,128)S(1)}, f32[128,1152]{1,0:T(8,128)S(1)}, bf16[1024,1152]{1,0:T(8,128)(2,1)}, bf16[2,1024,72]{2,1,0:T(8,128)(2,1)S(1)}...) custom-call(f32[128,1152]{1,0:T(8,128)S(1)} %fusion.1.x_ref, ...), custom_call_target="tpu_custom_call" | custom-call | tf_op jit(solution)/shard_map/pallas_call | solution.py:86
  141.3 1.2 fusion.9
  143.1 3.8 fusion.56
  146.8 34.6 %shard_map.345 = (f32[128,1152]{1,0:T(8,128)S(1)}, f32[128,1152]{1,0:T(8,128)S(1)}, bf16[1024,1152]{1,0:T(8,128)(2,1)}, bf16[1024,576]{1,0:T(8,128)(2,1)S(1)}, bf16[1024,576]{1,0:T(8,128)(2,1)S(1)}) custom-call(f32[128,1152]{1,0:T(8,128)S(1)} %get-tuple-element.72.x_ref, f32[8,1152]{1,0:T(8,128)S(1)} %get-tuple-element.266.vec_ref, ...), custom_call_target="tpu_custom_call" | custom-call | tf_op jit(solution)/shard_map/pallas_call | solution.py:86
  184.5 1.5 gather_fusion
  186.1 1.6 slice.366.wqkv_ref
  187.7 2.1 slice.367.wm_ref
  189.8 33.9 %shard_map.346 = (f32[112,1152]{1,0:T(8,128)S(1)}, f32[112,1152]{1,0:T(8,128)S(1)}, bf16[896,1152]{1,0:T(8,128)(2,1)}, bf16[2,896,72]{2,1,0:T(8,128)(2,1)S(1)}, ...) custom-call(f32[112,1152]{1,0:T(8,128)S(1)} %fusion.11.x_ref, ...), custom_call_target="tpu_custom_call" | custom-call | tf_op jit(solution)/shard_map/pallas_call | solution.py:86
  226.1 1.9 fusion.55
  227.9 32.5 %shard_map.347 = (f32[112,1152]{1,0:T(8,128)S(1)}, f32[112,1152]{1,0:T(8,128)S(1)}, bf16[896,1152]{1,0:T(8,128)(2,1)}, bf16[896,576]{1,0:T(8,128)(2,1)S(1)}, bf16[896,576]{1,0:T(8,128)(2,1)S(1)}) custom-call(f32[112,1152]{1,0:T(8,128)S(1)} %get-tuple-element.74.x_ref, f32[8,1152]{1,0:T(8,128)S(1)} %get-tuple-element.265.vec_ref, ...), custom_call_target="tpu_custom_call" | custom-call | tf_op jit(solution)/shard_map/pallas_call | solution.py:86
  263.3 2.1 gather_fusion.1
  265.4 1.3 fusion.53
  268.2 2.4 gather_fusion.2
  271.8 1.2 copy-done.20
  273.1 1.3 copy-done.22
  275.4 36.9 %shard_map.348 = (f32[112,1152]{1,0:T(8,128)S(1)}, f32[8,1152]{1,0:T(8,128)S(1)}, f32[1,576]{1,0:T(1,128)S(1)}, bf16[1152,1152]{1,0:T(8,128)(2,1)}) custom-call(f32[112,1152]{1,0:T(8,128)S(1)} %fusion.10.g_ref, f32[112,1152]{1,0:T(8,128)S(1)} %copy-done.14, f32[112,1152]{1,0:T(8,128)S(1)} %copy-done.40, f32[8,1152]{1,0:T(8,128)S(1)} %get-tuple-element.265.vec_ref, ...), custom_call_target="tpu_custom_call" | custom-call | tf_op jit(solution)/shard_map/pallas_call | solution.py:86
  312.4 34.0 %shard_map.349 = (f32[112,1152]{1,0:T(8,128)S(1)}, f32[8,1152]{1,0:T(8,128)S(1)}, f32[1,432]{1,0:T(1,128)S(1)}, bf16[1152,640]{1,0:T(8,128)(2,1)}) custom-call(f32[112,1152]{1,0:T(8,128)S(1)} %get-tuple-element.80.g_ref, f32[112,1152]{1,0:T(8,128)S(1)} %copy-done.10, f32[112,1152]{1,0:T(8,128)S(1)} %copy-done.38, f32[8,1152]{1,0:T(8,128)S(1)} %get-tuple-element.267.vec_ref, ...), custom_call_target="tpu_custom_call" | custom-call | tf_op jit(solution)/shard_map/pallas_call | solution.py:86
  346.4 1.7 pad_maximum_fusion.1
  348.3 72.5 %shard_map.353 = bf16[80,1792]{1,0:T(8,128)(2,1)S(1)} custom-call(bf16[16,80,1792]{2,1,0:T(8,128)(2,1)S(1)} %pad.40.g_ref), custom_call_target="tpu_custom_call" | custom-call | tf_op jit(solution)/shard_map/pallas_call | solution.py:86
  421.6 2.1 gather_fusion.3
  423.7 1.5 fusion.5.g_ref
  425.4 42.3 %shard_map.350 = (f32[128,1152]{1,0:T(8,128)S(1)}, f32[8,1152]{1,0:T(8,128)S(1)}, f32[1,576]{1,0:T(1,128)S(1)}, bf16[1152,1152]{1,0:T(8,128)(2,1)}) custom-call(f32[128,1152]{1,0:T(8,128)S(1)} %fusion.5.g_ref, f32[128,1152]{1,0:T(8,128)S(1)} %copy-done.12, f32[128,1152]{1,0:T(8,128)S(1)} %copy-done.26, f32[8,1152]{1,0:T(8,128)S(1)} %get-tuple-element.266.vec_ref, ...), custom_call_target="tpu_custom_call" | custom-call | tf_op jit(solution)/shard_map/pallas_call | solution.py:86
  467.8 38.8 %shard_map.351 = (f32[128,1152]{1,0:T(8,128)S(1)}, f32[8,1152]{1,0:T(8,128)S(1)}, f32[1,432]{1,0:T(1,128)S(1)}, bf16[1152,640]{1,0:T(8,128)(2,1)}) custom-call(f32[128,1152]{1,0:T(8,128)S(1)} %get-tuple-element.93.g_ref, f32[128,1152]{1,0:T(8,128)S(1)} %copy-done.8, f32[128,1152]{1,0:T(8,128)S(1)} %copy-done.24, f32[8,1152]{1,0:T(8,128)S(1)} %get-tuple-element.268.vec_ref, ...), custom_call_target="tpu_custom_call" | custom-call | tf_op jit(solution)/shard_map/pallas_call | solution.py:86
  506.7 1.7 pad_maximum_fusion
  508.7 78.0 %shard_map.352 = bf16[80,1792]{1,0:T(8,128)(2,1)S(1)} custom-call(bf16[16,80,1792]{2,1,0:T(8,128)(2,1)S(1)} %pad.39.g_ref), custom_call_target="tpu_custom_call" | custom-call | tf_op jit(solution)/shard_map/pallas_call | solution.py:86
  593.7 25.4 %shard_map.354 = (bf16[8,64,512]{2,1,0:T(8,128)(2,1)S(1)}, bf16[8,16,16,128]{3,2,1,0:T(8,128)(2,1)S(1)}, f32[8,128]{1,0:T(8,128)S(1)}) custom-call(bf16[8,64,512]{2,1,0:T(8,128)(2,1)S(1)} %pad.41.g_ref, f32[8,16,128]{2,1,0:T(8,128)S(1)} %bitcast.365, f32[16,8,8,128]{3,2,1,0:T(8,128)S(1)} %copy.264), custom_call_target="tpu_custom_call" | custom-call | tf_op jit(solution)/shard_map/pallas_call | solution.py:86
  628.9 1.7 convolution_bitcast_fusion.2
  (493 shorter events, 73.2 us)
Async XLA Ops:
  7.2 135.8 %all-gather.3.cloned.1.call-start = ((), (), s32[]{:S(2)}) async-start(), calls=%async_computation | async-start | bytes 2820096 | tf_op jit(solution)/shard_map/all_gather | solution.py:985
  54.6 131.5 %all-gather.5.cloned.1.call-start = ((), (), s32[]{:S(2)}) async-start(), calls=%async_computation.1 | async-start | bytes 4386816 | tf_op jit(solution)/shard_map/all_gather | solution.py:988
  56.4 31.5 %copy-start.55 = (bf16[1152,32]{1,0:T(8,128)(2,1)}, bf16[1152,32]{1,0:T(8,128)(2,1)S(1)}, u32[]{:S(2)}) copy-start(bf16[1152,32]{1,0:T(8,128)(2,1)S(1)} %reshape_reshape.13) | copy-start | bytes 221188
  88.0 12.7 %copy-start.2 = (bf16[1152,432]{1,0:T(8,128)(2,1)}, bf16[1152,432]{1,0:T(8,128)(2,1)S(1)}, u32[]{:S(2)}) copy-start(bf16[1152,432]{1,0:T(8,128)(2,1)S(1)} %slice.353.wqkv_ref) | copy-start | bytes 2985988
  88.2 12.4 %copy-start.5 = (bf16[1152,144]{1,0:T(8,128)(2,1)}, bf16[1152,144]{1,0:T(8,128)(2,1)S(1)}, u32[]{:S(2)}) copy-start(bf16[1152,144]{1,0:T(8,128)(2,1)S(1)} %slice.354.wm_ref) | copy-start | bytes 995332
  99.5 40.4 %copy-start.92 = (s32[112]{0:T(128)S(1)}, s32[112]{0:T(128)}, u32[]{:S(2)}) copy-start(s32[112]{0:T(128)} %scatter_custom_fusion) | copy-start | bytes 1348
  99.5 40.4 %copy-start.83 = (s32[1,128]{1,0:T(1,128)S(1)}, s32[1,128]{1,0:T(1,128)}, u32[]{:S(2)}) copy-start(s32[1,128]{1,0:T(1,128)} %copy-done.82) | copy-start | bytes 1540
  100.6 34.4 %copy-start.7 = (f32[128,1152]{1,0:T(8,128)}, f32[128,1152]{1,0:T(8,128)S(1)}, u32[]{:S(2)}) copy-start(f32[128,1152]{1,0:T(8,128)S(1)} %fusion.1.x_ref) | copy-start | bytes 1769476
  146.8 39.2 %copy-start.1 = (bf16[1152,576]{1,0:T(8,128)(2,1)}, bf16[1152,576]{1,0:T(8,128)(2,1)S(1)}, u32[]{:S(2)}) copy-start(bf16[1152,576]{1,0:T(8,128)(2,1)S(1)} %get-tuple-element.210.we_ref) | copy-start | bytes 3981316
  186.1 37.6 %copy-start.9 = (f32[112,1152]{1,0:T(8,128)}, f32[112,1152]{1,0:T(8,128)S(1)}, u32[]{:S(2)}) copy-start(f32[112,1152]{1,0:T(8,128)S(1)} %fusion.11.x_ref) | copy-start | bytes 1548292
  186.1 39.9 %copy-start.53 = (bf16[1152,1792]{1,0:T(8,128)(2,1)S(1)}, bf16[1152,1792]{1,0:T(8,128)(2,1)}, u32[]{:S(2)}) copy-start(bf16[1152,1792]{1,0:T(8,128)(2,1)} %all-gather.5.cloned.1.call-done) | copy-start | bytes 12386308
  187.7 40.2 %copy-start.3 = (bf16[1152,432]{1,0:T(8,128)(2,1)}, bf16[1152,432]{1,0:T(8,128)(2,1)S(1)}, u32[]{:S(2)}) copy-start(bf16[1152,432]{1,0:T(8,128)(2,1)S(1)} %slice.366.wqkv_ref) | copy-start | bytes 2985988
  275.4 36.9 %copy-start.4 = (bf16[1152,432]{1,0:T(8,128)(2,1)S(1)}, bf16[1152,432]{1,0:T(8,128)(2,1)}, u32[]{:S(2)}) copy-start(bf16[1152,432]{1,0:T(8,128)(2,1)} %copy-done.3) | copy-start | bytes 2985988
  275.4 36.9 %copy-start.10 = (f32[112,1152]{1,0:T(8,128)S(1)}, f32[112,1152]{1,0:T(8,128)}, u32[]{:S(2)}) copy-start(f32[112,1152]{1,0:T(8,128)} %copy-done.9) | copy-start | bytes 1548292
  275.4 36.9 %copy-start.38 = (f32[112,1152]{1,0:T(8,128)S(1)}, f32[112,1152]{1,0:T(8,128)}, u32[]{:S(2)}) copy-start(f32[112,1152]{1,0:T(8,128)} %copy-done.37) | copy-start | bytes 1548292
  275.4 36.9 %copy-start.42 = (bf16[2,896,72]{2,1,0:T(8,128)(2,1)S(1)}, bf16[2,896,72]{2,1,0:T(8,128)(2,1)}, u32[]{:S(2)}) copy-start(bf16[2,896,72]{2,1,0:T(8,128)(2,1)} %copy-done.41) | copy-start | bytes 774148
  275.4 37.0 %copy-start.44 = (bf16[2,896,72]{2,1,0:T(8,128)(2,1)S(1)}, bf16[2,896,72]{2,1,0:T(8,128)(2,1)}, u32[]{:S(2)}) copy-start(bf16[2,896,72]{2,1,0:T(8,128)(2,1)} %copy-done.43) | copy-start | bytes 774148
  275.4 37.0 %copy-start.46 = (bf16[2,896,72]{2,1,0:T(8,128)(2,1)S(1)}, bf16[2,896,72]{2,1,0:T(8,128)(2,1)}, u32[]{:S(2)}) copy-start(bf16[2,896,72]{2,1,0:T(8,128)(2,1)} %copy-done.45) | copy-start | bytes 774148
  275.4 37.0 %copy-start.48 = (f32[896,2]{1,0:T(8,128)S(1)}, f32[896,2]{1,0:T(8,128)}, u32[]{:S(2)}) copy-start(f32[896,2]{1,0:T(8,128)} %copy-done.47) | copy-start | bytes 21508
  275.4 37.0 %copy-start.50 = (bf16[896,144]{1,0:T(8,128)(2,1)S(1)}, bf16[896,144]{1,0:T(8,128)(2,1)}, u32[]{:S(2)}) copy-start(bf16[896,144]{1,0:T(8,128)(2,1)} %copy-done.49) | copy-start | bytes 774148
  312.4 34.0 %copy-start.57 = (bf16[1152,1152]{1,0:T(8,128)(2,1)S(1)}, bf16[1152,1152]{1,0:T(8,128)(2,1)}, u32[]{:S(2)}) copy-start(bf16[1152,1152]{1,0:T(8,128)(2,1)} %get-tuple-element.105) | copy-start | bytes 7962628
  425.4 42.4 %copy-start.6 = (bf16[1152,144]{1,0:T(8,128)(2,1)S(1)}, bf16[1152,144]{1,0:T(8,128)(2,1)}, u32[]{:S(2)}) copy-start(bf16[1152,144]{1,0:T(8,128)(2,1)} %copy-done.5) | copy-start | bytes 995332
  425.4 42.4 %copy-start.8 = (f32[128,1152]{1,0:T(8,128)S(1)}, f32[128,1152]{1,0:T(8,128)}, u32[]{:S(2)}) copy-start(f32[128,1152]{1,0:T(8,128)} %copy-done.7) | copy-start | bytes 1769476
  425.4 42.4 %copy-start.24 = (f32[128,1152]{1,0:T(8,128)S(1)}, f32[128,1152]{1,0:T(8,128)}, u32[]{:S(2)}) copy-start(f32[128,1152]{1,0:T(8,128)} %copy-done.23) | copy-start | bytes 1769476
  425.4 42.4 %copy-start.28 = (bf16[2,1024,72]{2,1,0:T(8,128)(2,1)S(1)}, bf16[2,1024,72]{2,1,0:T(8,128)(2,1)}, u32[]{:S(2)}) copy-start(bf16[2,1024,72]{2,1,0:T(8,128)(2,1)} %copy-done.27) | copy-start | bytes 884740
  425.4 42.4 %copy-start.30 = (bf16[2,1024,72]{2,1,0:T(8,128)(2,1)S(1)}, bf16[2,1024,72]{2,1,0:T(8,128)(2,1)}, u32[]{:S(2)}) copy-start(bf16[2,1024,72]{2,1,0:T(8,128)(2,1)} %copy-done.29) | copy-start | bytes 884740
  425.4 42.4 %copy-start.32 = (bf16[2,1024,72]{2,1,0:T(8,128)(2,1)S(1)}, bf16[2,1024,72]{2,1,0:T(8,128)(2,1)}, u32[]{:S(2)}) copy-start(bf16[2,1024,72]{2,1,0:T(8,128)(2,1)} %copy-done.31) | copy-start | bytes 884740
  425.4 42.4 %copy-start.34 = (f32[1024,2]{1,0:T(8,128)S(1)}, f32[1024,2]{1,0:T(8,128)}, u32[]{:S(2)}) copy-start(f32[1024,2]{1,0:T(8,128)} %copy-done.33) | copy-start | bytes 24580
  425.4 42.4 %copy-start.36 = (bf16[1024,144]{1,0:T(8,128)(2,1)S(1)}, bf16[1024,144]{1,0:T(8,128)(2,1)}, u32[]{:S(2)}) copy-start(bf16[1024,144]{1,0:T(8,128)(2,1)} %copy-done.35) | copy-start | bytes 884740
  467.8 38.9 %copy-start.58 = (bf16[1152,1152]{1,0:T(8,128)(2,1)S(1)}, bf16[1152,1152]{1,0:T(8,128)(2,1)}, u32[]{:S(2)}) copy-start(bf16[1152,1152]{1,0:T(8,128)(2,1)} %get-tuple-element.103) | copy-start | bytes 7962628
  508.6 78.2 %copy-start.64 = (bf16[72,1152]{1,0:T(8,128)(2,1)S(1)}, bf16[72,1152]{1,0:T(8,128)(2,1)}, u32[]{:S(2)}) copy-start(bf16[72,1152]{1,0:T(8,128)(2,1)} %slice.297) | copy-start | bytes 497668
  593.6 27.4 %copy-start.63 = (bf16[1,9,6912]{2,0,1:T(2,128)(2,1)S(1)}, bf16[1,9,6912]{2,0,1:T(2,128)(2,1)}, u32[]{:S(2)}) copy-start(bf16[1,9,6912]{2,0,1:T(2,128)(2,1)} %copy-done.62) | copy-start | bytes 373252
  (63 other events, 171.3 us)
Sparse Core Ops, SparseCore 0:
  54.7 59.4 all-gather.2
  117.0 50.8 all-gather.4

commit v3 on v2

--- a/solution.py
+++ b/solution.py
@@ -17,6 +17,7 @@
 DP_TX_TY = ("dp_0", "dp_1", "tx", "ty")
 MESH = pl.DeviceIdType.MESH
 VMEM = pl.BlockSpec(memory_space=pltpu.VMEM)
+FAR = pl.BlockSpec(memory_space=pl.ANY)
 F32 = jnp.float32
 BF16 = jnp.bfloat16
 ATT_COLS = 640
@@ -28,11 +29,19 @@
 SMALL_IN = (16 * 9, 9, 9 * 32, 2 * 18, 2 * 9, 2 * 36, 2 * 9)
 
 
-def enter(peers):
+def greet(peers):
     barrier = pltpu.get_barrier_semaphore()
     for peer in peers:
         pl.semaphore_signal(barrier, inc=1, device_id=peer, device_id_type=MESH)
-    pl.semaphore_wait(barrier, len(peers))
+
+
+def met(peers):
+    pl.semaphore_wait(pltpu.get_barrier_semaphore(), len(peers))
+
+
+def enter(peers):
+    greet(peers)
+    met(peers)
 
 
 def send(src, dst, sems, k, peer):
@@ -82,17 +91,37 @@
     return [pltpu.SemaphoreType.DMA((n,)), pltpu.SemaphoreType.DMA((n,))]
 
 
-def collective(kernel, cid, outs, scratch, *operands, vmem=48 << 20):
+def collective(kernel, cid, outs, scratch, *operands, far_in=0, far_out=0, vmem=56 << 20):
+    many = isinstance(outs, tuple)
+    near_in = len(operands) - far_in
+    near_out = (len(outs) if many else 1) - far_out
+    out_specs = (VMEM,) * near_out + (FAR,) * far_out
     return pl.pallas_call(
         kernel,
         out_shape=outs,
-        in_specs=[VMEM] * len(operands),
-        out_specs=jax.tree.map(lambda _: VMEM, outs),
+        in_specs=[VMEM] * near_in + [FAR] * far_in,
+        out_specs=out_specs if many else out_specs[0],
         scratch_shapes=scratch,
         compiler_params=pltpu.CompilerParams(
             collective_id=cid, has_side_effects=True, vmem_limit_bytes=vmem
         ),
     )(*operands)
+
+
+class Moves:
+    def __init__(self, sems):
+        self.sems, self.copies = sems, {}
+
+    def start(self, k, src, dst):
+        self.copies[k] = pltpu.make_async_copy(src, dst, self.sems.at[k])
+        self.copies[k].start()
+
+    def wait(self, *which):
+        for k in which:
+            self.copies.pop(k).wait()
+
+    def finish(self):
+        self.wait(*list(self.copies))
 
 
 def ring_peers():
@@ -148,55 +177,6 @@
     )
     scratch = [pltpu.VMEM((16, 128, 128), F32), pltpu.VMEM((8, 128, 128), F32)] + dma_sems(51)
     return collective(spread_kernel, 1, outs, scratch, weights, mods, small)
-
-
-def fetch_kernel(w_ref, o_ref, ss, rs):
-    image = image_peers()
-    enter([peer for peer, _ in image])
-    mine = own_image()
-    copies = [
-        send(w_ref, o_ref.at[mine], (ss, rs), k, peer) for k, (peer, _) in enumerate(image)
-    ]
-    o_ref[mine] = w_ref[...]
-    for copy in copies:
-        copy.wait()
-
-
-def fetch_rows(rows, cid):
-    padded = jnp.pad(rows, [(0, 8), (0, 0)])
-    out = jax.ShapeDtypeStruct((16, *padded.shape), BF16)
-    slabs = collective(fetch_kernel, cid, out, dma_sems(15), padded)
-    return slabs[:, :72].reshape(D, rows.shape[1])
-
-
-def reduce_kernel(g_ref, o_ref, got, ss, rs):
-    image = image_peers()
-    enter([peer for peer, _ in image])
-    mine = own_image()
-    copies = [
-        send(g_ref.at[at], got.at[mine], (ss, rs), k, peer) for k, (peer, at) in enumerate(image)
-    ]
-    got[mine] = g_ref[mine]
-    for copy in copies:
-        copy.wait_recv()
-
-    @pl.loop(0, g_ref.shape[1] // 16)
-    def _(piece):
-        rows = pl.ds(pl.multiple_of(piece * 16, 16), 16)
-        total = got[0, rows, :].astype(F32)
-        for k in range(1, 16):
-            total = total + got[k, rows, :].astype(F32)
-        o_ref[rows, :] = total.astype(BF16)
-
-    for copy in copies:
-        copy.wait_send()
-
-
-def reduce_rows(grads, cid):
-    slabs = jnp.pad(grads.reshape(16, 72, -1), [(0, 0), (0, 8), (0, 0)])
-    out = jax.ShapeDtypeStruct(slabs.shape[1:], BF16)
-    scratch = [pltpu.VMEM(slabs.shape, BF16)] + dma_sems(15)
-    return collective(reduce_kernel, cid, out, scratch, slabs)[:72]
 
 
 def finish_kernel(g_ref, m_ref, s_ref, g_out, m_out, s_out, m_got, s_got, s_mine, s_two, ss, rs):
@@ -343,6 +323,197 @@
     ]
 
 
+SLAB = 80
+PART = D // 16
+CUT = {ATT_COLS: 384, FFN_COLS: 640}
+
+
+def line_peers():
+    x, z = lax.axis_index("dp_0"), lax.axis_index("dp_1")
+    along_x = [({"dp_0": lax.rem(x + d, 4)}, lax.rem(x + d, 4)) for d in (2, 1, 3)]
+    along_z = [({"dp_1": lax.rem(z + d, 4)}, lax.rem(z + d, 4)) for d in (2, 1, 3)]
+    return along_x, along_z
+
+
+class RowsIn:
+    def __init__(self, left_ref, right_ref, scratch):
+        self.left, self.right = left_ref, right_ref
+        self.all_left, self.all_right = scratch[:2]
+        self.sems = tuple(scratch[2:4])
+        self.x, self.z = lax.axis_index("dp_0"), lax.axis_index("dp_1")
+        self.along_x, self.along_z = line_peers()
+
+    def peers(self):
+        return [peer for peer, _ in self.along_x + self.along_z]
+
+    def start(self):
+        x, z = self.x, self.z
+        self.first = []
+        for k, (peer, _) in enumerate(self.along_z):
+            self.first.append(send(self.left, self.all_left.at[x, z], self.sems, k, peer))
+        for k, (peer, _) in enumerate(self.along_x):
+            self.first.append(send(self.right, self.all_right.at[x, z], self.sems, 3 + k, peer))
+        self.all_left[x, z] = self.left[...]
+        self.all_right[x, z] = self.right[...]
+
+    def middle(self):
+        left, right = self.all_left.at[self.x], self.all_right.at[:, self.z]
+        self.second = []
+        for copy in self.first[:3]:
+            copy.wait_recv()
+        for k, (peer, _) in enumerate(self.along_x):
+            self.second.append(send(left, left, self.sems, 6 + k, peer))
+        for copy in self.first[3:]:
+            copy.wait_recv()
+        for k, (peer, _) in enumerate(self.along_z):
+            self.second.append(send(right, right, self.sems, 9 + k, peer))
+
+    def end(self, one_ref, two_ref):
+        for copy in self.second:
+            copy.wait_recv()
+        width, other = one_ref.shape[1], two_ref.shape[1]
+        cut = self.left.shape[1]
+
+        @pl.loop(0, 8)
+        def _(pair):
+            x, z = pair // 2, 2 * lax.rem(pair, 2)
+            both = []
+            for k in range(2):
+                parts = [self.all_left[x, z + k], self.all_right[x, z + k]]
+                both.append(jnp.concatenate(parts, axis=1).astype(F32)[:PART])
+            value = jnp.concatenate(both, axis=0).astype(BF16)
+            at = pl.ds(pl.multiple_of(pair * 2 * PART, 16), 2 * PART)
+            one_ref[at, :] = value[:, :width]
+            two_ref[at, :] = value[:, width : width + other]
+
+        for copy in self.first + self.second:
+            copy.wait_send()
+
+
+def rows_in_scratch(cols):
+    left = CUT[cols]
+    return [
+        pltpu.VMEM((4, 4, SLAB, left), BF16),
+        pltpu.VMEM((4, 4, SLAB, cols - left), BF16),
+    ] + dma_sems(12)
+
+
+class RowsOut:
+    def __init__(self, left_ref, right_ref, scratch):
+        self.left, self.right = left_ref, right_ref
+        self.got = scratch[0:2]
+        self.mine = scratch[2:4]
+        self.last = scratch[4:6]
+        self.sems = tuple(scratch[6:8])
+        self.x, self.z = lax.axis_index("dp_0"), lax.axis_index("dp_1")
+        self.along_x, self.along_z = line_peers()
+
+    def peers(self):
+        return [peer for peer, _ in self.along_x + self.along_z]
+
+    def start(self):
+        self.first = []
+        for k, (peer, at) in enumerate(self.along_x):
+            part = self.left.at[at]
+            self.first.append(send(part, self.got[0].at[k], self.sems, k, peer))
+        for k, (peer, at) in enumerate(self.along_z):
+            part = self.right.at[:, at]
+            self.first.append(send(part, self.got[1].at[k], self.sems, 3 + k, peer))
+
+    def middle(self):
+        self.second = []
+        for side, peers in ((0, self.along_z), (1, self.along_x)):
+            for copy in self.first[3 * side : 3 * side + 3]:
+                copy.wait_recv()
+            got, mine = self.got[side], self.mine[side]
+
+            @pl.loop(0, 4)
+            def _(k):
+                own = self.right[k, self.z] if side else self.left[self.x, k]
+                total = own.astype(F32)
+                for source in range(3):
+                    total = total + got[source, k].astype(F32)
+                mine[k] = total.astype(BF16)
+
+            for k, (peer, at) in enumerate(peers):
+                part = mine.at[at]
+                copy = send(part, self.last[side].at[k], self.sems, 6 + 3 * side + k, peer)
+                self.second.append(copy)
+
+    def end(self, out_ref):
+        cut = self.left.shape[3]
+        for copy in self.second:
+            copy.wait_recv()
+        for side, own, cols in ((0, self.z, slice(0, cut)), (1, self.x, slice(cut, None))):
+            total = self.mine[side][own].astype(F32)
+            for source in range(3):
+                total = total + self.last[side][source].astype(F32)
+            out_ref[:, cols] = total.astype(BF16)
+        for copy in self.first + self.second:
+            copy.wait_send()
+
+
+def rows_out_scratch(cols):
+    widths = (CUT[cols], cols - CUT[cols])
+    return (
+        [pltpu.VMEM((3, 4, SLAB, w), BF16) for w in widths]
+        + [pltpu.VMEM((4, SLAB, w), BF16) for w in widths]
+        + [pltpu.VMEM((3, SLAB, w), BF16) for w in widths]
+        + dma_sems(12)
+    )
+
+
+def slab_shapes(cols):
+    widths = (CUT[cols], cols - CUT[cols])
+    return tuple(jax.ShapeDtypeStruct((16, SLAB, w), BF16) for w in widths)
+
+
+def slabs(pair):
+    return [part.reshape(4, 4, *part.shape[1:]) for part in pair]
+
+
+def write_slabs(whole, left_ref, right_ref):
+    cut = left_ref.shape[2]
+
+    @pl.loop(0, 16)
+    def _(k):
+        rows = whole[pl.ds(pl.multiple_of(k * PART, 8), PART), :]
+        rows = jnp.concatenate([rows, jnp.zeros((SLAB - PART, rows.shape[1]), F32)], axis=0)
+        rows = rows.astype(BF16)
+        left_ref[k] = rows[:, :cut]
+        right_ref[k] = rows[:, cut:]
+
+
+def fetch_kernel(left_ref, right_ref, one_ref, two_ref, *scratch):
+    rows = RowsIn(left_ref, right_ref, scratch)
+    enter(rows.peers())
+    rows.start()
+    rows.middle()
+    rows.end(one_ref, two_ref)
+
+
+def weight_shapes(cols):
+    widths = (3 * HW, HW) if cols == ATT_COLS else (FW, FW)
+    return tuple(jax.ShapeDtypeStruct((D, w), BF16) for w in widths)
+
+
+def fetch_rows(pair, cols, cid):
+    return collective(fetch_kernel, cid, weight_shapes(cols), rows_in_scratch(cols), *pair)
+
+
+def reduce_kernel(left_ref, right_ref, out_ref, *scratch):
+    rows = RowsOut(left_ref, right_ref, scratch)
+    enter(rows.peers())
+    rows.start()
+    rows.middle()
+    rows.end(out_ref)
+
+
+def reduce_rows(pair, cols, cid):
+    out = jax.ShapeDtypeStruct((SLAB, cols), BF16)
+    return collective(reduce_kernel, cid, out, rows_out_scratch(cols), *slabs(pair))
+
+
 class Ring:
     def __init__(self, tokens, scratch):
         self.tokens = tokens
@@ -356,8 +527,8 @@
         self.other = [(1 - c) * 4 + lax.rem(y + d, 4) for d in range(4)]
         self.sent = []
 
-    def enter(self):
-        enter([self.sib, self.up, self.down])
+    def peers(self):
+        return [self.sib, self.up, self.down]
 
     def send(self, src, dst, k, peer):
         copy = send(src, dst, self.sems, k, peer)
@@ -369,7 +540,7 @@
         at = pl.multiple_of(index * self.tokens + start, 16)
         return pl.ds(at, stop - start)
 
-    def gather(self, x_ref, all_ref, visit):
+    def gather(self, x_ref, all_ref, prepare, visit, between=None):
         half, tokens = self.half, self.tokens
         me, above, across, below = self.own
         first, last = slice(0, half), slice(half, tokens)
@@ -388,6 +559,7 @@
         b2 = own_part(first, 3, self.down)
         s0 = self.send(x_ref, all_ref.at[self.rows(me)], 4, self.sib)
         all_ref[self.rows(me), :] = x_ref[...]
+        prepare()
         visit(True, 0)
         s0.wait_recv()
         visit(False, 0)
@@ -399,6 +571,8 @@
         s1 = pass_on(below, 7, self.sib)
         b2.wait_recv()
         s2 = pass_on(above, 8, self.sib)
+        if between:
+            between()
         visit(True, 3)
         visit(True, 1)
         s1.wait_recv()
@@ -486,15 +660,29 @@
     return value, slope
 
 
+def sum_rows(value):
+    return jnp.sum(value, axis=0, keepdims=True)
+
+
 def ffn_forward_kernel(
-    x_ref, vec_ref, bias_ref, we_ref, wr_ref, out_ref, mlp_ref, all_ref, hid_ref, slope_ref, x16, *scratch
+    x_ref, vec_ref, bias_ref, we_ref, wr_ref, next_left, next_right,
+    out_ref, mlp_ref, next_one, next_two, all_out, hid_out, slope_out,
+    x16, all_ref, hid_ref, slope_ref, move_sems, *scratch
 ):
     tokens = x_ref.shape[0]
-    ring = Ring(tokens, scratch)
+    ring = Ring(tokens, scratch[:9])
+    rows_in = RowsIn(next_left, next_right, scratch[9:]) if scratch[9:] else None
+    moves = Moves(move_sems)
+    peers = ring.peers() + (rows_in.peers() if rows_in else [])
+    greet(peers)
     normed, _ = layer_stats(x_ref[...])
     x16[...] = (normed * (1.0 + vec_ref[1:2]) + vec_ref[0:1]).astype(BF16)
-    ring.enter()
+    met(peers)
     ring.start_sums()
+
+    def prepare():
+        if rows_in:
+            rows_in.start()
 
     def visit(own, d):
         rows = ring.rows((ring.own if own else ring.other)[d])
@@ -507,43 +695,78 @@
         if not own and d == 1:
             ring.near()
 
-    ring.gather(x16, all_ref, visit)
+    ring.gather(x16, all_ref, prepare, visit, rows_in.middle if rows_in else None)
     ring.far()
+    moves.start(0, all_ref, all_out)
+    moves.start(1, hid_ref, hid_out)
+    moves.start(2, slope_ref, slope_out)
     ring.relay()
+    if rows_in:
+        rows_in.end(next_one, next_two)
     mlp = ring.total() + vec_ref[3:4]
     mlp_ref[...] = mlp
     out_ref[...] = x_ref[...] + vec_ref[2:3] * mlp
     ring.leave()
-
-
-def ffn_forward(x, vecs, bias, we, wr, cid):
+    moves.finish()
+
+
+def ffn_forward_last_kernel(
+    x_ref, vec_ref, bias_ref, we_ref, wr_ref, out_ref, mlp_ref, all_out, hid_out, slope_out, *scratch
+):
+    ffn_forward_kernel(
+        x_ref, vec_ref, bias_ref, we_ref, wr_ref, None, None,
+        out_ref, mlp_ref, None, None, all_out, hid_out, slope_out, *scratch
+    )
+
+
+def ffn_forward(x, vecs, bias, we, wr, following, cid):
     tokens = x.shape[0]
+    saved = [(8 * tokens, D), (8 * tokens, FW), (8 * tokens, FW)]
     outs = (
         jax.ShapeDtypeStruct((tokens, D), F32),
         jax.ShapeDtypeStruct((tokens, D), F32),
-        jax.ShapeDtypeStruct((8 * tokens, D), BF16),
-        jax.ShapeDtypeStruct((8 * tokens, FW), BF16),
-        jax.ShapeDtypeStruct((8 * tokens, FW), BF16),
-    )
-    scratch = [pltpu.VMEM((tokens, D), BF16)] + ring_scratch(tokens)
-    return collective(ffn_forward_kernel, cid, outs, scratch, x, vecs, bias, we, wr)
-
-
-def sum_rows(value):
-    return jnp.sum(value, axis=0, keepdims=True)
+        *(weight_shapes(ATT_COLS) if following else ()),
+        *(jax.ShapeDtypeStruct(shape, BF16) for shape in saved),
+    )
+    scratch = [pltpu.VMEM((tokens, D), BF16)]
+    scratch += [pltpu.VMEM(shape, BF16) for shape in saved]
+    scratch += [pltpu.SemaphoreType.DMA((3,))] + ring_scratch(tokens)
+    kernel = ffn_forward_last_kernel
+    if following:
+        scratch += rows_in_scratch(ATT_COLS)
+        kernel = ffn_forward_kernel
+    operands = (x, vecs, bias, we, wr, *following)
+    return collective(kernel, cid, outs, scratch, *operands, far_out=3)
 
 
 def ffn_backward_kernel(
-    g_ref, x_ref, mlp_ref, vec_ref, valid_ref, second_ref, hid_ref, slope_ref, we_ref, wr_ref,
-    out_ref, vecs_ref, bias_ref, dw_ref, g16, g_all, pre_all, *scratch
+    g_ref, x_ref, mlp_ref, vec_ref, valid_ref, we_ref, wr_ref, *refs
 ):
     tokens = x_ref.shape[0]
-    ring = Ring(tokens, scratch)
+    refs = list(refs)
+    pending = (refs.pop(0), refs.pop(0)) if len(refs) > 30 else None
+    second_in, hid_in, slope_in, out_ref, vecs_ref, bias_ref, dw_left, dw_right = refs[:8]
+    refs = refs[8:]
+    summed = refs.pop(0) if pending else None
+    g16, g_all, pre_all, second_ref, hid_ref, slope_ref, whole, move_sems = refs[:8]
+    ring = Ring(tokens, refs[8:17])
+    rows_out = RowsOut(*pending, refs[17:]) if pending else None
+    moves = Moves(move_sems)
+    peers = ring.peers() + (rows_out.peers() if rows_out else [])
+    greet(peers)
+    moves.start(0, slope_in, slope_ref)
+    moves.start(1, hid_in, hid_ref)
+    moves.start(2, second_in, second_ref)
     grad = g_ref[...] * valid_ref[...]
     g16[...] = (grad * vec_ref[2:3]).astype(BF16)
-    ring.enter()
+    met(peers)
     ring.start_sums()
     bias_ref[...] = jnp.zeros_like(bias_ref)
+
+    def prepare():
+        if rows_out:
+            rows_out.start()
+        moves.wait(0)
 
     def visit(own, d):
         rows = ring.rows((ring.own if own else ring.other)[d])
@@ -556,24 +779,30 @@
         if not own and d == 1:
             ring.near()
 
-    ring.gather(g16, g_all, visit)
+    ring.gather(g16, g_all, prepare, visit)
     ring.far()
     vecs_ref[2:3] = sum_rows(grad * mlp_ref[...])
     vecs_ref[3:4] = sum_rows(g16[...].astype(F32))
     vecs_ref[4:8] = jnp.zeros((4, D), F32)
+    if rows_out:
+        rows_out.middle()
     ring.relay()
+    moves.finish()
 
     @pl.loop(0, D // 128)
     def _(k):
         at = pl.ds(pl.multiple_of(k * 128, 128), 128)
-        dw_ref[at, :] = jnp.concatenate(
+        whole[at, :] = jnp.concatenate(
             [
                 dot_tn(second_ref[:, at], pre_all[...]),
                 dot_tn(g_all[:, at], hid_ref[...]),
             ],
             axis=1,
-        ).astype(BF16)
-
+        )
+
+    write_slabs(whole, dw_left, dw_right)
+    if rows_out:
+        rows_out.end(summed)
     second_grad = ring.total()
     normed, inv_std = layer_stats(x_ref[...])
     vecs_ref[0:1] = sum_rows(second_grad)
@@ -582,22 +811,29 @@
     ring.leave()
 
 
-def ffn_backward(g, x, mlp, vecs, valid, second, hid, slope, we, wr, cid):
+def ffn_backward(g, x, mlp, vecs, valid, second, hid, slope, we, wr, pending, cid):
     tokens = x.shape[0]
     outs = (
         jax.ShapeDtypeStruct((tokens, D), F32),
         jax.ShapeDtypeStruct((8, D), F32),
         jax.ShapeDtypeStruct((1, FW), F32),
-        jax.ShapeDtypeStruct((D, FFN_COLS), BF16),
+        *slab_shapes(FFN_COLS),
+        *((jax.ShapeDtypeStruct((SLAB, ATT_COLS), BF16),) if pending else ()),
     )
     scratch = [
         pltpu.VMEM((tokens, D), BF16),
         pltpu.VMEM((8 * tokens, D), BF16),
         pltpu.VMEM((8 * tokens, FW), BF16),
+        pltpu.VMEM((8 * tokens, D), BF16),
+        pltpu.VMEM((8 * tokens, FW), BF16),
+        pltpu.VMEM((8 * tokens, FW), BF16),
+        pltpu.VMEM((D, FFN_COLS), F32),
+        pltpu.SemaphoreType.DMA((3,)),
     ] + ring_scratch(tokens)
-    return collective(
-        ffn_backward_kernel, cid, outs, scratch, g, x, mlp, vecs, valid, second, hid, slope, we, wr
-    )
+    if pending:
+        scratch += rows_out_scratch(ATT_COLS)
+    operands = (g, x, mlp, vecs, valid, we, wr, *pending, second, hid, slope)
+    return collective(ffn_backward_kernel, cid, outs, scratch, *operands, far_in=3)
 
 
 HEAD = D // HEADS
@@ -609,14 +845,20 @@
 
 
 def attn_forward_kernel(
-    x_ref, vec_ref, bias_ref, mask_ref, wqkv_ref, wm_ref,
-    out_ref, branch_ref, all_ref, q_ref, k_ref, v_ref, lse_ref, att_ref, x16, *scratch
+    x_ref, vec_ref, bias_ref, mask_ref, wqkv_ref, wm_ref, next_left, next_right,
+    out_ref, branch_ref, next_one, next_two, *refs
 ):
+    outs, (x16, *kept, move_sems), scratch = refs[:6], refs[6:14], refs[14:]
+    all_ref, q_ref, k_ref, v_ref, lse_ref, att_ref = kept
     tokens = x_ref.shape[0]
-    ring = Ring(tokens, scratch)
+    ring = Ring(tokens, scratch[:9])
+    rows_in = RowsIn(next_left, next_right, scratch[9:])
+    moves = Moves(move_sems)
+    peers = ring.peers() + rows_in.peers()
+    greet(peers)
     normed, _ = layer_stats(x_ref[...])
     x16[...] = (normed * (1.0 + vec_ref[1:2]) + vec_ref[0:1]).astype(BF16)
-    ring.enter()
+    met(peers)
     ring.start_sums()
 
     def visit(own, d):
@@ -642,10 +884,12 @@
         att_ref[rows, :] = attended
         ring.put(own, d, dot_nt(attended, wm_ref[...]))
 
-    ring.gather(x16, all_ref, visit)
+    ring.gather(x16, all_ref, rows_in.start, visit, rows_in.middle)
     attend(False, 2)
     attend(True, 2)
     ring.far()
+    for k in range(4):
+        moves.start(k, kept[k], outs[k])
     for d in (1, 3):
         attend(False, d)
         attend(True, d)
@@ -653,41 +897,67 @@
     ring.relay()
     attend(False, 0)
     attend(True, 0)
+    for k in range(4, 6):
+        moves.start(k, kept[k], outs[k])
+    rows_in.end(next_one, next_two)
     branch = ring.total() + vec_ref[3:4]
     branch_ref[...] = branch
     out_ref[...] = x_ref[...] + vec_ref[2:3] * branch
     ring.leave()
-
-
-def attn_forward(x, vecs, bias, mask, wqkv, wm, cid):
+    moves.finish()
+
+
+def kept_shapes(tokens):
+    heads = ((2, 8 * tokens, HEAD), BF16)
+    return (
+        ((8 * tokens, D), BF16),
+        heads,
+        heads,
+        heads,
+        ((8 * tokens, 2), F32),
+        ((8 * tokens, HW), BF16),
+    )
+
+
+def attn_forward(x, vecs, bias, mask, wqkv, wm, following, cid):
     tokens = x.shape[0]
-    heads = jax.ShapeDtypeStruct((2, 8 * tokens, HEAD), BF16)
     outs = (
         jax.ShapeDtypeStruct((tokens, D), F32),
         jax.ShapeDtypeStruct((tokens, D), F32),
-        jax.ShapeDtypeStruct((8 * tokens, D), BF16),
-        heads,
-        heads,
-        heads,
-        jax.ShapeDtypeStruct((8 * tokens, 2), F32),
-        jax.ShapeDtypeStruct((8 * tokens, HW), BF16),
-    )
-    scratch = [pltpu.VMEM((tokens, D), BF16)] + ring_scratch(tokens)
-    return collective(attn_forward_kernel, cid, outs, scratch, x, vecs, bias, mask, wqkv, wm)
+        *weight_shapes(FFN_COLS),
+        *(jax.ShapeDtypeStruct(*shape) for shape in kept_shapes(tokens)),
+    )
+    scratch = [pltpu.VMEM((tokens, D), BF16)]
+    scratch += [pltpu.VMEM(*shape) for shape in kept_shapes(tokens)]
+    scratch += [pltpu.SemaphoreType.DMA((6,))] + ring_scratch(tokens) + rows_in_scratch(FFN_COLS)
+    operands = (x, vecs, bias, mask, wqkv, wm, *following)
+    return collective(attn_forward_kernel, cid, outs, scratch, *operands, far_out=6)
 
 
 def attn_backward_kernel(
-    g_ref, x_ref, branch_ref, vec_ref, mask_ref, in_ref, q_ref, k_ref, v_ref, lse_ref, att_ref,
-    wqkv_ref, wm_ref, out_ref, vecs_ref, bias_ref, dw_ref,
-    g16, g_all, joined, dk, dv, *scratch
+    g_ref, x_ref, branch_ref, vec_ref, mask_ref, wqkv_ref, wm_ref, pending_left, pending_right, *refs
 ):
+    ins, (out_ref, vecs_ref, bias_ref, dw_left, dw_right, summed) = refs[:6], refs[6:12]
+    g16, g_all, joined, dk, dv, whole = refs[12:18]
+    kept, move_sems, scratch = refs[18:24], refs[24], refs[25:]
+    in_ref, q_ref, k_ref, v_ref, lse_ref, att_ref = kept
     tokens = x_ref.shape[0]
-    ring = Ring(tokens, scratch)
+    ring = Ring(tokens, scratch[:9])
+    rows_out = RowsOut(pending_left, pending_right, scratch[9:])
+    moves = Moves(move_sems)
+    peers = ring.peers() + rows_out.peers()
+    greet(peers)
+    for k in (1, 2, 3, 4, 5, 0):
+        moves.start(k, ins[k], kept[k])
     g16[...] = (g_ref[...] * vec_ref[2:3]).astype(BF16)
-    ring.enter()
+    met(peers)
     ring.start_sums()
-    dk[...] = jnp.zeros_like(dk)
-    dv[...] = jnp.zeros_like(dv)
+
+    def prepare():
+        rows_out.start()
+        dk[...] = jnp.zeros_like(dk)
+        dv[...] = jnp.zeros_like(dv)
+        moves.wait(1, 2, 3, 4)
 
     def visit(own, d):
         rows = ring.rows((ring.own if own else ring.other)[d])
@@ -710,7 +980,7 @@
         rows = ring.rows((ring.own if own else ring.other)[d])
         ring.put(own, d, dot_nt(joined[rows, :], wqkv_ref[...]))
 
-    ring.gather(g16, g_all, visit)
+    ring.gather(g16, g_all, prepare, visit)
     later = [(dk[h] * SCALE).astype(BF16) for h in range(2)] + [dv[h].astype(BF16) for h in range(2)]
     joined[:, HW : 3 * HW] = jnp.concatenate(later, axis=1)
     back(False, 2)
@@ -722,24 +992,28 @@
     ring.near()
     back(False, 0)
     back(True, 0)
+    rows_out.middle()
+    ring.relay()
     bias_ref[...] = sum_rows(joined[...].astype(F32))
     vecs_ref[2:3] = sum_rows(g_ref[...] * branch_ref[...])
     vecs_ref[3:4] = sum_rows(g16[...].astype(F32))
     vecs_ref[4:8] = jnp.zeros((4, D), F32)
-    ring.relay()
+    moves.finish()
 
     @pl.loop(0, D // 128)
     def _(k):
         at = pl.ds(pl.multiple_of(k * 128, 128), 128)
-        dw_ref[at, :] = jnp.concatenate(
+        whole[at, :] = jnp.concatenate(
             [
                 dot_tn(in_ref[:, at], joined[...]),
                 dot_tn(g_all[:, at], att_ref[...]),
                 jnp.zeros((128, ATT_COLS - 4 * HW), F32),
             ],
             axis=1,
-        ).astype(BF16)
-
+        )
+
+    write_slabs(whole, dw_left, dw_right)
+    rows_out.end(summed)
     input_grad = ring.total()
     normed, inv_std = layer_stats(x_ref[...])
     vecs_ref[0:1] = sum_rows(input_grad)
@@ -748,13 +1022,14 @@
     ring.leave()
 
 
-def attn_backward(g, x, branch, vecs, mask, inputs, q, k, v, lse, att, wqkv, wm, cid):
+def attn_backward(g, x, branch, vecs, mask, kept, wqkv, wm, pending, cid):
     tokens = x.shape[0]
     outs = (
         jax.ShapeDtypeStruct((tokens, D), F32),
         jax.ShapeDtypeStruct((8, D), F32),
         jax.ShapeDtypeStruct((1, 3 * HW), F32),
-        jax.ShapeDtypeStruct((D, ATT_COLS), BF16),
+        *slab_shapes(ATT_COLS),
+        jax.ShapeDtypeStruct((SLAB, FFN_COLS), BF16),
     )
     scratch = [
         pltpu.VMEM((tokens, D), BF16),
@@ -762,13 +1037,15 @@
         pltpu.VMEM((8 * tokens, 3 * HW), BF16),
         pltpu.VMEM((2, 8 * tokens, HEAD), F32),
         pltpu.VMEM((2, 8 * tokens, HEAD), F32),
-    ] + ring_scratch(tokens)
-    operands = (g, x, branch, vecs, mask, inputs, q, k, v, lse, att, wqkv, wm)
-    return collective(attn_backward_kernel, cid, outs, scratch, *operands)
-
-
-def block_forward(x, mod, params, biases, mask, cid):
-    wqkv, wm, we, wr = params
+        pltpu.VMEM((D, ATT_COLS), F32),
+    ]
+    scratch += [pltpu.VMEM(*shape) for shape in kept_shapes(tokens)]
+    scratch += [pltpu.SemaphoreType.DMA((6,))] + ring_scratch(tokens) + rows_out_scratch(FFN_COLS)
+    operands = (g, x, branch, vecs, mask, wqkv, wm, *pending, *kept)
+    return collective(attn_backward_kernel, cid, outs, scratch, *operands, far_in=6)
+
+
+def block_forward(x, mod, attn_w, biases, mask, next_ffn, next_attn, cid):
     attn_b, merge_b, expand_b, reduce_b = (b.astype(F32) for b in biases)
     group = own_group()
     zeros = jnp.zeros((4, D), F32)
@@ -781,21 +1058,26 @@
             lax.dynamic_slice_in_dim(attn_b, D + group * HW, HW),
         ]
     )[None]
-    middle, branch, *kept = attn_forward(x, vec_one, bias, mask, wqkv, wm, cid)
+    middle, branch, we, wr, *kept = attn_forward(
+        x, vec_one, bias, mask, *attn_w, next_ffn, cid
+    )
     e_bias = lax.dynamic_slice_in_dim(expand_b, group * FW, FW)[None]
-    output, mlp, *more = ffn_forward(middle, vec_two, e_bias, we, wr, cid + 1)
-    return output, (x, vec_one, mask, middle, branch, kept, vec_two, mlp, more)
-
-
-def block_backward(grad, saved, params, valid, cid):
+    output, mlp, *more = ffn_forward(middle, vec_two, e_bias, we, wr, next_attn, cid + 1)
+    following, more = (more[:2], more[2:]) if next_attn else ((), more)
+    params = (*attn_w, we, wr)
+    return output, following, params, (x, vec_one, mask, middle, branch, kept, vec_two, mlp, more)
+
+
+def block_backward(grad, saved, params, valid, pending, cid):
     x, vec_one, mask, middle, branch, kept, vec_two, mlp, more = saved
     wqkv, wm, we, wr = params
     group = own_group()
-    grad, mod_two, bias_two, dw_ffn = ffn_backward(
-        grad, middle, mlp, vec_two, valid, *more, we, wr, cid + 2
-    )
-    grad, mod_one, bias_one, dw_attn = attn_backward(
-        grad, x, branch, vec_one, mask, *kept, wqkv, wm, cid + 3
+    grad, mod_two, bias_two, *dw_ffn = ffn_backward(
+        grad, middle, mlp, vec_two, valid, *more, we, wr, pending, cid + 2
+    )
+    dw_ffn, earlier = dw_ffn[:2], dw_ffn[2:]
+    grad, mod_one, bias_one, *dw_attn, ffn_rows = attn_backward(
+        grad, x, branch, vec_one, mask, kept, wqkv, wm, slabs(dw_ffn), cid + 3
     )
     grad_expand_b = lax.dynamic_update_slice_in_dim(
         jnp.zeros((FF,), F32), bias_two[0], group * FW, 0
@@ -808,7 +1090,7 @@
     )
     mod_grad = jnp.concatenate([mod_one[0:3].reshape(-1), mod_two[0:3].reshape(-1)])
     biases = (grad_attn_b, mod_one[3], grad_expand_b, mod_two[3])
-    return grad, mod_grad, (dw_attn, dw_ffn), biases
+    return grad, mod_grad, dw_attn, ffn_rows, earlier, biases
 
 
 def pack_weights(attention_weight, merge_weight, expand_weight, reduce_weight):
@@ -841,15 +1123,14 @@
     return unpack_pieces(packed).reshape(72, ALL_COLS)
 
 
-def block_params(attn, ffn):
-    return attn[:, : 3 * HW], attn[:, 3 * HW : 4 * HW], ffn[:, :FW], ffn[:, FW:]
-
-
-def pack_grads(one, two):
-    columns = jnp.concatenate(
-        [one[:, :ATT_COLS], two[:, :ATT_COLS], one[:, ATT_COLS:], two[:, ATT_COLS:]], axis=1
-    )
-    return pack_pieces(columns.reshape(8, 9, ALL_COLS))
+def pack_grads(attn_one, attn_two, ffn_one, ffn_two):
+    columns = jnp.concatenate([attn_one, attn_two, ffn_one, ffn_two], axis=1)
+    return pack_pieces(columns[:72].reshape(8, 9, ALL_COLS))
+
+
+def slab_pair(rows, start, cols):
+    part = jnp.pad(rows[:, start : start + cols], [(0, SLAB - PART), (0, 0)])
+    return part[:, : CUT[cols]], part[:, CUT[cols] :]
 
 
 def unpack_grads(packed):
@@ -981,18 +1262,10 @@
     expand_b = from_owner(pieces[5], (2, FF), 1)
     reduce_b = from_owner(pieces[6], (2, D), 1)
     rows = unpack_rows(packed)
-    first_attn = fetch_rows(rows[:, :ATT_COLS], 3)
-    first_ffn = lax.all_gather(
-        rows[:, 2 * ATT_COLS : 2 * ATT_COLS + FFN_COLS], DP, axis=0, tiled=True
-    )
-    second_all = lax.all_gather(
-        jnp.concatenate(
-            [rows[:, ATT_COLS : 2 * ATT_COLS], rows[:, 2 * ATT_COLS + FFN_COLS :]], axis=1
-        ),
-        DP,
-        axis=0,
-        tiled=True,
-    )
+    first_attn = fetch_rows(slab_pair(rows, 0, ATT_COLS), ATT_COLS, 3)
+    second_attn_rows = slab_pair(rows, ATT_COLS, ATT_COLS)
+    first_ffn_rows = slab_pair(rows, 2 * ATT_COLS, FFN_COLS)
+    second_ffn_rows = slab_pair(rows, 2 * ATT_COLS + FFN_COLS, FFN_COLS)
     placed = sincos_table(row_index.astype(jnp.float32), col_index.astype(jnp.float32), width)
     patches = to_patches(latent)
     initial_tokens = (
@@ -1000,19 +1273,31 @@
         + embed_b.astype(jnp.float32)
         + placed[None, :, :]
     )
-    first_params = block_params(first_attn, first_ffn)
-    second_params = block_params(second_all[:, :ATT_COLS], second_all[:, ATT_COLS:])
     first_biases = (attn_b[0], merge_b[0], expand_b[0], reduce_b[0])
     second_biases = (attn_b[1], merge_b[1], expand_b[1], reduce_b[1])
     mask_one = jnp.zeros((1, tiles * tile_tokens), F32)
     mask_two = jnp.where(routed_marks > 0, 0.0, -1e30).astype(F32)
-    middle_one, saved_one = block_forward(
-        initial_tokens[0], mod_one.reshape(6, D), first_params, first_biases, mask_one, 10
+    middle_one, second_attn, first_params, saved_one = block_forward(
+        initial_tokens[0],
+        mod_one.reshape(6, D),
+        first_attn,
+        first_biases,
+        mask_one,
+        first_ffn_rows,
+        second_attn_rows,
+        10,
     )
     middle_one = middle_one[None]
     selected_rows = pick_rows(middle_one, owner)
-    middle_two, saved_two = block_forward(
-        selected_rows[0], mod_two.reshape(6, D), second_params, second_biases, mask_two, 20
+    middle_two, _, second_params, saved_two = block_forward(
+        selected_rows[0],
+        mod_two.reshape(6, D),
+        second_attn,
+        second_biases,
+        mask_two,
+        second_ffn_rows,
+        (),
+        20,
     )
     middle_two = middle_two[None]
     keep_mask = routed[:, :, None] > 0
@@ -1036,16 +1321,15 @@
     )
     grad_ended = layer_back(grad_final * (1.0 + head_scale), normed_end, inv_end)
     grad_chosen = pick_rows(grad_ended, owner)
-    grad_two, mod_grad_two, weights_two, biases_two = block_backward(
-        grad_chosen[0], saved_two, second_params, valid[0][:, None], 20
-    )
-    summed_two = reduce_rows(jnp.concatenate(weights_two, axis=1), 4)
+    grad_two, mod_grad_two, dw_attn_two, ffn_two, _, biases_two = block_backward(
+        grad_chosen[0], saved_two, second_params, valid[0][:, None], (), 20
+    )
     grad_middle = jnp.where(keep_mask, pick_rows(grad_two[None], position), grad_ended)
-    grad_start, mod_grad_one, weights_one, biases_one = block_backward(
-        grad_middle[0], saved_one, first_params, everyone[0][:, None], 10
+    grad_start, mod_grad_one, dw_attn_one, ffn_one, (attn_two,), biases_one = block_backward(
+        grad_middle[0], saved_one, first_params, everyone[0][:, None], slabs(dw_attn_two), 10
     )
     grad_start = grad_start[None]
-    summed_one = reduce_rows(jnp.concatenate(weights_one, axis=1), 5)
+    attn_one = reduce_rows(dw_attn_one, ATT_COLS, 5)
     start_grad16 = grad_start.astype(jnp.bfloat16)
     grad_embed_w = jnp.einsum(
         "btp,btd->pd", patches, start_grad16, preferred_element_type=jnp.float32
@@ -1073,7 +1357,7 @@
     grad_mods = jnp.concatenate([mod_grad_one, mod_grad_two, head_grad_mod[0]])
     grad_mods = jnp.pad(grad_mods.reshape(8, MOD_ALL // 8), [(0, 0), (0, 2048 - MOD_ALL // 8)])
     packed_grads, mod_back, small_back = finish(
-        pack_grads(summed_one, summed_two),
+        pack_grads(attn_one, attn_two, ffn_one, ffn_two),
         grad_mods.reshape(8, 16, 128),
         small_out.reshape(16, 8, 8, 128),
     )

time: 659 us -> 495 us (0.75)
  Pallas kernels: 531 us -> 403 us
  local copies, waits for them, and re-layouts: 81.4 us -> 61.5 us
  between operations: 16.6 us -> 2.88 us
    pallas_call x13 -> x12, Pallas kernels: 531 us -> 403 us  [collective(): pl.pallas_call(kernel, out_shape=outs, in_specs=[VMEM] * near_in + [FAR]...]
    unnamed x209 -> x103, local copies, waits for them, and re-layouts: 25.1 us -> 12.2 us
    slice x13 -> x6, local copies, waits for them, and re-layouts: 11.1 us -> 2.71 us  [the longest x4 2.66 us: slab_pair(): return (part[:, :CUT[cols]], part[:, CUT[cols]:])]
  transfers between devices with their start and end apart: 2 -> 0, of which waited for: 0 -> 0; matrix products, arithmetic and copies ran while one was open for 4% -> 0% of each run, Pallas kernels for 15% -> 0%
where the time goes in v3:
time: 495 us; the launch traced here: 486 us
  Pallas kernels  403 us (81%)
  local copies, waits for them, and re-layouts  61.5 us (12%)
  other arithmetic  11.9 us (2%)
  matrix products  7.38 us (1%)
    pallas_call x12, Pallas kernels, collective(): pl.pallas_call(kernel, out_shape=outs, in_specs=[VMEM] * near_in + [FAR]...  403 us
    unnamed x103, local copies, waits for them, and re-layouts  12.2 us
    gather x6, local copies, waits for them, and re-layouts, pick_rows(): jnp.take(table, where, axis=0)  11.3 us

profile of v3, /device:TPU:1, one launch (start us, length us, event | category | flops | bytes accessed | tf_op | source)
XLA Modules:
  0.0 486.2 jit_solution(12218450422652747216)
XLA Ops:
  0.7 1.3 reshape.989
  3.3 1.2 concatenate.51
  7.7 1.2 copy.244
  10.1 39.6 %shard_map.342 = (bf16[8,64,512]{2,1,0:T(8,128)(2,1)}, f32[128,128]{1,0:T(8,128)}, bf16[8,16,16,128]{3,2,1,0:T(8,128)(2,1)}) custom-call(bf16[8,64,512]{2,1,0:T(8,128)(2,1)} %pad.38.w_ref, f32[16,128,128]{2,1,0:T(8,128)} %bitcast.367, bf16[16,128]{1,0:T(8,128)(2,1)} %pad_bitcast_fusion.3.s_ref), custom_call_target="tpu_custom_call" | custom-call | tf_op jit(solution)/shard_map/pallas_call | solution.py:99
  49.7 1.1 copy_bitcast_fusion.3
  55.3 1.1 fusion.1.x_ref
  62.5 23.5 %shard_map.343 = (bf16[1152,432]{1,0:T(8,128)(2,1)}, bf16[1152,144]{1,0:T(8,128)(2,1)}) custom-call(bf16[80,384]{1,0:T(8,128)(2,1)} %get-tuple-element.306.left_ref, bf16[80,256]{1,0:T(8,128)(2,1)} %get-tuple-element.304.right_ref), custom_call_target="tpu_custom_call" | custom-call | tf_op jit(solution)/shard_map/pallas_call | solution.py:99
  88.0 37.3 %shard_map.344 = (f32[128,1152]{1,0:T(8,128)}, f32[128,1152]{1,0:T(8,128)}, bf16[1152,576]{1,0:T(8,128)(2,1)}, bf16[1152,576]{1,0:T(8,128)(2,1)}, bf16[1024,1152...) custom-call(f32[128,1152]{1,0:T(8,128)} %fusion.1.x_ref, ...), custom_call_target="tpu_custom_call" | custom-call | tf_op jit(solution)/shard_map/pallas_call | solution.py:99
  126.4 35.2 %shard_map.345 = (f32[128,1152]{1,0:T(8,128)}, f32[128,1152]{1,0:T(8,128)}, bf16[1152,432]{1,0:T(8,128)(2,1)}, bf16[1152,144]{1,0:T(8,128)(2,1)}, bf16[1024,1152...) custom-call(f32[128,1152]{1,0:T(8,128)} %get-tuple-element.89.x_ref, ...), custom_call_target="tpu_custom_call" | custom-call | tf_op jit(solution)/shard_map/pallas_call | solution.py:99
  162.3 1.2 scatter_custom_fusion
  163.5 4.6 gather_fusion
  168.1 0.9 fusion.11.x_ref
  170.0 35.8 %shard_map.346 = (f32[112,1152]{1,0:T(8,128)}, f32[112,1152]{1,0:T(8,128)}, bf16[1152,576]{1,0:T(8,128)(2,1)}, bf16[1152,576]{1,0:T(8,128)(2,1)}, bf16[896,1152]...) custom-call(f32[112,1152]{1,0:T(8,128)} %fusion.11.x_ref, ...), custom_call_target="tpu_custom_call" | custom-call | tf_op jit(solution)/shard_map/pallas_call | solution.py:99
  206.7 32.2 %shard_map.347 = (f32[112,1152]{1,0:T(8,128)}, f32[112,1152]{1,0:T(8,128)}, bf16[896,1152]{1,0:T(8,128)(2,1)}, bf16[896,576]{1,0:T(8,128)(2,1)}, bf16[896,576]{1,0:T(8,128)(2,1)}) custom-call(f32[112,1152]{1,0:T(8,128)} %get-tuple-element.95.x_ref, f32[8,1152]{1,0:T(8,128)} %get-tuple-element.291.vec_ref, f32[1,576]{1,0:T(1,128)} %broadcast_in_dim.134.bias_ref, ...), custom_call_target="tpu_custom_call" | custom-call | tf_op jit(solution)/shard_map/pallas_call | solution.py:99
  239.0 2.7 gather_fusion.1
  245.2 1.5 gather_fusion.2
  246.7 0.9 fusion.10.g_ref
  248.3 1.3 fusion.22.valid_ref
  249.6 36.9 %shard_map.348 = (f32[112,1152]{1,0:T(8,128)}, f32[8,1152]{1,0:T(8,128)}, f32[1,576]{1,0:T(1,128)}, bf16[16,80,640]{2,1,0:T(8,128)(2,1)}, bf16[16,80,512]{2,1,0:T(8,128)(2,1)}) custom-call(f32[112,1152]{1,0:T(8,128)} %fusion.10.g_ref, f32[112,1152]{1,0:T(8,128)} %get-tuple-element.95.x_ref, f32[112,1152]{1,0:T(8,128)} %get-tuple-element.99.mlp_ref, ...), custom_call_target="tpu_custom_call" | custom-call | tf_op jit(solution)/shard_map/pallas_call | solution.py:99
  286.5 38.2 %shard_map.349 = (f32[112,1152]{1,0:T(8,128)}, f32[8,1152]{1,0:T(8,128)}, f32[1,432]{1,0:T(1,128)}, bf16[16,80,384]{2,1,0:T(8,128)(2,1)}, bf16[16,80,256]{2,1,0:T(8,128)(2,1)}, /*index=5*/bf16[80,1152]{1,0:T(8,128)(2,1)}) custom-call(f32[112,1152]{1,0:T(8,128)} %get-tuple-element.103.g_ref, f32[112,1152]{1,0:T(8,128)} %fusion.11.x_ref, ...), custom_call_target="tpu_custom_call" | custom-call | tf_op jit(solution)/shard_map/pallas_call | solution.py:99
  324.7 2.6 gather_fusion.3
  327.3 1.0 fusion.5.g_ref
  328.9 38.1 %shard_map.350 = (f32[128,1152]{1,0:T(8,128)}, f32[8,1152]{1,0:T(8,128)}, f32[1,576]{1,0:T(1,128)}, bf16[16,80,640]{2,1,0:T(8,128)(2,1)}, bf16[16,80,512]{2,1,0:T(8,128)(2,1)}, /*index=5*/bf16[80,640]{1,0:T(8,128)(2,1)}) custom-call(f32[128,1152]{1,0:T(8,128)} %fusion.5.g_ref, f32[128,1152]{1,0:T(8,128)} %get-tuple-element.89.x_ref, ...), custom_call_target="tpu_custom_call" | custom-call | tf_op jit(solution)/shard_map/pallas_call | solution.py:99
  367.0 40.0 %shard_map.351 = (f32[128,1152]{1,0:T(8,128)}, f32[8,1152]{1,0:T(8,128)}, f32[1,432]{1,0:T(1,128)}, bf16[16,80,384]{2,1,0:T(8,128)(2,1)}, bf16[16,80,256]{2,1,0:T(8,128)(2,1)}, /*index=5*/bf16[80,1152]{1,0:T(8,128)(2,1)}) custom-call(f32[128,1152]{1,0:T(8,128)} %get-tuple-element.120.g_ref, f32[128,1152]{1,0:T(8,128)} %fusion.1.x_ref, ...), custom_call_target="tpu_custom_call" | custom-call | tf_op jit(solution)/shard_map/pallas_call | solution.py:99
  407.1 2.0 convolution_bitcast_fusion.2
  410.4 22.2 %shard_map.352 = bf16[80,640]{1,0:T(8,128)(2,1)} custom-call(bf16[4,4,80,384]{3,2,1,0:T(8,128)(2,1)} %bitcast.396, bf16[4,4,80,256]{3,2,1,0:T(8,128)(2,1)} %bitcast.400), custom_call_target="tpu_custom_call" | custom-call | tf_op jit(solution)/shard_map/pallas_call | solution.py:99
  432.6 0.9 pad_maximum_fusion.1
  443.2 23.5 %shard_map.353 = (bf16[8,64,512]{2,1,0:T(8,128)(2,1)}, bf16[8,16,16,128]{3,2,1,0:T(8,128)(2,1)}, f32[8,128]{1,0:T(8,128)}) custom-call(bf16[8,64,512]{2,1,0:T(8,128)(2,1)} %pad.45.g_ref, f32[8,16,128]{2,1,0:T(8,128)} %bitcast.414, f32[16,8,8,128]{3,2,1,0:T(8,128)} %copy.264), custom_call_target="tpu_custom_call" | custom-call | tf_op jit(solution)/shard_map/pallas_call | solution.py:99
  466.7 1.3 reshape.1047
  472.2 1.2 copy.232
  479.3 1.0 copy.235
  481.3 1.0 copy.236
  (367 shorter events, 50.9 us)
Async XLA Ops:
  0.7 4.9 %copy-start = (bf16[9,2304]{1,0:T(8,128)(2,1)S(1)}, bf16[9,2304]{1,0:T(8,128)(2,1)}, u32[]{:S(2)}) copy-start(bf16[9,2304]{1,0:T(8,128)(2,1)} %param.39) | copy-start | bytes 124420
  0.7 1.8 copy-start.17
  0.7 2.1 copy-start.12
  0.7 2.3 copy-start.13
  5.6 1.5 copy-start.33
  5.6 1.8 copy-start.34
  7.6 1.3 copy-start.26
  7.6 1.4 copy-start.25
  7.6 1.5 copy-start.35
  7.6 1.5 copy-start.36
  7.6 1.6 copy-start.37
  7.7 1.7 copy-start.38
  7.7 1.8 copy-start.32
  49.7 1.6 copy-start.18
  52.2 1.3 copy-start.19
  53.8 3.2 copy-start.16
  56.4 4.1 copy-start.8
  126.4 35.4 %copy-start.24 = (s32[1,512]{1,0:T(1,128)S(1)}, s32[1,512]{1,0:T(1,128)}, u32[]{:S(2)}) copy-start(s32[1,512]{1,0:T(1,128)} %param.26) | copy-start | bytes 6148
  239.0 2.7 copy-start.1
  407.0 25.6 %copy-start.10 = (bf16[80,1152]{1,0:T(8,128)(2,1)S(1)}, bf16[80,1152]{1,0:T(8,128)(2,1)}, u32[]{:S(2)}) copy-start(bf16[80,1152]{1,0:T(8,128)(2,1)} %get-tuple-element.135) | copy-start | bytes 552964
  407.0 25.6 %copy-start.11 = (bf16[80,1152]{1,0:T(8,128)(2,1)S(1)}, bf16[80,1152]{1,0:T(8,128)(2,1)}, u32[]{:S(2)}) copy-start(bf16[80,1152]{1,0:T(8,128)(2,1)} %get-tuple-element.134) | copy-start | bytes 552964
  407.0 25.6 %copy-start.15 = (bf16[80,640]{1,0:T(8,128)(2,1)S(1)}, bf16[80,640]{1,0:T(8,128)(2,1)}, u32[]{:S(2)}) copy-start(bf16[80,640]{1,0:T(8,128)(2,1)} %get-tuple-element.133) | copy-start | bytes 307204
  434.2 1.3 copy-start.21
  434.2 1.3 copy-start.22
  434.4 2.2 copy-start.7
  437.0 1.7 copy-start.31
  437.3 2.9 copy-start.28
  437.3 3.1 copy-start.29
  466.7 2.4 copy-start.6
  468.0 1.3 copy-start.4
  468.1 2.3 copy-start.27
  472.2 2.1 copy-start.9
  (8 other events, 8.0 us)

commit v4 on v3

--- a/solution.py
+++ b/solution.py
@@ -2,6 +2,7 @@
 
 import jax
 import jax.numpy as jnp
+import numpy as np
 from jax import lax
 from jax.experimental import pallas as pl
 from jax.experimental.pallas import tpu as pltpu
@@ -134,110 +135,6 @@
     )
 
 
-def spread_kernel(w_ref, m_ref, s_ref, w_out, m_out, s_out, m_got, m_two, ss, rs):
-    group, image = group_peers(), image_peers()
-    enter([peer for peer, _ in group + image])
-    sems = (ss, rs)
-    me, mine = own_group(), own_image()
-    first = []
-    for k, (peer, at) in enumerate(image):
-        first.append(send(m_ref.at[at], m_got.at[mine], sems, k, peer))
-        first.append(send(s_ref, s_out.at[me, mine], sems, 15 + k, peer))
-    weights = [send(w_ref.at[at], w_out.at[me], sems, 30 + k, p) for k, (p, at) in enumerate(group)]
-    w_out[me] = w_ref[me]
-    s_out[me, mine] = s_ref[...]
-    m_got[mine] = m_ref[mine]
-    for copy in first:
-        copy.wait_recv()
-    total = m_got[0]
-    for k in range(1, 16):
-        total = total + m_got[k]
-    m_two[me] = total
-    second = []
-    for k, (peer, _) in enumerate(group):
-        second.append(send(m_two.at[me], m_two.at[me], sems, 37 + k, peer))
-        second.append(send(s_out.at[me], s_out.at[me], sems, 44 + k, peer))
-    for copy in second:
-        copy.wait_recv()
-    total = m_two[0]
-    for k in range(1, 8):
-        total = total + m_two[k]
-    m_out[...] = total
-    for copy in weights:
-        copy.wait_recv()
-    for copy in first + second + weights:
-        copy.wait_send()
-
-
-def spread(weights, mods, small):
-    outs = (
-        jax.ShapeDtypeStruct(weights.shape, BF16),
-        jax.ShapeDtypeStruct((128, 128), F32),
-        jax.ShapeDtypeStruct((8, 16, *small.shape), BF16),
-    )
-    scratch = [pltpu.VMEM((16, 128, 128), F32), pltpu.VMEM((8, 128, 128), F32)] + dma_sems(51)
-    return collective(spread_kernel, 1, outs, scratch, weights, mods, small)
-
-
-def finish_kernel(g_ref, m_ref, s_ref, g_out, m_out, s_out, m_got, s_got, s_mine, s_two, ss, rs):
-    group, image = group_peers(), image_peers()
-    enter([peer for peer, _ in group + image])
-    sems = (ss, rs)
-    me, mine = own_group(), own_image()
-    first = [send(m_ref.at[at], m_got.at[me], sems, k, p) for k, (p, at) in enumerate(group)]
-    small = [send(s_ref.at[at], s_got.at[mine], sems, 7 + k, p) for k, (p, at) in enumerate(image)]
-    weights = [send(g_ref.at[at], g_out.at[me], sems, 22 + k, p) for k, (p, at) in enumerate(group)]
-    m_got[me] = m_ref[me]
-    s_got[mine] = s_ref[mine]
-    g_out[me] = g_ref[me]
-    for copy in first:
-        copy.wait_recv()
-    total = m_got[0]
-    for k in range(1, 8):
-        total = total + m_got[k]
-    m_out[me, mine] = total.astype(BF16)
-    second = [
-        send(m_out.at[me, mine], m_out.at[me, mine], sems, 29 + k, p)
-        for k, (p, _) in enumerate(image)
-    ]
-    for copy in small:
-        copy.wait_recv()
-    total = s_got[0]
-    for k in range(1, 16):
-        total = total + s_got[k]
-    s_mine[...] = total
-    pieces = [send(s_mine.at[at], s_two.at[me], sems, 44 + k, p) for k, (p, at) in enumerate(group)]
-    s_two[me] = s_mine[me]
-    for copy in second:
-        copy.wait_recv()
-    third = [send(m_out.at[me], m_out.at[me], sems, 51 + k, p) for k, (p, _) in enumerate(group)]
-    for copy in pieces:
-        copy.wait_recv()
-    total = s_two[0]
-    for k in range(1, 8):
-        total = total + s_two[k]
-    s_out[...] = total
-    for copy in weights + third:
-        copy.wait_recv()
-    for copy in first + small + weights + second + pieces + third:
-        copy.wait_send()
-
-
-def finish(grads, mods, small):
-    outs = (
-        jax.ShapeDtypeStruct(grads.shape, BF16),
-        jax.ShapeDtypeStruct((8, 16, 16, 128), BF16),
-        jax.ShapeDtypeStruct((8, 128), F32),
-    )
-    scratch = [
-        pltpu.VMEM((8, 16, 128), F32),
-        pltpu.VMEM((16, 8, 8, 128), F32),
-        pltpu.VMEM((8, 8, 128), F32),
-        pltpu.VMEM((8, 8, 128), F32),
-    ] + dma_sems(58)
-    return collective(finish_kernel, 2, outs, scratch, grads, mods, small)
-
-
 def layer_stats(value_rows):
     centered = value_rows - jnp.mean(value_rows, axis=-1, keepdims=True)
     inv_std = lax.rsqrt(jnp.mean(centered * centered, axis=-1, keepdims=True) + 1e-06)
@@ -433,32 +330,45 @@
                 total = own.astype(F32)
                 for source in range(3):
                     total = total + got[source, k].astype(F32)
-                mine[k] = total.astype(BF16)
+                mine[k] = total.astype(mine.dtype)
 
             for k, (peer, at) in enumerate(peers):
                 part = mine.at[at]
                 copy = send(part, self.last[side].at[k], self.sems, 6 + 3 * side + k, peer)
                 self.second.append(copy)
 
-    def end(self, out_ref):
-        cut = self.left.shape[3]
+    def end(self):
         for copy in self.second:
             copy.wait_recv()
-        for side, own, cols in ((0, self.z, slice(0, cut)), (1, self.x, slice(cut, None))):
+        totals = []
+        for side, own in ((0, self.z), (1, self.x)):
             total = self.mine[side][own].astype(F32)
             for source in range(3):
                 total = total + self.last[side][source].astype(F32)
-            out_ref[:, cols] = total.astype(BF16)
+            totals.append(total)
+        return totals
+
+    def end_rows(self, out_ref):
+        cut = self.left.shape[3]
+        left, right = self.end()
+        out_ref[:, :cut] = left.astype(BF16)
+        out_ref[:, cut:] = right.astype(BF16)
+        self.leave()
+
+    def leave(self):
         for copy in self.first + self.second:
             copy.wait_send()
 
 
 def rows_out_scratch(cols):
-    widths = (CUT[cols], cols - CUT[cols])
+    return sum_scratch([(SLAB, CUT[cols]), (SLAB, cols - CUT[cols])], BF16)
+
+
+def sum_scratch(shapes, dtype):
     return (
-        [pltpu.VMEM((3, 4, SLAB, w), BF16) for w in widths]
-        + [pltpu.VMEM((4, SLAB, w), BF16) for w in widths]
-        + [pltpu.VMEM((3, SLAB, w), BF16) for w in widths]
+        [pltpu.VMEM((3, 4, *shape), dtype) for shape in shapes]
+        + [pltpu.VMEM((4, *shape), dtype) for shape in shapes]
+        + [pltpu.VMEM((3, *shape), dtype) for shape in shapes]
         + dma_sems(12)
     )
 
@@ -484,34 +394,14 @@
         right_ref[k] = rows[:, cut:]
 
 
-def fetch_kernel(left_ref, right_ref, one_ref, two_ref, *scratch):
-    rows = RowsIn(left_ref, right_ref, scratch)
-    enter(rows.peers())
-    rows.start()
-    rows.middle()
-    rows.end(one_ref, two_ref)
+def slab_views(rows_ref, start, cols):
+    cut = start + CUT[cols]
+    return rows_ref.at[:, start:cut], rows_ref.at[:, cut : start + cols]
 
 
 def weight_shapes(cols):
     widths = (3 * HW, HW) if cols == ATT_COLS else (FW, FW)
     return tuple(jax.ShapeDtypeStruct((D, w), BF16) for w in widths)
-
-
-def fetch_rows(pair, cols, cid):
-    return collective(fetch_kernel, cid, weight_shapes(cols), rows_in_scratch(cols), *pair)
-
-
-def reduce_kernel(left_ref, right_ref, out_ref, *scratch):
-    rows = RowsOut(left_ref, right_ref, scratch)
-    enter(rows.peers())
-    rows.start()
-    rows.middle()
-    rows.end(out_ref)
-
-
-def reduce_rows(pair, cols, cid):
-    out = jax.ShapeDtypeStruct((SLAB, cols), BF16)
-    return collective(reduce_kernel, cid, out, rows_out_scratch(cols), *slabs(pair))
 
 
 class Ring:
@@ -665,13 +555,15 @@
 
 
 def ffn_forward_kernel(
-    x_ref, vec_ref, bias_ref, we_ref, wr_ref, next_left, next_right,
+    x_ref, vec_ref, bias_ref, we_ref, wr_ref, rows_ref,
     out_ref, mlp_ref, next_one, next_two, all_out, hid_out, slope_out,
     x16, all_ref, hid_ref, slope_ref, move_sems, *scratch
 ):
     tokens = x_ref.shape[0]
     ring = Ring(tokens, scratch[:9])
-    rows_in = RowsIn(next_left, next_right, scratch[9:]) if scratch[9:] else None
+    rows_in = None
+    if scratch[9:]:
+        rows_in = RowsIn(*slab_views(rows_ref, ATT_COLS, ATT_COLS), scratch[9:])
     moves = Moves(move_sems)
     peers = ring.peers() + (rows_in.peers() if rows_in else [])
     greet(peers)
@@ -714,7 +606,7 @@
     x_ref, vec_ref, bias_ref, we_ref, wr_ref, out_ref, mlp_ref, all_out, hid_out, slope_out, *scratch
 ):
     ffn_forward_kernel(
-        x_ref, vec_ref, bias_ref, we_ref, wr_ref, None, None,
+        x_ref, vec_ref, bias_ref, we_ref, wr_ref, None,
         out_ref, mlp_ref, None, None, all_out, hid_out, slope_out, *scratch
     )
 
@@ -725,17 +617,17 @@
     outs = (
         jax.ShapeDtypeStruct((tokens, D), F32),
         jax.ShapeDtypeStruct((tokens, D), F32),
-        *(weight_shapes(ATT_COLS) if following else ()),
+        *(weight_shapes(ATT_COLS) if following is not None else ()),
         *(jax.ShapeDtypeStruct(shape, BF16) for shape in saved),
     )
     scratch = [pltpu.VMEM((tokens, D), BF16)]
     scratch += [pltpu.VMEM(shape, BF16) for shape in saved]
     scratch += [pltpu.SemaphoreType.DMA((3,))] + ring_scratch(tokens)
     kernel = ffn_forward_last_kernel
-    if following:
+    if following is not None:
         scratch += rows_in_scratch(ATT_COLS)
         kernel = ffn_forward_kernel
-    operands = (x, vecs, bias, we, wr, *following)
+    operands = (x, vecs, bias, we, wr) + (() if following is None else (following,))
     return collective(kernel, cid, outs, scratch, *operands, far_out=3)
 
 
@@ -802,7 +694,7 @@
 
     write_slabs(whole, dw_left, dw_right)
     if rows_out:
-        rows_out.end(summed)
+        rows_out.end_rows(summed)
     second_grad = ring.total()
     normed, inv_std = layer_stats(x_ref[...])
     vecs_ref[0:1] = sum_rows(second_grad)
@@ -836,6 +728,285 @@
     return collective(ffn_backward_kernel, cid, outs, scratch, *operands, far_in=3)
 
 
+def open_kernel(
+    w_ref, pick_ref, m_ref, s_ref, rows_ref, one_ref, two_ref, m_out, s_out,
+    w_got, m_got, m_sum, ss, rs, *scratch
+):
+    group = group_peers()
+    sib, up, down, far = ring_peers()
+    fetch = RowsIn(*slab_views(rows_ref, 0, ATT_COLS), scratch[:4])
+    mods = RowsOut(m_ref.at[:, :, 0:64], m_ref.at[:, :, 64:128], scratch[4:])
+    enter([peer for peer, _ in group] + fetch.peers())
+    sems = (ss, rs)
+    me, x, z = own_group(), lax.axis_index("dp_0"), lax.axis_index("dp_1")
+    weights = [send(w_ref.at[at], w_got.at[me], sems, k, p) for k, (p, at) in enumerate(group)]
+    small = s_out.at[me, x, z]
+    first = [send(s_ref, small, sems, 7 + k, p) for k, (p, _) in enumerate(fetch.along_z)]
+    mods.start()
+    w_got[me] = w_ref[me]
+    s_out[me, x, z] = s_ref[...]
+    for copy in first:
+        copy.wait_recv()
+    small = s_out.at[me, x]
+    second = [send(small, small, sems, 10 + k, p) for k, (p, _) in enumerate(fetch.along_x)]
+    for copy in weights:
+        copy.wait_recv()
+    received = w_got[...].reshape(8 * w_got.shape[1], PIECE)
+    for k in range(PIECES):
+        cols = slice(k * PIECE, (k + 1) * PIECE)
+        rows_ref[:, cols] = dot_nn(pick_ref[k], received).astype(BF16)
+    fetch.start()
+    for copy in second:
+        copy.wait_recv()
+    small = s_out.at[me]
+    third = [send(small, small, sems, 13 + k, p) for k, p in enumerate((up, down, far, sib))]
+    mods.middle()
+    fetch.middle()
+    left, right = mods.end()
+    m_sum[0:64] = left
+    m_sum[64:128] = right
+
+    def chunk(ref, index):
+        return ref.at[pl.ds(pl.multiple_of(index * 16, 16), 16)]
+
+    m_first = [
+        send(chunk(m_sum, at), m_got.at[me], sems, 20 + k, p) for k, (p, at) in enumerate(group)
+    ]
+    mine = pl.ds(pl.multiple_of(me * 16, 16), 16)
+    m_got[me] = m_sum[mine, :]
+    for copy in m_first:
+        copy.wait_recv()
+    total = m_got[0]
+    for k in range(1, 8):
+        total = total + m_got[k]
+    m_out[mine, :] = total
+    part = chunk(m_out, me)
+    m_second = [send(part, part, sems, 27 + k, p) for k, (p, _) in enumerate(group)]
+    c, y = lax.axis_index("tx"), lax.axis_index("ty")
+    fourth = []
+    for k, d in enumerate((3, 1, 2)):
+        third[k].wait_recv()
+        small = s_out.at[c * 4 + lax.rem(y + d, 4)]
+        fourth.append(send(small, small, sems, 17 + k, sib))
+    fetch.end(one_ref, two_ref)
+    for copy in m_second + fourth + third[3:]:
+        copy.wait_recv()
+    for copy in weights + first + second + third + fourth + m_first + m_second:
+        copy.wait_send()
+    mods.leave()
+
+
+def picking():
+    picks = np.zeros((PIECES, SLAB, 8 * 64), np.float32)
+    for k in range(PIECES):
+        for row in range(72):
+            picks[k, row, row // 9 * 64 + 9 * k + row % 9] = 1.0
+    return picks
+
+
+def open_up(weights, mods, small):
+    outs = (
+        jax.ShapeDtypeStruct((SLAB, ALL_COLS), BF16),
+        *weight_shapes(ATT_COLS),
+        jax.ShapeDtypeStruct((128, 128), F32),
+        jax.ShapeDtypeStruct((8, 4, 4, *small.shape), BF16),
+    )
+    scratch = [
+        pltpu.VMEM(weights.shape, BF16),
+        pltpu.VMEM((8, 16, 128), F32),
+        pltpu.VMEM((128, 128), F32),
+    ] + dma_sems(34)
+    scratch += rows_in_scratch(ATT_COLS) + sum_scratch([(64, 128), (64, 128)], F32)
+    picks = jnp.asarray(picking(), BF16)
+    return collective(open_kernel, 1, outs, scratch, weights, picks, mods, small)
+
+
+EARLY = ATT_COLS + 2 * FFN_COLS
+EARLY_PIECES = -(-EARLY // PIECE)
+LATE_PIECES = -(-ATT_COLS // PIECE)
+LATE_ROWS = 32
+
+
+def packed_rows(picks_ref, parts, pieces):
+    columns = jnp.concatenate(parts, axis=1)
+    spare = pieces * PIECE - columns.shape[1]
+    columns = jnp.concatenate([columns, jnp.zeros((SLAB, spare), BF16)], axis=1)
+    total = jnp.zeros((8 * 64, PIECE), F32)
+    for k in range(pieces):
+        total = total + dot_tn(picks_ref[k], columns[:, k * PIECE : (k + 1) * PIECE])
+    return total.astype(BF16).reshape(8, 64, PIECE)
+
+
+def finish_kernel(
+    left_ref, right_ref, attn_ref, ffn_one_ref, ffn_two_ref, picks_ref, m_ref, s_ref,
+    early_out, late_out, m_out, s_out,
+    early, late, m_got, s_mine, s_two, late_rows, ss, rs, *scratch
+):
+    group = group_peers()
+    sib, up, down, far = ring_peers()
+    rows = RowsOut(left_ref, right_ref, scratch[:8])
+    small = RowsOut(s_ref.at[:, :, 0:32], s_ref.at[:, :, 32:64], scratch[8:])
+    peers = [peer for peer, _ in group] + rows.peers()
+    greet(peers)
+    me, x, z = own_group(), lax.axis_index("dp_0"), lax.axis_index("dp_1")
+    sems = (ss, rs)
+    met(peers)
+    rows.start()
+    m_first = [send(m_ref.at[at], m_got.at[me], sems, k, p) for k, (p, at) in enumerate(group)]
+    small.start()
+    early[...] = packed_rows(
+        picks_ref, [attn_ref[...], ffn_one_ref[...], ffn_two_ref[...]], EARLY_PIECES
+    )
+    sent = [send(early.at[at], early_out.at[me], sems, 7 + k, p) for k, (p, at) in enumerate(group)]
+    early_out[me] = early[me]
+    m_got[me] = m_ref[me]
+    for copy in m_first:
+        copy.wait_recv()
+    total = m_got[0]
+    for k in range(1, 8):
+        total = total + m_got[k]
+    m_out[me, x, z] = total.astype(BF16)
+    part = m_out.at[me, x, z]
+    m_second = [send(part, part, sems, 14 + k, p) for k, (p, _) in enumerate(rows.along_z)]
+    small.middle()
+    for copy in m_second:
+        copy.wait_recv()
+    part = m_out.at[me, x]
+    m_third = [send(part, part, sems, 17 + k, p) for k, (p, _) in enumerate(rows.along_x)]
+    left, right = small.end()
+    s_mine[0:4] = left.reshape(4, 8, 128)
+    s_mine[4:8] = right.reshape(4, 8, 128)
+    s_last = [send(s_mine.at[at], s_two.at[me], sems, 20 + k, p) for k, (p, at) in enumerate(group)]
+    s_two[me] = s_mine[me]
+    for copy in m_third:
+        copy.wait_recv()
+    part = m_out.at[me]
+    m_fourth = [send(part, part, sems, 27 + k, p) for k, p in enumerate((up, down, far, sib))]
+    rows.middle()
+    c, y = lax.axis_index("tx"), lax.axis_index("ty")
+    m_fifth = []
+    for k, d in enumerate((3, 1, 2)):
+        m_fourth[k].wait_recv()
+        part = m_out.at[c * 4 + lax.rem(y + d, 4)]
+        m_fifth.append(send(part, part, sems, 31 + k, sib))
+    for copy in s_last:
+        copy.wait_recv()
+    total = s_two[0]
+    for k in range(1, 8):
+        total = total + s_two[k]
+    s_out[...] = total
+    rows.end_rows(late_rows)
+    late[...] = packed_rows(picks_ref, [late_rows[...]], LATE_PIECES)[:, :LATE_ROWS]
+    later = [send(late.at[at], late_out.at[me], sems, 34 + k, p) for k, (p, at) in enumerate(group)]
+    late_out[me] = late[me]
+    for copy in sent + m_fourth[3:] + m_fifth + later:
+        copy.wait_recv()
+    small.leave()
+    for copy in m_first + sent + m_second + m_third + s_last + m_fourth + m_fifth + later:
+        copy.wait_send()
+
+
+def finish(pair, attn, ffn_one, ffn_two, mods, small):
+    outs = (
+        jax.ShapeDtypeStruct((8, 64, PIECE), BF16),
+        jax.ShapeDtypeStruct((8, LATE_ROWS, PIECE), BF16),
+        jax.ShapeDtypeStruct((8, 4, 4, 16, 128), BF16),
+        jax.ShapeDtypeStruct((8, 128), F32),
+    )
+    scratch = [
+        pltpu.VMEM((8, 64, PIECE), BF16),
+        pltpu.VMEM((8, LATE_ROWS, PIECE), BF16),
+        pltpu.VMEM((8, 16, 128), F32),
+        pltpu.VMEM((8, 8, 128), F32),
+        pltpu.VMEM((8, 8, 128), F32),
+        pltpu.VMEM((SLAB, ATT_COLS), BF16),
+    ] + dma_sems(41)
+    scratch += rows_out_scratch(ATT_COLS) + sum_scratch([(32, 128), (32, 128)], F32)
+    picks = jnp.asarray(picking(), BF16)
+    operands = (*slabs(pair), attn, ffn_one, ffn_two, picks, mods, small)
+    return collective(finish_kernel, 2, outs, scratch, *operands)
+
+
+def unpicking(pieces, height):
+    picks = np.zeros((pieces, 128, 8 * height), np.float32)
+    for k in range(pieces):
+        for group in range(8):
+            for row in range(9):
+                picks[k, group * 16 + row, group * height + 9 * k + row] = 1.0
+    return picks
+
+
+def close_kernel(
+    early_ref, late_ref, early_picks, late_picks, g_ref, cond_ref, mod_ref, final_ref,
+    attn_ref, merge_ref, expand_ref, reduce_ref, mod_grad_ref, final_grad_ref, terms_ref, bias_ref,
+    early, late
+):
+    received = early_ref[...].reshape(8 * 64, PIECE)
+    for k in range(EARLY_PIECES):
+        early[:, k * PIECE : (k + 1) * PIECE] = dot_nn(early_picks[k], received)
+    received = late_ref[...].reshape(8 * LATE_ROWS, PIECE)
+    for k in range(LATE_PIECES):
+        late[:, k * PIECE : (k + 1) * PIECE] = dot_nn(late_picks[k], received)
+
+    def whole(source, start, width):
+        parts = [source[g * 16 : g * 16 + 16, start : start + width] for g in range(8)]
+        return jnp.concatenate(parts, axis=1)[:9]
+
+    for b, (source, start) in enumerate(((late, 0), (early, 0))):
+        for j in range(3):
+            attn_ref[b, j] = whole(source, start + j * HW, HW)
+        merge_ref[b] = whole(source, start + 3 * HW, HW)
+    for b, start in enumerate((ATT_COLS, ATT_COLS + FFN_COLS)):
+        expand_ref[b] = whole(early, start, FW)
+        reduce_ref[b] = whole(early, start + FW, FW)
+    terms = jnp.zeros((16, 9), F32)
+    for b in range(3):
+        grads = g_ref[:, 6 * b * D : min(6 * b + 6, 14) * D]
+        weights = mod_ref[b] if b < 2 else final_ref[...]
+        product = dot_tn(cond_ref[...], grads)
+        if b < 2:
+            mod_grad_ref[b] = product
+        else:
+            final_grad_ref[...] = product
+        terms = terms + dot_nt(grads, weights)
+    terms_ref[...] = terms
+    bias_ref[...] = sum_rows(g_ref[...].astype(F32))
+
+
+def close(early, late, grads, cond, mod_weight, final_weight):
+    outs = (
+        jax.ShapeDtypeStruct((2, 3, 9, D), F32),
+        jax.ShapeDtypeStruct((2, 9, D), F32),
+        jax.ShapeDtypeStruct((2, 9, FF), F32),
+        jax.ShapeDtypeStruct((2, 9, FF), F32),
+        jax.ShapeDtypeStruct((2, 9, 6 * D), F32),
+        jax.ShapeDtypeStruct((9, 2 * D), F32),
+        jax.ShapeDtypeStruct((16, 9), F32),
+        jax.ShapeDtypeStruct((1, 16384), F32),
+    )
+    operands = (
+        early,
+        late,
+        jnp.asarray(unpicking(EARLY_PIECES, 64), BF16),
+        jnp.asarray(unpicking(LATE_PIECES, LATE_ROWS), BF16),
+        grads,
+        cond,
+        mod_weight,
+        final_weight,
+    )
+    return pl.pallas_call(
+        close_kernel,
+        out_shape=outs,
+        in_specs=[VMEM] * len(operands),
+        out_specs=(VMEM,) * len(outs),
+        scratch_shapes=[
+            pltpu.VMEM((128, EARLY_PIECES * PIECE), F32),
+            pltpu.VMEM((128, LATE_PIECES * PIECE), F32),
+        ],
+        compiler_params=pltpu.CompilerParams(vmem_limit_bytes=32 << 20),
+    )(*operands)
+
+
 HEAD = D // HEADS
 SCALE = HEAD ** (-0.5)
 
@@ -845,14 +1016,14 @@
 
 
 def attn_forward_kernel(
-    x_ref, vec_ref, bias_ref, mask_ref, wqkv_ref, wm_ref, next_left, next_right,
-    out_ref, branch_ref, next_one, next_two, *refs
+    x_ref, vec_ref, bias_ref, mask_ref, wqkv_ref, wm_ref, rows_ref,
+    out_ref, branch_ref, next_one, next_two, *refs, start
 ):
     outs, (x16, *kept, move_sems), scratch = refs[:6], refs[6:14], refs[14:]
     all_ref, q_ref, k_ref, v_ref, lse_ref, att_ref = kept
     tokens = x_ref.shape[0]
     ring = Ring(tokens, scratch[:9])
-    rows_in = RowsIn(next_left, next_right, scratch[9:])
+    rows_in = RowsIn(*slab_views(rows_ref, start, FFN_COLS), scratch[9:])
     moves = Moves(move_sems)
     peers = ring.peers() + rows_in.peers()
     greet(peers)
@@ -919,7 +1090,7 @@
     )
 
 
-def attn_forward(x, vecs, bias, mask, wqkv, wm, following, cid):
+def attn_forward(x, vecs, bias, mask, wqkv, wm, rows, start, cid):
     tokens = x.shape[0]
     outs = (
         jax.ShapeDtypeStruct((tokens, D), F32),
@@ -930,8 +1101,9 @@
     scratch = [pltpu.VMEM((tokens, D), BF16)]
     scratch += [pltpu.VMEM(*shape) for shape in kept_shapes(tokens)]
     scratch += [pltpu.SemaphoreType.DMA((6,))] + ring_scratch(tokens) + rows_in_scratch(FFN_COLS)
-    operands = (x, vecs, bias, mask, wqkv, wm, *following)
-    return collective(attn_forward_kernel, cid, outs, scratch, *operands, far_out=6)
+    operands = (x, vecs, bias, mask, wqkv, wm, rows)
+    kernel = functools.partial(attn_forward_kernel, start=start)
+    return collective(kernel, cid, outs, scratch, *operands, far_out=6)
 
 
 def attn_backward_kernel(
@@ -1013,7 +1185,7 @@
         )
 
     write_slabs(whole, dw_left, dw_right)
-    rows_out.end(summed)
+    rows_out.end_rows(summed)
     input_grad = ring.total()
     normed, inv_std = layer_stats(x_ref[...])
     vecs_ref[0:1] = sum_rows(input_grad)
@@ -1045,7 +1217,7 @@
     return collective(attn_backward_kernel, cid, outs, scratch, *operands, far_in=6)
 
 
-def block_forward(x, mod, attn_w, biases, mask, next_ffn, next_attn, cid):
+def block_forward(x, mod, attn_w, biases, mask, rows, start, more_blocks, cid):
     attn_b, merge_b, expand_b, reduce_b = (b.astype(F32) for b in biases)
     group = own_group()
     zeros = jnp.zeros((4, D), F32)
@@ -1059,11 +1231,12 @@
         ]
     )[None]
     middle, branch, we, wr, *kept = attn_forward(
-        x, vec_one, bias, mask, *attn_w, next_ffn, cid
+        x, vec_one, bias, mask, *attn_w, rows, start, cid
     )
     e_bias = lax.dynamic_slice_in_dim(expand_b, group * FW, FW)[None]
-    output, mlp, *more = ffn_forward(middle, vec_two, e_bias, we, wr, next_attn, cid + 1)
-    following, more = (more[:2], more[2:]) if next_attn else ((), more)
+    next_rows = rows if more_blocks else None
+    output, mlp, *more = ffn_forward(middle, vec_two, e_bias, we, wr, next_rows, cid + 1)
+    following, more = (more[:2], more[2:]) if more_blocks else ((), more)
     params = (*attn_w, we, wr)
     return output, following, params, (x, vec_one, mask, middle, branch, kept, vec_two, mlp, more)
 
@@ -1112,41 +1285,6 @@
 def pack_pieces(columns):
     pieces = columns.reshape(8, 9, PIECES, PIECE).swapaxes(1, 2)
     return jnp.pad(pieces.reshape(8, 9 * PIECES, PIECE), [(0, 0), (0, 1), (0, 0)])
-
-
-def unpack_pieces(packed):
-    pieces = packed[:, : 9 * PIECES].reshape(8, PIECES, 9, PIECE)
-    return pieces.swapaxes(1, 2).reshape(8, 9, ALL_COLS)
-
-
-def unpack_rows(packed):
-    return unpack_pieces(packed).reshape(72, ALL_COLS)
-
-
-def pack_grads(attn_one, attn_two, ffn_one, ffn_two):
-    columns = jnp.concatenate([attn_one, attn_two, ffn_one, ffn_two], axis=1)
-    return pack_pieces(columns[:72].reshape(8, 9, ALL_COLS))
-
-
-def slab_pair(rows, start, cols):
-    part = jnp.pad(rows[:, start : start + cols], [(0, SLAB - PART), (0, 0)])
-    return part[:, : CUT[cols]], part[:, CUT[cols] :]
-
-
-def unpack_grads(packed):
-    columns = unpack_pieces(packed)
-
-    def whole(at, width, inner):
-        parts = columns[:, :, at : at + inner * width].reshape(8, 9, inner, width)
-        return parts.transpose(1, 2, 0, 3).reshape(9, inner, 8 * width).astype(F32)
-
-    starts = (0, ATT_COLS), (2 * ATT_COLS, 2 * ATT_COLS + FFN_COLS)
-    return (
-        jnp.stack([whole(at, HW, 3) for at in starts[0]]),
-        jnp.stack([whole(at + 3 * HW, HW, 1)[:, 0] for at in starts[0]]),
-        jnp.stack([whole(at, FW, 1)[:, 0] for at in starts[1]]),
-        jnp.stack([whole(at + FW, FW, 1)[:, 0] for at in starts[1]]),
-    )
 
 
 def pack_small(parts):
@@ -1227,7 +1365,6 @@
         reduce_bias,
     )
     cond_rows = jax.nn.silu(condition.astype(F32)).astype(BF16)
-    mod_cuts = (6 * D, 12 * D, 14 * D)
     mod_piece = modulation_bias.shape[1]
     final_piece = final_offsets.shape[0]
     placed_bias = jnp.zeros((MOD_ALL,), F32)
@@ -1247,12 +1384,14 @@
     )
     mod_parts = jnp.pad(mod_parts + placed_bias[None], [(0, 0), (0, 16384 - MOD_ALL)])
     packed = pack_weights(attention_weight, merge_weight, expand_weight, reduce_weight)
-    packed, mods, small = spread(packed, mod_parts.reshape(16, 128, 128), pack_small(small_parts))
+    rows, *first_attn, mods, small = open_up(
+        packed, mod_parts.reshape(4, 4, 128, 128), pack_small(small_parts)
+    )
     mods = mods.reshape(1, 16384)
     mod_one = mods[:, : 6 * D]
     mod_two = mods[:, 6 * D : 12 * D]
     head_mod = mods[:, 12 * D : 14 * D]
-    small = small.transpose(1, 0, 2, 3).reshape(128, 2048)
+    small = small.reshape(8, 16, 2048).swapaxes(0, 1).reshape(128, 2048)
     pieces = jnp.split(small, [sum(SMALL_IN[:k]) for k in range(1, 8)], axis=1)
     embed_w = from_owner(pieces[0], (16, D), 1)
     embed_b = from_owner(pieces[1], (D,), 0)
@@ -1261,11 +1400,6 @@
     merge_b = from_owner(pieces[4], (2, D), 1)
     expand_b = from_owner(pieces[5], (2, FF), 1)
     reduce_b = from_owner(pieces[6], (2, D), 1)
-    rows = unpack_rows(packed)
-    first_attn = fetch_rows(slab_pair(rows, 0, ATT_COLS), ATT_COLS, 3)
-    second_attn_rows = slab_pair(rows, ATT_COLS, ATT_COLS)
-    first_ffn_rows = slab_pair(rows, 2 * ATT_COLS, FFN_COLS)
-    second_ffn_rows = slab_pair(rows, 2 * ATT_COLS + FFN_COLS, FFN_COLS)
     placed = sincos_table(row_index.astype(jnp.float32), col_index.astype(jnp.float32), width)
     patches = to_patches(latent)
     initial_tokens = (
@@ -1283,8 +1417,9 @@
         first_attn,
         first_biases,
         mask_one,
-        first_ffn_rows,
-        second_attn_rows,
+        rows,
+        2 * ATT_COLS,
+        True,
         10,
     )
     middle_one = middle_one[None]
@@ -1295,8 +1430,9 @@
         second_attn,
         second_biases,
         mask_two,
-        second_ffn_rows,
-        (),
+        rows,
+        2 * ATT_COLS + FFN_COLS,
+        False,
         20,
     )
     middle_two = middle_two[None]
@@ -1329,7 +1465,6 @@
         grad_middle[0], saved_one, first_params, everyone[0][:, None], slabs(dw_attn_two), 10
     )
     grad_start = grad_start[None]
-    attn_one = reduce_rows(dw_attn_one, ATT_COLS, 5)
     start_grad16 = grad_start.astype(jnp.bfloat16)
     grad_embed_w = jnp.einsum(
         "btp,btd->pd", patches, start_grad16, preferred_element_type=jnp.float32
@@ -1355,45 +1490,31 @@
     )
     small_out = jnp.pad(small_out, [(0, 0), (0, 1024 - small_out.shape[1])])
     grad_mods = jnp.concatenate([mod_grad_one, mod_grad_two, head_grad_mod[0]])
-    grad_mods = jnp.pad(grad_mods.reshape(8, MOD_ALL // 8), [(0, 0), (0, 2048 - MOD_ALL // 8)])
-    packed_grads, mod_back, small_back = finish(
-        pack_grads(attn_one, attn_two, ffn_one, ffn_two),
+    grad_mods = jnp.pad(grad_mods, (0, 16384 - MOD_ALL))
+    early, late, mod_back, small_back = finish(
+        dw_attn_one,
+        attn_two,
+        ffn_one,
+        ffn_two,
         grad_mods.reshape(8, 16, 128),
-        small_out.reshape(16, 8, 8, 128),
-    )
+        small_out.reshape(4, 4, 64, 128),
+    )
+    mod_back = mod_back.reshape(8, 16, 2048).swapaxes(0, 1).reshape(16, 16384)
+    attn_grad, *closed = close(
+        early, late, mod_back, cond_rows, modulation_weight, final_modulation
+    )
+    merge_grad, expand_grad, reduce_grad, mod_weight_grad, final_mod_grad, cond_terms, bias_sum = closed
     small_back = small_back.reshape(1024)
     small_sizes = (*SMALL_IN, 32)
     small_sums = jnp.split(small_back, [sum(small_sizes[:k]) for k in range(1, 9)])
-    mod_back = mod_back.reshape(8, 16, 2048)[:, :, : MOD_ALL // 8]
-    mod_back = mod_back.transpose(1, 0, 2).reshape(16, MOD_ALL)
-    one16 = mod_back[:, : mod_cuts[0]]
-    two16 = mod_back[:, mod_cuts[0] : mod_cuts[1]]
-    head16 = mod_back[:, mod_cuts[1] :]
-    stacked = unpack_grads(packed_grads)
-    mod_weight_grad = jnp.stack(
-        [
-            jnp.einsum("id,ie->de", cond_rows, one16, preferred_element_type=jnp.float32),
-            jnp.einsum("id,ie->de", cond_rows, two16, preferred_element_type=jnp.float32),
-        ]
-    )
     mod_bias_grad = jnp.stack(
         [
-            lax.dynamic_slice_in_dim(
-                jnp.sum(one16.astype(jnp.float32), axis=0), whole_index * mod_piece, mod_piece
-            ),
-            lax.dynamic_slice_in_dim(
-                jnp.sum(two16.astype(jnp.float32), axis=0), whole_index * mod_piece, mod_piece
-            ),
+            lax.dynamic_slice_in_dim(bias_sum[0], at + whole_index * mod_piece, mod_piece)
+            for at in (0, 6 * D)
         ]
     )
-    final_mod_grad = jnp.einsum("id,ie->de", cond_rows, head16, preferred_element_type=jnp.float32)
     final_bias_grad = lax.dynamic_slice_in_dim(
-        jnp.sum(head16.astype(jnp.float32), axis=0), whole_index * final_piece, final_piece
-    )
-    cond_terms = (
-        jnp.einsum("ie,de->id", one16, modulation_weight[0], preferred_element_type=jnp.float32)
-        + jnp.einsum("ie,de->id", two16, modulation_weight[1], preferred_element_type=jnp.float32)
-        + jnp.einsum("ie,de->id", head16, final_modulation, preferred_element_type=jnp.float32)
+        bias_sum[0], 12 * D + whole_index * final_piece, final_piece
     )
     silu_value, silu_pull = jax.vjp(jax.nn.silu, condition.astype(jnp.float32))
     condition_grad = silu_pull(cond_terms)[0]
@@ -1405,13 +1526,13 @@
         small_sums[1],
         mod_weight_grad,
         mod_bias_grad,
-        stacked[0],
+        attn_grad.swapaxes(1, 2),
         small_sums[3].reshape(2, 18),
-        stacked[1],
+        merge_grad,
         small_sums[4].reshape(2, 9),
-        stacked[2],
+        expand_grad,
         small_sums[5].reshape(2, 36),
-        stacked[3],
+        reduce_grad,
         small_sums[6].reshape(2, 9),
         final_mod_grad,
         final_bias_grad,

time: 495 us -> 453 us (0.915)
  Pallas kernels: 403 us -> 373 us
    pallas_call x12 -> x10, Pallas kernels: 403 us -> 371 us  [collective(): pl.pallas_call(kernel, out_shape=outs, in_specs=[VMEM] * near_in + [FAR]...]
    unnamed x103 -> x97, local copies, waits for them, and re-layouts: 12.2 us -> 12.9 us
where the time goes in v4:
time: 453 us; the launch traced here: 448 us
  Pallas kernels  373 us (82%)
  local copies, waits for them, and re-layouts  56.8 us (13%)
  other arithmetic  11.1 us (2%)
  matrix products  4.85 us (1%)
    pallas_call x10, Pallas kernels, collective(): pl.pallas_call(kernel, out_shape=outs, in_specs=[VMEM] * near_in + [FAR]...  371 us
    unnamed x97, local copies, waits for them, and re-layouts  12.9 us
    gather x6, local copies, waits for them, and re-layouts, pick_rows(): jnp.take(table, where, axis=0)  10 us

profile of v4, /device:TPU:1, one launch (start us, length us, event | category | flops | bytes accessed | tf_op | source)
XLA Modules:
  0.0 448.5 jit_solution(13666332192242960719)
XLA Ops:
  0.7 1.3 reshape.836
  3.2 1.2 concatenate.48
  6.8 1.2 copy.226
  9.2 39.4 %shard_map.378 = (bf16[80,3584]{1,0:T(8,128)(2,1)}, bf16[1152,432]{1,0:T(8,128)(2,1)}, bf16[1152,144]{1,0:T(8,128)(2,1)}, f32[128,128]{1,0:T(8,128)}, bf16[8,4,4,16,128]{4,3,2,1,0:T(8,128)(2,1)}) custom-call(bf16[8,64,512]{2,1,0:T(8,128)(2,1)} %pad.21.w_ref, bf16[7,80,512]{2,1,0:T(8,128)(2,1)} %constant.193.clone.pick_ref.picks_ref, ...), custom_call_target="tpu_custom_call" | custom-call | tf_op jit(solution)/shard_map/pallas_call | solution.py:100
  48.6 1.3 reshape.850
  54.6 1.1 fusion.1.x_ref
  60.4 38.1 %shard_map.379 = (f32[128,1152]{1,0:T(8,128)}, f32[128,1152]{1,0:T(8,128)}, bf16[1152,576]{1,0:T(8,128)(2,1)}, bf16[1152,576]{1,0:T(8,128)(2,1)}, bf16[1024,1152...) custom-call(f32[128,1152]{1,0:T(8,128)} %fusion.1.x_ref, ...), custom_call_target="tpu_custom_call" | custom-call | tf_op jit(solution)/shard_map/pallas_call | solution.py:100
  99.6 35.2 %shard_map.380 = (f32[128,1152]{1,0:T(8,128)}, f32[128,1152]{1,0:T(8,128)}, bf16[1152,432]{1,0:T(8,128)(2,1)}, bf16[1152,144]{1,0:T(8,128)(2,1)}, bf16[1024,1152...) custom-call(f32[128,1152]{1,0:T(8,128)} %get-tuple-element.98.x_ref, ...), custom_call_target="tpu_custom_call" | custom-call | tf_op jit(solution)/shard_map/pallas_call | solution.py:100
  135.5 1.2 scatter_custom_fusion
  136.7 3.2 gather_fusion
  140.0 0.9 fusion.11.x_ref
  141.9 37.5 %shard_map.381 = (f32[112,1152]{1,0:T(8,128)}, f32[112,1152]{1,0:T(8,128)}, bf16[1152,576]{1,0:T(8,128)(2,1)}, bf16[1152,576]{1,0:T(8,128)(2,1)}, bf16[896,1152]...) custom-call(f32[112,1152]{1,0:T(8,128)} %fusion.11.x_ref, ...), custom_call_target="tpu_custom_call" | custom-call | tf_op jit(solution)/shard_map/pallas_call | solution.py:100
  180.3 32.5 %shard_map.382 = (f32[112,1152]{1,0:T(8,128)}, f32[112,1152]{1,0:T(8,128)}, bf16[896,1152]{1,0:T(8,128)(2,1)}, bf16[896,576]{1,0:T(8,128)(2,1)}, bf16[896,576]{1,0:T(8,128)(2,1)}) custom-call(f32[112,1152]{1,0:T(8,128)} %get-tuple-element.104.x_ref, f32[8,1152]{1,0:T(8,128)} %get-tuple-element.295.vec_ref, f32[1,576]{1,0:T(1,128)} %broadcast_in_dim.134.bias_ref, ...), custom_call_target="tpu_custom_call" | custom-call | tf_op jit(solution)/shard_map/pallas_call | solution.py:100
  212.9 2.7 gather_fusion.1
  219.4 1.5 gather_fusion.2
  222.5 1.3 fusion.17.valid_ref
  223.7 36.9 %shard_map.383 = (f32[112,1152]{1,0:T(8,128)}, f32[8,1152]{1,0:T(8,128)}, f32[1,576]{1,0:T(1,128)}, bf16[16,80,640]{2,1,0:T(8,128)(2,1)}, bf16[16,80,512]{2,1,0:T(8,128)(2,1)}) custom-call(f32[112,1152]{1,0:T(8,128)} %fusion.10.g_ref, f32[112,1152]{1,0:T(8,128)} %get-tuple-element.104.x_ref, f32[112,1152]{1,0:T(8,128)} %get-tuple-element.108.mlp_ref, ...), custom_call_target="tpu_custom_call" | custom-call | tf_op jit(solution)/shard_map/pallas_call | solution.py:100
  260.7 37.5 %shard_map.384 = (f32[112,1152]{1,0:T(8,128)}, f32[8,1152]{1,0:T(8,128)}, f32[1,432]{1,0:T(1,128)}, bf16[16,80,384]{2,1,0:T(8,128)(2,1)}, bf16[16,80,256]{2,1,0:T(8,128)(2,1)}, /*index=5*/bf16[80,1152]{1,0:T(8,128)(2,1)}) custom-call(f32[112,1152]{1,0:T(8,128)} %get-tuple-element.112.g_ref, f32[112,1152]{1,0:T(8,128)} %fusion.11.x_ref, ...), custom_call_target="tpu_custom_call" | custom-call | tf_op jit(solution)/shard_map/pallas_call | solution.py:100
  298.2 2.6 gather_fusion.3
  300.8 1.0 fusion.5.g_ref
  302.4 38.6 %shard_map.385 = (f32[128,1152]{1,0:T(8,128)}, f32[8,1152]{1,0:T(8,128)}, f32[1,576]{1,0:T(1,128)}, bf16[16,80,640]{2,1,0:T(8,128)(2,1)}, bf16[16,80,512]{2,1,0:T(8,128)(2,1)}, /*index=5*/bf16[80,640]{1,0:T(8,128)(2,1)}) custom-call(f32[128,1152]{1,0:T(8,128)} %fusion.5.g_ref, f32[128,1152]{1,0:T(8,128)} %get-tuple-element.98.x_ref, ...), custom_call_target="tpu_custom_call" | custom-call | tf_op jit(solution)/shard_map/pallas_call | solution.py:100
  341.0 39.7 %shard_map.386 = (f32[128,1152]{1,0:T(8,128)}, f32[8,1152]{1,0:T(8,128)}, f32[1,432]{1,0:T(1,128)}, bf16[16,80,384]{2,1,0:T(8,128)(2,1)}, bf16[16,80,256]{2,1,0:T(8,128)(2,1)}, /*index=5*/bf16[80,1152]{1,0:T(8,128)(2,1)}) custom-call(f32[128,1152]{1,0:T(8,128)} %get-tuple-element.129.g_ref, f32[128,1152]{1,0:T(8,128)} %fusion.1.x_ref, ...), custom_call_target="tpu_custom_call" | custom-call | tf_op jit(solution)/shard_map/pallas_call | solution.py:100
  380.8 2.1 convolution_bitcast_fusion
  391.5 36.0 %shard_map.387 = (bf16[8,64,512]{2,1,0:T(8,128)(2,1)}, bf16[8,32,512]{2,1,0:T(8,128)(2,1)}, bf16[8,4,4,16,128]{4,3,2,1,0:T(8,128)(2,1)}, f32[8,128]{1,0:T(8,128)}) custom-call(bf16[4,4,80,384]{3,2,1,0:T(8,128)(2,1)} %bitcast.296, bf16[4,4,80,256]{3,2,1,0:T(8,128)(2,1)} %bitcast.300, bf16[80,640]{1,0:T(8,128)(2,1)} %get-tuple-element.142.attn_ref, ...), custom_call_target="tpu_custom_call" | custom-call | tf_op jit(solution)/shard_map/pallas_call | solution.py:100
  427.5 1.3 reshape.892
  429.0 1.0 copy-done.1
  430.0 0.9 copy-done.5
  431.8 1.8 shard_map.388
  436.9 1.2 copy.217
  442.3 1.0 copy.220
  444.0 1.0 copy.221
  445.6 1.3 fusion.28
  (321 shorter events, 42.5 us)
Async XLA Ops:
  0.7 1.8 copy-start.17
  0.7 2.1 copy-start.13
  0.7 2.3 copy-start.14
  4.4 1.1 copy-start.4
  4.4 1.1 copy-start.15
  4.4 1.3 copy-start.12
  4.7 1.5 copy-start.33
  4.7 1.8 copy-start.34
  6.7 1.3 copy-start.26
  6.7 1.4 copy-start.25
  6.7 1.5 copy-start.35
  6.7 1.5 copy-start.36
  6.8 1.6 copy-start.37
  6.8 1.7 copy-start.38
  6.8 1.8 copy-start.32
  48.6 2.0 copy-start.18
  50.6 1.3 copy-start.9
  51.5 1.4 copy-start.19
  53.1 3.2 copy-start.16
  99.6 35.4 %copy-start.24 = (s32[1,512]{1,0:T(1,128)S(1)}, s32[1,512]{1,0:T(1,128)}, u32[]{:S(2)}) copy-start(s32[1,512]{1,0:T(1,128)} %param.30) | copy-start | bytes 6148
  212.9 2.7 copy-start.8
  380.7 3.4 copy-start.23
  380.7 3.4 copy-start.21
  380.7 3.5 copy-start.22
  380.8 3.5 copy-start.20
  380.8 4.4 copy-start.11
  385.6 1.7 copy-start.31
  385.9 2.9 copy-start.28
  385.9 3.1 copy-start.29
  427.5 1.4 copy-start
  428.9 6.7 %copy-start.27 = (f32[8,128]{1,0:T(8,128)S(1)}, f32[8,128]{1,0:T(8,128)}, u32[]{:S(2)}) copy-start(f32[8,128]{1,0:T(8,128)} %get-tuple-element.157) | copy-start | bytes 12292
  435.0 4.3 copy-start.3
  (8 other events, 7.0 us)

commit v5 on v4

--- a/solution.py
+++ b/solution.py
@@ -69,23 +69,8 @@
     return found
 
 
-def image_peers():
-    x, z = lax.axis_index("dp_0"), lax.axis_index("dp_1")
-    found = []
-    for dx in range(4):
-        for dz in range(4):
-            if dx or dz:
-                ox, oz = lax.rem(x + dx, 4), lax.rem(z + dz, 4)
-                found.append(({"dp_0": ox, "dp_1": oz}, ox * 4 + oz))
-    return found
-
-
 def own_group():
     return lax.axis_index("tx") * 4 + lax.axis_index("ty")
-
-
-def own_image():
-    return lax.axis_index("dp_0") * 4 + lax.axis_index("dp_1")
 
 
 def dma_sems(n):
@@ -109,22 +94,6 @@
     )(*operands)
 
 
-class Moves:
-    def __init__(self, sems):
-        self.sems, self.copies = sems, {}
-
-    def start(self, k, src, dst):
-        self.copies[k] = pltpu.make_async_copy(src, dst, self.sems.at[k])
-        self.copies[k].start()
-
-    def wait(self, *which):
-        for k in which:
-            self.copies.pop(k).wait()
-
-    def finish(self):
-        self.wait(*list(self.copies))
-
-
 def ring_peers():
     c, y = lax.axis_index("tx"), lax.axis_index("ty")
     return (
@@ -182,42 +151,22 @@
     return shaped.transpose(0, 1, 3, 2, 4, 5).reshape(count, 2 * tile_rows, 2 * tile_cols, depth)
 
 
-def compact_plan(routed, capacity):
-    count, tokens = routed.shape
-    flags = routed > 0
-    position = jnp.cumsum(flags.astype(jnp.int32), axis=1) - 1
-    slots = jnp.where(flags, position, capacity)
-    batch_index = jnp.broadcast_to(jnp.arange(count, dtype=jnp.int32)[:, None], (count, tokens))
-    token_ids = jnp.arange(tokens, dtype=jnp.int32)[None, :]
-    owner = (
-        jnp.zeros((count, capacity), jnp.int32).at[batch_index, slots].set(token_ids, mode="drop")
-    )
-    filled = jnp.sum(flags.astype(jnp.int32), axis=1, keepdims=True)
-    valid = (jnp.arange(capacity, dtype=jnp.int32)[None, :] < filled).astype(jnp.float32)
-    return (jnp.where(flags, position, 0), owner, valid)
-
-
-def pick_rows(value_rows, index):
-    return jax.vmap(lambda table, where: jnp.take(table, where, axis=0))(value_rows, index)
-
-
-def rows_at(index, tokens):
-    return pl.ds(pl.multiple_of(index * tokens, 16), tokens)
-
-
-def ring_scratch(tokens):
-    half = (tokens // 2 + 15) // 16 * 16
+def ring_local(tokens):
     return [
         pltpu.VMEM((4, tokens, D), F32),
         pltpu.VMEM((4, tokens, D), BF16),
+        pltpu.VMEM((3, tokens, D), BF16),
+    ]
+
+
+def ring_remote(tokens):
+    half = (tokens // 2 + 15) // 16 * 16
+    return [
         pltpu.VMEM((4, tokens, D), BF16),
-        pltpu.VMEM((3, tokens, D), BF16),
         pltpu.VMEM((2, tokens, D), BF16),
         pltpu.VMEM((half, D), BF16),
         pltpu.VMEM((tokens - half, D), BF16),
-        pltpu.SemaphoreType.DMA((20,)),
-        pltpu.SemaphoreType.DMA((20,)),
-    ]
+    ] + dma_sems(20)
 
 
 SLAB = 80
@@ -373,27 +322,6 @@
     )
 
 
-def slab_shapes(cols):
-    widths = (CUT[cols], cols - CUT[cols])
-    return tuple(jax.ShapeDtypeStruct((16, SLAB, w), BF16) for w in widths)
-
-
-def slabs(pair):
-    return [part.reshape(4, 4, *part.shape[1:]) for part in pair]
-
-
-def write_slabs(whole, left_ref, right_ref):
-    cut = left_ref.shape[2]
-
-    @pl.loop(0, 16)
-    def _(k):
-        rows = whole[pl.ds(pl.multiple_of(k * PART, 8), PART), :]
-        rows = jnp.concatenate([rows, jnp.zeros((SLAB - PART, rows.shape[1]), F32)], axis=0)
-        rows = rows.astype(BF16)
-        left_ref[k] = rows[:, :cut]
-        right_ref[k] = rows[:, cut:]
-
-
 def slab_views(rows_ref, start, cols):
     cut = start + CUT[cols]
     return rows_ref.at[:, start:cut], rows_ref.at[:, cut : start + cols]
@@ -405,12 +333,12 @@
 
 
 class Ring:
-    def __init__(self, tokens, scratch):
+    def __init__(self, tokens, local, remote):
         self.tokens = tokens
         self.half = (tokens // 2 + 15) // 16 * 16
-        self.kept, self.sib_out, self.sib_in, self.out, self.got = scratch[:5]
-        self.far_low, self.far_high = scratch[5:7]
-        self.sems = tuple(scratch[7:9])
+        self.kept, self.sib_out, self.out = local
+        self.sib_in, self.got, self.far_low, self.far_high = remote[:4]
+        self.sems = tuple(remote[4:6])
         c, y = lax.axis_index("tx"), lax.axis_index("ty")
         self.sib, self.up, self.down, _ = ring_peers()
         self.own = [c * 4 + lax.rem(y + d, 4) for d in range(4)]
@@ -552,180 +480,6 @@
 
 def sum_rows(value):
     return jnp.sum(value, axis=0, keepdims=True)
-
-
-def ffn_forward_kernel(
-    x_ref, vec_ref, bias_ref, we_ref, wr_ref, rows_ref,
-    out_ref, mlp_ref, next_one, next_two, all_out, hid_out, slope_out,
-    x16, all_ref, hid_ref, slope_ref, move_sems, *scratch
-):
-    tokens = x_ref.shape[0]
-    ring = Ring(tokens, scratch[:9])
-    rows_in = None
-    if scratch[9:]:
-        rows_in = RowsIn(*slab_views(rows_ref, ATT_COLS, ATT_COLS), scratch[9:])
-    moves = Moves(move_sems)
-    peers = ring.peers() + (rows_in.peers() if rows_in else [])
-    greet(peers)
-    normed, _ = layer_stats(x_ref[...])
-    x16[...] = (normed * (1.0 + vec_ref[1:2]) + vec_ref[0:1]).astype(BF16)
-    met(peers)
-    ring.start_sums()
-
-    def prepare():
-        if rows_in:
-            rows_in.start()
-
-    def visit(own, d):
-        rows = ring.rows((ring.own if own else ring.other)[d])
-        pre = dot_nn(all_ref[rows, :], we_ref[...]) + bias_ref[...]
-        value, slope = gelu_both(pre)
-        hidden = value.astype(BF16)
-        hid_ref[rows, :] = hidden
-        slope_ref[rows, :] = slope.astype(BF16)
-        ring.put(own, d, dot_nt(hidden, wr_ref[...]))
-        if not own and d == 1:
-            ring.near()
-
-    ring.gather(x16, all_ref, prepare, visit, rows_in.middle if rows_in else None)
-    ring.far()
-    moves.start(0, all_ref, all_out)
-    moves.start(1, hid_ref, hid_out)
-    moves.start(2, slope_ref, slope_out)
-    ring.relay()
-    if rows_in:
-        rows_in.end(next_one, next_two)
-    mlp = ring.total() + vec_ref[3:4]
-    mlp_ref[...] = mlp
-    out_ref[...] = x_ref[...] + vec_ref[2:3] * mlp
-    ring.leave()
-    moves.finish()
-
-
-def ffn_forward_last_kernel(
-    x_ref, vec_ref, bias_ref, we_ref, wr_ref, out_ref, mlp_ref, all_out, hid_out, slope_out, *scratch
-):
-    ffn_forward_kernel(
-        x_ref, vec_ref, bias_ref, we_ref, wr_ref, None,
-        out_ref, mlp_ref, None, None, all_out, hid_out, slope_out, *scratch
-    )
-
-
-def ffn_forward(x, vecs, bias, we, wr, following, cid):
-    tokens = x.shape[0]
-    saved = [(8 * tokens, D), (8 * tokens, FW), (8 * tokens, FW)]
-    outs = (
-        jax.ShapeDtypeStruct((tokens, D), F32),
-        jax.ShapeDtypeStruct((tokens, D), F32),
-        *(weight_shapes(ATT_COLS) if following is not None else ()),
-        *(jax.ShapeDtypeStruct(shape, BF16) for shape in saved),
-    )
-    scratch = [pltpu.VMEM((tokens, D), BF16)]
-    scratch += [pltpu.VMEM(shape, BF16) for shape in saved]
-    scratch += [pltpu.SemaphoreType.DMA((3,))] + ring_scratch(tokens)
-    kernel = ffn_forward_last_kernel
-    if following is not None:
-        scratch += rows_in_scratch(ATT_COLS)
-        kernel = ffn_forward_kernel
-    operands = (x, vecs, bias, we, wr) + (() if following is None else (following,))
-    return collective(kernel, cid, outs, scratch, *operands, far_out=3)
-
-
-def ffn_backward_kernel(
-    g_ref, x_ref, mlp_ref, vec_ref, valid_ref, we_ref, wr_ref, *refs
-):
-    tokens = x_ref.shape[0]
-    refs = list(refs)
-    pending = (refs.pop(0), refs.pop(0)) if len(refs) > 30 else None
-    second_in, hid_in, slope_in, out_ref, vecs_ref, bias_ref, dw_left, dw_right = refs[:8]
-    refs = refs[8:]
-    summed = refs.pop(0) if pending else None
-    g16, g_all, pre_all, second_ref, hid_ref, slope_ref, whole, move_sems = refs[:8]
-    ring = Ring(tokens, refs[8:17])
-    rows_out = RowsOut(*pending, refs[17:]) if pending else None
-    moves = Moves(move_sems)
-    peers = ring.peers() + (rows_out.peers() if rows_out else [])
-    greet(peers)
-    moves.start(0, slope_in, slope_ref)
-    moves.start(1, hid_in, hid_ref)
-    moves.start(2, second_in, second_ref)
-    grad = g_ref[...] * valid_ref[...]
-    g16[...] = (grad * vec_ref[2:3]).astype(BF16)
-    met(peers)
-    ring.start_sums()
-    bias_ref[...] = jnp.zeros_like(bias_ref)
-
-    def prepare():
-        if rows_out:
-            rows_out.start()
-        moves.wait(0)
-
-    def visit(own, d):
-        rows = ring.rows((ring.own if own else ring.other)[d])
-        pre_grad = (
-            dot_nn(g_all[rows, :], wr_ref[...]) * slope_ref[rows, :].astype(F32)
-        ).astype(BF16)
-        pre_all[rows, :] = pre_grad
-        bias_ref[...] += sum_rows(pre_grad.astype(F32))
-        ring.put(own, d, dot_nt(pre_grad, we_ref[...]))
-        if not own and d == 1:
-            ring.near()
-
-    ring.gather(g16, g_all, prepare, visit)
-    ring.far()
-    vecs_ref[2:3] = sum_rows(grad * mlp_ref[...])
-    vecs_ref[3:4] = sum_rows(g16[...].astype(F32))
-    vecs_ref[4:8] = jnp.zeros((4, D), F32)
-    if rows_out:
-        rows_out.middle()
-    ring.relay()
-    moves.finish()
-
-    @pl.loop(0, D // 128)
-    def _(k):
-        at = pl.ds(pl.multiple_of(k * 128, 128), 128)
-        whole[at, :] = jnp.concatenate(
-            [
-                dot_tn(second_ref[:, at], pre_all[...]),
-                dot_tn(g_all[:, at], hid_ref[...]),
-            ],
-            axis=1,
-        )
-
-    write_slabs(whole, dw_left, dw_right)
-    if rows_out:
-        rows_out.end_rows(summed)
-    second_grad = ring.total()
-    normed, inv_std = layer_stats(x_ref[...])
-    vecs_ref[0:1] = sum_rows(second_grad)
-    vecs_ref[1:2] = sum_rows(second_grad * normed)
-    out_ref[...] = grad + layer_back(second_grad * (1.0 + vec_ref[1:2]), normed, inv_std)
-    ring.leave()
-
-
-def ffn_backward(g, x, mlp, vecs, valid, second, hid, slope, we, wr, pending, cid):
-    tokens = x.shape[0]
-    outs = (
-        jax.ShapeDtypeStruct((tokens, D), F32),
-        jax.ShapeDtypeStruct((8, D), F32),
-        jax.ShapeDtypeStruct((1, FW), F32),
-        *slab_shapes(FFN_COLS),
-        *((jax.ShapeDtypeStruct((SLAB, ATT_COLS), BF16),) if pending else ()),
-    )
-    scratch = [
-        pltpu.VMEM((tokens, D), BF16),
-        pltpu.VMEM((8 * tokens, D), BF16),
-        pltpu.VMEM((8 * tokens, FW), BF16),
-        pltpu.VMEM((8 * tokens, D), BF16),
-        pltpu.VMEM((8 * tokens, FW), BF16),
-        pltpu.VMEM((8 * tokens, FW), BF16),
-        pltpu.VMEM((D, FFN_COLS), F32),
-        pltpu.SemaphoreType.DMA((3,)),
-    ] + ring_scratch(tokens)
-    if pending:
-        scratch += rows_out_scratch(ATT_COLS)
-    operands = (g, x, mlp, vecs, valid, we, wr, *pending, second, hid, slope)
-    return collective(ffn_backward_kernel, cid, outs, scratch, *operands, far_in=3)
 
 
 def open_kernel(
@@ -923,7 +677,7 @@
     ] + dma_sems(41)
     scratch += rows_out_scratch(ATT_COLS) + sum_scratch([(32, 128), (32, 128)], F32)
     picks = jnp.asarray(picking(), BF16)
-    operands = (*slabs(pair), attn, ffn_one, ffn_two, picks, mods, small)
+    operands = (*pair, attn, ffn_one, ffn_two, picks, mods, small)
     return collective(finish_kernel, 2, outs, scratch, *operands)
 
 
@@ -1015,52 +769,150 @@
     return slice(start + h * HEAD, start + (h + 1) * HEAD)
 
 
-def attn_forward_kernel(
-    x_ref, vec_ref, bias_ref, mask_ref, wqkv_ref, wm_ref, rows_ref,
-    out_ref, branch_ref, next_one, next_two, *refs, start
-):
-    outs, (x16, *kept, move_sems), scratch = refs[:6], refs[6:14], refs[14:]
-    all_ref, q_ref, k_ref, v_ref, lse_ref, att_ref = kept
-    tokens = x_ref.shape[0]
-    ring = Ring(tokens, scratch[:9])
-    rows_in = RowsIn(*slab_views(rows_ref, start, FFN_COLS), scratch[9:])
-    moves = Moves(move_sems)
-    peers = ring.peers() + rows_in.peers()
+class Refs:
+    pass
+
+
+def make_specs(entry):
+    return list(entry) if isinstance(entry, list) else [entry]
+
+
+def launch(body, cid, near, far, outs, kept, scratch, vmem=60 << 20):
+    twins = {name: (value.shape, value.dtype) for name, value in far.items()}
+    twins.update(kept)
+    groups = {name: make_specs(entry) for name, entry in scratch.items()}
+
+    def kernel(*refs):
+        refs = iter(refs)
+        r = Refs()
+        r.hbm = {}
+        for name in near:
+            setattr(r, name, next(refs))
+        for name in far:
+            r.hbm[name] = next(refs)
+        for name in outs:
+            setattr(r, name, next(refs))
+        for name in kept:
+            r.hbm[name] = next(refs)
+        for name in twins:
+            setattr(r, name, next(refs))
+        r.move_sems = next(refs)
+        for name, specs in groups.items():
+            found = [next(refs) for _ in specs]
+            setattr(r, name, found if isinstance(scratch[name], list) else found[0])
+        r.index = {name: k for k, name in enumerate(twins)}
+        r.moving = {}
+        body(r)
+
+    shapes = [jax.ShapeDtypeStruct(*spec) for spec in (*outs.values(), *kept.values())]
+    results = pl.pallas_call(
+        kernel,
+        out_shape=tuple(shapes),
+        in_specs=[VMEM] * len(near) + [FAR] * len(far),
+        out_specs=(VMEM,) * len(outs) + (FAR,) * len(kept),
+        scratch_shapes=[pltpu.VMEM(*spec) for spec in twins.values()]
+        + [pltpu.SemaphoreType.DMA((len(twins),))]
+        + [spec for specs in groups.values() for spec in specs],
+        compiler_params=pltpu.CompilerParams(
+            collective_id=cid, has_side_effects=True, vmem_limit_bytes=vmem
+        ),
+    )(*near.values(), *far.values())
+    return dict(zip((*outs, *kept), results))
+
+
+def load(r, *names):
+    for name in names:
+        copy = pltpu.make_async_copy(r.hbm[name], getattr(r, name), r.move_sems.at[r.index[name]])
+        copy.start()
+        r.moving[name] = copy
+
+
+def load_into(r, name, ref):
+    copy = pltpu.make_async_copy(r.hbm[name], ref, r.move_sems.at[r.index[name]])
+    copy.start()
+    r.moving[name] = copy
+
+
+def save(r, *names):
+    for name in names:
+        copy = pltpu.make_async_copy(getattr(r, name), r.hbm[name], r.move_sems.at[r.index[name]])
+        copy.start()
+        r.moving[name] = copy
+
+
+def settle(r, *names):
+    for name in names or tuple(r.moving):
+        r.moving.pop(name).wait()
+
+
+def exact(left, right, dims):
+    return lax.dot_general(
+        left,
+        right,
+        ((dims[:1], dims[1:]), ((), ())),
+        precision=lax.Precision.HIGHEST,
+        preferred_element_type=F32,
+    )
+
+
+def choice(place_ref, capacity):
+    tokens = place_ref.shape[1]
+    slots = lax.broadcasted_iota(jnp.int32, (capacity, tokens), 0)
+    return jnp.where(slots == place_ref[...], 1.0, 0.0).astype(F32)
+
+
+def spread_back(picks, chosen, others):
+    used = exact(picks, jnp.ones((picks.shape[0], 128), F32), (0, 0))[:, :1]
+    return exact(picks, chosen, (0, 0)) + others * (1.0 - used)
+
+
+def modulated(x, vec_ref):
+    normed, _ = layer_stats(x)
+    return (normed * (1.0 + vec_ref[1:2]) + vec_ref[0:1]).astype(BF16)
+
+
+def forward_body(r, tokens, start, last):
+    ring = Ring(tokens, r.ring_local, r.ring_one)
+    fetch = RowsIn(*slab_views(r.rows, start, FFN_COLS), r.fetch_one)
+    peers = ring.peers() + fetch.peers()
     greet(peers)
-    normed, _ = layer_stats(x_ref[...])
-    x16[...] = (normed * (1.0 + vec_ref[1:2]) + vec_ref[0:1]).astype(BF16)
+    if last:
+        r.x[...] = exact(choice(r.place, tokens), r.first[...], (1, 0))
+    else:
+        r.x[...] = dot_nn(r.patches[...], r.embed_w[...]) + r.embed_b[...] + r.placed[...]
+    r.x16[...] = modulated(r.x[...], r.vec_one)
     met(peers)
+    save(r, "x")
     ring.start_sums()
 
     def visit(own, d):
         rows = ring.rows((ring.own if own else ring.other)[d])
-        joined = (dot_nn(all_ref[rows, :], wqkv_ref[...]) + bias_ref[...]).astype(BF16)
+        joined = (dot_nn(r.in_all[rows, :], r.wqkv[...]) + r.bias_one[...]).astype(BF16)
         for h in range(2):
-            q_ref[h, rows, :] = joined[:, head_cols(h)]
-            k_ref[h, rows, :] = joined[:, head_cols(h, HW)]
-            v_ref[h, rows, :] = joined[:, head_cols(h, 2 * HW)]
+            r.q[h, rows, :] = joined[:, head_cols(h)]
+            r.k[h, rows, :] = joined[:, head_cols(h, HW)]
+            r.v[h, rows, :] = joined[:, head_cols(h, 2 * HW)]
 
     def attend(own, d):
         rows = ring.rows((ring.own if own else ring.other)[d])
         parts = []
         for h in range(2):
-            scores = dot_nt(q_ref[h, rows, :], k_ref[h]) * SCALE + mask_ref[...]
+            scores = dot_nt(r.q[h, rows, :], r.k[h]) * SCALE + r.mask[...]
             highest = jnp.max(scores, axis=-1, keepdims=True)
             shifted = jnp.exp(scores - highest)
             summed = jnp.sum(shifted, axis=-1, keepdims=True)
             probs = (shifted * (1.0 / summed)).astype(BF16)
-            lse_ref[rows, h : h + 1] = highest + jnp.log(summed)
-            parts.append(dot_nn(probs, v_ref[h]).astype(BF16))
+            r.lse[rows, h : h + 1] = highest + jnp.log(summed)
+            parts.append(dot_nn(probs, r.v[h]).astype(BF16))
         attended = jnp.concatenate(parts, axis=1)
-        att_ref[rows, :] = attended
-        ring.put(own, d, dot_nt(attended, wm_ref[...]))
-
-    ring.gather(x16, all_ref, rows_in.start, visit, rows_in.middle)
+        r.att[rows, :] = attended
+        ring.put(own, d, dot_nt(attended, r.wm[...]))
+
+    ring.gather(r.x16, r.in_all, fetch.start, visit, fetch.middle)
     attend(False, 2)
     attend(True, 2)
     ring.far()
-    for k in range(4):
-        moves.start(k, kept[k], outs[k])
+    save(r, "in_all", "q", "k", "v")
     for d in (1, 3):
         attend(False, d)
         attend(True, d)
@@ -1068,93 +920,183 @@
     ring.relay()
     attend(False, 0)
     attend(True, 0)
-    for k in range(4, 6):
-        moves.start(k, kept[k], outs[k])
-    rows_in.end(next_one, next_two)
-    branch = ring.total() + vec_ref[3:4]
-    branch_ref[...] = branch
-    out_ref[...] = x_ref[...] + vec_ref[2:3] * branch
+    save(r, "lse", "att")
+    fetch.end(r.we, r.wr)
+    save(r, "we", "wr")
+    branch = ring.total() + r.vec_one[3:4]
+    r.branch[...] = branch
+    middle = r.x[...] + r.vec_one[2:3] * branch
+    r.middle[...] = middle
+    save(r, "branch", "middle")
     ring.leave()
-    moves.finish()
+
+    ring = Ring(tokens, r.ring_local, r.ring_two)
+    fetch = None
+    if not last:
+        fetch = RowsIn(*slab_views(r.rows, ATT_COLS, ATT_COLS), r.fetch_two)
+    r.x16[...] = modulated(middle, r.vec_two)
+    ring.start_sums()
+
+    def prepare():
+        if fetch:
+            fetch.start()
+
+    def expand(own, d):
+        rows = ring.rows((ring.own if own else ring.other)[d])
+        pre = dot_nn(r.second[rows, :], r.we[...]) + r.bias_two[...]
+        value, slope = gelu_both(pre)
+        hidden = value.astype(BF16)
+        r.hid[rows, :] = hidden
+        r.slope[rows, :] = slope.astype(BF16)
+        ring.put(own, d, dot_nt(hidden, r.wr[...]))
+        if not own and d == 1:
+            ring.near()
+
+    ring.gather(r.x16, r.second, prepare, expand, fetch.middle if fetch else None)
+    ring.far()
+    save(r, "second", "hid", "slope")
+    ring.relay()
+    if fetch:
+        fetch.end(r.next_wqkv, r.next_wm)
+    mlp = ring.total() + r.vec_two[3:4]
+    r.mlp[...] = mlp
+    save(r, "mlp")
+    r.out[...] = r.middle[...] + r.vec_two[2:3] * mlp
+    ring.leave()
+    settle(r)
 
 
 def kept_shapes(tokens):
     heads = ((2, 8 * tokens, HEAD), BF16)
-    return (
-        ((8 * tokens, D), BF16),
-        heads,
-        heads,
-        heads,
-        ((8 * tokens, 2), F32),
-        ((8 * tokens, HW), BF16),
-    )
-
-
-def attn_forward(x, vecs, bias, mask, wqkv, wm, rows, start, cid):
-    tokens = x.shape[0]
-    outs = (
-        jax.ShapeDtypeStruct((tokens, D), F32),
-        jax.ShapeDtypeStruct((tokens, D), F32),
-        *weight_shapes(FFN_COLS),
-        *(jax.ShapeDtypeStruct(*shape) for shape in kept_shapes(tokens)),
-    )
-    scratch = [pltpu.VMEM((tokens, D), BF16)]
-    scratch += [pltpu.VMEM(*shape) for shape in kept_shapes(tokens)]
-    scratch += [pltpu.SemaphoreType.DMA((6,))] + ring_scratch(tokens) + rows_in_scratch(FFN_COLS)
-    operands = (x, vecs, bias, mask, wqkv, wm, rows)
-    kernel = functools.partial(attn_forward_kernel, start=start)
-    return collective(kernel, cid, outs, scratch, *operands, far_out=6)
-
-
-def attn_backward_kernel(
-    g_ref, x_ref, branch_ref, vec_ref, mask_ref, wqkv_ref, wm_ref, pending_left, pending_right, *refs
-):
-    ins, (out_ref, vecs_ref, bias_ref, dw_left, dw_right, summed) = refs[:6], refs[6:12]
-    g16, g_all, joined, dk, dv, whole = refs[12:18]
-    kept, move_sems, scratch = refs[18:24], refs[24], refs[25:]
-    in_ref, q_ref, k_ref, v_ref, lse_ref, att_ref = kept
-    tokens = x_ref.shape[0]
-    ring = Ring(tokens, scratch[:9])
-    rows_out = RowsOut(pending_left, pending_right, scratch[9:])
-    moves = Moves(move_sems)
-    peers = ring.peers() + rows_out.peers()
+    wide, tile = ((8 * tokens, D), BF16), ((tokens, D), F32)
+    hidden = ((8 * tokens, FW), BF16)
+    return {
+        "x": tile,
+        "in_all": wide,
+        "q": heads,
+        "k": heads,
+        "v": heads,
+        "lse": ((8 * tokens, 2), F32),
+        "att": ((8 * tokens, HW), BF16),
+        "branch": tile,
+        "middle": tile,
+        "second": wide,
+        "hid": hidden,
+        "slope": hidden,
+        "mlp": tile,
+        "we": ((D, FW), BF16),
+        "wr": ((D, FW), BF16),
+    }
+
+
+def block_forward(near, tokens, start, last, cid):
+    outs = {"out": ((tokens, D), F32)}
+    scratch = {
+        "x16": pltpu.VMEM((tokens, D), BF16),
+        "ring_local": ring_local(tokens),
+        "ring_one": ring_remote(tokens),
+        "ring_two": ring_remote(tokens),
+        "fetch_one": rows_in_scratch(FFN_COLS),
+    }
+    if not last:
+        outs["next_wqkv"] = ((D, 3 * HW), BF16)
+        outs["next_wm"] = ((D, HW), BF16)
+        scratch["fetch_two"] = rows_in_scratch(ATT_COLS)
+    body = functools.partial(forward_body, tokens=tokens, start=start, last=last)
+    return launch(body, cid, near, {}, outs, kept_shapes(tokens), scratch)
+
+
+def backward_body(r, tokens, last):
+    ring = Ring(tokens, r.ring_local, r.ring_one)
+    sums = None if last else RowsOut(r.pending_left, r.pending_right, r.sums_one)
+    peers = ring.peers() + line_only(line_peers())
     greet(peers)
-    for k in (1, 2, 3, 4, 5, 0):
-        moves.start(k, ins[k], kept[k])
-    g16[...] = (g_ref[...] * vec_ref[2:3]).astype(BF16)
+    load(r, "slope", "wr", "we", "hid", "second", "mlp", "middle")
+    load(r, "q", "k", "v", "lse", "att", "x", "branch")
+    if not last:
+        picks = choice(r.place, r.grad_two.shape[0])
+        r.g[...] = spread_back(picks, r.grad_two[...], r.grad_ended[...])
+    else:
+        r.g[...] = r.grad_in[...]
+    r.g16[...] = (r.g[...] * r.vec_two[2:3]).astype(BF16)
     met(peers)
     ring.start_sums()
+    r.bias_two[...] = jnp.zeros_like(r.bias_two)
 
     def prepare():
-        rows_out.start()
-        dk[...] = jnp.zeros_like(dk)
-        dv[...] = jnp.zeros_like(dv)
-        moves.wait(1, 2, 3, 4)
+        if sums:
+            sums.start()
+        settle(r, "slope", "wr", "we")
 
     def visit(own, d):
         rows = ring.rows((ring.own if own else ring.other)[d])
-        grad = dot_nn(g_all[rows, :], wm_ref[...]).astype(BF16)
+        pre_grad = (
+            dot_nn(r.g_one[rows, :], r.wr[...]) * r.slope[rows, :].astype(F32)
+        ).astype(BF16)
+        r.pre_all[rows, :] = pre_grad
+        r.bias_two[...] += sum_rows(pre_grad.astype(F32))
+        ring.put(own, d, dot_nt(pre_grad, r.we[...]))
+        if not own and d == 1:
+            ring.near()
+
+    ring.gather(r.g16, r.g_one, prepare, visit)
+    ring.far()
+    settle(r, "hid", "second", "mlp", "middle")
+    weight_grads(r.g_one, r.hid, r.whole_two, FW)
+    ring.relay()
+    if sums:
+        sums.middle()
+    r.vecs_two[2:3] = sum_rows(r.g[...] * r.mlp[...])
+    r.vecs_two[3:4] = sum_rows(r.g16[...].astype(F32))
+    r.vecs_two[4:8] = jnp.zeros((4, D), F32)
+    weight_grads(r.second, r.pre_all, r.whole_one, FW)
+    load_into(r, "in_all", r.second)
+    write_slabs((r.whole_one, FW), (r.whole_two, FW), r.ffn_left, r.ffn_right)
+    if sums:
+        sums.end_rows(r.attn_rows)
+    second_grad = ring.total()
+    normed, inv_std = layer_stats(r.middle[...])
+    r.vecs_two[0:1] = sum_rows(second_grad)
+    r.vecs_two[1:2] = sum_rows(second_grad * normed)
+    r.g[...] += layer_back(second_grad * (1.0 + r.vec_two[1:2]), normed, inv_std)
+    ring.leave()
+
+    ring = Ring(tokens, r.ring_local, r.ring_two)
+    sums = RowsOut(r.ffn_left, r.ffn_right, r.sums_two)
+    r.g16[...] = (r.g[...] * r.vec_one[2:3]).astype(BF16)
+    ring.start_sums()
+
+    def prepare_attention():
+        sums.start()
+        r.dk[...] = jnp.zeros_like(r.dk)
+        r.dv[...] = jnp.zeros_like(r.dv)
+        settle(r, "q", "k", "v", "lse")
+
+    def attend(own, d):
+        rows = ring.rows((ring.own if own else ring.other)[d])
+        grad = dot_nn(r.g_two[rows, :], r.wm[...]).astype(BF16)
         queries = []
         for h in range(2):
             part = grad[:, head_cols(h)]
-            query = q_ref[h, rows, :]
-            scores = dot_nt(query, k_ref[h]) * SCALE + mask_ref[...]
-            probs = jnp.exp(scores - lse_ref[rows, h : h + 1])
-            grad_probs = dot_nt(part, v_ref[h])
+            query = r.q[h, rows, :]
+            scores = dot_nt(query, r.k[h]) * SCALE + r.mask[...]
+            probs = jnp.exp(scores - r.lse[rows, h : h + 1])
+            grad_probs = dot_nt(part, r.v[h])
             weighted = jnp.sum(probs * grad_probs, axis=-1, keepdims=True)
             score_grad = (probs * (grad_probs - weighted)).astype(BF16)
-            queries.append((dot_nn(score_grad, k_ref[h]) * SCALE).astype(BF16))
-            dk[h] += dot_tn(score_grad, query)
-            dv[h] += dot_tn(probs.astype(BF16), part)
-        joined[rows, 0:HW] = jnp.concatenate(queries, axis=1)
+            queries.append((dot_nn(score_grad, r.k[h]) * SCALE).astype(BF16))
+            r.dk[h] += dot_tn(score_grad, query)
+            r.dv[h] += dot_tn(probs.astype(BF16), part)
+        r.joined[rows, 0:HW] = jnp.concatenate(queries, axis=1)
 
     def back(own, d):
         rows = ring.rows((ring.own if own else ring.other)[d])
-        ring.put(own, d, dot_nt(joined[rows, :], wqkv_ref[...]))
-
-    ring.gather(g16, g_all, prepare, visit)
-    later = [(dk[h] * SCALE).astype(BF16) for h in range(2)] + [dv[h].astype(BF16) for h in range(2)]
-    joined[:, HW : 3 * HW] = jnp.concatenate(later, axis=1)
+        ring.put(own, d, dot_nt(r.joined[rows, :], r.wqkv[...]))
+
+    ring.gather(r.g16, r.g_two, prepare_attention, attend)
+    later = [(r.dk[h] * SCALE).astype(BF16) for h in range(2)]
+    later += [r.dv[h].astype(BF16) for h in range(2)]
+    r.joined[:, HW : 3 * HW] = jnp.concatenate(later, axis=1)
     back(False, 2)
     back(True, 2)
     ring.far()
@@ -1164,106 +1106,144 @@
     ring.near()
     back(False, 0)
     back(True, 0)
-    rows_out.middle()
+    settle(r)
+    weight_grads(r.g_two, r.att, r.whole_two, HW)
     ring.relay()
-    bias_ref[...] = sum_rows(joined[...].astype(F32))
-    vecs_ref[2:3] = sum_rows(g_ref[...] * branch_ref[...])
-    vecs_ref[3:4] = sum_rows(g16[...].astype(F32))
-    vecs_ref[4:8] = jnp.zeros((4, D), F32)
-    moves.finish()
-
+    sums.middle()
+    r.bias_one[...] = sum_rows(r.joined[...].astype(F32))
+    r.vecs_one[2:3] = sum_rows(r.g[...] * r.branch[...])
+    r.vecs_one[3:4] = sum_rows(r.g16[...].astype(F32))
+    r.vecs_one[4:8] = jnp.zeros((4, D), F32)
+    weight_grads(r.second, r.joined, r.whole_one, 3 * HW)
+    write_slabs((r.whole_one, 3 * HW), (r.whole_two, HW), r.attn_left, r.attn_right)
+    sums.end_rows(r.ffn_rows)
+    input_grad = ring.total()
+    normed, inv_std = layer_stats(r.x[...])
+    r.vecs_one[0:1] = sum_rows(input_grad)
+    r.vecs_one[1:2] = sum_rows(input_grad * normed)
+    grad = r.g[...] + layer_back(input_grad * (1.0 + r.vec_one[1:2]), normed, inv_std)
+    if last:
+        r.out[...] = grad
+    else:
+        grad16 = grad.astype(BF16)
+        r.embed_w_grad[...] = dot_tn(r.patches[...], grad16)
+        r.embed_b_grad[...] = sum_rows(grad16.astype(F32))
+        r.latent[...] = dot_nt(grad16, r.embed_w[...])
+    ring.leave()
+
+
+def weight_grads(left_ref, right_ref, whole_ref, width):
     @pl.loop(0, D // 128)
     def _(k):
         at = pl.ds(pl.multiple_of(k * 128, 128), 128)
-        whole[at, :] = jnp.concatenate(
-            [
-                dot_tn(in_ref[:, at], joined[...]),
-                dot_tn(g_all[:, at], att_ref[...]),
-                jnp.zeros((128, ATT_COLS - 4 * HW), F32),
-            ],
-            axis=1,
-        )
-
-    write_slabs(whole, dw_left, dw_right)
-    rows_out.end_rows(summed)
-    input_grad = ring.total()
-    normed, inv_std = layer_stats(x_ref[...])
-    vecs_ref[0:1] = sum_rows(input_grad)
-    vecs_ref[1:2] = sum_rows(input_grad * normed)
-    out_ref[...] = g_ref[...] + layer_back(input_grad * (1.0 + vec_ref[1:2]), normed, inv_std)
-    ring.leave()
-
-
-def attn_backward(g, x, branch, vecs, mask, kept, wqkv, wm, pending, cid):
-    tokens = x.shape[0]
+        whole_ref[at, :width] = dot_tn(left_ref[:, at], right_ref[...])
+
+
+def write_slabs(one, two, left_ref, right_ref):
+    cut = left_ref.shape[3]
+    cols = cut + right_ref.shape[3]
+
+    @pl.loop(0, 16)
+    def _(k):
+        at = pl.ds(pl.multiple_of(k * PART, 8), PART)
+        parts = [ref[at, :width] for ref, width in (one, two)]
+        spare = cols - one[1] - two[1]
+        if spare:
+            parts.append(jnp.zeros((PART, spare), F32))
+        rows = jnp.concatenate(parts, axis=1)
+        rows = jnp.concatenate([rows, jnp.zeros((SLAB - PART, cols), F32)], axis=0).astype(BF16)
+        x, z = k // 4, lax.rem(k, 4)
+        left_ref[x, z] = rows[:, :cut]
+        right_ref[x, z] = rows[:, cut:]
+
+
+def line_only(lines):
+    return [peer for peer, _ in lines[0] + lines[1]]
+
+
+def slab_specs(cols):
+    widths = (CUT[cols], cols - CUT[cols])
+    return [((4, 4, SLAB, width), BF16) for width in widths]
+
+
+def block_backward(near, far, tokens, last, cid):
+    vecs = ((8, D), F32)
+    attn_left, attn_right = slab_specs(ATT_COLS)
+    outs = {
+        "vecs_one": vecs,
+        "vecs_two": vecs,
+        "bias_one": ((1, 3 * HW), F32),
+        "bias_two": ((1, FW), F32),
+        "attn_left": attn_left,
+        "attn_right": attn_right,
+        "ffn_rows": ((SLAB, FFN_COLS), BF16),
+    }
+    wide, tile = (8 * tokens, D), (tokens, D)
+    scratch = {
+        "g16": pltpu.VMEM(tile, BF16),
+        "g_one": pltpu.VMEM(wide, BF16),
+        "g_two": pltpu.VMEM(wide, BF16),
+        "pre_all": pltpu.VMEM((8 * tokens, FW), BF16),
+        "joined": pltpu.VMEM((8 * tokens, 3 * HW), BF16),
+        "dk": pltpu.VMEM((2, 8 * tokens, HEAD), F32),
+        "dv": pltpu.VMEM((2, 8 * tokens, HEAD), F32),
+        "whole_one": pltpu.VMEM((D, FW), F32),
+        "whole_two": pltpu.VMEM((D, FW), F32),
+        "ffn_left": pltpu.VMEM(*slab_specs(FFN_COLS)[0]),
+        "ffn_right": pltpu.VMEM(*slab_specs(FFN_COLS)[1]),
+        "ring_local": ring_local(tokens),
+        "ring_one": ring_remote(tokens),
+        "ring_two": ring_remote(tokens),
+        "sums_two": rows_out_scratch(FFN_COLS),
+    }
+    if last:
+        outs["out"] = (tile, F32)
+        scratch["g"] = pltpu.VMEM(tile, F32)
+    else:
+        outs["attn_rows"] = ((SLAB, ATT_COLS), BF16)
+        outs["embed_w_grad"] = ((16, D), F32)
+        outs["embed_b_grad"] = ((1, D), F32)
+        outs["latent"] = ((tokens, 16), F32)
+        scratch["g"] = pltpu.VMEM(tile, F32)
+        scratch["sums_one"] = rows_out_scratch(ATT_COLS)
+    body = functools.partial(backward_body, tokens=tokens, last=last)
+    return launch(body, cid, near, far, outs, {}, scratch, vmem=62 << 20)
+
+
+def head_kernel(
+    first_ref, two_ref, place_ref, vec_ref, unpatch_ref, bias_ref, cot_ref,
+    out_ref, unpatch_grad_ref, vecs_ref, ended_ref, chosen_ref
+):
+    picks = choice(place_ref, two_ref.shape[0])
+    ended = spread_back(picks, two_ref[...], first_ref[...])
+    normed, inv_std = layer_stats(ended)
+    final16 = (normed * (1.0 + vec_ref[1:2]) + vec_ref[0:1]).astype(BF16)
+    out_ref[...] = (dot_nn(final16, unpatch_ref[...]) + bias_ref[...]).astype(BF16)
+    unpatch_grad_ref[...] = dot_tn(final16, cot_ref[...])
+    grad = dot_nt(cot_ref[...], unpatch_ref[...])
+    vecs_ref[0:1] = sum_rows(grad)
+    vecs_ref[1:2] = sum_rows(grad * normed)
+    grad = layer_back(grad * (1.0 + vec_ref[1:2]), normed, inv_std)
+    ended_ref[...] = grad
+    chosen_ref[...] = exact(picks, grad, (1, 0))
+
+
+def head(first, two, place, vecs, unpatch, bias, cotangent):
+    tokens, capacity = first.shape[0], two.shape[0]
     outs = (
+        jax.ShapeDtypeStruct((tokens, 32), BF16),
+        jax.ShapeDtypeStruct((D, 32), F32),
+        jax.ShapeDtypeStruct((2, D), F32),
         jax.ShapeDtypeStruct((tokens, D), F32),
-        jax.ShapeDtypeStruct((8, D), F32),
-        jax.ShapeDtypeStruct((1, 3 * HW), F32),
-        *slab_shapes(ATT_COLS),
-        jax.ShapeDtypeStruct((SLAB, FFN_COLS), BF16),
-    )
-    scratch = [
-        pltpu.VMEM((tokens, D), BF16),
-        pltpu.VMEM((8 * tokens, D), BF16),
-        pltpu.VMEM((8 * tokens, 3 * HW), BF16),
-        pltpu.VMEM((2, 8 * tokens, HEAD), F32),
-        pltpu.VMEM((2, 8 * tokens, HEAD), F32),
-        pltpu.VMEM((D, ATT_COLS), F32),
-    ]
-    scratch += [pltpu.VMEM(*shape) for shape in kept_shapes(tokens)]
-    scratch += [pltpu.SemaphoreType.DMA((6,))] + ring_scratch(tokens) + rows_out_scratch(FFN_COLS)
-    operands = (g, x, branch, vecs, mask, wqkv, wm, *pending, *kept)
-    return collective(attn_backward_kernel, cid, outs, scratch, *operands, far_in=6)
-
-
-def block_forward(x, mod, attn_w, biases, mask, rows, start, more_blocks, cid):
-    attn_b, merge_b, expand_b, reduce_b = (b.astype(F32) for b in biases)
-    group = own_group()
-    zeros = jnp.zeros((4, D), F32)
-    vec_one = jnp.concatenate([mod[0:3], merge_b[None], zeros])
-    vec_two = jnp.concatenate([mod[3:6], reduce_b[None], zeros])
-    bias = jnp.concatenate(
-        [
-            lax.dynamic_slice_in_dim(attn_b, group * HW, HW),
-            jnp.zeros((HW,), F32),
-            lax.dynamic_slice_in_dim(attn_b, D + group * HW, HW),
-        ]
-    )[None]
-    middle, branch, we, wr, *kept = attn_forward(
-        x, vec_one, bias, mask, *attn_w, rows, start, cid
-    )
-    e_bias = lax.dynamic_slice_in_dim(expand_b, group * FW, FW)[None]
-    next_rows = rows if more_blocks else None
-    output, mlp, *more = ffn_forward(middle, vec_two, e_bias, we, wr, next_rows, cid + 1)
-    following, more = (more[:2], more[2:]) if more_blocks else ((), more)
-    params = (*attn_w, we, wr)
-    return output, following, params, (x, vec_one, mask, middle, branch, kept, vec_two, mlp, more)
-
-
-def block_backward(grad, saved, params, valid, pending, cid):
-    x, vec_one, mask, middle, branch, kept, vec_two, mlp, more = saved
-    wqkv, wm, we, wr = params
-    group = own_group()
-    grad, mod_two, bias_two, *dw_ffn = ffn_backward(
-        grad, middle, mlp, vec_two, valid, *more, we, wr, pending, cid + 2
-    )
-    dw_ffn, earlier = dw_ffn[:2], dw_ffn[2:]
-    grad, mod_one, bias_one, *dw_attn, ffn_rows = attn_backward(
-        grad, x, branch, vec_one, mask, kept, wqkv, wm, slabs(dw_ffn), cid + 3
-    )
-    grad_expand_b = lax.dynamic_update_slice_in_dim(
-        jnp.zeros((FF,), F32), bias_two[0], group * FW, 0
-    )
-    grad_attn_b = lax.dynamic_update_slice_in_dim(
-        jnp.zeros((2 * D,), F32), bias_one[0, :HW], group * HW, 0
-    )
-    grad_attn_b = lax.dynamic_update_slice_in_dim(
-        grad_attn_b, bias_one[0, 2 * HW :], D + group * HW, 0
-    )
-    mod_grad = jnp.concatenate([mod_one[0:3].reshape(-1), mod_two[0:3].reshape(-1)])
-    biases = (grad_attn_b, mod_one[3], grad_expand_b, mod_two[3])
-    return grad, mod_grad, dw_attn, ffn_rows, earlier, biases
+        jax.ShapeDtypeStruct((capacity, D), F32),
+    )
+    return pl.pallas_call(
+        head_kernel,
+        out_shape=outs,
+        in_specs=[VMEM] * 7,
+        out_specs=(VMEM,) * 5,
+        compiler_params=pltpu.CompilerParams(vmem_limit_bytes=32 << 20),
+    )(first, two, place, vecs, unpatch, bias, cotangent)
 
 
 def pack_weights(attention_weight, merge_weight, expand_weight, reduce_weight):
@@ -1351,9 +1331,8 @@
     )
     routed_marks = jnp.arange(capacity, dtype=jnp.int32)[None, None, :] < tile_loads[:, :, None]
     routed_marks = routed_marks.astype(jnp.float32).reshape(count, tiles * capacity)
-    everyone = jnp.ones((count, tile_tokens), jnp.float32)
-    position, owner, valid = compact_plan(routed, capacity)
-    width = D
+    flags = routed[0] > 0
+    place = jnp.where(flags, jnp.cumsum(flags.astype(jnp.int32)) - 1, -1)[None]
     whole_index = lax.axis_index(DP_TX_TY)
     small_parts = (
         embed_weight,
@@ -1400,80 +1379,90 @@
     merge_b = from_owner(pieces[4], (2, D), 1)
     expand_b = from_owner(pieces[5], (2, FF), 1)
     reduce_b = from_owner(pieces[6], (2, D), 1)
-    placed = sincos_table(row_index.astype(jnp.float32), col_index.astype(jnp.float32), width)
-    patches = to_patches(latent)
-    initial_tokens = (
-        jnp.einsum("btp,pd->btd", patches, embed_w, preferred_element_type=jnp.float32)
-        + embed_b.astype(jnp.float32)
-        + placed[None, :, :]
-    )
-    first_biases = (attn_b[0], merge_b[0], expand_b[0], reduce_b[0])
-    second_biases = (attn_b[1], merge_b[1], expand_b[1], reduce_b[1])
+    placed = sincos_table(row_index.astype(F32), col_index.astype(F32), D)
+    patches = to_patches(latent)[0]
     mask_one = jnp.zeros((1, tiles * tile_tokens), F32)
     mask_two = jnp.where(routed_marks > 0, 0.0, -1e30).astype(F32)
-    middle_one, second_attn, first_params, saved_one = block_forward(
-        initial_tokens[0],
-        mod_one.reshape(6, D),
-        first_attn,
-        first_biases,
-        mask_one,
-        rows,
-        2 * ATT_COLS,
+    group = own_group()
+    zeros = jnp.zeros((4, D), F32)
+
+    def own_cols(bias, start, cols):
+        return lax.dynamic_slice_in_dim(bias, start + group * cols, cols).astype(F32)
+
+    def block_near(b, mod, wqkv, wm, mask):
+        vecs = mod.reshape(6, D)
+        bias = [own_cols(attn_b[b], 0, HW), jnp.zeros((HW,), F32), own_cols(attn_b[b], D, HW)]
+        return {
+            "vec_one": jnp.concatenate([vecs[0:3], merge_b[b].astype(F32)[None], zeros]),
+            "vec_two": jnp.concatenate([vecs[3:6], reduce_b[b].astype(F32)[None], zeros]),
+            "mask": mask,
+            "wqkv": wqkv,
+            "wm": wm,
+        }, {
+            "bias_one": jnp.concatenate(bias)[None],
+            "bias_two": own_cols(expand_b[b], 0, FW)[None],
+            "rows": rows,
+        }
+
+    near_one, more_one = block_near(0, mod_one, *first_attn, mask_one)
+    start_one = {"patches": patches, "embed_w": embed_w, "embed_b": embed_b.astype(F32)[None]}
+    kept_one = block_forward(
+        {**near_one, **more_one, **start_one, "placed": placed}, tile_tokens, 2 * ATT_COLS, False, 10
+    )
+    near_two, more_two = block_near(
+        1, mod_two, kept_one.pop("next_wqkv"), kept_one.pop("next_wm"), mask_two
+    )
+    first = kept_one.pop("out")
+    kept_two = block_forward(
+        {**near_two, **more_two, "first": first, "place": place},
+        capacity,
+        2 * ATT_COLS + FFN_COLS,
         True,
-        10,
-    )
-    middle_one = middle_one[None]
-    selected_rows = pick_rows(middle_one, owner)
-    middle_two, _, second_params, saved_two = block_forward(
-        selected_rows[0],
-        mod_two.reshape(6, D),
-        second_attn,
-        second_biases,
-        mask_two,
-        rows,
-        2 * ATT_COLS + FFN_COLS,
-        False,
-        20,
-    )
-    middle_two = middle_two[None]
-    keep_mask = routed[:, :, None] > 0
-    ended = jnp.where(keep_mask, pick_rows(middle_two, position), middle_one)
-    head_shift = head_mod[:, None, :width]
-    head_scale = head_mod[:, None, width:]
-    normed_end, inv_end = layer_stats(ended)
-    final16 = (normed_end * (1.0 + head_scale) + head_shift).astype(jnp.bfloat16)
-    outputs = jnp.einsum(
-        "btd,do->bto", final16, unpatch_w, preferred_element_type=jnp.float32
-    ) + unpatch_bias.astype(jnp.float32)
-    predicted = from_patches(outputs.astype(jnp.bfloat16), tile_rows, tile_cols)
-    cotangent = to_patches(pred_cotangent)
-    grad_unpatch_w = jnp.einsum(
-        "btd,bto->do", final16, cotangent, preferred_element_type=jnp.float32
-    )
-    grad_unpatch_b = jnp.sum(cotangent.astype(jnp.float32), axis=(0, 1))
-    grad_final = jnp.einsum("bto,do->btd", cotangent, unpatch_w, preferred_element_type=jnp.float32)
-    head_grad_mod = jnp.concatenate(
-        [jnp.sum(grad_final, axis=1), jnp.sum(grad_final * normed_end, axis=1)], axis=-1
-    )
-    grad_ended = layer_back(grad_final * (1.0 + head_scale), normed_end, inv_end)
-    grad_chosen = pick_rows(grad_ended, owner)
-    grad_two, mod_grad_two, dw_attn_two, ffn_two, _, biases_two = block_backward(
-        grad_chosen[0], saved_two, second_params, valid[0][:, None], (), 20
-    )
-    grad_middle = jnp.where(keep_mask, pick_rows(grad_two[None], position), grad_ended)
-    grad_start, mod_grad_one, dw_attn_one, ffn_one, (attn_two,), biases_one = block_backward(
-        grad_middle[0], saved_one, first_params, everyone[0][:, None], slabs(dw_attn_two), 10
-    )
-    grad_start = grad_start[None]
-    start_grad16 = grad_start.astype(jnp.bfloat16)
-    grad_embed_w = jnp.einsum(
-        "btp,btd->pd", patches, start_grad16, preferred_element_type=jnp.float32
-    )
-    grad_embed_b = jnp.sum(start_grad16.astype(jnp.float32), axis=(0, 1))
-    latent_tokens = jnp.einsum(
-        "btd,pd->btp", start_grad16, embed_w, preferred_element_type=jnp.float32
-    )
-    latent_grad = from_patches(latent_tokens, tile_rows, tile_cols)
+        11,
+    )
+    cotangent = to_patches(pred_cotangent)[0]
+    outputs, grad_unpatch_w, head_grad_mod, grad_ended, grad_chosen = head(
+        first,
+        kept_two.pop("out"),
+        place,
+        head_mod.reshape(2, D),
+        unpatch_w,
+        unpatch_bias.astype(F32)[None],
+        cotangent,
+    )
+    predicted = from_patches(outputs[None], tile_rows, tile_cols)
+    grad_unpatch_b = jnp.sum(cotangent.astype(F32), axis=0)
+    back_two = block_backward({**near_two, "grad_in": grad_chosen}, kept_two, capacity, True, 12)
+    later = {
+        "pending_left": back_two["attn_left"],
+        "pending_right": back_two["attn_right"],
+        "grad_two": back_two["out"],
+        "grad_ended": grad_ended,
+        "place": place,
+        "patches": patches,
+        "embed_w": embed_w,
+    }
+    back_one = block_backward({**near_one, **later}, kept_one, tile_tokens, False, 13)
+    latent_grad = from_patches(back_one["latent"][None], tile_rows, tile_cols)
+    grad_embed_w, grad_embed_b = back_one["embed_w_grad"], back_one["embed_b_grad"][0]
+
+    def placed_cols(parts, length):
+        whole = jnp.zeros((length,), F32)
+        for part, at in parts:
+            whole = lax.dynamic_update_slice_in_dim(whole, part, at, 0)
+        return whole
+
+    def bias_parts(back):
+        one, two = back["bias_one"][0], back["bias_two"][0]
+        return (
+            placed_cols([(one[:HW], group * HW), (one[2 * HW :], D + group * HW)], 2 * D),
+            back["vecs_one"][3],
+            placed_cols([(two, group * FW)], FF),
+            back["vecs_two"][3],
+        )
+
+    biases_one, biases_two = bias_parts(back_one), bias_parts(back_two)
+    mod_grads = [back[name][0:3].reshape(-1) for back in (back_one, back_two) for name in ("vecs_one", "vecs_two")]
     bias_grads = [jnp.stack([biases_one[member], biases_two[member]]) for member in range(4)]
     small_out = jnp.concatenate(
         [
@@ -1489,13 +1478,13 @@
         axis=1,
     )
     small_out = jnp.pad(small_out, [(0, 0), (0, 1024 - small_out.shape[1])])
-    grad_mods = jnp.concatenate([mod_grad_one, mod_grad_two, head_grad_mod[0]])
+    grad_mods = jnp.concatenate([*mod_grads, head_grad_mod.reshape(-1)])
     grad_mods = jnp.pad(grad_mods, (0, 16384 - MOD_ALL))
     early, late, mod_back, small_back = finish(
-        dw_attn_one,
-        attn_two,
-        ffn_one,
-        ffn_two,
+        (back_one["attn_left"], back_one["attn_right"]),
+        back_one["attn_rows"],
+        back_one["ffn_rows"],
+        back_two["ffn_rows"],
         grad_mods.reshape(8, 16, 128),
         small_out.reshape(4, 4, 64, 128),
     )

time: 453 us -> 420 us (0.927)
  Pallas kernels: 373 us -> 352 us
  local copies, waits for them, and re-layouts: 56.8 us -> 50.7 us
    pallas_call x10 -> x2, Pallas kernels: 371 us -> 74.9 us  [collective(): pl.pallas_call(kernel, out_shape=outs, in_specs=[VMEM] * near_in + [FAR]...]
    pallas_call x0 -> x5, Pallas kernels: none -> 276 us  [the longest x4 274 us: launch(): pl.pallas_call(kernel, out_shape=tuple(shapes), in_specs=[VMEM] * len(nea...]
    gather x6 -> x0, local copies, waits for them, and re-layouts: 10 us -> none  [pick_rows(): jnp.take(table, where, axis=0)]
    unnamed x97 -> x109, local copies, waits for them, and re-layouts: 12.9 us -> 15.5 us
where the time goes in v5:
time: 420 us; the launch traced here: 415 us
  Pallas kernels  352 us (84%)
  local copies, waits for them, and re-layouts  50.7 us (12%)
  other arithmetic  8.74 us (2%)
    pallas_call x4, Pallas kernels, launch(): pl.pallas_call(kernel, out_shape=tuple(shapes), in_specs=[VMEM] * len(nea...  274 us
    pallas_call x2, Pallas kernels, collective(): pl.pallas_call(kernel, out_shape=outs, in_specs=[VMEM] * near_in + [FAR]...  74.9 us
    unnamed x109, local copies, waits for them, and re-layouts  15.5 us

profile of v5, /device:TPU:1, one launch (start us, length us, event | category | flops | bytes accessed | tf_op | source)
XLA Modules:
  0.0 415.3 jit_solution(3932478466976659214)
XLA Ops:
  3.0 1.0 copy.173.mod_ref
  4.0 0.9 fusion
  5.4 1.2 copy.223
  8.3 1.2 concatenate.42
  9.8 0.9 pad.20.w_ref
  11.9 39.3 %shard_map.378 = (bf16[80,3584]{1,0:T(8,128)(2,1)}, bf16[1152,432]{1,0:T(8,128)(2,1)}, bf16[1152,144]{1,0:T(8,128)(2,1)}, f32[128,128]{1,0:T(8,128)}, bf16[8,4,4,16,128]{4,3,2,1,0:T(8,128)(2,1)}) custom-call(bf16[8,64,512]{2,1,0:T(8,128)(2,1)} %pad.20.w_ref, bf16[7,80,512]{2,1,0:T(8,128)(2,1)} %constant.157.clone.pick_ref.picks_ref, ...), custom_call_target="tpu_custom_call" | custom-call | tf_op jit(solution)/shard_map/pallas_call | solution.py:85
  51.2 1.3 reshape.576
  58.8 1.2 reshape.584.refs_9_.refs_11_
  60.1 0.8 reshape.621.refs_10_
  61.5 1.0 maximum_bitcast_fusion.refs_11_
  64.7 68.0 %shard_map.379 = (f32[128,1152]{1,0:T(8,128)}, bf16[1152,432]{1,0:T(8,128)(2,1)}, bf16[1152,144]{1,0:T(8,128)(2,1)}, f32[128,1152]{1,0:T(8,128)}, bf16[1024,1152...) custom-call(f32[8,1152]{1,0:T(8,128)} %get-tuple-element.288.refs_0_, ...), custom_call_target="tpu_custom_call" | custom-call | tf_op jit(solution)/shard_map/pallas_call | solution.py:808
  135.4 64.1 %shard_map.380 = (f32[112,1152]{1,0:T(8,128)}, f32[112,1152]{1,0:T(8,128)}, bf16[896,1152]{1,0:T(8,128)(2,1)}, bf16[2,896,72]{2,1,0:T(8,128)(2,1)}, bf16[2,896,7...) custom-call(f32[8,1152]{1,0:T(8,128)} %get-tuple-element.287.refs_0_, ...), custom_call_target="tpu_custom_call" | custom-call | tf_op jit(solution)/shard_map/pallas_call | solution.py:808
  200.6 2.1 shard_map.381
  202.7 0.8 copy-done.2
  203.5 0.8 copy-done.4
  205.0 68.5 %shard_map.382 = (f32[8,1152]{1,0:T(8,128)}, f32[8,1152]{1,0:T(8,128)}, f32[1,432]{1,0:T(1,128)}, f32[1,576]{1,0:T(1,128)}, bf16[4,4,80,384]{3,2,1,0:T(8,128)(2,...) custom-call(f32[8,1152]{1,0:T(8,128)} %get-tuple-element.287.refs_0_, ...), custom_call_target="tpu_custom_call" | custom-call | tf_op jit(solution)/shard_map/pallas_call | solution.py:808
  273.5 73.0 %shard_map.383 = (f32[8,1152]{1,0:T(8,128)}, f32[8,1152]{1,0:T(8,128)}, f32[1,432]{1,0:T(1,128)}, f32[1,576]{1,0:T(1,128)}, bf16[4,4,80,384]{3,2,1,0:T(8,128)(2,...) custom-call(f32[8,1152]{1,0:T(8,128)} %get-tuple-element.288.refs_0_, ...), custom_call_target="tpu_custom_call" | custom-call | tf_op jit(solution)/shard_map/pallas_call | solution.py:808
  346.5 0.8 slice.182
  347.8 0.8 dynamic_update_slice.46
  352.1 0.9 reshape.596
  354.5 0.9 reshape.606.s_ref
  356.2 35.6 %shard_map.384 = (bf16[8,64,512]{2,1,0:T(8,128)(2,1)}, bf16[8,32,512]{2,1,0:T(8,128)(2,1)}, bf16[8,4,4,16,128]{4,3,2,1,0:T(8,128)(2,1)}, f32[8,128]{1,0:T(8,128)}) custom-call(bf16[4,4,80,384]{3,2,1,0:T(8,128)(2,1)} %get-tuple-element.140.left_ref, bf16[4,4,80,256]{3,2,1,0:T(8,128)(2,1)} %get-tuple-element.141.right_ref, ...), custom_call_target="tpu_custom_call" | custom-call | tf_op jit(solution)/shard_map/pallas_call | solution.py:85
  391.9 1.3 reshape.607
  393.3 1.0 copy-done.3
  394.3 0.9 copy-done.9
  395.3 1.8 shard_map.385
  400.4 1.2 copy.215
  401.6 1.0 copy.218
  402.6 1.0 copy.219
  403.6 0.8 copy.216
  405.1 1.2 fusion.11
  413.0 0.8 copy.214
  (292 shorter events, 37.0 us)
Async XLA Ops:
  0.7 4.2 %copy-start.20 = (bf16[16,9]{1,0:T(8,128)(2,1)S(1)}, bf16[16,9]{1,0:T(8,128)(2,1)}, u32[]{:S(2)}) copy-start(bf16[16,9]{1,0:T(8,128)(2,1)} %param.25) | copy-start | bytes 868
  0.7 4.4 %copy-start.8 = (bf16[9,2304]{1,0:T(8,128)(2,1)S(1)}, bf16[9,2304]{1,0:T(8,128)(2,1)}, u32[]{:S(2)}) copy-start(bf16[9,2304]{1,0:T(8,128)(2,1)} %final_ref.1) | copy-start | bytes 124420
  5.4 1.2 copy-start.19
  6.6 1.2 copy-start.18
  9.5 1.3 copy-start.41
  9.5 1.4 copy-start.42
  9.5 1.5 copy-start.43
  9.5 1.5 copy-start.44
  9.6 1.6 copy-start.40
  52.4 4.9 %copy-start.24 = (f32[128,128]{1,0:T(8,128)S(1)}, f32[128,128]{1,0:T(8,128)}, u32[]{:S(2)}) copy-start(f32[128,128]{1,0:T(8,128)} %get-tuple-element.94) | copy-start | bytes 196612
  58.8 3.7 copy-start.27
  64.7 68.7 %copy-start.32 = (s32[1,512]{1,0:T(1,128)S(1)}, s32[1,512]{1,0:T(1,128)}, u32[]{:S(2)}) copy-start(s32[1,512]{1,0:T(1,128)} %param.26) | copy-start | bytes 6148
  135.4 64.6 %copy-start.26 = (bf16[1,32,16,8]{1,3,2,0:T(8,128)(2,1)S(1)}, bf16[1,32,16,8]{1,3,2,0:T(8,128)(2,1)}, u32[]{:S(2)}) copy-start(bf16[1,32,16,8]{1,3,2,0:T(8,128)(2,1)} %param.43) | copy-start | bytes 24580
  135.4 65.0 %copy-start.45 = (bf16[32]{0:T(256)(128)(2,1)S(1)}, bf16[32]{0:T(256)(128)(2,1)}, u32[]{:S(2)}) copy-start(bf16[32]{0:T(256)(128)(2,1)} %param.42) | copy-start | bytes 196
  135.4 65.0 %copy-start = (f32[128,1152]{1,0:T(8,128)S(1)}, f32[128,1152]{1,0:T(8,128)}, u32[]{:S(2)}) copy-start(f32[128,1152]{1,0:T(8,128)} %get-tuple-element.99.refs_8_.first_ref) | copy-start | bytes 1769476
  135.4 65.0 %copy-start.15 = (s32[1,128]{1,0:T(1,128)S(1)}, s32[1,128]{1,0:T(1,128)}, u32[]{:S(2)}) copy-start(s32[1,128]{1,0:T(1,128)} %bitcast_select_fusion.refs_9_.place_ref) | copy-start | bytes 1540
  273.5 73.9 %copy-start.28 = (f32[8,1152]{1,0:T(8,128)S(1)}, f32[8,1152]{1,0:T(8,128)}, u32[]{:S(2)}) copy-start(f32[8,1152]{1,0:T(8,128)} %get-tuple-element.148) | copy-start | bytes 110596
  273.5 75.2 %copy-start.37 = (f32[1,576]{1,0:T(1,128)S(1)}, f32[1,576]{1,0:T(1,128)}, u32[]{:S(2)}) copy-start(f32[1,576]{1,0:T(1,128)} %get-tuple-element.156) | copy-start | bytes 6916
  273.5 76.6 %copy-start.29 = (f32[8,1152]{1,0:T(8,128)S(1)}, f32[8,1152]{1,0:T(8,128)}, u32[]{:S(2)}) copy-start(f32[8,1152]{1,0:T(8,128)} %get-tuple-element.147) | copy-start | bytes 110596
  346.5 4.0 copy-start.39
  346.5 4.6 %copy-start.38 = (f32[1,432]{1,0:T(1,128)S(1)}, f32[1,432]{1,0:T(1,128)}, u32[]{:S(2)}) copy-start(f32[1,432]{1,0:T(1,128)} %get-tuple-element.154) | copy-start | bytes 5188
  346.5 5.6 %copy-start.22 = (f32[16,1152]{1,0:T(8,128)S(1)}, f32[16,1152]{1,0:T(8,128)}, u32[]{:S(2)}) copy-start(f32[16,1152]{1,0:T(8,128)} %get-tuple-element.150) | copy-start | bytes 221188
  351.9 1.6 copy-start.33
  354.2 1.3 copy-start.30
  391.8 1.4 copy-start.1
  391.9 1.4 copy-start.12
  400.4 3.1 copy-start.7
  401.6 2.8 copy-start.11
  401.6 4.7 %copy-start.21 = (bf16[16,9]{1,0:T(8,128)(2,1)S(1)}, bf16[16,9]{1,0:T(8,128)(2,1)}, u32[]{:S(2)}) copy-start(bf16[16,9]{1,0:T(8,128)(2,1)} %param.25) | copy-start | bytes 868
  401.6 5.3 %copy-start.36 = (f32[8,128]{1,0:T(8,128)S(1)}, f32[8,128]{1,0:T(8,128)}, u32[]{:S(2)}) copy-start(f32[8,128]{1,0:T(8,128)} %get-tuple-element.161) | copy-start | bytes 12292
  401.6 10.7 %copy-start.23 = (f32[128,16]{1,0:T(8,128)S(1)}, f32[128,16]{1,0:T(8,128)}, u32[]{:S(2)}) copy-start(f32[128,16]{1,0:T(8,128)} %get-tuple-element.139) | copy-start | bytes 24580
  402.6 11.2 %copy-start.14 = (bf16[128,32]{1,0:T(8,128)(2,1)S(1)}, bf16[128,32]{1,0:T(8,128)(2,1)}, u32[]{:S(2)}) copy-start(bf16[128,32]{1,0:T(8,128)(2,1)} %copy-done.13) | copy-start | bytes 24580
  (14 other events, 12.8 us)

commit v6 on v5

v6 whole, which is shorter than its diff:
```python
import functools

import jax
import jax.numpy as jnp
import numpy as np
from jax import lax
from jax.experimental import pallas as pl
from jax.experimental.pallas import tpu as pltpu
from jax.sharding import Mesh
from jax.sharding import PartitionSpec as P

D = 1152
HEADS = 16
FF = 4608
HW = D // 8
FW = FF // 8
DP = ("dp_0", "dp_1")
DP_TX_TY = ("dp_0", "dp_1", "tx", "ty")
MESH = pl.DeviceIdType.MESH
VMEM = pl.BlockSpec(memory_space=pltpu.VMEM)
FAR = pl.BlockSpec(memory_space=pl.ANY)
F32 = jnp.float32
BF16 = jnp.bfloat16
ATT_COLS = 640
FFN_COLS = 2 * FW
ALL_COLS = 2 * (ATT_COLS + FFN_COLS)
PIECE = 512
PIECES = ALL_COLS // PIECE


def greet(peers):
    barrier = pltpu.get_barrier_semaphore()
    for peer in peers:
        pl.semaphore_signal(barrier, inc=1, device_id=peer, device_id_type=MESH)


def met(peers):
    pl.semaphore_wait(pltpu.get_barrier_semaphore(), len(peers))


def enter(peers):
    greet(peers)
    met(peers)


def send(src, dst, sems, k, peer):
    copy = pltpu.make_async_remote_copy(
        src_ref=src,
        dst_ref=dst,
        send_sem=sems[0].at[k],
        recv_sem=sems[1].at[k],
        device_id=peer,
        device_id_type=MESH,
    )
    copy.start()
    return copy


def group_peers():
    c, y = lax.axis_index("tx"), lax.axis_index("ty")
    found = []
    for dc in range(2):
        for dy in range(4):
            if dc or dy:
                oc, oy = lax.rem(c + dc, 2), lax.rem(y + dy, 4)
                found.append(({"tx": oc, "ty": oy}, oc * 4 + oy))
    return found


def own_group():
    return lax.axis_index("tx") * 4 + lax.axis_index("ty")


def dma_sems(n):
    return [pltpu.SemaphoreType.DMA((n,)), pltpu.SemaphoreType.DMA((n,))]


def ring_peers():
    c, y = lax.axis_index("tx"), lax.axis_index("ty")
    return (
        {"tx": 1 - c},
        {"ty": lax.rem(y + 1, 4)},
        {"ty": lax.rem(y + 3, 4)},
        {"ty": lax.rem(y + 2, 4)},
    )


def layer_stats(value_rows):
    centered = value_rows - jnp.mean(value_rows, axis=-1, keepdims=True)
    inv_std = lax.rsqrt(jnp.mean(centered * centered, axis=-1, keepdims=True) + 1e-06)
    return (centered * inv_std, inv_std)


def layer_back(upstream, normed, inv_std):
    return inv_std * (
        upstream
        - jnp.mean(upstream, axis=-1, keepdims=True)
        - normed * jnp.mean(upstream * normed, axis=-1, keepdims=True)
    )


def sincos_table(row_pos, col_pos, width):
    quarter = width // 4
    freqs = jnp.power(10000.0, -jnp.arange(quarter, dtype=jnp.float32) / quarter)
    row_angle = row_pos[:, None] * freqs[None, :]
    col_angle = col_pos[:, None] * freqs[None, :]
    row_embed = jnp.concatenate([jnp.sin(row_angle), jnp.cos(row_angle)], axis=-1)
    col_embed = jnp.concatenate([jnp.sin(col_angle), jnp.cos(col_angle)], axis=-1)
    row_full = jnp.broadcast_to(
        row_embed[:, None, :], (row_pos.shape[0], col_pos.shape[0], width // 2)
    )
    col_full = jnp.broadcast_to(
        col_embed[None, :, :], (row_pos.shape[0], col_pos.shape[0], width // 2)
    )
    return jnp.concatenate([row_full, col_full], axis=-1).reshape(
        row_pos.shape[0] * col_pos.shape[0], width
    )


def ring_local(tokens):
    return [
        pltpu.VMEM((4, tokens, D), F32),
        pltpu.VMEM((4, tokens, D), BF16),
        pltpu.VMEM((3, tokens, D), BF16),
    ]


def ring_remote(tokens):
    half = (tokens // 2 + 15) // 16 * 16
    return [
        pltpu.VMEM((4, tokens, D), BF16),
        pltpu.VMEM((2, tokens, D), BF16),
        pltpu.VMEM((half, D), BF16),
        pltpu.VMEM((tokens - half, D), BF16),
    ] + dma_sems(24)


SLAB = 80
PART = D // 16
CUT = {ATT_COLS: 384, FFN_COLS: 640}


def line_peers():
    x, z = lax.axis_index("dp_0"), lax.axis_index("dp_1")
    along_x = [({"dp_0": lax.rem(x + d, 4)}, lax.rem(x + d, 4)) for d in (2, 1, 3)]
    along_z = [({"dp_1": lax.rem(z + d, 4)}, lax.rem(z + d, 4)) for d in (2, 1, 3)]
    return along_x, along_z


class RowsIn:
    def __init__(self, left_ref, right_ref, scratch):
        self.left, self.right = left_ref, right_ref
        self.all_left, self.all_right = scratch[:2]
        self.sems = tuple(scratch[2:4])
        self.x, self.z = lax.axis_index("dp_0"), lax.axis_index("dp_1")
        self.along_x, self.along_z = line_peers()

    def peers(self):
        return [peer for peer, _ in self.along_x + self.along_z]

    def start(self):
        x, z = self.x, self.z
        self.first = []
        for k, (peer, _) in enumerate(self.along_z):
            self.first.append(send(self.left, self.all_left.at[x, z], self.sems, k, peer))
        for k, (peer, _) in enumerate(self.along_x):
            self.first.append(send(self.right, self.all_right.at[x, z], self.sems, 3 + k, peer))
        self.all_left[x, z] = self.left[...]
        self.all_right[x, z] = self.right[...]

    def middle(self):
        left, right = self.all_left.at[self.x], self.all_right.at[:, self.z]
        self.second = []
        for copy in self.first[:3]:
            copy.wait_recv()
        for k, (peer, _) in enumerate(self.along_x):
            self.second.append(send(left, left, self.sems, 6 + k, peer))
        for copy in self.first[3:]:
            copy.wait_recv()
        for k, (peer, _) in enumerate(self.along_z):
            self.second.append(send(right, right, self.sems, 9 + k, peer))

    def end(self, one_ref, two_ref):
        for copy in self.second:
            copy.wait_recv()
        width, other = one_ref.shape[1], two_ref.shape[1]
        cut = self.left.shape[1]

        @pl.loop(0, 8)
        def _(pair):
            x, z = pair // 2, 2 * lax.rem(pair, 2)
            both = []
            for k in range(2):
                parts = [self.all_left[x, z + k], self.all_right[x, z + k]]
                both.append(jnp.concatenate(parts, axis=1).astype(F32)[:PART])
            value = jnp.concatenate(both, axis=0).astype(BF16)
            at = pl.ds(pl.multiple_of(pair * 2 * PART, 16), 2 * PART)
            one_ref[at, :] = value[:, :width]
            two_ref[at, :] = value[:, width : width + other]

        for copy in self.first + self.second:
            copy.wait_send()


def rows_in_scratch(cols):
    left = CUT[cols]
    return [
        pltpu.VMEM((4, 4, SLAB, left), BF16),
        pltpu.VMEM((4, 4, SLAB, cols - left), BF16),
    ] + dma_sems(12)


class RowsOut:
    def __init__(self, left_ref, right_ref, scratch):
        self.left, self.right = left_ref, right_ref
        self.got = scratch[0:2]
        self.mine = scratch[2:4]
        self.last = scratch[4:6]
        self.sems = tuple(scratch[6:8])
        self.x, self.z = lax.axis_index("dp_0"), lax.axis_index("dp_1")
        self.along_x, self.along_z = line_peers()

    def peers(self):
        return [peer for peer, _ in self.along_x + self.along_z]

    def start(self):
        self.first = []
        for k, (peer, at) in enumerate(self.along_x):
            part = self.left.at[at]
            self.first.append(send(part, self.got[0].at[k], self.sems, k, peer))
        for k, (peer, at) in enumerate(self.along_z):
            part = self.right.at[:, at]
            self.first.append(send(part, self.got[1].at[k], self.sems, 3 + k, peer))

    def middle(self):
        self.second = []
        for side, peers in ((0, self.along_z), (1, self.along_x)):
            for copy in self.first[3 * side : 3 * side + 3]:
                copy.wait_recv()
            got, mine = self.got[side], self.mine[side]

            @pl.loop(0, 4)
            def _(k):
                own = self.right[k, self.z] if side else self.left[self.x, k]
                across, below, above = (got[source, k].astype(F32) for source in range(3))
                total = (own.astype(F32) + across) + (below + above)
                mine[k] = total.astype(mine.dtype)

            for k, (peer, at) in enumerate(peers):
                part = mine.at[at]
                copy = send(part, self.last[side].at[k], self.sems, 6 + 3 * side + k, peer)
                self.second.append(copy)

    def end(self):
        for copy in self.second:
            copy.wait_recv()
        totals = []
        for side, own in ((0, self.z), (1, self.x)):
            across, below, above = (self.last[side][source].astype(F32) for source in range(3))
            totals.append((self.mine[side][own].astype(F32) + across) + (below + above))
        return totals

    def end_rows(self, out_ref):
        cut = self.left.shape[3]
        left, right = self.end()
        out_ref[:, :cut] = left.astype(BF16)
        out_ref[:, cut:] = right.astype(BF16)
        self.leave()

    def leave(self):
        for copy in self.first + self.second:
            copy.wait_send()


def rows_out_scratch(cols):
    return sum_scratch([(SLAB, CUT[cols]), (SLAB, cols - CUT[cols])], BF16)


def sum_scratch(shapes, dtype):
    return (
        [pltpu.VMEM((3, 4, *shape), dtype) for shape in shapes]
        + [pltpu.VMEM((4, *shape), dtype) for shape in shapes]
        + [pltpu.VMEM((3, *shape), dtype) for shape in shapes]
        + dma_sems(12)
    )


def slab_views(rows_ref, start, cols):
    cut = start + CUT[cols]
    return rows_ref.at[:, start:cut], rows_ref.at[:, cut : start + cols]


def weight_shapes(cols):
    widths = (3 * HW, HW) if cols == ATT_COLS else (FW, FW)
    return tuple(jax.ShapeDtypeStruct((D, w), BF16) for w in widths)


class Ring:
    def __init__(self, tokens, local, remote):
        self.tokens = tokens
        self.half = (tokens // 2 + 15) // 16 * 16
        self.kept, self.sib_out, self.out = local
        self.sib_in, self.got, self.far_low, self.far_high = remote[:4]
        self.sems = tuple(remote[4:6])
        c, y = lax.axis_index("tx"), lax.axis_index("ty")
        self.sib, self.up, self.down, _ = ring_peers()
        self.own = [c * 4 + lax.rem(y + d, 4) for d in range(4)]
        self.other = [(1 - c) * 4 + lax.rem(y + d, 4) for d in range(4)]
        self.sent = []

    def peers(self):
        return [self.sib, self.up, self.down]

    def send(self, src, dst, k, peer):
        copy = send(src, dst, self.sems, k, peer)
        self.sent.append(copy)
        return copy

    def rows(self, index, start=0, stop=None):
        stop = self.tokens if stop is None else stop
        at = pl.multiple_of(index * self.tokens + start, 16)
        return pl.ds(at, stop - start)

    def gather(self, x_ref, all_ref, prepare, visit, between=None):
        half, tokens = self.half, self.tokens
        me, above, across, below = self.own
        first, last = slice(0, half), slice(half, tokens)

        def pass_on(index, k, peer, start=0, stop=None):
            part = all_ref.at[self.rows(index, start, stop)]
            return self.send(part, part, k, peer)

        def own_part(rows, k, peer):
            part = all_ref.at[self.rows(me, rows.start, rows.stop)]
            return self.send(x_ref.at[rows], part, k, peer)

        a1 = own_part(first, 0, self.up)
        b1 = own_part(last, 1, self.down)
        a2 = own_part(last, 2, self.up)
        b2 = own_part(first, 3, self.down)
        s0 = self.send(x_ref, all_ref.at[self.rows(me)], 4, self.sib)
        all_ref[self.rows(me), :] = x_ref[...]
        prepare()
        visit(True, 0)
        s0.wait_recv()
        visit(False, 0)
        a1.wait_recv()
        f1 = pass_on(below, 5, self.up, 0, half)
        b1.wait_recv()
        f2 = pass_on(above, 6, self.down, half, tokens)
        a2.wait_recv()
        s1 = pass_on(below, 7, self.sib)
        b2.wait_recv()
        s2 = pass_on(above, 8, self.sib)
        if between:
            between()
        visit(True, 3)
        visit(True, 1)
        s1.wait_recv()
        visit(False, 3)
        s2.wait_recv()
        visit(False, 1)
        f1.wait_recv()
        f2.wait_recv()
        s3 = pass_on(across, 9, self.sib)
        visit(True, 2)
        s3.wait_recv()
        visit(False, 2)

    def put(self, own, d, value):
        if own:
            self.kept[d] = value
        else:
            self.sib_out[d] = value.astype(BF16)
            self.swaps[d] = self.send(self.sib_out.at[d], self.sib_in.at[d], 10 + d, self.sib)

    def start_sums(self):
        self.swaps = {}

    def chip_sum(self, d):
        self.swaps[d].wait_recv()
        return self.kept[d] + self.sib_in[d].astype(F32)

    def near(self):
        half = self.half
        first, last = slice(0, half), slice(half, self.tokens)
        total = self.chip_sum(1)
        self.kept[1] = total
        self.out[0, last] = total[half:].astype(BF16)
        self.n1 = self.send(self.out.at[0, last], self.got.at[0, last], 14, self.up)
        total = self.chip_sum(3)
        self.kept[3] = total
        self.out[1, first] = total[:half].astype(BF16)
        self.n2 = self.send(self.out.at[1, first], self.got.at[1, first], 15, self.down)

    def far(self):
        half = self.half
        self.out[2] = self.chip_sum(2).astype(BF16)
        self.low, self.high = [], []
        for k, (start, stop) in enumerate(((0, 32), (32, half))):
            part = self.out.at[2, start:stop]
            self.low.append(self.send(part, self.far_low.at[start:stop], 16 + k, self.up))
        for k, (start, stop) in enumerate(((half, half + 32), (half + 32, self.tokens))):
            part = self.out.at[2, start:stop]
            landing = self.far_high.at[start - half : stop - half]
            self.high.append(self.send(part, landing, 18 + k, self.down))

    def relay(self):
        half, self.last = self.half, []
        for k in range(2):
            rows = slice(0, 32) if k == 0 else slice(32, half)
            self.low[k].wait_recv()
            value = self.kept[1, rows] + self.far_low[rows].astype(F32)
            self.out[0, rows] = value.astype(BF16)
            part = self.out.at[0, rows]
            self.last.append(self.send(part, self.got.at[0, rows], 20 + k, self.up))
            rows = slice(half, half + 32) if k == 0 else slice(half + 32, self.tokens)
            self.high[k].wait_recv()
            landed = self.far_high[rows.start - half : rows.stop - half]
            self.out[1, rows] = (self.kept[3, rows] + landed.astype(F32)).astype(BF16)
            part = self.out.at[1, rows]
            self.last.append(self.send(part, self.got.at[1, rows], 22 + k, self.down))

    def total(self):
        value = self.chip_sum(0)
        for copy in [self.n1, self.n2] + self.last:
            copy.wait_recv()
        return value + self.got[0].astype(F32) + self.got[1].astype(F32)

    def leave(self):
        for copy in self.sent:
            copy.wait_send()


def dot_nn(left, right):
    return lax.dot_general(left, right, (((1,), (0,)), ((), ())), preferred_element_type=F32)


def dot_nt(left, right):
    return lax.dot_general(left, right, (((1,), (1,)), ((), ())), preferred_element_type=F32)


def dot_tn(left, right):
    return lax.dot_general(left, right, (((0,), (0,)), ((), ())), preferred_element_type=F32)


def gelu_both(pre):
    root = 0.7978845608028654
    square = pre * pre
    bent = jnp.tanh(root * pre * (1.0 + 0.044715 * square))
    value = 0.5 * pre * (1.0 + bent)
    slope = 0.5 * (1.0 + bent) + 0.5 * pre * (1.0 - bent * bent) * root * (1.0 + 0.134145 * square)
    return value, slope


def sum_rows(value):
    return jnp.sum(value, axis=0, keepdims=True)


HEAD = D // HEADS
SCALE = HEAD ** (-0.5)


def head_cols(h, start=0):
    return slice(start + h * HEAD, start + (h + 1) * HEAD)


class Refs:
    pass


class Results(dict):
    __getattr__ = dict.__getitem__


def make_specs(entry):
    return list(entry) if isinstance(entry, list) else [entry]


def launch(body, cid, near, far, outs, kept, scratch, vmem=60 << 20):
    twins = {name: (value.shape, value.dtype) for name, value in far.items()}
    twins.update(kept)
    groups = {name: make_specs(entry) for name, entry in scratch.items()}

    def kernel(*refs):
        refs = iter(refs)
        r, hbm = Refs(), {}
        for name in near:
            setattr(r, name, next(refs))
        for name in far:
            hbm[name] = next(refs)
        for name in outs:
            setattr(r, name, next(refs))
        for name in kept:
            hbm[name] = next(refs)
        r.moves, r.moving = {}, {}
        for k, name in enumerate(twins):
            ref = next(refs)
            setattr(r, name, ref)
            r.moves[id(ref)] = (hbm[name], k)
        if twins:
            r.move_sems = next(refs)
        for name, specs in groups.items():
            found = [next(refs) for _ in specs]
            setattr(r, name, found if isinstance(scratch[name], list) else found[0])
        body(r)

    shapes = [jax.ShapeDtypeStruct(*spec) for spec in (*outs.values(), *kept.values())]
    results = pl.pallas_call(
        kernel,
        out_shape=tuple(shapes),
        in_specs=[VMEM] * len(near) + [FAR] * len(far),
        out_specs=(VMEM,) * len(outs) + (FAR,) * len(kept),
        scratch_shapes=[pltpu.VMEM(*spec) for spec in twins.values()]
        + ([pltpu.SemaphoreType.DMA((len(twins),))] if twins else [])
        + [spec for specs in groups.values() for spec in specs],
        compiler_params=pltpu.CompilerParams(
            collective_id=cid, has_side_effects=cid is not None, vmem_limit_bytes=vmem
        ),
    )(*near.values(), *far.values())
    return Results(zip(outs, results)), Results(zip(kept, results[len(outs) :]))


def load_into(r, ref, target):
    source, k = r.moves[id(ref)]
    r.moving[id(ref)] = pltpu.make_async_copy(source, target, r.move_sems.at[k])
    r.moving[id(ref)].start()


def load(r, *refs):
    for ref in refs:
        load_into(r, ref, ref)


def save(r, *refs):
    for ref in refs:
        target, k = r.moves[id(ref)]
        r.moving[id(ref)] = pltpu.make_async_copy(ref, target, r.move_sems.at[k])
        r.moving[id(ref)].start()


def settle(r, *refs):
    for key in [id(ref) for ref in refs] or list(r.moving):
        r.moving.pop(key).wait()


def exact(left, right, dims):
    return lax.dot_general(
        left,
        right,
        ((dims[:1], dims[1:]), ((), ())),
        precision=lax.Precision.HIGHEST,
        preferred_element_type=F32,
    )


def choice(place_ref, capacity):
    tokens = place_ref.shape[1]
    slots = lax.broadcasted_iota(jnp.int32, (capacity, tokens), 0)
    return jnp.where(slots == place_ref[...], 1.0, 0.0).astype(F32)


def spread_back(picks, chosen, others):
    used = exact(picks, jnp.ones((picks.shape[0], 128), F32), (0, 0))[:, :1]
    return exact(picks, chosen, (0, 0)) + others * (1.0 - used)


def modulated(x, vec_ref):
    normed, _ = layer_stats(x)
    return (normed * (1.0 + vec_ref[1:2]) + vec_ref[0:1]).astype(BF16)


def full_width(parts, at):
    height = parts[0].shape[0]
    used = at + sum(part.shape[1] for part in parts)
    if at:
        parts = [jnp.zeros((height, at), F32), *parts]
    if used < 128:
        parts = [*parts, jnp.zeros((height, 128 - used), F32)]
    return jnp.concatenate(parts, axis=1)


def to_tokens(pixels_ref, square, tokens_ref, at):
    wide, depth, high = pixels_ref.shape
    square[...] = jnp.zeros_like(square)
    square[: wide * depth, :high] = pixels_ref[...].astype(F32).reshape(wide * depth, high)
    square[...] = jnp.transpose(square[...])
    size = 2 * depth
    lines = [square[pl.ds(line, high // 2, stride=2), :] for line in range(2)]
    for c in range(wide // 2):
        parts = [value[:, c * size : (c + 1) * size] for value in lines]
        tokens_ref[pl.ds(c, high // 2, stride=wide // 2), :] = full_width(parts, at)


def to_pixels(tokens_ref, square, pixels_ref, at):
    wide, depth, high = pixels_ref.shape
    square[...] = jnp.zeros_like(square)
    size = 2 * depth
    columns = [tokens_ref[pl.ds(c, high // 2, stride=wide // 2), :] for c in range(wide // 2)]
    for line in range(2):
        start = at + line * size
        parts = [value[:, start : start + size] for value in columns]
        square[pl.ds(line, high // 2, stride=2), :] = full_width(parts, 0)
    value = jnp.transpose(square[...])[: wide * depth, :high].reshape(wide, depth, high)
    pixels_ref[...] = value.astype(pixels_ref.dtype)


UNPATCH, EMBED, BLOCKS, EMBED_BIAS = 0, 32, 48, 64
WHOLE = 16384


def own_targets():
    group = own_group()
    return group * (D // 16), group * (D // 8)


def bias_table():
    table = np.zeros((8, 1024), np.int32)
    for col in range(3 * HW):
        part, e = divmod(col, HW)
        table[0, col] = (e // 18 + (64 if part == 2 else 0)) * 9 + e % 9 if part != 1 else -(1 << 20)
        table[1, col] = e % 18 // 9
    for e in range(FW):
        table[0, 3 * HW + e] = e // 36 * 9 + e % 9
        table[1, 3 * HW + e] = e % 36 // 9
    return table


def bias_picks(table_ref, cols, shift):
    rows = lax.broadcasted_iota(jnp.int32, (D, cols.stop - cols.start), 0)
    return jnp.where(rows == table_ref[0:1, cols] + shift, 1.0, 0.0).astype(F32)


ATT_BIAS = slice(0, 3 * HW)
FFN_BIAS = slice(3 * HW, 3 * HW + FW)


def mod_places(index):
    e = lax.broadcasted_iota(jnp.int32, (1, 128), 1)
    at = jnp.where(e < 108, 6 * D - 54 + index * 54 + e, 12 * D - 108 + index * 18 + e)
    at = jnp.where(e < 54, index * 54 + e, at)
    at = jnp.where(e < 126, at, -1)
    lines = lax.broadcasted_iota(jnp.int32, (128, 128), 0)
    return lines == lax.shift_right_arithmetic(at, 7), lines == jnp.bitwise_and(at, 127)


def whole_index():
    x, z = lax.axis_index("dp_0"), lax.axis_index("dp_1")
    return (x * 4 + z) * 8 + own_group()


def route(r):
    token = lax.broadcasted_iota(jnp.int32, (128, 512), 0)
    row = lax.axis_index("tx") * 16 + token // 8
    col = lax.axis_index("ty") * 8 + lax.rem(token, 8)
    hits = jnp.where(row * 32 + col == r.ids[...], 1.0, 0.0).astype(BF16)
    flags = dot_nt(jnp.ones((8, 512), BF16), hits)
    lines = lax.broadcasted_iota(jnp.int32, (128, 128), 0)
    lanes = lax.broadcasted_iota(jnp.int32, (128, 128), 1)
    before = dot_nn(flags.astype(BF16), jnp.where(lines <= lanes, 1.0, 0.0).astype(BF16))
    r.place[...] = jnp.where(flags > 0, before - 1.0, -1.0)[0:1].astype(jnp.int32)
    tile = r.ids[...] // 512 * 4 + lax.rem(r.ids[...], 32) // 8
    slot = lax.broadcasted_iota(jnp.int32, r.mask.shape, 1)
    capacity = r.mask.shape[1] // 8
    used = slot < 0
    for k in range(8):
        load_k = jnp.sum(jnp.where(tile == k, 1.0, 0.0), axis=1, keepdims=True).astype(jnp.int32)
        at = slot - k * capacity
        used = used | ((at >= 0) & (at < capacity) & (at < load_k))
    r.mask[...] = jnp.where(used, 0.0, -1e30)


def open_body(r):
    group = group_peers()
    sib, up, down, far = ring_peers()
    fetch = RowsIn(*slab_views(r.rows, 0, ATT_COLS), r.fetch)
    mods = RowsOut(r.m_mine.at[:, :, 0:64], r.m_mine.at[:, :, 64:128], r.mods)
    peers = [peer for peer, _ in group] + fetch.peers()
    greet(peers)
    r.pack[...] = jnp.zeros_like(r.pack)
    attn = [[r.attn_w[:, j, b, :] for j in range(3)] for b in range(2)]
    merge = [r.merge_w[:, b, :] for b in range(2)]
    expand = [r.expand_w[:, b, :] for b in range(2)]
    reduce = [r.reduce_w[:, b, :] for b in range(2)]
    spare = jnp.zeros((9, ATT_COLS - 4 * HW), BF16)
    for p in range(8):
        narrow, wide = slice(p * HW, (p + 1) * HW), slice(p * FW, (p + 1) * FW)
        parts = []
        for b in range(2):
            parts += [attn[b][j][:, narrow] for j in range(3)] + [merge[b][:, narrow], spare]
        for b in range(2):
            parts += [expand[b][:, wide], reduce[b][:, wide]]
        r.pack[p * 16 : p * 16 + 9, :] = jnp.concatenate(parts, axis=1)
    packed = jnp.zeros((8 * 64, PIECE), F32)
    for k in range(PIECES):
        packed = packed + dot_tn(r.unpicks[k], r.pack[:, k * PIECE : (k + 1) * PIECE])
    r.w_mine[...] = packed.astype(BF16).reshape(8, 64, PIECE)
    r.lines[...] = jnp.zeros_like(r.lines)
    r.lines[EMBED : EMBED + 16, 0:9] = r.embed_w[...].astype(F32)
    for b in range(2):
        at = BLOCKS + 8 * b
        for j in range(2):
            r.lines[at + j : at + j + 1, 0:9] = r.attn_b[b : b + 1, 9 * j : 9 * j + 9].astype(F32)
        for j in range(4):
            value = r.expand_b[b : b + 1, 9 * j : 9 * j + 9].astype(F32)
            r.lines[at + 2 + j : at + 3 + j, 0:9] = value
        r.lines[at + 6 : at + 7, 0:9] = r.merge_b[b : b + 1].astype(F32)
        r.lines[at + 7 : at + 8, 0:9] = r.reduce_b[b : b + 1].astype(F32)
    r.lines[EMBED_BIAS : EMBED_BIAS + 1, 0:9] = r.embed_b[...].astype(F32)
    r.block[...] = jnp.transpose(r.lines[...])[0:16]
    r.block[0:9, UNPATCH : UNPATCH + 32] = r.unpatch_w[...].astype(F32)
    me, x, z = own_group(), lax.axis_index("dp_0"), lax.axis_index("dp_1")
    r.small[x, z, me] = r.block[...].astype(BF16)
    met(peers)
    sems = (r.ss, r.rs)
    weights = [
        send(r.w_mine.at[at], r.w_got.at[me], sems, k, p) for k, (p, at) in enumerate(group)
    ]
    small = r.small.at[x, z, me]
    first = [send(small, small, sems, 7 + k, p) for k, (p, _) in enumerate(fetch.along_z)]
    r.w_got[me] = r.w_mine[me]

    condition = r.condition[...].astype(F32)
    cond16 = (condition / (1.0 + jnp.exp(-condition))).astype(BF16)
    on_line, on_lane = mod_places(whole_index())
    r.places[...] = jnp.zeros_like(r.places)
    r.places[0:1, 0:54] = r.mod_b[0:1].astype(F32)
    r.places[0:1, 54:108] = r.mod_b[1:2].astype(F32)
    r.places[0:1, 108:126] = r.final_b[...].astype(F32)
    left = jnp.where(on_line, r.places[0:1], 0.0).astype(BF16)
    right = jnp.where(on_lane, 1.0, 0.0).astype(BF16)
    r.placed_bias[...] = dot_nt(left, right)
    r.m_mine[:, :, 126:128] = jnp.zeros((4, 4, 2, 128), F32)
    for b in range(3):
        weight = r.mod_w[:, b, :] if b < 2 else r.final_w[...]
        part = dot_nn(cond16, weight)
        for k in range(part.shape[1] // 128):
            line = 54 * b + k
            value = part[:, k * 128 : (k + 1) * 128] + r.placed_bias[line : line + 1]
            r.m_mine[:, :, line, :] = value.reshape(4, 4, 128)
    mods.start()
    for copy in first:
        copy.wait_recv()
    small = r.small.at[x, :, me]
    second = [send(small, small, sems, 10 + k, p) for k, (p, _) in enumerate(fetch.along_x)]
    for copy in weights:
        copy.wait_recv()
    received = r.w_got[...].reshape(8 * 64, PIECE)
    for k in range(PIECES):
        r.rows[:, k * PIECE : (k + 1) * PIECE] = dot_nn(r.picks[k], received).astype(BF16)
    fetch.start()
    for copy in second:
        copy.wait_recv()
    small = r.small.at[:, :, me]
    third = [send(small, small, sems, 13 + k, p) for k, p in enumerate((up, down, far, sib))]
    mods.middle()
    fetch.middle()
    route(r)
    r.m_sum[0:64], r.m_sum[64:128] = mods.end()

    def chunk(ref, index):
        return ref.at[pl.ds(pl.multiple_of(index * 16, 16), 16)]

    m_first = [
        send(chunk(r.m_sum, at), r.m_got.at[me], sems, 20 + k, p) for k, (p, at) in enumerate(group)
    ]
    mine = pl.ds(pl.multiple_of(me * 16, 16), 16)
    r.m_got[me] = r.m_sum[mine, :]
    for copy in m_first:
        copy.wait_recv()
    total = r.m_got[0]
    for k in range(1, 8):
        total = total + r.m_got[k]
    r.m_all[mine, :] = total
    part = chunk(r.m_all, me)
    m_second = [send(part, part, sems, 27 + k, p) for k, (p, _) in enumerate(group)]
    c, y = lax.axis_index("tx"), lax.axis_index("ty")
    fourth = []
    for k, d in enumerate((3, 1, 2)):
        third[k].wait_recv()
        small = r.small.at[:, :, c * 4 + lax.rem(y + d, 4)]
        fourth.append(send(small, small, sems, 17 + k, sib))
    for copy in fourth + third[3:]:
        copy.wait_recv()

    @pl.loop(0, 16)
    def _(k):
        got = r.small[k // 4, lax.rem(k, 4)].reshape(128, 128)
        at = pl.ds(pl.multiple_of(k * PART, 8), PART)
        r.feat32[at, :] = dot_nn(r.pick_small[...], got)[:PART]

    r.feat[...] = r.feat32[...].astype(BF16)
    for k in range(9):
        cols = slice(k * 128, (k + 1) * 128)
        r.turned[:, cols] = jnp.transpose(r.feat32[cols, :])
    attn_at, ffn_at = own_targets()
    picks = bias_picks(r.table, ATT_BIAS, attn_at).astype(BF16)
    blocks = r.turned[BLOCKS : BLOCKS + 16].astype(BF16)
    narrow = dot_nn(blocks, picks)
    wide = dot_nn(blocks, bias_picks(r.table, FFN_BIAS, ffn_at).astype(BF16))
    for b, (one, two) in enumerate(((r.bias_one_0, r.bias_two_0), (r.bias_one_1, r.bias_two_1))):
        at, which = 8 * b, r.table[1:2, ATT_BIAS]
        one[...] = jnp.where(which == 0, narrow[at : at + 1], narrow[at + 1 : at + 2])
        value, which = wide[at + 2 : at + 3], r.table[1:2, FFN_BIAS]
        for j in range(1, 4):
            value = jnp.where(which == j, wide[at + 2 + j : at + 3 + j], value)
        two[...] = value
    for copy in m_second:
        copy.wait_recv()

    def mod_line(k):
        return jnp.concatenate([r.m_all[9 * k + i : 9 * k + i + 1] for i in range(9)], axis=1)

    vecs = (r.vec_one_0, r.vec_two_0, r.vec_one_1, r.vec_two_1)
    for k, ref in enumerate(vecs):
        for i in range(3):
            ref[i : i + 1] = mod_line(3 * k + i)
        at = BLOCKS + 8 * (k // 2) + 6 + k % 2
        ref[3:4] = r.turned[at : at + 1]
        ref[4:5] = r.turned[EMBED_BIAS : EMBED_BIAS + 1]
        ref[5:8] = jnp.zeros((3, D), F32)
    r.head_vec[0:1] = mod_line(12)
    r.head_vec[1:2] = mod_line(13)
    fetch.end(r.wqkv, r.wm)
    for copy in weights + first + second + third + fourth + m_first + m_second:
        copy.wait_send()
    mods.leave()


def picking():
    picks = np.zeros((PIECES, SLAB, 8 * 64), np.float32)
    for k in range(PIECES):
        for row in range(72):
            picks[k, row, row // 9 * 64 + 9 * k + row % 9] = 1.0
    return picks


def picking_small():
    picks = np.zeros((SLAB, 128), np.float32)
    for row in range(72):
        picks[row, row // 9 * 16 + row % 9] = 1.0
    return picks


def open_up(arguments):
    near = dict(
        **arguments,
        unpicks=jnp.asarray(unpicking(PIECES, 64), BF16),
        picks=jnp.asarray(picking(), BF16),
        pick_small=jnp.asarray(picking_small(), BF16),
        table=jnp.asarray(bias_table()),
    )
    vec = ((8, D), F32)
    outs = dict(
        rows=((SLAB, ALL_COLS), BF16),
        wqkv=((D, 3 * HW), BF16),
        wm=((D, HW), BF16),
        feat=((D, 128), BF16),
        vec_one_0=vec,
        vec_two_0=vec,
        vec_one_1=vec,
        vec_two_1=vec,
        head_vec=((2, D), F32),
        place=((1, 128), jnp.int32),
        mask=((1, 8 * 112), F32),
        bias_one_0=((1, 3 * HW), F32),
        bias_one_1=((1, 3 * HW), F32),
        bias_two_0=((1, FW), F32),
        bias_two_1=((1, FW), F32),
    )
    scratch = dict(
        pack=pltpu.VMEM((128, ALL_COLS), BF16),
        w_mine=pltpu.VMEM((8, 64, PIECE), BF16),
        w_got=pltpu.VMEM((8, 64, PIECE), BF16),
        lines=pltpu.VMEM((128, 128), F32),
        block=pltpu.VMEM((16, 128), F32),
        small=pltpu.VMEM((4, 4, 8, 16, 128), BF16),
        places=pltpu.VMEM((8, 128), F32),
        placed_bias=pltpu.VMEM((128, 128), F32),
        m_mine=pltpu.VMEM((4, 4, 128, 128), F32),
        m_sum=pltpu.VMEM((128, 128), F32),
        m_got=pltpu.VMEM((8, 16, 128), F32),
        m_all=pltpu.VMEM((128, 128), F32),
        feat32=pltpu.VMEM((D, 128), F32),
        turned=pltpu.VMEM((128, D), F32),
        ss=dma_sems(34)[0],
        rs=dma_sems(34)[1],
        fetch=rows_in_scratch(ATT_COLS),
        mods=sum_scratch([(64, 128), (64, 128)], F32),
    )
    return launch(open_body, 1, near, {}, outs, {}, scratch)[0]


EARLY = ATT_COLS + 2 * FFN_COLS
EARLY_PIECES = -(-EARLY // PIECE)
LATE_PIECES = -(-ATT_COLS // PIECE)
LATE_ROWS = 32


def packed_rows(picks_ref, parts, pieces):
    columns = jnp.concatenate(parts, axis=1)
    spare = pieces * PIECE - columns.shape[1]
    columns = jnp.concatenate([columns, jnp.zeros((SLAB, spare), BF16)], axis=1)
    total = jnp.zeros((8 * 64, PIECE), F32)
    for k in range(pieces):
        total = total + dot_tn(picks_ref[k], columns[:, k * PIECE : (k + 1) * PIECE])
    return total.astype(BF16).reshape(8, 64, PIECE)


def bias_lines(table_ref, cols, shift, biases, count):
    which = table_ref[1:2, cols]
    parts = []
    for bias in biases:
        rest = jnp.concatenate(
            [jnp.where(which == j, bias, 0.0) for j in range(count)]
            + [jnp.zeros((8 - count, bias.shape[1]), F32)],
            axis=0,
        )
        for _ in range(3):
            part = rest.astype(BF16).astype(F32)
            parts.append(part)
            rest = rest - part
    parts = jnp.concatenate(parts, axis=0).astype(BF16)
    found = dot_nt(parts, bias_picks(table_ref, cols, shift).astype(BF16))
    sums = [found[24 * k : 24 * k + 8] for k in range(2)]
    return [
        (sums[k] + found[24 * k + 8 : 24 * k + 16] + found[24 * k + 16 : 24 * k + 24])[:count]
        for k in range(2)
    ]


def finish_body(r):
    group = group_peers()
    sib, up, down, far = ring_peers()
    rows = RowsOut(r.left, r.right, r.rows_sums)
    small = RowsOut(r.small.at[:, :, 0:40], r.small.at[:, :, 40:80], r.small_sums)
    peers = [peer for peer, _ in group] + rows.peers()
    greet(peers)
    me, x, z = own_group(), lax.axis_index("dp_0"), lax.axis_index("dp_1")
    sems = (r.ss, r.rs)
    r.m_mine[...] = jnp.zeros_like(r.m_mine)
    vecs = (r.vecs_one_0, r.vecs_two_0, r.vecs_one_1, r.vecs_two_1, r.head_vecs)
    for k, ref in enumerate(vecs):
        for i in range(3 if k < 4 else 2):
            for j in range(9):
                line = 27 * k + 9 * i + j
                r.m_mine[line // 16, line % 16 : line % 16 + 1] = ref[
                    i : i + 1, j * 128 : (j + 1) * 128
                ]
    met(peers)
    rows.start()
    m_first = [send(r.m_mine.at[at], r.m_got.at[me], sems, k, p) for k, (p, at) in enumerate(group)]
    r.m_got[me] = r.m_mine[me]
    attn_at, ffn_at = own_targets()
    biases = (r.bias_one_0[...], r.bias_one_1[...])
    narrow = bias_lines(r.table, ATT_BIAS, attn_at, biases, 2)
    biases = (r.bias_two_0[...], r.bias_two_1[...])
    wide = bias_lines(r.table, FFN_BIAS, ffn_at, biases, 4)
    vecs = ((r.vecs_one_0, r.vecs_two_0), (r.vecs_one_1, r.vecs_two_1))
    for k in range(2):
        r.bias_rows[k, 0:2] = narrow[k]
        r.bias_rows[k, 2:6] = wide[k]
        r.bias_rows[k, 6:7] = vecs[k][0][3:4]
        r.bias_rows[k, 7:8] = vecs[k][1][3:4]
    r.turned[...] = jnp.zeros_like(r.turned)
    for k in range(9):
        cols = slice(k * 128, (k + 1) * 128)
        r.lines[...] = jnp.zeros_like(r.lines)
        r.lines[0:32] = r.unpatch_rows[:, cols]
        r.lines[32:48] = r.embed_rows[0:16, cols]
        r.lines[48:56] = r.bias_rows[0, :, cols]
        r.lines[56:64] = r.bias_rows[1, :, cols]
        r.lines[64:72] = r.embed_rows[16:24, cols]
        r.turned[cols, :] = jnp.transpose(r.lines[...])
    for k in range(16):
        r.small[k // 4, k % 4, 0:72] = r.turned[k * PART : (k + 1) * PART, :]
        r.small[k // 4, k % 4, 72:80] = r.unpatch_bias[...]
    small.start()
    r.early[...] = packed_rows(
        r.picks, [r.attn_rows[...], r.ffn_rows_0[...], r.ffn_rows_1[...]], EARLY_PIECES
    )
    sent = [
        send(r.early.at[at], r.early_out.at[me], sems, 7 + k, p) for k, (p, at) in enumerate(group)
    ]
    r.early_out[me] = r.early[me]
    for copy in m_first:
        copy.wait_recv()
    total = r.m_got[0]
    for k in range(1, 8):
        total = total + r.m_got[k]
    r.m_out[me, x, z] = total.astype(BF16)
    part = r.m_out.at[me, x, z]
    m_second = [send(part, part, sems, 14 + k, p) for k, (p, _) in enumerate(rows.along_z)]
    small.middle()
    for copy in m_second:
        copy.wait_recv()
    part = r.m_out.at[me, x]
    m_third = [send(part, part, sems, 17 + k, p) for k, (p, _) in enumerate(rows.along_x)]
    r.s_total[0:40], r.s_total[40:80] = small.end()
    for g in range(8):
        r.s_mine[g, 0:9] = r.s_total[9 * g : 9 * g + 9]
        r.s_mine[g, 9:16] = r.s_total[72:79]
    s_last = [
        send(r.s_mine.at[at], r.s_two.at[me], sems, 20 + k, p) for k, (p, at) in enumerate(group)
    ]
    r.s_two[me] = r.s_mine[me]
    for copy in m_third:
        copy.wait_recv()
    part = r.m_out.at[me]
    m_fourth = [send(part, part, sems, 27 + k, p) for k, p in enumerate((up, down, far, sib))]
    rows.middle()
    c, y = lax.axis_index("tx"), lax.axis_index("ty")
    m_fifth = []
    for k, d in enumerate((3, 1, 2)):
        m_fourth[k].wait_recv()
        part = r.m_out.at[c * 4 + lax.rem(y + d, 4)]
        m_fifth.append(send(part, part, sems, 31 + k, sib))
    for copy in s_last:
        copy.wait_recv()
    total = r.s_two[0]
    for k in range(1, 8):
        total = total + r.s_two[k]
    r.s_out[...] = total
    rows.end_rows(r.late_rows)
    r.late[...] = packed_rows(r.picks, [r.late_rows[...]], LATE_PIECES)[:, :LATE_ROWS]
    later = [
        send(r.late.at[at], r.late_out.at[me], sems, 34 + k, p) for k, (p, at) in enumerate(group)
    ]
    r.late_out[me] = r.late[me]
    for copy in sent + m_fourth[3:] + m_fifth + later:
        copy.wait_recv()
    small.leave()
    for copy in m_first + sent + m_second + m_third + s_last + m_fourth + m_fifth + later:
        copy.wait_send()


def finish(near):
    near = dict(near, picks=jnp.asarray(picking(), BF16))
    outs = dict(
        early_out=((8, 64, PIECE), BF16),
        late_out=((8, LATE_ROWS, PIECE), BF16),
        m_out=((8, 4, 4, 16, 128), BF16),
        s_out=((16, 128), F32),
    )
    scratch = dict(
        early=pltpu.VMEM((8, 64, PIECE), BF16),
        late=pltpu.VMEM((8, LATE_ROWS, PIECE), BF16),
        m_mine=pltpu.VMEM((8, 16, 128), F32),
        m_got=pltpu.VMEM((8, 16, 128), F32),
        lines=pltpu.VMEM((128, 128), F32),
        bias_rows=pltpu.VMEM((2, 8, D), F32),
        turned=pltpu.VMEM((D, 128), F32),
        small=pltpu.VMEM((4, 4, 80, 128), F32),
        s_total=pltpu.VMEM((80, 128), F32),
        s_mine=pltpu.VMEM((8, 16, 128), F32),
        s_two=pltpu.VMEM((8, 16, 128), F32),
        late_rows=pltpu.VMEM((SLAB, ATT_COLS), BF16),
        ss=dma_sems(41)[0],
        rs=dma_sems(41)[1],
        rows_sums=rows_out_scratch(ATT_COLS),
        small_sums=sum_scratch([(40, 128), (40, 128)], F32),
    )
    return launch(finish_body, 2, near, {}, outs, {}, scratch)[0]


def unpicking(pieces, height):
    picks = np.zeros((pieces, 128, 8 * height), np.float32)
    for k in range(pieces):
        for group in range(8):
            for row in range(9):
                picks[k, group * 16 + row, group * height + 9 * k + row] = 1.0
    return picks


def close_body(r):
    load(r, r.early_in, r.late_in, r.m_in)
    settle(r, r.early_in, r.late_in)
    received = r.early_in[...].reshape(8 * 64, PIECE)
    for k in range(EARLY_PIECES):
        r.early[:, k * PIECE : (k + 1) * PIECE] = dot_nn(r.early_picks[k], received)
    received = r.late_in[...].reshape(8 * LATE_ROWS, PIECE)
    for k in range(LATE_PIECES):
        r.late[:, k * PIECE : (k + 1) * PIECE] = dot_nn(r.late_picks[k], received)

    def whole(source, start, width):
        parts = [source[g * 16 : g * 16 + 16, start : start + width] for g in range(8)]
        return jnp.concatenate(parts, axis=1)[:9]

    for b, (source, start) in enumerate(((r.late, 0), (r.early, 0))):
        for j in range(3):
            r.attn[:, j, b, :] = whole(source, start + j * HW, HW)
        r.merge[:, b, :] = whole(source, start + 3 * HW, HW)
    for b, start in enumerate((ATT_COLS, ATT_COLS + FFN_COLS)):
        r.expand[:, b, :] = whole(r.early, start, FW)
        r.reduce[:, b, :] = whole(r.early, start + FW, FW)
    settle(r, r.m_in)
    for k in range(128):
        value = r.m_in[k // 16, :, :, k % 16, :]
        r.grads[:, k * 128 : (k + 1) * 128] = value.reshape(16, 128)
        r.sums[k : k + 1] = sum_rows(value.reshape(16, 128).astype(F32))
    condition = r.condition[...].astype(F32)
    gate = 1.0 / (1.0 + jnp.exp(-condition))
    cond16 = (condition / (1.0 + jnp.exp(-condition))).astype(BF16)
    terms = jnp.zeros((16, 9), F32)
    for b in range(3):
        grads = r.grads[:, 6 * b * D : min(6 * b + 6, 14) * D]
        weights = r.mod_w[:, b, :] if b < 2 else r.final_w[...]
        product = dot_tn(cond16, grads)
        if b < 2:
            r.mod_grad[:, b, :] = product
        else:
            r.final_grad[...] = product
        terms = terms + dot_nt(grads, weights)
    r.condition_grad[...] = terms * (gate * (1.0 + condition * (1.0 - gate)))
    on_line, on_lane = mod_places(whole_index())
    found = exact(r.sums[...], jnp.where(on_lane, 1.0, 0.0).astype(F32), (1, 0))
    found = sum_rows(jnp.where(on_line, found, 0.0))
    r.mod_b[0:1] = found[:, 0:54]
    r.mod_b[1:2] = found[:, 54:108]
    r.final_b[...] = found[:, 108:126]
    r.square[...] = jnp.zeros_like(r.square)
    r.square[0:16] = r.s_in[...]
    turned = jnp.transpose(r.square[...])
    r.unpatch_w[...] = r.s_in[0:9, 0:32]
    r.unpatch_b[...] = r.s_in[9:10, 0:32]
    r.embed_w[...] = turned[32:48, 0:9]
    r.embed_b[...] = turned[64:65, 0:9]
    for b in range(2):
        at = BLOCKS + 8 * b
        for j in range(2):
            r.attn_b[b : b + 1, 9 * j : 9 * j + 9] = turned[at + j : at + j + 1, 0:9]
        for j in range(4):
            r.expand_b[b : b + 1, 9 * j : 9 * j + 9] = turned[at + 2 + j : at + 3 + j, 0:9]
        r.merge_b[b : b + 1] = turned[at + 6 : at + 7, 0:9]
        r.reduce_b[b : b + 1] = turned[at + 7 : at + 8, 0:9]


def close(near, far):
    near = dict(
        **near,
        early_picks=jnp.asarray(unpicking(EARLY_PIECES, 64), BF16),
        late_picks=jnp.asarray(unpicking(LATE_PIECES, LATE_ROWS), BF16),
    )
    outs = dict(
        attn=((9, 3, 2, D), F32),
        merge=((9, 2, D), F32),
        expand=((9, 2, FF), F32),
        reduce=((9, 2, FF), F32),
        mod_grad=((9, 2, 6 * D), F32),
        final_grad=((9, 2 * D), F32),
        condition_grad=((16, 9), F32),
        mod_b=((2, 54), F32),
        final_b=((1, 18), F32),
        unpatch_w=((9, 32), F32),
        unpatch_b=((1, 32), F32),
        embed_w=((16, 9), F32),
        embed_b=((1, 9), F32),
        attn_b=((2, 18), F32),
        expand_b=((2, 36), F32),
        merge_b=((2, 9), F32),
        reduce_b=((2, 9), F32),
    )
    scratch = dict(
        early=pltpu.VMEM((128, EARLY_PIECES * PIECE), F32),
        late=pltpu.VMEM((128, LATE_PIECES * PIECE), F32),
        grads=pltpu.VMEM((16, WHOLE), BF16),
        sums=pltpu.VMEM((128, 128), F32),
        square=pltpu.VMEM((128, 128), F32),
    )
    return launch(close_body, None, near, far, outs, {}, scratch, vmem=40 << 20)[0]


def forward_body(r, tokens, start, last):
    ring = Ring(tokens, r.ring_local, r.ring_one)
    fetch = RowsIn(*slab_views(r.rows, start, FFN_COLS), r.fetch_one)
    peers = ring.peers() + fetch.peers()
    greet(peers)
    if last:
        r.x[...] = exact(choice(r.place, tokens), r.first[...], (1, 0))
    else:
        r.token_cols[...] = jnp.zeros_like(r.token_cols)
        to_tokens(r.pixels, r.square, r.token_cols, EMBED)
        r.patches[...] = r.token_cols[...].astype(BF16)
        r.x[...] = dot_nt(r.patches[...], r.feat[...]) + r.vec_one[4:5] + r.placed[...]
    r.x16[...] = modulated(r.x[...], r.vec_one)
    met(peers)
    save(r, r.x)
    ring.start_sums()

    def visit(own, d):
        rows = ring.rows((ring.own if own else ring.other)[d])
        joined = (dot_nn(r.in_all[rows, :], r.wqkv[...]) + r.bias_one[...]).astype(BF16)
        for h in range(2):
            r.q[h, rows, :] = joined[:, head_cols(h)]
            r.k[h, rows, :] = joined[:, head_cols(h, HW)]
            r.v[h, rows, :] = joined[:, head_cols(h, 2 * HW)]

    def attend(own, d):
        rows = ring.rows((ring.own if own else ring.other)[d])
        parts = []
        for h in range(2):
            scores = dot_nt(r.q[h, rows, :], r.k[h]) * SCALE
            if last:
                scores = scores + r.mask[...]
            highest = jnp.max(scores, axis=-1, keepdims=True)
            shifted = jnp.exp(scores - highest)
            summed = jnp.sum(shifted, axis=-1, keepdims=True)
            probs = (shifted * (1.0 / summed)).astype(BF16)
            r.lse[rows, h : h + 1] = highest + jnp.log(summed)
            parts.append(dot_nn(probs, r.v[h]).astype(BF16))
        attended = jnp.concatenate(parts, axis=1)
        r.att[rows, :] = attended
        ring.put(own, d, dot_nt(attended, r.wm[...]))

    ring.gather(r.x16, r.in_all, fetch.start, visit, fetch.middle)
    attend(False, 2)
    attend(True, 2)
    ring.far()
    save(r, r.in_all, r.q, r.k, r.v)
    for d in (1, 3):
        attend(False, d)
        attend(True, d)
    ring.near()
    ring.relay()
    attend(False, 0)
    attend(True, 0)
    save(r, r.lse, r.att)
    fetch.end(r.we, r.wr)
    save(r, r.we, r.wr)
    branch = ring.total() + r.vec_one[3:4]
    r.branch[...] = branch
    middle = r.x[...] + r.vec_one[2:3] * branch
    r.middle[...] = middle
    save(r, r.branch, r.middle)
    ring.leave()

    ring = Ring(tokens, r.ring_local, r.ring_two)
    fetch = None
    if not last:
        fetch = RowsIn(*slab_views(r.rows, ATT_COLS, ATT_COLS), r.fetch_two)
    r.x16[...] = modulated(middle, r.vec_two)
    ring.start_sums()

    def prepare():
        if fetch:
            fetch.start()

    def expand(own, d):
        rows = ring.rows((ring.own if own else ring.other)[d])
        pre = dot_nn(r.second[rows, :], r.we[...]) + r.bias_two[...]
        value, slope = gelu_both(pre)
        hidden = value.astype(BF16)
        r.hid[rows, :] = hidden
        r.slope[rows, :] = slope.astype(BF16)
        ring.put(own, d, dot_nt(hidden, r.wr[...]))
        if not own and d == 1:
            ring.near()

    ring.gather(r.x16, r.second, prepare, expand, fetch.middle if fetch else None)
    ring.far()
    save(r, r.second, r.hid, r.slope)
    ring.relay()
    if fetch:
        fetch.end(r.next_wqkv, r.next_wm)
    mlp = ring.total() + r.vec_two[3:4]
    r.mlp[...] = mlp
    save(r, r.mlp)
    r.out[...] = r.middle[...] + r.vec_two[2:3] * mlp
    ring.leave()
    settle(r)


def kept_shapes(tokens):
    heads = ((2, 8 * tokens, HEAD), BF16)
    wide, tile = ((8 * tokens, D), BF16), ((tokens, D), F32)
    hidden = ((8 * tokens, FW), BF16)
    return dict(
        x=tile,
        in_all=wide,
        q=heads,
        k=heads,
        v=heads,
        lse=((8 * tokens, 2), F32),
        att=((8 * tokens, HW), BF16),
        branch=tile,
        middle=tile,
        second=wide,
        hid=hidden,
        slope=hidden,
        mlp=tile,
        we=((D, FW), BF16),
        wr=((D, FW), BF16),
    )


def block_forward(near, tokens, start, last, cid):
    outs = dict(out=((tokens, D), F32))
    scratch = dict(
        x16=pltpu.VMEM((tokens, D), BF16),
        ring_local=ring_local(tokens),
        ring_one=ring_remote(tokens),
        ring_two=ring_remote(tokens),
        fetch_one=rows_in_scratch(FFN_COLS),
    )
    if not last:
        outs.update(next_wqkv=((D, 3 * HW), BF16))
        outs.update(next_wm=((D, HW), BF16))
        outs.update(patches=((128, 128), BF16))
        scratch.update(square=pltpu.VMEM((128, 128), F32), token_cols=pltpu.VMEM((128, 128), F32))
        scratch.update(fetch_two=rows_in_scratch(ATT_COLS))
    body = functools.partial(forward_body, tokens=tokens, start=start, last=last)
    return launch(body, cid, near, {}, outs, kept_shapes(tokens), scratch)


def head(r):
    picks = choice(r.place, r.two.shape[0])
    ended = spread_back(picks, r.two[...], r.first[...])
    normed, inv_std = layer_stats(ended)
    final16 = (normed * (1.0 + r.head_vec[1:2]) + r.head_vec[0:1]).astype(BF16)
    unpatch = r.feat[:, UNPATCH : UNPATCH + 32]
    r.token_cols[...] = jnp.zeros_like(r.token_cols)
    r.token_cols[:, 0:32] = dot_nn(final16, unpatch) + r.unpatch_b[...].astype(F32)
    to_pixels(r.token_cols, r.square, r.predicted, 0)
    to_tokens(r.cotangent_pixels, r.square, r.token_cols, 0)
    r.cotangent[...] = r.token_cols[:, 0:32].astype(BF16)
    r.unpatch_rows[...] = dot_tn(r.cotangent[...], final16)
    r.unpatch_bias[...] = jnp.zeros_like(r.unpatch_bias)
    r.unpatch_bias[0:1, 0:32] = sum_rows(r.cotangent[...].astype(F32))
    grad = dot_nt(r.cotangent[...], unpatch)
    r.head_vecs[0:1] = sum_rows(grad)
    r.head_vecs[1:2] = sum_rows(grad * normed)
    grad = layer_back(grad * (1.0 + r.head_vec[1:2]), normed, inv_std)
    r.grad_ended[...] = grad
    r.g[...] = exact(picks, grad, (1, 0))


def backward_body(r, tokens, last):
    ring = Ring(tokens, r.ring_local, r.ring_one)
    sums = None if last else RowsOut(r.pending_left, r.pending_right, r.sums_one)
    peers = ring.peers() + line_only(line_peers())
    greet(peers)
    if last:
        load(r, r.first, r.two, r.slope, r.wr, r.we)
    else:
        load(r, r.grad_two, r.grad_ended, r.slope, r.wr, r.we, r.pending_left, r.pending_right)
    load(r, r.hid, r.second, r.mlp, r.middle)
    load(r, r.q, r.k, r.v, r.lse, r.wm, r.wqkv, r.att, r.x, r.branch)
    if last:
        settle(r, r.first, r.two)
        head(r)
    else:
        settle(r, r.grad_two, r.grad_ended)
        picks = choice(r.place, r.grad_two.shape[0])
        r.g[...] = spread_back(picks, r.grad_two[...], r.grad_ended[...])
    r.g16[...] = (r.g[...] * r.vec_two[2:3]).astype(BF16)
    met(peers)
    ring.start_sums()
    r.bias_two[...] = jnp.zeros_like(r.bias_two)

    def prepare():
        if sums:
            settle(r, r.pending_left, r.pending_right)
            sums.start()
        settle(r, r.slope, r.wr, r.we)

    def visit(own, d):
        rows = ring.rows((ring.own if own else ring.other)[d])
        pre_grad = (
            dot_nn(r.g_one[rows, :], r.wr[...]) * r.slope[rows, :].astype(F32)
        ).astype(BF16)
        r.pre_all[rows, :] = pre_grad
        r.bias_two[...] += sum_rows(pre_grad.astype(F32))
        ring.put(own, d, dot_nt(pre_grad, r.we[...]))
        if not own and d == 1:
            ring.near()

    ring.gather(r.g16, r.g_one, prepare, visit)
    ring.far()
    settle(r, r.hid, r.second, r.mlp, r.middle)
    weight_grads(r.g_one, r.hid, r.whole_two, FW)
    ring.relay()
    if sums:
        sums.middle()
    r.vecs_two[2:3] = sum_rows(r.g[...] * r.mlp[...])
    r.vecs_two[3:4] = sum_rows(r.g16[...].astype(F32))
    r.vecs_two[4:8] = jnp.zeros((4, D), F32)
    weight_grads(r.second, r.pre_all, r.whole_one, FW)
    load_into(r, r.in_all, r.second)
    write_slabs((r.whole_one, FW), (r.whole_two, FW), r.ffn_left, r.ffn_right)
    if sums:
        sums.end_rows(r.attn_rows)
    second_grad = ring.total()
    normed, inv_std = layer_stats(r.middle[...])
    r.vecs_two[0:1] = sum_rows(second_grad)
    r.vecs_two[1:2] = sum_rows(second_grad * normed)
    r.g[...] += layer_back(second_grad * (1.0 + r.vec_two[1:2]), normed, inv_std)
    ring.leave()

    ring = Ring(tokens, r.ring_local, r.ring_two)
    sums = RowsOut(r.ffn_left, r.ffn_right, r.sums_two)
    r.g16[...] = (r.g[...] * r.vec_one[2:3]).astype(BF16)
    ring.start_sums()

    def prepare_attention():
        sums.start()
        r.dk[...] = jnp.zeros_like(r.dk)
        r.dv[...] = jnp.zeros_like(r.dv)
        settle(r, r.q, r.k, r.v, r.lse, r.wm)

    def attend(own, d):
        rows = ring.rows((ring.own if own else ring.other)[d])
        grad = dot_nn(r.g_two[rows, :], r.wm[...]).astype(BF16)
        queries = []
        for h in range(2):
            part = grad[:, head_cols(h)]
            query = r.q[h, rows, :]
            scores = dot_nt(query, r.k[h]) * SCALE
            if last:
                scores = scores + r.mask[...]
            probs = jnp.exp(scores - r.lse[rows, h : h + 1])
            grad_probs = dot_nt(part, r.v[h])
            weighted = jnp.sum(probs * grad_probs, axis=-1, keepdims=True)
            score_grad = (probs * (grad_probs - weighted)).astype(BF16)
            queries.append((dot_nn(score_grad, r.k[h]) * SCALE).astype(BF16))
            r.dk[h] += dot_tn(score_grad, query)
            r.dv[h] += dot_tn(probs.astype(BF16), part)
        r.joined[rows, 0:HW] = jnp.concatenate(queries, axis=1)

    def back(own, d):
        rows = ring.rows((ring.own if own else ring.other)[d])
        ring.put(own, d, dot_nt(r.joined[rows, :], r.wqkv[...]))

    ring.gather(r.g16, r.g_two, prepare_attention, attend)
    settle(r, r.wqkv)
    later = [(r.dk[h] * SCALE).astype(BF16) for h in range(2)]
    later += [r.dv[h].astype(BF16) for h in range(2)]
    r.joined[:, HW : 3 * HW] = jnp.concatenate(later, axis=1)
    back(False, 2)
    back(True, 2)
    ring.far()
    for d in (1, 3):
        back(False, d)
        back(True, d)
    ring.near()
    back(False, 0)
    back(True, 0)
    settle(r)
    weight_grads(r.g_two, r.att, r.whole_two, HW)
    ring.relay()
    sums.middle()
    r.bias_one[...] = sum_rows(r.joined[...].astype(F32))
    r.vecs_one[2:3] = sum_rows(r.g[...] * r.branch[...])
    r.vecs_one[3:4] = sum_rows(r.g16[...].astype(F32))
    r.vecs_one[4:8] = jnp.zeros((4, D), F32)
    weight_grads(r.second, r.joined, r.whole_one, 3 * HW)
    write_slabs((r.whole_one, 3 * HW), (r.whole_two, HW), r.attn_left, r.attn_right)
    sums.end_rows(r.ffn_rows)
    input_grad = ring.total()
    normed, inv_std = layer_stats(r.x[...])
    r.vecs_one[0:1] = sum_rows(input_grad)
    r.vecs_one[1:2] = sum_rows(input_grad * normed)
    grad = r.g[...] + layer_back(input_grad * (1.0 + r.vec_one[1:2]), normed, inv_std)
    if last:
        r.out[...] = grad
    else:
        grad16 = grad.astype(BF16)
        r.embed_rows[0:16] = dot_tn(r.patches[...], grad16)[EMBED : EMBED + 16]
        r.embed_rows[16:17] = sum_rows(grad16.astype(F32))
        r.embed_rows[17:24] = jnp.zeros((7, D), F32)
        r.token_cols[...] = dot_nn(grad16, r.feat[...])
        to_pixels(r.token_cols, r.square, r.latent, EMBED)
    ring.leave()


def weight_grads(left_ref, right_ref, whole_ref, width):
    @pl.loop(0, D // 128)
    def _(k):
        at = pl.ds(pl.multiple_of(k * 128, 128), 128)
        whole_ref[at, :width] = dot_tn(left_ref[:, at], right_ref[...])


def write_slabs(one, two, left_ref, right_ref):
    cut = left_ref.shape[3]
    cols = cut + right_ref.shape[3]

    @pl.loop(0, 16)
    def _(k):
        at = pl.ds(pl.multiple_of(k * PART, 8), PART)
        parts = [ref[at, :width] for ref, width in (one, two)]
        spare = cols - one[1] - two[1]
        if spare:
            parts.append(jnp.zeros((PART, spare), F32))
        rows = jnp.concatenate(parts, axis=1)
        rows = jnp.concatenate([rows, jnp.zeros((SLAB - PART, cols), F32)], axis=0).astype(BF16)
        x, z = k // 4, lax.rem(k, 4)
        left_ref[x, z] = rows[:, :cut]
        right_ref[x, z] = rows[:, cut:]


def line_only(lines):
    return [peer for peer, _ in lines[0] + lines[1]]


def slab_specs(cols):
    widths = (CUT[cols], cols - CUT[cols])
    return [((4, 4, SLAB, width), BF16) for width in widths]


def block_backward(near, far, tokens, last, cid):
    vecs = ((8, D), F32)
    attn_left, attn_right = slab_specs(ATT_COLS)
    outs = dict(
        vecs_one=vecs,
        vecs_two=vecs,
        bias_one=((1, 3 * HW), F32),
        bias_two=((1, FW), F32),
        attn_left=attn_left,
        attn_right=attn_right,
        ffn_rows=((SLAB, FFN_COLS), BF16),
    )
    wide, tile = (8 * tokens, D), (tokens, D)
    scratch = dict(
        g16=pltpu.VMEM(tile, BF16),
        square=pltpu.VMEM((128, 128), F32),
        token_cols=pltpu.VMEM((128, 128), F32),
        g_one=pltpu.VMEM(wide, BF16),
        g_two=pltpu.VMEM(wide, BF16),
        pre_all=pltpu.VMEM((8 * tokens, FW), BF16),
        joined=pltpu.VMEM((8 * tokens, 3 * HW), BF16),
        dk=pltpu.VMEM((2, 8 * tokens, HEAD), F32),
        dv=pltpu.VMEM((2, 8 * tokens, HEAD), F32),
        whole_one=pltpu.VMEM((D, FW), F32),
        whole_two=pltpu.VMEM((D, FW), F32),
        ffn_left=pltpu.VMEM(*slab_specs(FFN_COLS)[0]),
        ffn_right=pltpu.VMEM(*slab_specs(FFN_COLS)[1]),
        ring_local=ring_local(tokens),
        ring_one=ring_remote(tokens),
        ring_two=ring_remote(tokens),
        sums_two=rows_out_scratch(FFN_COLS),
    )
    if last:
        outs.update(out=(tile, F32))
        outs.update(predicted=((16, 8, 32), BF16))
        outs.update(unpatch_rows=((32, D), F32))
        outs.update(unpatch_bias=((8, 128), F32))
        outs.update(head_vecs=((2, D), F32))
        scratch.update(cotangent=pltpu.VMEM((128, 32), BF16))
        outs.update(grad_ended=((128, D), F32))
        scratch.update(g=pltpu.VMEM(tile, F32))
    else:
        outs.update(attn_rows=((SLAB, ATT_COLS), BF16))
        outs.update(embed_rows=((24, D), F32))
        outs.update(latent=((16, 4, 32), F32))
        scratch.update(g=pltpu.VMEM(tile, F32))
        scratch.update(sums_one=rows_out_scratch(ATT_COLS))
    body = functools.partial(backward_body, tokens=tokens, last=last)
    return launch(body, cid, near, far, outs, {}, scratch, vmem=62 << 20)[0]


def shards(
    latent,
    condition,
    routed_ids,
    embed_weight,
    embed_bias,
    modulation_weight,
    modulation_bias,
    attention_weight,
    attention_bias,
    merge_weight,
    merge_bias,
    expand_weight,
    expand_bias,
    reduce_weight,
    reduce_bias,
    final_modulation,
    final_offsets,
    unpatch_weight,
    unpatch_bias,
    pred_cotangent,
):
    tile_rows = latent.shape[1] // 2
    tile_cols = latent.shape[2] // 2
    tile_tokens = tile_rows * tile_cols
    capacity = 7 * tile_tokens // 8
    row_index = lax.axis_index("tx") * tile_rows + jnp.arange(tile_rows, dtype=jnp.int32)
    col_index = lax.axis_index("ty") * tile_cols + jnp.arange(tile_cols, dtype=jnp.int32)
    placed = sincos_table(row_index.astype(F32), col_index.astype(F32), D)
    mod_w = modulation_weight.swapaxes(0, 1)
    got = open_up(
        dict(
            condition=condition,
            ids=routed_ids,
            mod_w=mod_w,
            final_w=final_modulation,
            attn_w=attention_weight.transpose(1, 2, 0, 3),
            merge_w=merge_weight.swapaxes(0, 1),
            expand_w=expand_weight.swapaxes(0, 1),
            reduce_w=reduce_weight.swapaxes(0, 1),
            embed_w=embed_weight,
            embed_b=embed_bias[None],
            unpatch_w=unpatch_weight,
            attn_b=attention_bias,
            merge_b=merge_bias,
            expand_b=expand_bias,
            reduce_b=reduce_bias,
            mod_b=modulation_bias,
            final_b=final_offsets[None],
        )
    )
    vecs_one = dict(vec_one=got.vec_one_0, vec_two=got.vec_two_0)
    vecs_two = dict(vec_one=got.vec_one_1, vec_two=got.vec_two_1, mask=got.mask)
    outs_one, kept_one = block_forward(
        dict(
            vecs_one,
            bias_one=got.bias_one_0,
            bias_two=got.bias_two_0,
            rows=got.rows,
            wqkv=got.wqkv,
            wm=got.wm,
            pixels=latent.transpose(0, 2, 3, 1)[0],
            feat=got.feat,
            placed=placed,
        ),
        tile_tokens,
        2 * ATT_COLS,
        False,
        10,
    )
    outs_two, kept_two = block_forward(
        dict(
            vecs_two,
            bias_one=got.bias_one_1,
            bias_two=got.bias_two_1,
            rows=got.rows,
            wqkv=outs_one.next_wqkv,
            wm=outs_one.next_wm,
            first=outs_one.out,
            place=got.place,
        ),
        capacity,
        2 * ATT_COLS + FFN_COLS,
        True,
        11,
    )
    back_two = block_backward(
        dict(
            vecs_two,
            place=got.place,
            head_vec=got.head_vec,
            feat=got.feat,
            unpatch_b=unpatch_bias[None],
            cotangent_pixels=pred_cotangent.transpose(0, 2, 3, 1)[0],
        ),
        dict(
            kept_two,
            first=outs_one.out,
            two=outs_two.out,
            wqkv=outs_one.next_wqkv,
            wm=outs_one.next_wm,
        ),
        capacity,
        True,
        12,
    )
    back_one = block_backward(
        dict(vecs_one, place=got.place, patches=outs_one.patches, feat=got.feat),
        dict(
            kept_one,
            wqkv=got.wqkv,
            wm=got.wm,
            pending_left=back_two.attn_left,
            pending_right=back_two.attn_right,
            grad_two=back_two.out,
            grad_ended=back_two.grad_ended,
        ),
        tile_tokens,
        False,
        13,
    )
    ended = finish(
        dict(
            left=back_one.attn_left,
            right=back_one.attn_right,
            attn_rows=back_one.attn_rows,
            ffn_rows_0=back_one.ffn_rows,
            ffn_rows_1=back_two.ffn_rows,
            vecs_one_0=back_one.vecs_one,
            vecs_two_0=back_one.vecs_two,
            vecs_one_1=back_two.vecs_one,
            vecs_two_1=back_two.vecs_two,
            head_vecs=back_two.head_vecs,
            unpatch_rows=back_two.unpatch_rows,
            embed_rows=back_one.embed_rows,
            bias_one_0=back_one.bias_one,
            bias_two_0=back_one.bias_two,
            bias_one_1=back_two.bias_one,
            bias_two_1=back_two.bias_two,
            table=jnp.asarray(bias_table()),
            unpatch_bias=back_two.unpatch_bias,
        )
    )
    last = close(
        dict(s_in=ended.s_out, condition=condition, mod_w=mod_w, final_w=final_modulation),
        dict(early_in=ended.early_out, late_in=ended.late_out, m_in=ended.m_out),
    )
    return (
        back_two.predicted.transpose(2, 0, 1)[None],
        back_one.latent.transpose(2, 0, 1)[None],
        last.condition_grad,
        last.embed_w,
        last.embed_b[0],
        last.mod_grad.swapaxes(0, 1),
        last.mod_b,
        last.attn.transpose(2, 0, 1, 3),
        last.attn_b,
        last.merge.swapaxes(0, 1),
        last.merge_b,
        last.expand.swapaxes(0, 1),
        last.expand_b,
        last.reduce.swapaxes(0, 1),
        last.reduce_b,
        last.final_grad,
        last.final_b[0],
        last.unpatch_w,
        last.unpatch_b[0],
    )


def solution(mesh):
    torus = Mesh(
        mesh.devices.reshape(4, 4, mesh.shape["tx"], mesh.shape["ty"]), ("dp_0", "dp_1", "tx", "ty")
    )
    return jax.shard_map(
        shards,
        mesh=torus,
        in_specs=(
            P(DP, "tx", "ty", None),
            P(None, DP_TX_TY),
            P(DP, None),
            P(None, DP_TX_TY),
            P(DP_TX_TY),
            P(None, DP_TX_TY, None),
            P(None, DP_TX_TY),
            P(None, DP_TX_TY, None, None),
            P(None, DP_TX_TY),
            P(None, DP_TX_TY, None),
            P(None, DP_TX_TY),
            P(None, DP_TX_TY, None),
            P(None, DP_TX_TY),
            P(None, DP_TX_TY, None),
            P(None, DP_TX_TY),
            P(DP_TX_TY, None),
            P(DP_TX_TY),
            P(DP_TX_TY, None),
            P(),
            P(DP, "tx", "ty", None),
        ),
        out_specs=(
            P(DP, "tx", "ty", None),
            P(DP, "tx", "ty", None),
            P(None, DP_TX_TY),
            P(None, DP_TX_TY),
            P(DP_TX_TY),
            P(None, DP_TX_TY, None),
            P(None, DP_TX_TY),
            P(None, DP_TX_TY, None, None),
            P(None, DP_TX_TY),
            P(None, DP_TX_TY, None),
            P(None, DP_TX_TY),
            P(None, DP_TX_TY, None),
            P(None, DP_TX_TY),
            P(None, DP_TX_TY, None),
            P(None, DP_TX_TY),
            P(DP_TX_TY, None),
            P(DP_TX_TY),
            P(DP_TX_TY, None),
            P(),
        ),
        check_vma=False,
    )
```

time: 420 us -> 366 us (0.87)
  local copies, waits for them, and re-layouts: 50.7 us -> 5.04 us
  other arithmetic: 8.74 us -> 1.45 us
    pallas_call x4 -> x7, Pallas kernels: 274 us -> 354 us  [launch(): pl.pallas_call(kernel, out_shape=tuple(shapes), in_specs=[VMEM] * len(nea...]
    pallas_call x4 -> x0, Pallas kernels: 78.8 us -> none  [the longest x2 74.9 us: collective(): pl.pallas_call(kernel, out_shape=outs, in_specs=[VMEM] * near_in + [FAR]...]
    reshape x50 -> x0, local copies, waits for them, and re-layouts: 13.4 us -> none  [the longest x5 1.64 us: by_owner(): parts = array.reshape(*before, 128, array.shape[dim] // 128, *after)]
    unnamed x109 -> x24, local copies, waits for them, and re-layouts: 15.5 us -> 4.99 us
where the time goes in v6:
time: 366 us; the launch traced here: 362 us
  Pallas kernels  354 us (97%)
  local copies, waits for them, and re-layouts  5.04 us (1%)
    pallas_call x7, Pallas kernels, launch(): pl.pallas_call(kernel, out_shape=tuple(shapes), in_specs=[VMEM] * len(nea...  354 us

profile of v6, /device:TPU:1, one launch (start us, length us, event | category | flops | bytes accessed | tf_op | source)
XLA Modules:
  0.0 361.6 jit_solution(11131462428431473352)
XLA Ops:
  0.7 0.1 multiply_sine_fusion.1
  0.8 0.1 pad_maximum_fusion.1
  0.9 0.2 multiply_sine_fusion
  1.1 0.1 pad_maximum_fusion
  1.2 1.0 maximum_bitcast_fusion.refs_9_
  2.2 39.7 %shard_map.411 = (bf16[80,3584]{1,0:T(8,128)(2,1)}, bf16[1152,432]{1,0:T(8,128)(2,1)}, bf16[1152,144]{1,0:T(8,128)(2,1)}, bf16[1152,128]{1,0:T(8,128)(2,1)}, f32...) custom-call(bf16[16,9]{1,0:T(8,128)(2,1)} %refs_1_.3, ...), custom_call_target="tpu_custom_call" | custom-call | tf_op jit(solution)/shard_map/pallas_call | solution.py:509
  41.9 66.2 %shard_map.412 = (f32[128,1152]{1,0:T(8,128)}, bf16[1152,432]{1,0:T(8,128)(2,1)}, bf16[1152,144]{1,0:T(8,128)(2,1)}, bf16[128,128]{1,0:T(8,128)(2,1)}, f32[128,1...) custom-call(f32[8,1152]{1,0:T(8,128)} %get-tuple-element.122.refs_0_, ...), custom_call_target="tpu_custom_call" | custom-call | tf_op jit(solution)/shard_map/pallas_call | solution.py:509
  108.1 62.5 %shard_map.413 = (f32[112,1152]{1,0:T(8,128)}, f32[112,1152]{1,0:T(8,128)}, bf16[896,1152]{1,0:T(8,128)(2,1)}, bf16[2,896,72]{2,1,0:T(8,128)(2,1)}, bf16[2,896,7...) custom-call(f32[8,1152]{1,0:T(8,128)} %get-tuple-element.113.refs_0_, ...), custom_call_target="tpu_custom_call" | custom-call | tf_op jit(solution)/shard_map/pallas_call | solution.py:509
  170.5 71.7 %shard_map.414 = (f32[8,1152]{1,0:T(8,128)}, f32[8,1152]{1,0:T(8,128)}, f32[1,432]{1,0:T(1,128)}, f32[1,576]{1,0:T(1,128)}, bf16[4,4,80,384]{3,2,1,0:T(8,128)(2,...) custom-call(f32[8,1152]{1,0:T(8,128)} %get-tuple-element.113.refs_0_, ...), custom_call_target="tpu_custom_call" | custom-call | tf_op jit(solution)/shard_map/pallas_call | solution.py:509
  242.2 72.7 %shard_map.415 = (f32[8,1152]{1,0:T(8,128)}, f32[8,1152]{1,0:T(8,128)}, f32[1,432]{1,0:T(1,128)}, f32[1,576]{1,0:T(1,128)}, bf16[4,4,80,384]{3,2,1,0:T(8,128)(2,...) custom-call(f32[8,1152]{1,0:T(8,128)} %get-tuple-element.122.refs_0_, ...), custom_call_target="tpu_custom_call" | custom-call | tf_op jit(solution)/shard_map/pallas_call | solution.py:509
  314.9 0.0 copy-start
  314.9 0.0 copy-start.1
  315.0 0.0 copy-start.4
  315.0 0.0 copy-start.6
  315.0 0.0 copy-start.7
  315.0 0.0 copy-start.9
  315.0 0.0 copy-start.10
  315.0 36.7 %shard_map.416 = (bf16[8,64,512]{2,1,0:T(8,128)(2,1)}, bf16[8,32,512]{2,1,0:T(8,128)(2,1)}, bf16[8,4,4,16,128]{4,3,2,1,0:T(8,128)(2,1)}, f32[16,128]{1,0:T(8,128)}) custom-call(bf16[4,4,80,384]{3,2,1,0:T(8,128)(2,1)} %get-tuple-element.169.refs_0_, bf16[4,4,80,256]{3,2,1,0:T(8,128)(2,1)} %get-tuple-element.170.refs_1_, ...), custom_call_target="tpu_custom_call" | custom-call | tf_op jit(solution)/shard_map/pallas_call | solution.py:509
  351.7 0.0 copy-done
  351.7 0.0 copy-done.1
  351.7 0.0 copy-done.4
  351.7 0.0 copy-done.6
  351.8 0.0 copy-done.7
  351.8 0.0 copy-start.2
  351.8 1.0 copy-done.2
  352.8 1.0 copy-done.3
  353.8 0.9 copy-done.5
  354.8 0.7 copy-done.8
  355.5 4.5 %shard_map.417 = (f32[9,3,2,1152]{3,2,1,0:T(2,128)}, f32[9,2,1152]{2,1,0:T(2,128)}, f32[9,2,4608]{2,1,0:T(2,128)}, f32[9,2,4608]{2,1,0:T(2,128)}, f32[9,2,6912]{...) custom-call(f32[16,128]{1,0:T(8,128)S(1)} %copy-done.8, ...), custom_call_target="tpu_custom_call" | custom-call | tf_op jit(solution)/shard_map/pallas_call | solution.py:509
  360.0 0.0 copy-done.9
  360.0 0.6 copy.49
  360.6 0.6 copy.50
  (9 shorter events, 0.1 us)
Async XLA Ops:
  314.9 36.8 %copy-start = (bf16[2,9,6912]{2,0,1:T(2,128)(2,1)S(1)}, bf16[2,9,6912]{2,0,1:T(2,128)(2,1)}, u32[]{:S(2)}) copy-start(bf16[2,9,6912]{2,0,1:T(2,128)(2,1)} %param.33) | copy-start | bytes 746500
  314.9 36.8 %copy-start.1 = (bf16[6,128,512]{2,1,0:T(8,128)(2,1)S(1)}, bf16[6,128,512]{2,1,0:T(8,128)(2,1)}, u32[]{:S(2)}) copy-start(bf16[6,128,512]{2,1,0:T(8,128)(2,1)} %constant.34.clone.refs_4_) | copy-start | bytes 2359300
  315.0 36.8 %copy-start.4 = (bf16[9,2304]{1,0:T(8,128)(2,1)S(1)}, bf16[9,2304]{1,0:T(8,128)(2,1)}, u32[]{:S(2)}) copy-start(bf16[9,2304]{1,0:T(8,128)(2,1)} %refs_3_.3) | copy-start | bytes 124420
  315.0 36.8 %copy-start.6 = (bf16[2,128,256]{2,1,0:T(8,128)(2,1)S(1)}, bf16[2,128,256]{2,1,0:T(8,128)(2,1)}, u32[]{:S(2)}) copy-start(bf16[2,128,256]{2,1,0:T(8,128)(2,1)} %constant.35.clone.refs_5_) | copy-start | bytes 393220
  315.0 36.8 %copy-start.7 = (bf16[16,9]{1,0:T(8,128)(2,1)S(1)}, bf16[16,9]{1,0:T(8,128)(2,1)}, u32[]{:S(2)}) copy-start(bf16[16,9]{1,0:T(8,128)(2,1)} %refs_1_.3) | copy-start | bytes 868
  315.0 45.0 %copy-start.9 = (bf16[16,8,32]{2,1,0:T(8,128)(2,1)S(1)}, bf16[16,8,32]{2,1,0:T(8,128)(2,1)}, u32[]{:S(2)}) copy-start(bf16[16,8,32]{2,1,0:T(8,128)(2,1)} %get-tuple-element.147) | copy-start | bytes 24580
  315.0 45.6 %copy-start.10 = (f32[16,4,32]{2,1,0:T(4,128)S(1)}, f32[16,4,32]{2,1,0:T(4,128)}, u32[]{:S(2)}) copy-start(f32[16,4,32]{2,1,0:T(4,128)} %get-tuple-element.168) | copy-start | bytes 24580
  351.8 1.0 copy-start.2
  352.8 1.0 copy-start.3
  353.8 0.9 copy-start.5
  354.8 0.7 copy-start.8

commit v7 on v6

--- a/solution.py
+++ b/solution.py
@@ -117,24 +117,6 @@
     )
 
 
-def ring_local(tokens):
-    return [
-        pltpu.VMEM((4, tokens, D), F32),
-        pltpu.VMEM((4, tokens, D), BF16),
-        pltpu.VMEM((3, tokens, D), BF16),
-    ]
-
-
-def ring_remote(tokens):
-    half = (tokens // 2 + 15) // 16 * 16
-    return [
-        pltpu.VMEM((4, tokens, D), BF16),
-        pltpu.VMEM((2, tokens, D), BF16),
-        pltpu.VMEM((half, D), BF16),
-        pltpu.VMEM((tokens - half, D), BF16),
-    ] + dma_sems(24)
-
-
 SLAB = 80
 PART = D // 16
 CUT = {ATT_COLS: 384, FFN_COLS: 640}
@@ -295,143 +277,6 @@
     return tuple(jax.ShapeDtypeStruct((D, w), BF16) for w in widths)
 
 
-class Ring:
-    def __init__(self, tokens, local, remote):
-        self.tokens = tokens
-        self.half = (tokens // 2 + 15) // 16 * 16
-        self.kept, self.sib_out, self.out = local
-        self.sib_in, self.got, self.far_low, self.far_high = remote[:4]
-        self.sems = tuple(remote[4:6])
-        c, y = lax.axis_index("tx"), lax.axis_index("ty")
-        self.sib, self.up, self.down, _ = ring_peers()
-        self.own = [c * 4 + lax.rem(y + d, 4) for d in range(4)]
-        self.other = [(1 - c) * 4 + lax.rem(y + d, 4) for d in range(4)]
-        self.sent = []
-
-    def peers(self):
-        return [self.sib, self.up, self.down]
-
-    def send(self, src, dst, k, peer):
-        copy = send(src, dst, self.sems, k, peer)
-        self.sent.append(copy)
-        return copy
-
-    def rows(self, index, start=0, stop=None):
-        stop = self.tokens if stop is None else stop
-        at = pl.multiple_of(index * self.tokens + start, 16)
-        return pl.ds(at, stop - start)
-
-    def gather(self, x_ref, all_ref, prepare, visit, between=None):
-        half, tokens = self.half, self.tokens
-        me, above, across, below = self.own
-        first, last = slice(0, half), slice(half, tokens)
-
-        def pass_on(index, k, peer, start=0, stop=None):
-            part = all_ref.at[self.rows(index, start, stop)]
-            return self.send(part, part, k, peer)
-
-        def own_part(rows, k, peer):
-            part = all_ref.at[self.rows(me, rows.start, rows.stop)]
-            return self.send(x_ref.at[rows], part, k, peer)
-
-        a1 = own_part(first, 0, self.up)
-        b1 = own_part(last, 1, self.down)
-        a2 = own_part(last, 2, self.up)
-        b2 = own_part(first, 3, self.down)
-        s0 = self.send(x_ref, all_ref.at[self.rows(me)], 4, self.sib)
-        all_ref[self.rows(me), :] = x_ref[...]
-        prepare()
-        visit(True, 0)
-        s0.wait_recv()
-        visit(False, 0)
-        a1.wait_recv()
-        f1 = pass_on(below, 5, self.up, 0, half)
-        b1.wait_recv()
-        f2 = pass_on(above, 6, self.down, half, tokens)
-        a2.wait_recv()
-        s1 = pass_on(below, 7, self.sib)
-        b2.wait_recv()
-        s2 = pass_on(above, 8, self.sib)
-        if between:
-            between()
-        visit(True, 3)
-        visit(True, 1)
-        s1.wait_recv()
-        visit(False, 3)
-        s2.wait_recv()
-        visit(False, 1)
-        f1.wait_recv()
-        f2.wait_recv()
-        s3 = pass_on(across, 9, self.sib)
-        visit(True, 2)
-        s3.wait_recv()
-        visit(False, 2)
-
-    def put(self, own, d, value):
-        if own:
-            self.kept[d] = value
-        else:
-            self.sib_out[d] = value.astype(BF16)
-            self.swaps[d] = self.send(self.sib_out.at[d], self.sib_in.at[d], 10 + d, self.sib)
-
-    def start_sums(self):
-        self.swaps = {}
-
-    def chip_sum(self, d):
-        self.swaps[d].wait_recv()
-        return self.kept[d] + self.sib_in[d].astype(F32)
-
-    def near(self):
-        half = self.half
-        first, last = slice(0, half), slice(half, self.tokens)
-        total = self.chip_sum(1)
-        self.kept[1] = total
-        self.out[0, last] = total[half:].astype(BF16)
-        self.n1 = self.send(self.out.at[0, last], self.got.at[0, last], 14, self.up)
-        total = self.chip_sum(3)
-        self.kept[3] = total
-        self.out[1, first] = total[:half].astype(BF16)
-        self.n2 = self.send(self.out.at[1, first], self.got.at[1, first], 15, self.down)
-
-    def far(self):
-        half = self.half
-        self.out[2] = self.chip_sum(2).astype(BF16)
-        self.low, self.high = [], []
-        for k, (start, stop) in enumerate(((0, 32), (32, half))):
-            part = self.out.at[2, start:stop]
-            self.low.append(self.send(part, self.far_low.at[start:stop], 16 + k, self.up))
-        for k, (start, stop) in enumerate(((half, half + 32), (half + 32, self.tokens))):
-            part = self.out.at[2, start:stop]
-            landing = self.far_high.at[start - half : stop - half]
-            self.high.append(self.send(part, landing, 18 + k, self.down))
-
-    def relay(self):
-        half, self.last = self.half, []
-        for k in range(2):
-            rows = slice(0, 32) if k == 0 else slice(32, half)
-            self.low[k].wait_recv()
-            value = self.kept[1, rows] + self.far_low[rows].astype(F32)
-            self.out[0, rows] = value.astype(BF16)
-            part = self.out.at[0, rows]
-            self.last.append(self.send(part, self.got.at[0, rows], 20 + k, self.up))
-            rows = slice(half, half + 32) if k == 0 else slice(half + 32, self.tokens)
-            self.high[k].wait_recv()
-            landed = self.far_high[rows.start - half : rows.stop - half]
-            self.out[1, rows] = (self.kept[3, rows] + landed.astype(F32)).astype(BF16)
-            part = self.out.at[1, rows]
-            self.last.append(self.send(part, self.got.at[1, rows], 22 + k, self.down))
-
-    def total(self):
-        value = self.chip_sum(0)
-        for copy in [self.n1, self.n2] + self.last:
-            copy.wait_recv()
-        return value + self.got[0].astype(F32) + self.got[1].astype(F32)
-
-    def leave(self):
-        for copy in self.sent:
-            copy.wait_send()
-
-
 def dot_nn(left, right):
     return lax.dot_general(left, right, (((1,), (0,)), ((), ())), preferred_element_type=F32)
 
@@ -473,14 +318,10 @@
     __getattr__ = dict.__getitem__
 
 
-def make_specs(entry):
-    return list(entry) if isinstance(entry, list) else [entry]
-
-
 def launch(body, cid, near, far, outs, kept, scratch, vmem=60 << 20):
     twins = {name: (value.shape, value.dtype) for name, value in far.items()}
     twins.update(kept)
-    groups = {name: make_specs(entry) for name, entry in scratch.items()}
+    groups, tree = jax.tree.flatten(scratch, is_leaf=lambda entry: not isinstance(entry, (dict, list)))
 
     def kernel(*refs):
         refs = iter(refs)
@@ -500,9 +341,8 @@
             r.moves[id(ref)] = (hbm[name], k)
         if twins:
             r.move_sems = next(refs)
-        for name, specs in groups.items():
-            found = [next(refs) for _ in specs]
-            setattr(r, name, found if isinstance(scratch[name], list) else found[0])
+        for name, entry in jax.tree.unflatten(tree, list(refs)).items():
+            setattr(r, name, entry)
         body(r)
 
     shapes = [jax.ShapeDtypeStruct(*spec) for spec in (*outs.values(), *kept.values())]
@@ -513,7 +353,7 @@
         out_specs=(VMEM,) * len(outs) + (FAR,) * len(kept),
         scratch_shapes=[pltpu.VMEM(*spec) for spec in twins.values()]
         + ([pltpu.SemaphoreType.DMA((len(twins),))] if twins else [])
-        + [spec for specs in groups.values() for spec in specs],
+        + groups,
         compiler_params=pltpu.CompilerParams(
             collective_id=cid, has_side_effects=cid is not None, vmem_limit_bytes=vmem
         ),
@@ -605,6 +445,230 @@
     pixels_ref[...] = value.astype(pixels_ref.dtype)
 
 
+FIRST = 64
+PIECE_ROWS = 32
+
+
+def half_sizes(tokens):
+    return FIRST, tokens - FIRST
+
+
+def half_local(size):
+    return [
+        pltpu.VMEM((4, size, D), F32),
+        pltpu.VMEM((4, size, D), BF16),
+        pltpu.VMEM((3, size, D), BF16),
+    ]
+
+
+def half_remote(size):
+    return [
+        pltpu.VMEM((4, size, D), BF16),
+        pltpu.VMEM((2, size, D), BF16),
+        pltpu.VMEM((PIECE_ROWS, D), BF16),
+        pltpu.VMEM((size - PIECE_ROWS, D), BF16),
+    ] + dma_sems(20)
+
+
+class Half:
+    def __init__(self, which, tokens, x_ref, all_ref, local, remote):
+        sizes = half_sizes(tokens)
+        self.size = sizes[which]
+        self.own = slice(which * FIRST, which * FIRST + self.size)
+        self.base = which * 8 * FIRST
+        self.x, self.all = x_ref, all_ref
+        self.kept, self.sib_out, self.out = local
+        self.sib_in, self.got, self.far_low, self.far_high = remote[:4]
+        self.sems = tuple(remote[4:6])
+        self.sib, self.up, self.down, _ = ring_peers()
+        self.low, self.high = slice(0, PIECE_ROWS), slice(PIECE_ROWS, self.size)
+        self.sent, self.swaps = [], {}
+
+    def peers(self):
+        return [self.sib, self.up, self.down]
+
+    def send(self, src, dst, k, peer):
+        copy = send(src, dst, self.sems, k, peer)
+        self.sent.append(copy)
+        return copy
+
+    def pair(self, d):
+        start = self.base + 2 * d * self.size
+        return slice(start, start + 2 * self.size)
+
+    def slot(self, d, other, rows=None):
+        start = self.base + (2 * d + other) * self.size
+        rows = slice(0, self.size) if rows is None else rows
+        return self.all.at[start + rows.start : start + rows.stop]
+
+    def source(self, rows):
+        return self.x.at[self.own.start + rows.start : self.own.start + rows.stop]
+
+    def issue(self):
+        low, high = self.low, self.high
+        self.a1 = self.send(self.source(low), self.slot(3, 0, low), 0, self.up)
+        self.b1 = self.send(self.source(high), self.slot(1, 0, high), 1, self.down)
+        whole = slice(0, self.size)
+        self.arrive = {0: self.send(self.source(whole), self.slot(0, 1), 4, self.sib)}
+        start = self.base
+        self.all[start : start + self.size, :] = self.x[self.own, :]
+
+    def issue_rest(self):
+        low, high = self.low, self.high
+        self.a2 = self.send(self.source(high), self.slot(3, 0, high), 2, self.up)
+        self.b2 = self.send(self.source(low), self.slot(1, 0, low), 3, self.down)
+
+    def forward(self):
+        low, high = self.low, self.high
+        self.a1.wait_recv()
+        self.f1 = self.send(self.slot(3, 0, low), self.slot(2, 0, low), 5, self.up)
+        self.b1.wait_recv()
+        self.f2 = self.send(self.slot(1, 0, high), self.slot(2, 0, high), 6, self.down)
+
+    def near_arrive(self):
+        self.a2.wait_recv()
+        self.arrive[3] = self.send(self.slot(3, 0), self.slot(3, 1), 7, self.sib)
+        self.b2.wait_recv()
+        self.arrive[1] = self.send(self.slot(1, 0), self.slot(1, 1), 8, self.sib)
+
+    def far_arrive(self):
+        self.f1.wait_recv()
+        self.f2.wait_recv()
+        self.arrive[2] = self.send(self.slot(2, 0), self.slot(2, 1), 9, self.sib)
+
+    def ready(self, d):
+        self.arrive[d].wait_recv()
+
+    def put(self, d, value):
+        self.kept[d] = value[: self.size]
+        self.sib_out[d] = value[self.size :].astype(BF16)
+        self.swaps[d] = self.send(self.sib_out.at[d], self.sib_in.at[d], 10 + d, self.sib)
+
+    def chip_sum(self, d):
+        self.swaps[d].wait_recv()
+        return self.kept[d] + self.sib_in[d].astype(F32)
+
+    def near(self):
+        low, high = self.low, self.high
+        total = self.chip_sum(1)
+        self.kept[1] = total
+        self.out[0, high] = total[high].astype(BF16)
+        self.n1 = self.send(self.out.at[0, high], self.got.at[0, high], 14, self.up)
+        total = self.chip_sum(3)
+        self.kept[3] = total
+        self.out[1, low] = total[low].astype(BF16)
+        self.n2 = self.send(self.out.at[1, low], self.got.at[1, low], 15, self.down)
+
+    def far(self):
+        self.out[2] = self.chip_sum(2).astype(BF16)
+        self.low_sent = self.send(self.out.at[2, self.low], self.far_low, 16, self.up)
+        self.high_sent = self.send(self.out.at[2, self.high], self.far_high, 17, self.down)
+
+    def relay(self):
+        low, high = self.low, self.high
+        self.low_sent.wait_recv()
+        self.out[0, low] = (self.kept[1, low] + self.far_low[...].astype(F32)).astype(BF16)
+        self.r1 = self.send(self.out.at[0, low], self.got.at[0, low], 18, self.up)
+        self.high_sent.wait_recv()
+        self.out[1, high] = (self.kept[3, high] + self.far_high[...].astype(F32)).astype(BF16)
+        self.r2 = self.send(self.out.at[1, high], self.got.at[1, high], 19, self.down)
+
+    def total(self):
+        value = self.chip_sum(0)
+        for copy in (self.n1, self.n2, self.r1, self.r2):
+            copy.wait_recv()
+        value = value + self.got[0].astype(F32) + self.got[1].astype(F32)
+        for copy in self.sent:
+            copy.wait_send()
+        return value
+
+
+def gather_both(a, b, prepare, visit, between):
+    prepare()
+    a.ready(0)
+    visit(a, 0)
+    a.forward()
+    b.issue_rest()
+    b.ready(0)
+    visit(b, 0)
+    a.near_arrive()
+    b.forward()
+    between()
+    a.ready(3)
+    visit(a, 3)
+    a.ready(1)
+    visit(a, 1)
+    a.far_arrive()
+    b.near_arrive()
+    b.ready(3)
+    visit(b, 3)
+    a.ready(2)
+    visit(a, 2)
+    b.ready(1)
+    visit(b, 1)
+    b.far_arrive()
+    b.ready(2)
+    visit(b, 2)
+
+
+def gather_and_sum(a, b, prepare, visit, between):
+    prepare()
+    a.ready(0)
+    visit(a, 0)
+    a.forward()
+    b.issue_rest()
+    b.ready(0)
+    visit(b, 0)
+    a.near_arrive()
+    b.forward()
+    between()
+    a.ready(3)
+    visit(a, 3)
+    a.ready(1)
+    visit(a, 1)
+    a.far_arrive()
+    b.near_arrive()
+    a.near()
+    b.ready(3)
+    visit(b, 3)
+    a.ready(2)
+    visit(a, 2)
+    b.ready(1)
+    visit(b, 1)
+    a.far()
+    b.far_arrive()
+    b.near()
+    b.ready(2)
+    visit(b, 2)
+    a.relay()
+    b.far()
+
+
+def sum_both(a, b, make):
+    make(a, 2)
+    make(b, 2)
+    a.far()
+    make(a, 1)
+    b.far()
+    make(a, 3)
+    make(a, 0)
+    a.near()
+    make(b, 1)
+    a.relay()
+    make(b, 3)
+    make(b, 0)
+    b.near()
+    b.relay()
+
+
+def nothing():
+    pass
+
+
+def halves(r, tokens, x_ref, all_ref, remote):
+    return [Half(k, tokens, x_ref, all_ref, r.local[k], remote[k]) for k in range(2)]
+
+
 UNPATCH, EMBED, BLOCKS, EMBED_BIAS = 0, 32, 48, 64
 WHOLE = 16384
 
@@ -659,14 +723,17 @@
     lanes = lax.broadcasted_iota(jnp.int32, (128, 128), 1)
     before = dot_nn(flags.astype(BF16), jnp.where(lines <= lanes, 1.0, 0.0).astype(BF16))
     r.place[...] = jnp.where(flags > 0, before - 1.0, -1.0)[0:1].astype(jnp.int32)
-    tile = r.ids[...] // 512 * 4 + lax.rem(r.ids[...], 32) // 8
+    row, col = r.ids[...] // 512, lax.rem(r.ids[...], 32) // 8
+    chip = lax.rem(col - lax.axis_index("ty") + 4, 4)
+    other = jnp.where(row == lax.axis_index("tx"), 0, 1)
+    tile = chip * 2 + other
     slot = lax.broadcasted_iota(jnp.int32, r.mask.shape, 1)
-    capacity = r.mask.shape[1] // 8
     used = slot < 0
     for k in range(8):
-        load_k = jnp.sum(jnp.where(tile == k, 1.0, 0.0), axis=1, keepdims=True).astype(jnp.int32)
-        at = slot - k * capacity
-        used = used | ((at >= 0) & (at < capacity) & (at < load_k))
+        count = jnp.sum(jnp.where(tile == k, 1.0, 0.0), axis=1, keepdims=True).astype(jnp.int32)
+        for which, size in enumerate(half_sizes(r.mask.shape[1] // 8)):
+            at = slot - which * 8 * FIRST - k * size
+            used = used | ((at >= 0) & (at < size) & (at + which * FIRST < count))
     r.mask[...] = jnp.where(used, 0.0, -1e30)
 
 
@@ -677,7 +744,10 @@
     mods = RowsOut(r.m_mine.at[:, :, 0:64], r.m_mine.at[:, :, 64:128], r.mods)
     peers = [peer for peer, _ in group] + fetch.peers()
     greet(peers)
+    load(r, r.attn_w, r.merge_w, r.expand_w, r.reduce_w, r.unpicks)
+    load(r, r.mod_w, r.final_w, r.picks, r.table)
     r.pack[...] = jnp.zeros_like(r.pack)
+    settle(r, r.attn_w, r.merge_w, r.expand_w, r.reduce_w)
     attn = [[r.attn_w[:, j, b, :] for j in range(3)] for b in range(2)]
     merge = [r.merge_w[:, b, :] for b in range(2)]
     expand = [r.expand_w[:, b, :] for b in range(2)]
@@ -691,6 +761,7 @@
         for b in range(2):
             parts += [expand[b][:, wide], reduce[b][:, wide]]
         r.pack[p * 16 : p * 16 + 9, :] = jnp.concatenate(parts, axis=1)
+    settle(r, r.unpicks)
     packed = jnp.zeros((8 * 64, PIECE), F32)
     for k in range(PIECES):
         packed = packed + dot_tn(r.unpicks[k], r.pack[:, k * PIECE : (k + 1) * PIECE])
@@ -731,6 +802,7 @@
     right = jnp.where(on_lane, 1.0, 0.0).astype(BF16)
     r.placed_bias[...] = dot_nt(left, right)
     r.m_mine[:, :, 126:128] = jnp.zeros((4, 4, 2, 128), F32)
+    settle(r, r.mod_w, r.final_w)
     for b in range(3):
         weight = r.mod_w[:, b, :] if b < 2 else r.final_w[...]
         part = dot_nn(cond16, weight)
@@ -745,10 +817,12 @@
     second = [send(small, small, sems, 10 + k, p) for k, (p, _) in enumerate(fetch.along_x)]
     for copy in weights:
         copy.wait_recv()
+    settle(r, r.picks, r.table)
     received = r.w_got[...].reshape(8 * 64, PIECE)
     for k in range(PIECES):
         r.rows[:, k * PIECE : (k + 1) * PIECE] = dot_nn(r.picks[k], received).astype(BF16)
     fetch.start()
+    save(r, r.rows)
     for copy in second:
         copy.wait_recv()
     small = r.small.at[:, :, me]
@@ -790,6 +864,7 @@
         r.feat32[at, :] = dot_nn(r.pick_small[...], got)[:PART]
 
     r.feat[...] = r.feat32[...].astype(BF16)
+    save(r, r.feat)
     for k in range(9):
         cols = slice(k * 128, (k + 1) * 128)
         r.turned[:, cols] = jnp.transpose(r.feat32[cols, :])
@@ -822,9 +897,11 @@
     r.head_vec[0:1] = mod_line(12)
     r.head_vec[1:2] = mod_line(13)
     fetch.end(r.wqkv, r.wm)
+    save(r, r.wqkv, r.wm)
     for copy in weights + first + second + third + fourth + m_first + m_second:
         copy.wait_send()
     mods.leave()
+    settle(r)
 
 
 def picking():
@@ -842,20 +919,16 @@
     return picks
 
 
-def open_up(arguments):
-    near = dict(
-        **arguments,
+def open_up(near, far):
+    near = dict(near, pick_small=jnp.asarray(picking_small(), BF16))
+    far = dict(
+        far,
         unpicks=jnp.asarray(unpicking(PIECES, 64), BF16),
         picks=jnp.asarray(picking(), BF16),
-        pick_small=jnp.asarray(picking_small(), BF16),
         table=jnp.asarray(bias_table()),
     )
     vec = ((8, D), F32)
     outs = dict(
-        rows=((SLAB, ALL_COLS), BF16),
-        wqkv=((D, 3 * HW), BF16),
-        wm=((D, HW), BF16),
-        feat=((D, 128), BF16),
         vec_one_0=vec,
         vec_two_0=vec,
         vec_one_1=vec,
@@ -867,6 +940,12 @@
         bias_one_1=((1, 3 * HW), F32),
         bias_two_0=((1, FW), F32),
         bias_two_1=((1, FW), F32),
+    )
+    kept = dict(
+        rows=((SLAB, ALL_COLS), BF16),
+        wqkv=((D, 3 * HW), BF16),
+        wm=((D, HW), BF16),
+        feat=((D, 128), BF16),
     )
     scratch = dict(
         pack=pltpu.VMEM((128, ALL_COLS), BF16),
@@ -888,7 +967,8 @@
         fetch=rows_in_scratch(ATT_COLS),
         mods=sum_scratch([(64, 128), (64, 128)], F32),
     )
-    return launch(open_body, 1, near, {}, outs, {}, scratch)[0]
+    near_outs, far_outs = launch(open_body, 1, near, far, outs, kept, scratch)
+    return Results(near_outs, **far_outs)
 
 
 EARLY = ATT_COLS + 2 * FFN_COLS
@@ -938,6 +1018,8 @@
     greet(peers)
     me, x, z = own_group(), lax.axis_index("dp_0"), lax.axis_index("dp_1")
     sems = (r.ss, r.rs)
+    load(r, r.left, r.right, r.picks, r.attn_rows, r.ffn_rows_0, r.ffn_rows_1)
+    load(r, r.unpatch_rows, r.embed_rows, r.table)
     r.m_mine[...] = jnp.zeros_like(r.m_mine)
     vecs = (r.vecs_one_0, r.vecs_two_0, r.vecs_one_1, r.vecs_two_1, r.head_vecs)
     for k, ref in enumerate(vecs):
@@ -948,9 +1030,11 @@
                     i : i + 1, j * 128 : (j + 1) * 128
                 ]
     met(peers)
+    settle(r, r.left, r.right)
     rows.start()
     m_first = [send(r.m_mine.at[at], r.m_got.at[me], sems, k, p) for k, (p, at) in enumerate(group)]
     r.m_got[me] = r.m_mine[me]
+    settle(r)
     attn_at, ffn_at = own_targets()
     biases = (r.bias_one_0[...], r.bias_one_1[...])
     narrow = bias_lines(r.table, ATT_BIAS, attn_at, biases, 2)
@@ -1034,8 +1118,8 @@
         copy.wait_send()
 
 
-def finish(near):
-    near = dict(near, picks=jnp.asarray(picking(), BF16))
+def finish(near, far):
+    far = dict(far, picks=jnp.asarray(picking(), BF16), table=jnp.asarray(bias_table()))
     outs = dict(
         early_out=((8, 64, PIECE), BF16),
         late_out=((8, LATE_ROWS, PIECE), BF16),
@@ -1060,7 +1144,7 @@
         rows_sums=rows_out_scratch(ATT_COLS),
         small_sums=sum_scratch([(40, 128), (40, 128)], F32),
     )
-    return launch(finish_body, 2, near, {}, outs, {}, scratch)[0]
+    return launch(finish_body, 2, near, far, outs, {}, scratch)[0]
 
 
 def unpicking(pieces, height):
@@ -1073,8 +1157,8 @@
 
 
 def close_body(r):
-    load(r, r.early_in, r.late_in, r.m_in)
-    settle(r, r.early_in, r.late_in)
+    load(r, r.early_in, r.early_picks, r.late_in, r.late_picks, r.m_in, r.mod_w, r.final_w)
+    settle(r, r.early_in, r.late_in, r.early_picks, r.late_picks)
     received = r.early_in[...].reshape(8 * 64, PIECE)
     for k in range(EARLY_PIECES):
         r.early[:, k * PIECE : (k + 1) * PIECE] = dot_nn(r.early_picks[k], received)
@@ -1093,7 +1177,8 @@
     for b, start in enumerate((ATT_COLS, ATT_COLS + FFN_COLS)):
         r.expand[:, b, :] = whole(r.early, start, FW)
         r.reduce[:, b, :] = whole(r.early, start + FW, FW)
-    settle(r, r.m_in)
+    save(r, r.attn, r.merge, r.expand, r.reduce)
+    settle(r, r.m_in, r.mod_w, r.final_w)
     for k in range(128):
         value = r.m_in[k // 16, :, :, k % 16, :]
         r.grads[:, k * 128 : (k + 1) * 128] = value.reshape(16, 128)
@@ -1111,6 +1196,9 @@
         else:
             r.final_grad[...] = product
         terms = terms + dot_nt(grads, weights)
+    save(r, r.mod_grad, r.final_grad)
+    r.predicted[...] = r.predicted_in[...]
+    r.latent[...] = r.latent_in[...]
     r.condition_grad[...] = terms * (gate * (1.0 + condition * (1.0 - gate)))
     on_line, on_lane = mod_places(whole_index())
     found = exact(r.sums[...], jnp.where(on_lane, 1.0, 0.0).astype(F32), (1, 0))
@@ -1133,21 +1221,26 @@
             r.expand_b[b : b + 1, 9 * j : 9 * j + 9] = turned[at + 2 + j : at + 3 + j, 0:9]
         r.merge_b[b : b + 1] = turned[at + 6 : at + 7, 0:9]
         r.reduce_b[b : b + 1] = turned[at + 7 : at + 8, 0:9]
+    settle(r)
 
 
 def close(near, far):
-    near = dict(
-        **near,
+    far = dict(
+        far,
         early_picks=jnp.asarray(unpicking(EARLY_PIECES, 64), BF16),
         late_picks=jnp.asarray(unpicking(LATE_PIECES, LATE_ROWS), BF16),
     )
-    outs = dict(
+    kept = dict(
         attn=((9, 3, 2, D), F32),
         merge=((9, 2, D), F32),
         expand=((9, 2, FF), F32),
         reduce=((9, 2, FF), F32),
         mod_grad=((9, 2, 6 * D), F32),
         final_grad=((9, 2 * D), F32),
+    )
+    outs = dict(
+        predicted=((16, 8, 32), BF16),
+        latent=((16, 4, 32), F32),
         condition_grad=((16, 9), F32),
         mod_b=((2, 54), F32),
         final_b=((1, 18), F32),
@@ -1167,36 +1260,49 @@
         sums=pltpu.VMEM((128, 128), F32),
         square=pltpu.VMEM((128, 128), F32),
     )
-    return launch(close_body, None, near, far, outs, {}, scratch, vmem=40 << 20)[0]
+    near_outs, far_outs = launch(close_body, None, near, far, outs, kept, scratch)
+    return Results(near_outs, **far_outs)
 
 
 def forward_body(r, tokens, start, last):
-    ring = Ring(tokens, r.ring_local, r.ring_one)
+    a, b = halves(r, tokens, r.x16, r.in_all, r.remote_one)
     fetch = RowsIn(*slab_views(r.rows, start, FFN_COLS), r.fetch_one)
-    peers = ring.peers() + fetch.peers()
+    peers = a.peers() + fetch.peers()
     greet(peers)
     if last:
+        load(r, r.first, r.wqkv, r.rows, r.wm)
+        settle(r, r.first)
         r.x[...] = exact(choice(r.place, tokens), r.first[...], (1, 0))
     else:
+        load(r, r.feat, r.placed, r.wqkv, r.rows, r.wm)
+        settle(r, r.feat, r.placed)
         r.token_cols[...] = jnp.zeros_like(r.token_cols)
         to_tokens(r.pixels, r.square, r.token_cols, EMBED)
         r.patches[...] = r.token_cols[...].astype(BF16)
         r.x[...] = dot_nt(r.patches[...], r.feat[...]) + r.vec_one[4:5] + r.placed[...]
     r.x16[...] = modulated(r.x[...], r.vec_one)
     met(peers)
+    a.issue()
+    a.issue_rest()
+    b.issue()
     save(r, r.x)
-    ring.start_sums()
-
-    def visit(own, d):
-        rows = ring.rows((ring.own if own else ring.other)[d])
+    if not last:
+        save(r, r.patches)
+
+    def prepare():
+        settle(r, r.wqkv, r.rows)
+        fetch.start()
+
+    def visit(half, d):
+        rows = half.pair(d)
         joined = (dot_nn(r.in_all[rows, :], r.wqkv[...]) + r.bias_one[...]).astype(BF16)
         for h in range(2):
             r.q[h, rows, :] = joined[:, head_cols(h)]
             r.k[h, rows, :] = joined[:, head_cols(h, HW)]
             r.v[h, rows, :] = joined[:, head_cols(h, 2 * HW)]
 
-    def attend(own, d):
-        rows = ring.rows((ring.own if own else ring.other)[d])
+    def attend(half, d):
+        rows = half.pair(d)
         parts = []
         for h in range(2):
             scores = dot_nt(r.q[h, rows, :], r.k[h]) * SCALE
@@ -1210,64 +1316,64 @@
             parts.append(dot_nn(probs, r.v[h]).astype(BF16))
         attended = jnp.concatenate(parts, axis=1)
         r.att[rows, :] = attended
-        ring.put(own, d, dot_nt(attended, r.wm[...]))
-
-    ring.gather(r.x16, r.in_all, fetch.start, visit, fetch.middle)
-    attend(False, 2)
-    attend(True, 2)
-    ring.far()
+        half.put(d, dot_nt(attended, r.wm[...]))
+
+    gather_both(a, b, prepare, visit, fetch.middle)
+    settle(r, r.wm)
     save(r, r.in_all, r.q, r.k, r.v)
-    for d in (1, 3):
-        attend(False, d)
-        attend(True, d)
-    ring.near()
-    ring.relay()
-    attend(False, 0)
-    attend(True, 0)
+    sum_both(a, b, attend)
     save(r, r.lse, r.att)
     fetch.end(r.we, r.wr)
     save(r, r.we, r.wr)
-    branch = ring.total() + r.vec_one[3:4]
-    r.branch[...] = branch
-    middle = r.x[...] + r.vec_one[2:3] * branch
-    r.middle[...] = middle
+    follow = halves(r, tokens, r.x16, r.second, r.remote_two)
+
+    def finish_half(half, after):
+        branch = half.total() + r.vec_one[3:4]
+        middle = r.x[half.own, :] + r.vec_one[2:3] * branch
+        r.x16[half.own, :] = modulated(middle, r.vec_two)
+        after.issue()
+        r.branch[half.own, :] = branch
+        r.middle[half.own, :] = middle
+
+    finish_half(a, follow[0])
+    follow[0].issue_rest()
+    finish_half(b, follow[1])
     save(r, r.branch, r.middle)
-    ring.leave()
-
-    ring = Ring(tokens, r.ring_local, r.ring_two)
+    a, b = follow
     fetch = None
     if not last:
         fetch = RowsIn(*slab_views(r.rows, ATT_COLS, ATT_COLS), r.fetch_two)
-    r.x16[...] = modulated(middle, r.vec_two)
-    ring.start_sums()
-
-    def prepare():
-        if fetch:
-            fetch.start()
-
-    def expand(own, d):
-        rows = ring.rows((ring.own if own else ring.other)[d])
+
+    def expand(half, d):
+        rows = half.pair(d)
         pre = dot_nn(r.second[rows, :], r.we[...]) + r.bias_two[...]
         value, slope = gelu_both(pre)
         hidden = value.astype(BF16)
         r.hid[rows, :] = hidden
         r.slope[rows, :] = slope.astype(BF16)
-        ring.put(own, d, dot_nt(hidden, r.wr[...]))
-        if not own and d == 1:
-            ring.near()
-
-    ring.gather(r.x16, r.second, prepare, expand, fetch.middle if fetch else None)
-    ring.far()
+        half.put(d, dot_nt(hidden, r.wr[...]))
+
+    if fetch:
+        gather_and_sum(a, b, fetch.start, expand, fetch.middle)
+    else:
+        gather_and_sum(a, b, nothing, expand, nothing)
     save(r, r.second, r.hid, r.slope)
-    ring.relay()
+    b.relay()
     if fetch:
         fetch.end(r.next_wqkv, r.next_wm)
-    mlp = ring.total() + r.vec_two[3:4]
-    r.mlp[...] = mlp
-    save(r, r.mlp)
-    r.out[...] = r.middle[...] + r.vec_two[2:3] * mlp
-    ring.leave()
+        save(r, r.next_wqkv, r.next_wm)
+    for half in (a, b):
+        mlp = half.total() + r.vec_two[3:4]
+        r.mlp[half.own, :] = mlp
+        r.out[half.own, :] = r.middle[half.own, :] + r.vec_two[2:3] * mlp
+    save(r, r.mlp, r.out)
     settle(r)
+
+
+def ring_scratch(tokens):
+    sizes = half_sizes(tokens)
+    remote = [half_remote(size) for size in sizes]
+    return dict(local=[half_local(size) for size in sizes], remote_one=remote, remote_two=remote)
 
 
 def kept_shapes(tokens):
@@ -1293,23 +1399,24 @@
     )
 
 
-def block_forward(near, tokens, start, last, cid):
-    outs = dict(out=((tokens, D), F32))
+def block_forward(near, far, tokens, start, last, cid):
+    kept = dict(kept_shapes(tokens), out=((tokens, D), F32))
     scratch = dict(
         x16=pltpu.VMEM((tokens, D), BF16),
-        ring_local=ring_local(tokens),
-        ring_one=ring_remote(tokens),
-        ring_two=ring_remote(tokens),
+        **ring_scratch(tokens),
         fetch_one=rows_in_scratch(FFN_COLS),
     )
     if not last:
-        outs.update(next_wqkv=((D, 3 * HW), BF16))
-        outs.update(next_wm=((D, HW), BF16))
-        outs.update(patches=((128, 128), BF16))
-        scratch.update(square=pltpu.VMEM((128, 128), F32), token_cols=pltpu.VMEM((128, 128), F32))
-        scratch.update(fetch_two=rows_in_scratch(ATT_COLS))
+        kept.update(
+            next_wqkv=((D, 3 * HW), BF16), next_wm=((D, HW), BF16), patches=((128, 128), BF16)
+        )
+        scratch.update(
+            square=pltpu.VMEM((128, 128), F32),
+            token_cols=pltpu.VMEM((128, 128), F32),
+            fetch_two=rows_in_scratch(ATT_COLS),
+        )
     body = functools.partial(forward_body, tokens=tokens, start=start, last=last)
-    return launch(body, cid, near, {}, outs, kept_shapes(tokens), scratch)
+    return launch(body, cid, near, far, {}, kept, scratch)[1]
 
 
 def head(r):
@@ -1335,18 +1442,19 @@
 
 
 def backward_body(r, tokens, last):
-    ring = Ring(tokens, r.ring_local, r.ring_one)
+    a, b = halves(r, tokens, r.g16, r.g_one, r.remote_one)
     sums = None if last else RowsOut(r.pending_left, r.pending_right, r.sums_one)
-    peers = ring.peers() + line_only(line_peers())
+    peers = a.peers() + line_only(line_peers())
     greet(peers)
     if last:
-        load(r, r.first, r.two, r.slope, r.wr, r.we)
+        load(r, r.first, r.two, r.feat, r.slope, r.wr, r.we)
     else:
         load(r, r.grad_two, r.grad_ended, r.slope, r.wr, r.we, r.pending_left, r.pending_right)
+        load(r, r.feat, r.patches)
     load(r, r.hid, r.second, r.mlp, r.middle)
     load(r, r.q, r.k, r.v, r.lse, r.wm, r.wqkv, r.att, r.x, r.branch)
     if last:
-        settle(r, r.first, r.two)
+        settle(r, r.first, r.two, r.feat)
         head(r)
     else:
         settle(r, r.grad_two, r.grad_ended)
@@ -1354,7 +1462,9 @@
         r.g[...] = spread_back(picks, r.grad_two[...], r.grad_ended[...])
     r.g16[...] = (r.g[...] * r.vec_two[2:3]).astype(BF16)
     met(peers)
-    ring.start_sums()
+    a.issue()
+    a.issue_rest()
+    b.issue()
     r.bias_two[...] = jnp.zeros_like(r.bias_two)
 
     def prepare():
@@ -1363,43 +1473,52 @@
             sums.start()
         settle(r, r.slope, r.wr, r.we)
 
-    def visit(own, d):
-        rows = ring.rows((ring.own if own else ring.other)[d])
+    def visit(half, d):
+        rows = half.pair(d)
         pre_grad = (
             dot_nn(r.g_one[rows, :], r.wr[...]) * r.slope[rows, :].astype(F32)
         ).astype(BF16)
         r.pre_all[rows, :] = pre_grad
         r.bias_two[...] += sum_rows(pre_grad.astype(F32))
-        ring.put(own, d, dot_nt(pre_grad, r.we[...]))
-        if not own and d == 1:
-            ring.near()
-
-    ring.gather(r.g16, r.g_one, prepare, visit)
-    ring.far()
+        half.put(d, dot_nt(pre_grad, r.we[...]))
+
+    if last:
+        save(r, r.grad_ended, r.unpatch_rows)
+    gather_and_sum(a, b, prepare, visit, nothing)
     settle(r, r.hid, r.second, r.mlp, r.middle)
-    weight_grads(r.g_one, r.hid, r.whole_two, FW)
-    ring.relay()
-    if sums:
-        sums.middle()
     r.vecs_two[2:3] = sum_rows(r.g[...] * r.mlp[...])
     r.vecs_two[3:4] = sum_rows(r.g16[...].astype(F32))
     r.vecs_two[4:8] = jnp.zeros((4, D), F32)
+    if sums:
+        sums.middle()
+    b.relay()
+    weight_grads(r.g_one, r.hid, r.whole_two, FW)
+    follow = halves(r, tokens, r.g16, r.g_two, r.remote_two)
+
+    def finish_half(half, after):
+        second_grad = half.total()
+        normed, inv_std = layer_stats(r.middle[half.own, :])
+        grad = r.g[half.own, :] + layer_back(
+            second_grad * (1.0 + r.vec_two[1:2]), normed, inv_std
+        )
+        r.g[half.own, :] = grad
+        r.g16[half.own, :] = (grad * r.vec_one[2:3]).astype(BF16)
+        after.issue()
+        return sum_rows(second_grad), sum_rows(second_grad * normed)
+
+    shift_a, scale_a = finish_half(a, follow[0])
+    follow[0].issue_rest()
+    shift_b, scale_b = finish_half(b, follow[1])
+    r.vecs_two[0:1] = shift_a + shift_b
+    r.vecs_two[1:2] = scale_a + scale_b
     weight_grads(r.second, r.pre_all, r.whole_one, FW)
     load_into(r, r.in_all, r.second)
     write_slabs((r.whole_one, FW), (r.whole_two, FW), r.ffn_left, r.ffn_right)
     if sums:
         sums.end_rows(r.attn_rows)
-    second_grad = ring.total()
-    normed, inv_std = layer_stats(r.middle[...])
-    r.vecs_two[0:1] = sum_rows(second_grad)
-    r.vecs_two[1:2] = sum_rows(second_grad * normed)
-    r.g[...] += layer_back(second_grad * (1.0 + r.vec_two[1:2]), normed, inv_std)
-    ring.leave()
-
-    ring = Ring(tokens, r.ring_local, r.ring_two)
+        save(r, r.attn_rows)
+    a, b = follow
     sums = RowsOut(r.ffn_left, r.ffn_right, r.sums_two)
-    r.g16[...] = (r.g[...] * r.vec_one[2:3]).astype(BF16)
-    ring.start_sums()
 
     def prepare_attention():
         sums.start()
@@ -1407,8 +1526,8 @@
         r.dv[...] = jnp.zeros_like(r.dv)
         settle(r, r.q, r.k, r.v, r.lse, r.wm)
 
-    def attend(own, d):
-        rows = ring.rows((ring.own if own else ring.other)[d])
+    def attend(half, d):
+        rows = half.pair(d)
         grad = dot_nn(r.g_two[rows, :], r.wm[...]).astype(BF16)
         queries = []
         for h in range(2):
@@ -1426,56 +1545,55 @@
             r.dv[h] += dot_tn(probs.astype(BF16), part)
         r.joined[rows, 0:HW] = jnp.concatenate(queries, axis=1)
 
-    def back(own, d):
-        rows = ring.rows((ring.own if own else ring.other)[d])
-        ring.put(own, d, dot_nt(r.joined[rows, :], r.wqkv[...]))
-
-    ring.gather(r.g16, r.g_two, prepare_attention, attend)
+    def back(half, d):
+        half.put(d, dot_nt(r.joined[half.pair(d), :], r.wqkv[...]))
+
+    gather_both(a, b, prepare_attention, attend, nothing)
     settle(r, r.wqkv)
     later = [(r.dk[h] * SCALE).astype(BF16) for h in range(2)]
     later += [r.dv[h].astype(BF16) for h in range(2)]
     r.joined[:, HW : 3 * HW] = jnp.concatenate(later, axis=1)
-    back(False, 2)
-    back(True, 2)
-    ring.far()
-    for d in (1, 3):
-        back(False, d)
-        back(True, d)
-    ring.near()
-    back(False, 0)
-    back(True, 0)
+    sum_both(a, b, back)
     settle(r)
-    weight_grads(r.g_two, r.att, r.whole_two, HW)
-    ring.relay()
     sums.middle()
     r.bias_one[...] = sum_rows(r.joined[...].astype(F32))
     r.vecs_one[2:3] = sum_rows(r.g[...] * r.branch[...])
     r.vecs_one[3:4] = sum_rows(r.g16[...].astype(F32))
     r.vecs_one[4:8] = jnp.zeros((4, D), F32)
+    weight_grads(r.g_two, r.att, r.whole_two, HW)
     weight_grads(r.second, r.joined, r.whole_one, 3 * HW)
     write_slabs((r.whole_one, 3 * HW), (r.whole_two, HW), r.attn_left, r.attn_right)
+    save(r, r.attn_left, r.attn_right)
     sums.end_rows(r.ffn_rows)
-    input_grad = ring.total()
-    normed, inv_std = layer_stats(r.x[...])
-    r.vecs_one[0:1] = sum_rows(input_grad)
-    r.vecs_one[1:2] = sum_rows(input_grad * normed)
-    grad = r.g[...] + layer_back(input_grad * (1.0 + r.vec_one[1:2]), normed, inv_std)
+    save(r, r.ffn_rows)
+    shift, scale = 0.0, 0.0
+    for half in (a, b):
+        input_grad = half.total()
+        normed, inv_std = layer_stats(r.x[half.own, :])
+        shift = shift + sum_rows(input_grad)
+        scale = scale + sum_rows(input_grad * normed)
+        scaled = input_grad * (1.0 + r.vec_one[1:2])
+        r.g[half.own, :] = r.g[half.own, :] + layer_back(scaled, normed, inv_std)
+    r.vecs_one[0:1] = shift
+    r.vecs_one[1:2] = scale
     if last:
-        r.out[...] = grad
+        r.out[...] = r.g[...]
+        save(r, r.out)
     else:
-        grad16 = grad.astype(BF16)
+        grad16 = r.g[...].astype(BF16)
         r.embed_rows[0:16] = dot_tn(r.patches[...], grad16)[EMBED : EMBED + 16]
         r.embed_rows[16:17] = sum_rows(grad16.astype(F32))
         r.embed_rows[17:24] = jnp.zeros((7, D), F32)
+        save(r, r.embed_rows)
         r.token_cols[...] = dot_nn(grad16, r.feat[...])
         to_pixels(r.token_cols, r.square, r.latent, EMBED)
-    ring.leave()
+    settle(r)
 
 
 def weight_grads(left_ref, right_ref, whole_ref, width):
-    @pl.loop(0, D // 128)
+    @pl.loop(0, D // 384)
     def _(k):
-        at = pl.ds(pl.multiple_of(k * 128, 128), 128)
+        at = pl.ds(pl.multiple_of(k * 384, 128), 384)
         whole_ref[at, :width] = dot_tn(left_ref[:, at], right_ref[...])
 
 
@@ -1509,17 +1627,12 @@
 def block_backward(near, far, tokens, last, cid):
     vecs = ((8, D), F32)
     attn_left, attn_right = slab_specs(ATT_COLS)
-    outs = dict(
-        vecs_one=vecs,
-        vecs_two=vecs,
-        bias_one=((1, 3 * HW), F32),
-        bias_two=((1, FW), F32),
-        attn_left=attn_left,
-        attn_right=attn_right,
-        ffn_rows=((SLAB, FFN_COLS), BF16),
-    )
     wide, tile = (8 * tokens, D), (tokens, D)
+    outs = dict(vecs_one=vecs, vecs_two=vecs)
+    outs.update(bias_one=((1, 3 * HW), F32), bias_two=((1, FW), F32))
+    kept = dict(attn_left=attn_left, attn_right=attn_right, ffn_rows=((SLAB, FFN_COLS), BF16))
     scratch = dict(
+        g=pltpu.VMEM(tile, F32),
         g16=pltpu.VMEM(tile, BF16),
         square=pltpu.VMEM((128, 128), F32),
         token_cols=pltpu.VMEM((128, 128), F32),
@@ -1533,28 +1646,22 @@
         whole_two=pltpu.VMEM((D, FW), F32),
         ffn_left=pltpu.VMEM(*slab_specs(FFN_COLS)[0]),
         ffn_right=pltpu.VMEM(*slab_specs(FFN_COLS)[1]),
-        ring_local=ring_local(tokens),
-        ring_one=ring_remote(tokens),
-        ring_two=ring_remote(tokens),
+        **ring_scratch(tokens),
         sums_two=rows_out_scratch(FFN_COLS),
     )
     if last:
-        outs.update(out=(tile, F32))
-        outs.update(predicted=((16, 8, 32), BF16))
-        outs.update(unpatch_rows=((32, D), F32))
-        outs.update(unpatch_bias=((8, 128), F32))
-        outs.update(head_vecs=((2, D), F32))
+        outs.update(
+            predicted=((16, 8, 32), BF16), unpatch_bias=((8, 128), F32), head_vecs=((2, D), F32)
+        )
+        kept.update(out=(tile, F32), unpatch_rows=((32, D), F32), grad_ended=((128, D), F32))
         scratch.update(cotangent=pltpu.VMEM((128, 32), BF16))
-        outs.update(grad_ended=((128, D), F32))
-        scratch.update(g=pltpu.VMEM(tile, F32))
     else:
-        outs.update(attn_rows=((SLAB, ATT_COLS), BF16))
-        outs.update(embed_rows=((24, D), F32))
         outs.update(latent=((16, 4, 32), F32))
-        scratch.update(g=pltpu.VMEM(tile, F32))
+        kept.update(attn_rows=((SLAB, ATT_COLS), BF16), embed_rows=((24, D), F32))
         scratch.update(sums_one=rows_out_scratch(ATT_COLS))
     body = functools.partial(backward_body, tokens=tokens, last=last)
-    return launch(body, cid, near, far, outs, {}, scratch, vmem=62 << 20)[0]
+    near_outs, far_outs = launch(body, cid, near, far, outs, kept, scratch, vmem=62 << 20)
+    return Results(near_outs, **far_outs)
 
 
 def shards(
@@ -1591,12 +1698,6 @@
         dict(
             condition=condition,
             ids=routed_ids,
-            mod_w=mod_w,
-            final_w=final_modulation,
-            attn_w=attention_weight.transpose(1, 2, 0, 3),
-            merge_w=merge_weight.swapaxes(0, 1),
-            expand_w=expand_weight.swapaxes(0, 1),
-            reduce_w=reduce_weight.swapaxes(0, 1),
             embed_w=embed_weight,
             embed_b=embed_bias[None],
             unpatch_w=unpatch_weight,
@@ -1606,69 +1707,71 @@
             reduce_b=reduce_bias,
             mod_b=modulation_bias,
             final_b=final_offsets[None],
-        )
+        ),
+        dict(
+            mod_w=mod_w,
+            final_w=final_modulation,
+            attn_w=attention_weight.transpose(1, 2, 0, 3),
+            merge_w=merge_weight.swapaxes(0, 1),
+            expand_w=expand_weight.swapaxes(0, 1),
+            reduce_w=reduce_weight.swapaxes(0, 1),
+        ),
     )
     vecs_one = dict(vec_one=got.vec_one_0, vec_two=got.vec_two_0)
     vecs_two = dict(vec_one=got.vec_one_1, vec_two=got.vec_two_1, mask=got.mask)
-    outs_one, kept_one = block_forward(
+    kept_one = block_forward(
         dict(
             vecs_one,
             bias_one=got.bias_one_0,
             bias_two=got.bias_two_0,
-            rows=got.rows,
-            wqkv=got.wqkv,
-            wm=got.wm,
             pixels=latent.transpose(0, 2, 3, 1)[0],
-            feat=got.feat,
-            placed=placed,
         ),
+        dict(feat=got.feat, placed=placed, rows=got.rows, wqkv=got.wqkv, wm=got.wm),
         tile_tokens,
         2 * ATT_COLS,
         False,
         10,
     )
-    outs_two, kept_two = block_forward(
-        dict(
-            vecs_two,
-            bias_one=got.bias_one_1,
-            bias_two=got.bias_two_1,
-            rows=got.rows,
-            wqkv=outs_one.next_wqkv,
-            wm=outs_one.next_wm,
-            first=outs_one.out,
-            place=got.place,
-        ),
+    weights_two = dict(wqkv=kept_one.next_wqkv, wm=kept_one.next_wm)
+    kept_two = block_forward(
+        dict(vecs_two, bias_one=got.bias_one_1, bias_two=got.bias_two_1, place=got.place),
+        dict(weights_two, rows=got.rows, first=kept_one.out),
         capacity,
         2 * ATT_COLS + FFN_COLS,
         True,
         11,
     )
+
+    def saved(kept, tokens):
+        return {name: kept[name] for name in kept_shapes(tokens)}
+
     back_two = block_backward(
         dict(
             vecs_two,
             place=got.place,
             head_vec=got.head_vec,
-            feat=got.feat,
             unpatch_b=unpatch_bias[None],
             cotangent_pixels=pred_cotangent.transpose(0, 2, 3, 1)[0],
         ),
         dict(
-            kept_two,
-            first=outs_one.out,
-            two=outs_two.out,
-            wqkv=outs_one.next_wqkv,
-            wm=outs_one.next_wm,
+            saved(kept_two, capacity),
+            **weights_two,
+            feat=got.feat,
+            first=kept_one.out,
+            two=kept_two.out,
         ),
         capacity,
         True,
         12,
     )
     back_one = block_backward(
-        dict(vecs_one, place=got.place, patches=outs_one.patches, feat=got.feat),
+        dict(vecs_one, place=got.place),
         dict(
-            kept_one,
+            saved(kept_one, tile_tokens),
             wqkv=got.wqkv,
             wm=got.wm,
+            feat=got.feat,
+            patches=kept_one.patches,
             pending_left=back_two.attn_left,
             pending_right=back_two.attn_right,
             grad_two=back_two.out,
@@ -1680,33 +1783,45 @@
     )
     ended = finish(
         dict(
+            vecs_one_0=back_one.vecs_one,
+            vecs_two_0=back_one.vecs_two,
+            vecs_one_1=back_two.vecs_one,
+            vecs_two_1=back_two.vecs_two,
+            head_vecs=back_two.head_vecs,
+            bias_one_0=back_one.bias_one,
+            bias_two_0=back_one.bias_two,
+            bias_one_1=back_two.bias_one,
+            bias_two_1=back_two.bias_two,
+            unpatch_bias=back_two.unpatch_bias,
+        ),
+        dict(
             left=back_one.attn_left,
             right=back_one.attn_right,
             attn_rows=back_one.attn_rows,
             ffn_rows_0=back_one.ffn_rows,
             ffn_rows_1=back_two.ffn_rows,
-            vecs_one_0=back_one.vecs_one,
-            vecs_two_0=back_one.vecs_two,
-            vecs_one_1=back_two.vecs_one,
-            vecs_two_1=back_two.vecs_two,
-            head_vecs=back_two.head_vecs,
             unpatch_rows=back_two.unpatch_rows,
             embed_rows=back_one.embed_rows,
-            bias_one_0=back_one.bias_one,
-            bias_two_0=back_one.bias_two,
-            bias_one_1=back_two.bias_one,
-            bias_two_1=back_two.bias_two,
-            table=jnp.asarray(bias_table()),
-            unpatch_bias=back_two.unpatch_bias,
-        )
+        ),
     )
     last = close(
-        dict(s_in=ended.s_out, condition=condition, mod_w=mod_w, final_w=final_modulation),
-        dict(early_in=ended.early_out, late_in=ended.late_out, m_in=ended.m_out),
+        dict(
+            s_in=ended.s_out,
+            condition=condition,
+            predicted_in=back_two.predicted,
+            latent_in=back_one.latent,
+        ),
+        dict(
+            early_in=ended.early_out,
+            late_in=ended.late_out,
+            m_in=ended.m_out,
+            mod_w=mod_w,
+            final_w=final_modulation,
+        ),
     )
     return (
-        back_two.predicted.transpose(2, 0, 1)[None],
-        back_one.latent.transpose(2, 0, 1)[None],
+        last.predicted.transpose(2, 0, 1)[None],
+        last.latent.transpose(2, 0, 1)[None],
         last.condition_grad,
         last.embed_w,
         last.embed_b[0],

time: 366 us -> 353 us (0.964)
  Pallas kernels: 354 us -> 345 us
  local copies, waits for them, and re-layouts: 5.04 us -> 0.05 us
    pallas_call x7, Pallas kernels: 354 us -> 345 us  [launch(): pl.pallas_call(kernel, out_shape=tuple(shapes), in_specs=[VMEM] * len(nea...]
    unnamed x24 -> x0, local copies, waits for them, and re-layouts: 4.99 us -> none
where the time goes in v7:
time: 353 us; the launch traced here: 348 us
  Pallas kernels  345 us (98%)
    pallas_call x7, Pallas kernels, launch(): pl.pallas_call(kernel, out_shape=tuple(shapes), in_specs=[VMEM] * len(nea...  345 us

profile of v7, /device:TPU:1, one launch (start us, length us, event | category | flops | bytes accessed | tf_op | source)
XLA Modules:
  0.0 348.0 jit_solution(2876694017176305121)
XLA Ops:
  0.7 0.1 multiply_sine_fusion.1
  0.8 0.1 pad_maximum_fusion.1
  0.9 0.2 multiply_sine_fusion
  1.1 0.1 pad_maximum_fusion
  1.2 1.0 maximum_bitcast_fusion.refs_6_
  2.2 41.0 %shard_map.411 = (f32[8,1152]{1,0:T(8,128)}, f32[8,1152]{1,0:T(8,128)}, f32[8,1152]{1,0:T(8,128)}, f32[8,1152]{1,0:T(8,128)}, f32[2,1152]{1,0:T(2,128)}, /*index...) custom-call(bf16[16,9]{1,0:T(8,128)(2,1)} %refs_1_.3, ...), custom_call_target="tpu_custom_call" | custom-call | tf_op jit(solution)/shard_map/pallas_call | solution.py:349
  43.2 59.7 %shard_map.412 = (f32[128,1152]{1,0:T(8,128)}, bf16[1024,1152]{1,0:T(8,128)(2,1)}, bf16[2,1024,72]{2,1,0:T(8,128)(2,1)}, bf16[2,1024,72]{2,1,0:T(8,128)(2,1)}, b...) custom-call(f32[8,1152]{1,0:T(8,128)} %get-tuple-element.115.refs_0_, ...), custom_call_target="tpu_custom_call" | custom-call | tf_op jit(solution)/shard_map/pallas_call | solution.py:349
  102.9 59.4 %shard_map.413 = (f32[112,1152]{1,0:T(8,128)}, bf16[896,1152]{1,0:T(8,128)(2,1)}, bf16[2,896,72]{2,1,0:T(8,128)(2,1)}, bf16[2,896,72]{2,1,0:T(8,128)(2,1)}, bf16...) custom-call(f32[8,1152]{1,0:T(8,128)} %get-tuple-element.140.refs_0_, ...), custom_call_target="tpu_custom_call" | custom-call | tf_op jit(solution)/shard_map/pallas_call | solution.py:349
  162.3 72.6 %shard_map.414 = (f32[8,1152]{1,0:T(8,128)}, f32[8,1152]{1,0:T(8,128)}, f32[1,432]{1,0:T(1,128)}, f32[1,576]{1,0:T(1,128)}, bf16[16,8,32]{2,1,0:T(8,128)(2,1)}, ...) custom-call(f32[8,1152]{1,0:T(8,128)} %get-tuple-element.140.refs_0_, ...), custom_call_target="tpu_custom_call" | custom-call | tf_op jit(solution)/shard_map/pallas_call | solution.py:349
  234.9 70.8 %shard_map.415 = (f32[8,1152]{1,0:T(8,128)}, f32[8,1152]{1,0:T(8,128)}, f32[1,432]{1,0:T(1,128)}, f32[1,576]{1,0:T(1,128)}, f32[16,4,32]{2,1,0:T(4,128)}, /*inde...) custom-call(f32[8,1152]{1,0:T(8,128)} %get-tuple-element.115.refs_0_, ...), custom_call_target="tpu_custom_call" | custom-call | tf_op jit(solution)/shard_map/pallas_call | solution.py:349
  305.7 35.6 %shard_map.416 = (bf16[8,64,512]{2,1,0:T(8,128)(2,1)}, bf16[8,32,512]{2,1,0:T(8,128)(2,1)}, bf16[8,4,4,16,128]{4,3,2,1,0:T(8,128)(2,1)}, f32[16,128]{1,0:T(8,128)}) custom-call(f32[8,1152]{1,0:T(8,128)} %get-tuple-element.169.refs_0_, f32[8,1152]{1,0:T(8,128)} %get-tuple-element.170.refs_1_, f32[8,1152]{1,0:T(8,128)} %get-tuple-element.171.refs_2_, ...), custom_call_target="tpu_custom_call" | custom-call | tf_op jit(solution)/shard_map/pallas_call | solution.py:349
  341.3 6.3 %shard_map.417 = (bf16[16,8,32]{2,1,0:T(8,128)(2,1)}, f32[16,4,32]{2,1,0:T(4,128)}, f32[16,9]{1,0:T(8,128)}, f32[2,54]{1,0:T(2,128)}, f32[1,18]{1,0:T(1,128)}, /...) custom-call(f32[16,128]{1,0:T(8,128)} %get-tuple-element.186.refs_0_, ...), custom_call_target="tpu_custom_call" | custom-call | tf_op jit(solution)/shard_map/pallas_call | solution.py:349
  (5 shorter events, 0.1 us)

commit v8 on v7

--- a/solution.py
+++ b/solution.py
@@ -904,11 +904,11 @@
     settle(r)
 
 
-def picking():
-    picks = np.zeros((PIECES, SLAB, 8 * 64), np.float32)
-    for k in range(PIECES):
+def picking(pieces, height):
+    picks = np.zeros((pieces, SLAB, 8 * height), np.float32)
+    for k in range(pieces):
         for row in range(72):
-            picks[k, row, row // 9 * 64 + 9 * k + row % 9] = 1.0
+            picks[k, row, row // 9 * height + 9 * k + row % 9] = 1.0
     return picks
 
 
@@ -924,7 +924,7 @@
     far = dict(
         far,
         unpicks=jnp.asarray(unpicking(PIECES, 64), BF16),
-        picks=jnp.asarray(picking(), BF16),
+        picks=jnp.asarray(picking(PIECES, 64), BF16),
         table=jnp.asarray(bias_table()),
     )
     vec = ((8, D), F32)
@@ -973,18 +973,21 @@
 
 EARLY = ATT_COLS + 2 * FFN_COLS
 EARLY_PIECES = -(-EARLY // PIECE)
-LATE_PIECES = -(-ATT_COLS // PIECE)
-LATE_ROWS = 32
-
-
-def packed_rows(picks_ref, parts, pieces):
+LATE_PIECE = 128
+LATE_PIECES = ATT_COLS // LATE_PIECE
+LATE_ROWS = 48
+
+
+def packed_rows(picks_ref, parts, piece):
+    pieces, _, height = picks_ref.shape
     columns = jnp.concatenate(parts, axis=1)
-    spare = pieces * PIECE - columns.shape[1]
-    columns = jnp.concatenate([columns, jnp.zeros((SLAB, spare), BF16)], axis=1)
-    total = jnp.zeros((8 * 64, PIECE), F32)
+    spare = pieces * piece - columns.shape[1]
+    if spare:
+        columns = jnp.concatenate([columns, jnp.zeros((SLAB, spare), BF16)], axis=1)
+    total = jnp.zeros((height, piece), F32)
     for k in range(pieces):
-        total = total + dot_tn(picks_ref[k], columns[:, k * PIECE : (k + 1) * PIECE])
-    return total.astype(BF16).reshape(8, 64, PIECE)
+        total = total + dot_tn(picks_ref[k], columns[:, k * piece : (k + 1) * piece])
+    return total.astype(BF16).reshape(8, height // 8, piece)
 
 
 def bias_lines(table_ref, cols, shift, biases, count):
@@ -1018,7 +1021,7 @@
     greet(peers)
     me, x, z = own_group(), lax.axis_index("dp_0"), lax.axis_index("dp_1")
     sems = (r.ss, r.rs)
-    load(r, r.left, r.right, r.picks, r.attn_rows, r.ffn_rows_0, r.ffn_rows_1)
+    load(r, r.left, r.right, r.picks, r.late_picks, r.attn_rows, r.ffn_rows_0, r.ffn_rows_1)
     load(r, r.unpatch_rows, r.embed_rows, r.table)
     r.m_mine[...] = jnp.zeros_like(r.m_mine)
     vecs = (r.vecs_one_0, r.vecs_two_0, r.vecs_one_1, r.vecs_two_1, r.head_vecs)
@@ -1061,7 +1064,7 @@
         r.small[k // 4, k % 4, 72:80] = r.unpatch_bias[...]
     small.start()
     r.early[...] = packed_rows(
-        r.picks, [r.attn_rows[...], r.ffn_rows_0[...], r.ffn_rows_1[...]], EARLY_PIECES
+        r.picks, [r.attn_rows[...], r.ffn_rows_0[...], r.ffn_rows_1[...]], PIECE
     )
     sent = [
         send(r.early.at[at], r.early_out.at[me], sems, 7 + k, p) for k, (p, at) in enumerate(group)
@@ -1075,6 +1078,7 @@
     r.m_out[me, x, z] = total.astype(BF16)
     part = r.m_out.at[me, x, z]
     m_second = [send(part, part, sems, 14 + k, p) for k, (p, _) in enumerate(rows.along_z)]
+    rows.middle()
     small.middle()
     for copy in m_second:
         copy.wait_recv()
@@ -1092,7 +1096,12 @@
         copy.wait_recv()
     part = r.m_out.at[me]
     m_fourth = [send(part, part, sems, 27 + k, p) for k, p in enumerate((up, down, far, sib))]
-    rows.middle()
+    rows.end_rows(r.late_rows)
+    r.late[...] = packed_rows(r.late_picks, [r.late_rows[...]], LATE_PIECE)
+    later = [
+        send(r.late.at[at], r.late_out.at[me], sems, 34 + k, p) for k, (p, at) in enumerate(group)
+    ]
+    r.late_out[me] = r.late[me]
     c, y = lax.axis_index("tx"), lax.axis_index("ty")
     m_fifth = []
     for k, d in enumerate((3, 1, 2)):
@@ -1105,12 +1114,6 @@
     for k in range(1, 8):
         total = total + r.s_two[k]
     r.s_out[...] = total
-    rows.end_rows(r.late_rows)
-    r.late[...] = packed_rows(r.picks, [r.late_rows[...]], LATE_PIECES)[:, :LATE_ROWS]
-    later = [
-        send(r.late.at[at], r.late_out.at[me], sems, 34 + k, p) for k, (p, at) in enumerate(group)
-    ]
-    r.late_out[me] = r.late[me]
     for copy in sent + m_fourth[3:] + m_fifth + later:
         copy.wait_recv()
     small.leave()
@@ -1119,16 +1122,21 @@
 
 
 def finish(near, far):
-    far = dict(far, picks=jnp.asarray(picking(), BF16), table=jnp.asarray(bias_table()))
+    far = dict(
+        far,
+        picks=jnp.asarray(picking(EARLY_PIECES, 64), BF16),
+        late_picks=jnp.asarray(picking(LATE_PIECES, LATE_ROWS), BF16),
+        table=jnp.asarray(bias_table()),
+    )
     outs = dict(
         early_out=((8, 64, PIECE), BF16),
-        late_out=((8, LATE_ROWS, PIECE), BF16),
+        late_out=((8, LATE_ROWS, LATE_PIECE), BF16),
         m_out=((8, 4, 4, 16, 128), BF16),
         s_out=((16, 128), F32),
     )
     scratch = dict(
         early=pltpu.VMEM((8, 64, PIECE), BF16),
-        late=pltpu.VMEM((8, LATE_ROWS, PIECE), BF16),
+        late=pltpu.VMEM((8, LATE_ROWS, LATE_PIECE), BF16),
         m_mine=pltpu.VMEM((8, 16, 128), F32),
         m_got=pltpu.VMEM((8, 16, 128), F32),
         lines=pltpu.VMEM((128, 128), F32),
@@ -1162,9 +1170,9 @@
     received = r.early_in[...].reshape(8 * 64, PIECE)
     for k in range(EARLY_PIECES):
         r.early[:, k * PIECE : (k + 1) * PIECE] = dot_nn(r.early_picks[k], received)
-    received = r.late_in[...].reshape(8 * LATE_ROWS, PIECE)
+    received = r.late_in[...].reshape(8 * LATE_ROWS, LATE_PIECE)
     for k in range(LATE_PIECES):
-        r.late[:, k * PIECE : (k + 1) * PIECE] = dot_nn(r.late_picks[k], received)
+        r.late[:, k * LATE_PIECE : (k + 1) * LATE_PIECE] = dot_nn(r.late_picks[k], received)
 
     def whole(source, start, width):
         parts = [source[g * 16 : g * 16 + 16, start : start + width] for g in range(8)]
@@ -1255,7 +1263,7 @@
     )
     scratch = dict(
         early=pltpu.VMEM((128, EARLY_PIECES * PIECE), F32),
-        late=pltpu.VMEM((128, LATE_PIECES * PIECE), F32),
+        late=pltpu.VMEM((128, ATT_COLS), F32),
         grads=pltpu.VMEM((16, WHOLE), BF16),
         sums=pltpu.VMEM((128, 128), F32),
         square=pltpu.VMEM((128, 128), F32),
@@ -1489,10 +1497,8 @@
     r.vecs_two[2:3] = sum_rows(r.g[...] * r.mlp[...])
     r.vecs_two[3:4] = sum_rows(r.g16[...].astype(F32))
     r.vecs_two[4:8] = jnp.zeros((4, D), F32)
-    if sums:
-        sums.middle()
+    weight_grads(r.g_one, r.hid, r.whole_two, FW)
     b.relay()
-    weight_grads(r.g_one, r.hid, r.whole_two, FW)
     follow = halves(r, tokens, r.g16, r.g_two, r.remote_two)
 
     def finish_half(half, after):
@@ -1508,10 +1514,12 @@
 
     shift_a, scale_a = finish_half(a, follow[0])
     follow[0].issue_rest()
+    if sums:
+        sums.middle()
+    weight_grads(r.second, r.pre_all, r.whole_one, FW)
     shift_b, scale_b = finish_half(b, follow[1])
     r.vecs_two[0:1] = shift_a + shift_b
     r.vecs_two[1:2] = scale_a + scale_b
-    weight_grads(r.second, r.pre_all, r.whole_one, FW)
     load_into(r, r.in_all, r.second)
     write_slabs((r.whole_one, FW), (r.whole_two, FW), r.ffn_left, r.ffn_right)
     if sums:

time: 353 us -> 346 us (0.980)
  Pallas kernels: 345 us -> 338 us
    pallas_call x7, Pallas kernels: 345 us -> 338 us  [launch(): pl.pallas_call(kernel, out_shape=tuple(shapes), in_specs=[VMEM] * len(nea...]
where the time goes in v8:
time: 346 us; the launch traced here: 341 us
  Pallas kernels  338 us (98%)
    pallas_call x7, Pallas kernels, launch(): pl.pallas_call(kernel, out_shape=tuple(shapes), in_specs=[VMEM] * len(nea...  338 us

profile of v8, /device:TPU:1, one launch (start us, length us, event | category | flops | bytes accessed | tf_op | source)
XLA Modules:
  0.0 340.8 jit_solution(10383581934687699130)
XLA Ops:
  0.7 0.1 multiply_sine_fusion.1
  0.8 0.1 pad_maximum_fusion.1
  0.9 0.2 multiply_sine_fusion
  1.1 0.1 pad_maximum_fusion
  1.2 1.0 maximum_bitcast_fusion.refs_6_
  2.2 41.0 %shard_map.420 = (f32[8,1152]{1,0:T(8,128)}, f32[8,1152]{1,0:T(8,128)}, f32[8,1152]{1,0:T(8,128)}, f32[8,1152]{1,0:T(8,128)}, f32[2,1152]{1,0:T(2,128)}, /*index...) custom-call(bf16[16,9]{1,0:T(8,128)(2,1)} %refs_1_.3, ...), custom_call_target="tpu_custom_call" | custom-call | tf_op jit(solution)/shard_map/pallas_call | solution.py:349
  43.2 59.7 %shard_map.421 = (f32[128,1152]{1,0:T(8,128)}, bf16[1024,1152]{1,0:T(8,128)(2,1)}, bf16[2,1024,72]{2,1,0:T(8,128)(2,1)}, bf16[2,1024,72]{2,1,0:T(8,128)(2,1)}, b...) custom-call(f32[8,1152]{1,0:T(8,128)} %get-tuple-element.115.refs_0_, ...), custom_call_target="tpu_custom_call" | custom-call | tf_op jit(solution)/shard_map/pallas_call | solution.py:349
  102.9 59.4 %shard_map.422 = (f32[112,1152]{1,0:T(8,128)}, bf16[896,1152]{1,0:T(8,128)(2,1)}, bf16[2,896,72]{2,1,0:T(8,128)(2,1)}, bf16[2,896,72]{2,1,0:T(8,128)(2,1)}, bf16...) custom-call(f32[8,1152]{1,0:T(8,128)} %get-tuple-element.140.refs_0_, ...), custom_call_target="tpu_custom_call" | custom-call | tf_op jit(solution)/shard_map/pallas_call | solution.py:349
  162.3 69.8 %shard_map.423 = (f32[8,1152]{1,0:T(8,128)}, f32[8,1152]{1,0:T(8,128)}, f32[1,432]{1,0:T(1,128)}, f32[1,576]{1,0:T(1,128)}, bf16[16,8,32]{2,1,0:T(8,128)(2,1)}, ...) custom-call(f32[8,1152]{1,0:T(8,128)} %get-tuple-element.140.refs_0_, ...), custom_call_target="tpu_custom_call" | custom-call | tf_op jit(solution)/shard_map/pallas_call | solution.py:349
  232.0 69.2 %shard_map.424 = (f32[8,1152]{1,0:T(8,128)}, f32[8,1152]{1,0:T(8,128)}, f32[1,432]{1,0:T(1,128)}, f32[1,576]{1,0:T(1,128)}, f32[16,4,32]{2,1,0:T(4,128)}, /*inde...) custom-call(f32[8,1152]{1,0:T(8,128)} %get-tuple-element.115.refs_0_, ...), custom_call_target="tpu_custom_call" | custom-call | tf_op jit(solution)/shard_map/pallas_call | solution.py:349
  301.2 32.6 %shard_map.425 = (bf16[8,64,512]{2,1,0:T(8,128)(2,1)}, bf16[8,48,128]{2,1,0:T(8,128)(2,1)}, bf16[8,4,4,16,128]{4,3,2,1,0:T(8,128)(2,1)}, f32[16,128]{1,0:T(8,128)}) custom-call(f32[8,1152]{1,0:T(8,128)} %get-tuple-element.169.refs_0_, f32[8,1152]{1,0:T(8,128)} %get-tuple-element.170.refs_1_, f32[8,1152]{1,0:T(8,128)} %get-tuple-element.171.refs_2_, ...), custom_call_target="tpu_custom_call" | custom-call | tf_op jit(solution)/shard_map/pallas_call | solution.py:349
  333.9 6.4 %shard_map.426 = (bf16[16,8,32]{2,1,0:T(8,128)(2,1)}, f32[16,4,32]{2,1,0:T(4,128)}, f32[16,9]{1,0:T(8,128)}, f32[2,54]{1,0:T(2,128)}, f32[1,18]{1,0:T(1,128)}, /...) custom-call(f32[16,128]{1,0:T(8,128)} %get-tuple-element.186.refs_0_, ...), custom_call_target="tpu_custom_call" | custom-call | tf_op jit(solution)/shard_map/pallas_call | solution.py:349
  (5 shorter events, 0.1 us)

commit v9 on v8

--- a/solution.py
+++ b/solution.py
@@ -447,6 +447,7 @@
 
 FIRST = 64
 PIECE_ROWS = 32
+PLACE_OF = {0: 0, 3: 1, 1: 2, 2: 3}
 
 
 def half_sizes(tokens):
@@ -492,12 +493,12 @@
         self.sent.append(copy)
         return copy
 
-    def pair(self, d):
-        start = self.base + 2 * d * self.size
-        return slice(start, start + 2 * self.size)
+    def pair(self, d, count=1):
+        start = self.base + 2 * PLACE_OF[d] * self.size
+        return slice(start, start + 2 * count * self.size)
 
     def slot(self, d, other, rows=None):
-        start = self.base + (2 * d + other) * self.size
+        start = self.base + (2 * PLACE_OF[d] + other) * self.size
         rows = slice(0, self.size) if rows is None else rows
         return self.all.at[start + rows.start : start + rows.stop]
 
@@ -726,7 +727,8 @@
     row, col = r.ids[...] // 512, lax.rem(r.ids[...], 32) // 8
     chip = lax.rem(col - lax.axis_index("ty") + 4, 4)
     other = jnp.where(row == lax.axis_index("tx"), 0, 1)
-    tile = chip * 2 + other
+    place = jnp.where(chip == 1, 2, jnp.where(chip == 2, 3, jnp.where(chip == 3, 1, 0)))
+    tile = place * 2 + other
     slot = lax.broadcasted_iota(jnp.int32, r.mask.shape, 1)
     used = slot < 0
     for k in range(8):
@@ -1535,7 +1537,7 @@
         settle(r, r.q, r.k, r.v, r.lse, r.wm)
 
     def attend(half, d):
-        rows = half.pair(d)
+        rows = half.pair(0 if d == 3 else 1, 2)
         grad = dot_nn(r.g_two[rows, :], r.wm[...]).astype(BF16)
         queries = []
         for h in range(2):
@@ -1556,7 +1558,26 @@
     def back(half, d):
         half.put(d, dot_nt(r.joined[half.pair(d), :], r.wqkv[...]))
 
-    gather_both(a, b, prepare_attention, attend, nothing)
+    prepare_attention()
+    a.forward()
+    b.issue_rest()
+    a.near_arrive()
+    b.forward()
+    a.ready(0)
+    a.ready(3)
+    attend(a, 3)
+    a.far_arrive()
+    b.near_arrive()
+    b.ready(0)
+    b.ready(3)
+    attend(b, 3)
+    a.ready(1)
+    a.ready(2)
+    b.far_arrive()
+    attend(a, 2)
+    b.ready(1)
+    b.ready(2)
+    attend(b, 2)
     settle(r, r.wqkv)
     later = [(r.dk[h] * SCALE).astype(BF16) for h in range(2)]
     later += [r.dv[h].astype(BF16) for h in range(2)]

time: 346 us -> 341 us (0.986)
  Pallas kernels: 338 us -> 333 us
    pallas_call x7, Pallas kernels: 338 us -> 333 us  [launch(): pl.pallas_call(kernel, out_shape=tuple(shapes), in_specs=[VMEM] * len(nea...]
where the time goes in v9:
time: 341 us; the launch traced here: 336 us
  Pallas kernels  333 us (98%)
    pallas_call x7, Pallas kernels, launch(): pl.pallas_call(kernel, out_shape=tuple(shapes), in_specs=[VMEM] * len(nea...  333 us

profile of v9, /device:TPU:1, one launch (start us, length us, event | category | flops | bytes accessed | tf_op | source)
XLA Modules:
  0.0 335.9 jit_solution(6434736776289704189)
XLA Ops:
  0.7 0.1 multiply_sine_fusion.1
  0.8 0.1 pad_maximum_fusion.1
  0.9 0.2 multiply_sine_fusion
  1.1 0.1 pad_maximum_fusion
  1.2 1.0 maximum_bitcast_fusion.refs_6_
  2.2 41.0 %shard_map.420 = (f32[8,1152]{1,0:T(8,128)}, f32[8,1152]{1,0:T(8,128)}, f32[8,1152]{1,0:T(8,128)}, f32[8,1152]{1,0:T(8,128)}, f32[2,1152]{1,0:T(2,128)}, /*index...) custom-call(bf16[16,9]{1,0:T(8,128)(2,1)} %refs_1_.3, ...), custom_call_target="tpu_custom_call" | custom-call | tf_op jit(solution)/shard_map/pallas_call | solution.py:349
  43.2 59.7 %shard_map.421 = (f32[128,1152]{1,0:T(8,128)}, bf16[1024,1152]{1,0:T(8,128)(2,1)}, bf16[2,1024,72]{2,1,0:T(8,128)(2,1)}, bf16[2,1024,72]{2,1,0:T(8,128)(2,1)}, b...) custom-call(f32[8,1152]{1,0:T(8,128)} %get-tuple-element.115.refs_0_, ...), custom_call_target="tpu_custom_call" | custom-call | tf_op jit(solution)/shard_map/pallas_call | solution.py:349
  102.9 59.4 %shard_map.422 = (f32[112,1152]{1,0:T(8,128)}, bf16[896,1152]{1,0:T(8,128)(2,1)}, bf16[2,896,72]{2,1,0:T(8,128)(2,1)}, bf16[2,896,72]{2,1,0:T(8,128)(2,1)}, bf16...) custom-call(f32[8,1152]{1,0:T(8,128)} %get-tuple-element.140.refs_0_, ...), custom_call_target="tpu_custom_call" | custom-call | tf_op jit(solution)/shard_map/pallas_call | solution.py:349
  162.3 66.4 %shard_map.423 = (f32[8,1152]{1,0:T(8,128)}, f32[8,1152]{1,0:T(8,128)}, f32[1,432]{1,0:T(1,128)}, f32[1,576]{1,0:T(1,128)}, bf16[16,8,32]{2,1,0:T(8,128)(2,1)}, ...) custom-call(f32[8,1152]{1,0:T(8,128)} %get-tuple-element.140.refs_0_, ...), custom_call_target="tpu_custom_call" | custom-call | tf_op jit(solution)/shard_map/pallas_call | solution.py:349
  228.7 67.3 %shard_map.424 = (f32[8,1152]{1,0:T(8,128)}, f32[8,1152]{1,0:T(8,128)}, f32[1,432]{1,0:T(1,128)}, f32[1,576]{1,0:T(1,128)}, f32[16,4,32]{2,1,0:T(4,128)}, /*inde...) custom-call(f32[8,1152]{1,0:T(8,128)} %get-tuple-element.115.refs_0_, ...), custom_call_target="tpu_custom_call" | custom-call | tf_op jit(solution)/shard_map/pallas_call | solution.py:349
  296.0 33.0 %shard_map.425 = (bf16[8,64,512]{2,1,0:T(8,128)(2,1)}, bf16[8,48,128]{2,1,0:T(8,128)(2,1)}, bf16[8,4,4,16,128]{4,3,2,1,0:T(8,128)(2,1)}, f32[16,128]{1,0:T(8,128)}) custom-call(f32[8,1152]{1,0:T(8,128)} %get-tuple-element.169.refs_0_, f32[8,1152]{1,0:T(8,128)} %get-tuple-element.170.refs_1_, f32[8,1152]{1,0:T(8,128)} %get-tuple-element.171.refs_2_, ...), custom_call_target="tpu_custom_call" | custom-call | tf_op jit(solution)/shard_map/pallas_call | solution.py:349
  329.0 6.4 %shard_map.426 = (bf16[16,8,32]{2,1,0:T(8,128)(2,1)}, f32[16,4,32]{2,1,0:T(4,128)}, f32[16,9]{1,0:T(8,128)}, f32[2,54]{1,0:T(2,128)}, f32[1,18]{1,0:T(1,128)}, /...) custom-call(f32[16,128]{1,0:T(8,128)} %get-tuple-element.186.refs_0_, ...), custom_call_target="tpu_custom_call" | custom-call | tf_op jit(solution)/shard_map/pallas_call | solution.py:349
  (5 shorter events, 0.1 us)

commit v10 on v9

--- a/solution.py
+++ b/solution.py
@@ -1555,8 +1555,10 @@
             r.dv[h] += dot_tn(probs.astype(BF16), part)
         r.joined[rows, 0:HW] = jnp.concatenate(queries, axis=1)
 
-    def back(half, d):
-        half.put(d, dot_nt(r.joined[half.pair(d), :], r.wqkv[...]))
+    def back(half, low, high):
+        value = dot_nt(r.joined[half.pair(low, 2), :], r.wqkv[...])
+        half.put(high, value[2 * half.size :])
+        half.put(low, value[: 2 * half.size])
 
     prepare_attention()
     a.forward()
@@ -1582,7 +1584,16 @@
     later = [(r.dk[h] * SCALE).astype(BF16) for h in range(2)]
     later += [r.dv[h].astype(BF16) for h in range(2)]
     r.joined[:, HW : 3 * HW] = jnp.concatenate(later, axis=1)
-    sum_both(a, b, back)
+    back(a, 1, 2)
+    back(b, 1, 2)
+    a.far()
+    back(a, 0, 3)
+    b.far()
+    a.near()
+    back(b, 0, 3)
+    a.relay()
+    b.near()
+    b.relay()
     settle(r)
     sums.middle()
     r.bias_one[...] = sum_rows(r.joined[...].astype(F32))

time: 341 us -> 338 us (level)
  no operation moved by 1% of the time
where the time goes in v10:
time: 338 us; the launch traced here: 333 us
  Pallas kernels  330 us (98%)
    pallas_call x7, Pallas kernels, launch(): pl.pallas_call(kernel, out_shape=tuple(shapes), in_specs=[VMEM] * len(nea...  330 us

profile of v10, /device:TPU:1, one launch (start us, length us, event | category | flops | bytes accessed | tf_op | source)
XLA Modules:
  0.0 332.7 jit_solution(6665647957503527789)
XLA Ops:
  0.7 0.1 multiply_sine_fusion.1
  0.8 0.1 pad_maximum_fusion.1
  0.9 0.2 multiply_sine_fusion
  1.1 0.1 pad_maximum_fusion
  1.2 1.0 maximum_bitcast_fusion.refs_6_
  2.2 41.0 %shard_map.420 = (f32[8,1152]{1,0:T(8,128)}, f32[8,1152]{1,0:T(8,128)}, f32[8,1152]{1,0:T(8,128)}, f32[8,1152]{1,0:T(8,128)}, f32[2,1152]{1,0:T(2,128)}, /*index...) custom-call(bf16[16,9]{1,0:T(8,128)(2,1)} %refs_1_.3, ...), custom_call_target="tpu_custom_call" | custom-call | tf_op jit(solution)/shard_map/pallas_call | solution.py:349
  43.2 59.7 %shard_map.421 = (f32[128,1152]{1,0:T(8,128)}, bf16[1024,1152]{1,0:T(8,128)(2,1)}, bf16[2,1024,72]{2,1,0:T(8,128)(2,1)}, bf16[2,1024,72]{2,1,0:T(8,128)(2,1)}, b...) custom-call(f32[8,1152]{1,0:T(8,128)} %get-tuple-element.115.refs_0_, ...), custom_call_target="tpu_custom_call" | custom-call | tf_op jit(solution)/shard_map/pallas_call | solution.py:349
  102.9 59.4 %shard_map.422 = (f32[112,1152]{1,0:T(8,128)}, bf16[896,1152]{1,0:T(8,128)(2,1)}, bf16[2,896,72]{2,1,0:T(8,128)(2,1)}, bf16[2,896,72]{2,1,0:T(8,128)(2,1)}, bf16...) custom-call(f32[8,1152]{1,0:T(8,128)} %get-tuple-element.140.refs_0_, ...), custom_call_target="tpu_custom_call" | custom-call | tf_op jit(solution)/shard_map/pallas_call | solution.py:349
  162.3 63.1 %shard_map.423 = (f32[8,1152]{1,0:T(8,128)}, f32[8,1152]{1,0:T(8,128)}, f32[1,432]{1,0:T(1,128)}, f32[1,576]{1,0:T(1,128)}, bf16[16,8,32]{2,1,0:T(8,128)(2,1)}, ...) custom-call(f32[8,1152]{1,0:T(8,128)} %get-tuple-element.140.refs_0_, ...), custom_call_target="tpu_custom_call" | custom-call | tf_op jit(solution)/shard_map/pallas_call | solution.py:349
  225.4 64.1 %shard_map.424 = (f32[8,1152]{1,0:T(8,128)}, f32[8,1152]{1,0:T(8,128)}, f32[1,432]{1,0:T(1,128)}, f32[1,576]{1,0:T(1,128)}, f32[16,4,32]{2,1,0:T(4,128)}, /*inde...) custom-call(f32[8,1152]{1,0:T(8,128)} %get-tuple-element.115.refs_0_, ...), custom_call_target="tpu_custom_call" | custom-call | tf_op jit(solution)/shard_map/pallas_call | solution.py:349
  289.5 36.3 %shard_map.425 = (bf16[8,64,512]{2,1,0:T(8,128)(2,1)}, bf16[8,48,128]{2,1,0:T(8,128)(2,1)}, bf16[8,4,4,16,128]{4,3,2,1,0:T(8,128)(2,1)}, f32[16,128]{1,0:T(8,128)}) custom-call(f32[8,1152]{1,0:T(8,128)} %get-tuple-element.169.refs_0_, f32[8,1152]{1,0:T(8,128)} %get-tuple-element.170.refs_1_, f32[8,1152]{1,0:T(8,128)} %get-tuple-element.171.refs_2_, ...), custom_call_target="tpu_custom_call" | custom-call | tf_op jit(solution)/shard_map/pallas_call | solution.py:349
  325.9 6.4 %shard_map.426 = (bf16[16,8,32]{2,1,0:T(8,128)(2,1)}, f32[16,4,32]{2,1,0:T(4,128)}, f32[16,9]{1,0:T(8,128)}, f32[2,54]{1,0:T(2,128)}, f32[1,18]{1,0:T(1,128)}, /...) custom-call(f32[16,128]{1,0:T(8,128)} %get-tuple-element.186.refs_0_, ...), custom_call_target="tpu_custom_call" | custom-call | tf_op jit(solution)/shard_map/pallas_call | solution.py:349
  (5 shorter events, 0.1 us)
